TPU v7x, 32 devices: a whole 2x2x4 slice. The times are simulated.
32 devices in a mesh: dp: 4 (over z), fsdp: 2 (over y), tensor: 4 (over x, core).
Axes of the slice: x: 2, y: 2, z: 4, core: 2. Of those that a mesh axis runs over, the one named last changes fastest.
Arguments:
- activations: bfloat16 [9216, 1024], P(('dp', 'fsdp')), may hold values from -6 to 6
- cotangent: bfloat16 [9216, 1024], P(('dp', 'fsdp', 'tensor')), may hold values from -6 to 6
- lengths: int32 [40], P(('dp', 'fsdp')), may hold values from 32 to 512, as said below
- w_qkv: bfloat16 [2, 3, 1024, 1024], P(None, None, 'fsdp', 'tensor'), may hold values from -0.1875 to 0.1875
- w_out: bfloat16 [2, 1024, 1024], P(None, 'tensor', 'fsdp'), may hold values from -1.5 to 1.5
- w_up: bfloat16 [2, 1024, 4096], P(None, 'fsdp', 'tensor'), may hold values from -0.1875 to 0.1875
- w_down: bfloat16 [2, 4096, 1024], P(None, 'tensor', 'fsdp'), may hold values from -0.09375 to 0.09375
- b_qv: bfloat16 [2, 2, 16, 64], P(None, None, 'tensor', 'fsdp'), may hold values from -3 to 3
- b_up: bfloat16 [2, 32, 128], P(None, 'tensor', 'fsdp'), may hold values from -3 to 3
- norm_gains: bfloat16 [2, 2, 1024], P(None, None, 'fsdp'), may hold values from 0.099609375 to 1.8984375
- layer_biases: bfloat16 [2, 4, 1024], P(None, None, 'fsdp'), may hold values from -2 to 2
Outputs:
- layer_out: bfloat16 [9216, 1024], P(('dp', 'fsdp', 'tensor'))
- input_grad: float32 [9216, 1024], P(('dp', 'fsdp', 'tensor'))
- grad_qkv: float32 [2, 3, 1024, 1024], P(None, None, 'fsdp', 'tensor')
- grad_out: float32 [2, 1024, 1024], P(None, 'tensor', 'fsdp')
- grad_up: float32 [2, 1024, 4096], P(None, 'fsdp', 'tensor')
- grad_down: float32 [2, 4096, 1024], P(None, 'tensor', 'fsdp')
- grad_bias_qv: float32 [2, 2, 16, 64], P(None, None, 'tensor', 'fsdp')
- grad_bias_up: float32 [2, 32, 128], P(None, 'tensor', 'fsdp')
- grad_gains: float32 [2, 2, 1024], P(None, None, 'fsdp')
- grad_biases: float32 [2, 4, 1024], P(None, None, 'fsdp')
Inputs may be any that keep to these rules, and one draw needn't show every extreme that they name: `lengths`: page i of a data group's 5 pages has 512 slots if i < 1, 256 if i < 2, else 128; it holds between a quarter of its slots and all of them; in each of the three buckets some page is full, and some page of the third bucket holds exactly a quarter of its slots.
All inputs are finite; a program needn't handle non-finite values.
Results may differ from a plain program's by a relative error of at most 0.028.
Values may be sent and summed in bfloat16 or wider, within the bound.
No kernel may reach another device: no remote copies, remote signals or barrier semaphores. Data moves between devices by JAX's collectives and lax.ppermute only.
A program may use at most 192 MiB of HBM per device.

v0:
```python
import jax
import jax.numpy as jnp
from jax import lax
from jax.sharding import PartitionSpec as P

HEAD = 64
LAYERS = 2
LEN_A = 512
LEN_B = 256
LEN_C = 128
PAGES_A = 1
PAGES_B = 1
PAGES_C = 3


def layer_norm(hidden, gain_row, bias_row):
    center = hidden - jnp.mean(hidden, -1, keepdims=True)
    inverse = lax.rsqrt(jnp.mean(center * center, -1, keepdims=True) + 1e-05)
    normed = center * inverse
    return (normed * gain_row + bias_row, normed, inverse)


def norm_back(grad_result, normed, inverse, gain_row):
    grad_norm = grad_result * gain_row
    mean_one = jnp.mean(grad_norm, -1, keepdims=True)
    mean_two = jnp.mean(grad_norm * normed, -1, keepdims=True)
    grad_in = inverse * (grad_norm - mean_one - normed * mean_two)
    return (grad_in, jnp.sum(grad_result * normed, 0), jnp.sum(grad_result, 0))


def gelu_parts(upward):
    cdf_val = 0.5 * (1.0 + lax.erf(upward * 0.7071067811865476))
    density = jnp.exp(-0.5 * upward * upward) * 0.3989422804014327
    return (upward * cdf_val, cdf_val + upward * density)


def fetch_layer(w_proj, w_mix, w_grow, w_shrink, bias_heads, bias_grow, gain_pair, bias_set):
    return (
        lax.all_gather(w_proj, "fsdp", axis=1, tiled=True),
        lax.all_gather(w_mix, "fsdp", axis=1, tiled=True),
        lax.all_gather(w_grow, "fsdp", axis=0, tiled=True),
        lax.all_gather(w_shrink, "fsdp", axis=1, tiled=True),
        lax.all_gather(bias_heads, "fsdp", axis=2, tiled=True),
        lax.all_gather(bias_grow, "fsdp", axis=1, tiled=True),
        lax.all_gather(gain_pair, "fsdp", axis=1, tiled=True),
        lax.all_gather(bias_set, "fsdp", axis=1, tiled=True),
    )


def refetch_layer(w_proj, w_mix, w_grow, w_shrink, bias_heads, bias_grow, gain_pair, bias_set):
    return (
        lax.all_gather(w_proj, "fsdp", axis=1, tiled=True),
        lax.all_gather(w_mix, "fsdp", axis=1, tiled=True),
        lax.all_gather(w_grow, "fsdp", axis=0, tiled=True),
        lax.all_gather(w_shrink, "fsdp", axis=1, tiled=True),
        lax.all_gather(bias_heads, "fsdp", axis=2, tiled=True),
        lax.all_gather(bias_grow, "fsdp", axis=1, tiled=True),
        lax.all_gather(gain_pair, "fsdp", axis=1, tiled=True),
        lax.all_gather(bias_set, "fsdp", axis=1, tiled=True),
    )


def spread_rows(share_low):
    return lax.all_gather(share_low, "tensor", axis=0, tiled=True)


def spread_back(share_low):
    return lax.all_gather(share_low, "tensor", axis=0, tiled=True)


def reduce_rows(term_fn, share_rows):
    return lax.psum_scatter(
        term_fn(jnp.int32(0), lax.axis_size("tensor") * share_rows).astype(jnp.bfloat16),
        "tensor",
        scatter_dimension=0,
        tiled=True,
    ).astype(jnp.float32)


def reduce_back(term_fn, share_rows):
    return lax.psum_scatter(
        term_fn(jnp.int32(0), lax.axis_size("tensor") * share_rows).astype(jnp.bfloat16),
        "tensor",
        scatter_dimension=0,
        tiled=True,
    ).astype(jnp.float32)


def bucket_scores(query_heads, key_heads, page_lengths, length):
    scores = jnp.einsum(
        "plhe,pmhe->phlm", query_heads, key_heads, preferred_element_type=jnp.float32
    ) * HEAD ** (-0.5)
    valid_keys = (
        jnp.arange(length, dtype=jnp.int32)[None, None, None, :] < page_lengths[:, None, None, None]
    )
    return jnp.where(valid_keys, scores, -1000000000.0)


def attention_forward(queries, keys_b, values_b, page_lengths):
    heads_here = queries.shape[1] // HEAD
    outputs = []
    log_totals = []
    row_at = 0
    page_at = 0
    for amount, length in ((PAGES_A, LEN_A), (PAGES_B, LEN_B), (PAGES_C, LEN_C)):
        span_rows = amount * length
        head_shape = (amount, length, heads_here, HEAD)
        query_heads = queries[row_at : row_at + span_rows].reshape(head_shape)
        key_heads = keys_b[row_at : row_at + span_rows].reshape(head_shape)
        value_heads = values_b[row_at : row_at + span_rows].reshape(head_shape)
        scores = bucket_scores(
            query_heads, key_heads, page_lengths[page_at : page_at + amount], length
        )
        row_peak = jnp.max(scores, -1, keepdims=True)
        exponent = jnp.exp(scores - row_peak)
        row_total = jnp.sum(exponent, -1, keepdims=True)
        attn_low = (exponent / row_total).astype(jnp.bfloat16)
        context = jnp.einsum(
            "phlm,pmhe->plhe", attn_low, value_heads, preferred_element_type=jnp.float32
        )
        outputs.append(context.reshape(span_rows, heads_here * HEAD))
        log_totals.append(row_peak + jnp.log(row_total))
        row_at += span_rows
        page_at += amount
    return (jnp.concatenate(outputs, 0).astype(jnp.bfloat16), log_totals)


def attention_backward(queries, keys_b, values_b, page_lengths, log_totals, grad_context):
    heads_here = queries.shape[1] // HEAD
    grad_q_list = []
    grad_k_list = []
    grad_v_list = []
    row_at = 0
    page_at = 0
    bucket_index = 0
    for amount, length in ((PAGES_A, LEN_A), (PAGES_B, LEN_B), (PAGES_C, LEN_C)):
        span_rows = amount * length
        head_shape = (amount, length, heads_here, HEAD)
        query_heads = queries[row_at : row_at + span_rows].reshape(head_shape)
        key_heads = keys_b[row_at : row_at + span_rows].reshape(head_shape)
        value_heads = values_b[row_at : row_at + span_rows].reshape(head_shape)
        grad_heads = grad_context[row_at : row_at + span_rows].reshape(head_shape)
        scores = bucket_scores(
            query_heads, key_heads, page_lengths[page_at : page_at + amount], length
        )
        attn_probs = jnp.exp(scores - log_totals[bucket_index])
        attn_low = attn_probs.astype(jnp.bfloat16)
        grad_values = jnp.einsum(
            "phlm,plhe->pmhe", attn_low, grad_heads, preferred_element_type=jnp.float32
        )
        grad_probs = jnp.einsum(
            "plhe,pmhe->phlm", grad_heads, value_heads, preferred_element_type=jnp.float32
        )
        grad_scores = (
            attn_probs * (grad_probs - jnp.sum(attn_probs * grad_probs, -1, keepdims=True))
        ).astype(jnp.bfloat16)
        grad_queries = jnp.einsum(
            "phlm,pmhe->plhe", grad_scores, key_heads, preferred_element_type=jnp.float32
        ) * HEAD ** (-0.5)
        grad_keys = jnp.einsum(
            "phlm,plhe->pmhe", grad_scores, query_heads, preferred_element_type=jnp.float32
        ) * HEAD ** (-0.5)
        grad_q_list.append(grad_queries.reshape(span_rows, heads_here * HEAD))
        grad_k_list.append(grad_keys.reshape(span_rows, heads_here * HEAD))
        grad_v_list.append(grad_values.reshape(span_rows, heads_here * HEAD))
        row_at += span_rows
        page_at += amount
        bucket_index += 1
    return (
        jnp.concatenate(grad_q_list, 0).astype(jnp.bfloat16),
        jnp.concatenate(grad_k_list, 0).astype(jnp.bfloat16),
        jnp.concatenate(grad_v_list, 0).astype(jnp.bfloat16),
    )


def layer_forward(weights, inputs_low, inputs_share, page_lengths, share_rows):
    w_proj, w_mix, w_grow, w_shrink, bias_heads, bias_grow, gain_pair, bias_set = weights
    width_here = w_proj.shape[2]
    gain_f = gain_pair.astype(jnp.float32)
    biases = bias_set.astype(jnp.float32)
    projected = jnp.einsum("td,kdc->ktc", inputs_low, w_proj, preferred_element_type=jnp.float32)
    head_bias = bias_heads.reshape(2, width_here).astype(jnp.float32)
    queries = (projected[0] + head_bias[0]).astype(jnp.bfloat16)
    keys_b = projected[1].astype(jnp.bfloat16)
    values_b = (projected[2] + head_bias[1]).astype(jnp.bfloat16)
    context, log_totals = attention_forward(queries, keys_b, values_b, page_lengths)
    attn_share = reduce_rows(
        lambda offset, amount: jnp.dot(context, w_mix, preferred_element_type=jnp.float32),
        share_rows,
    )
    y_one, normed_one, inverse_one = layer_norm(
        inputs_share + attn_share + biases[0], gain_f[0], biases[2]
    )
    middle_full = spread_rows(y_one.astype(jnp.bfloat16))
    upward = jnp.dot(middle_full, w_grow, preferred_element_type=jnp.float32) + bias_grow.reshape(
        -1
    ).astype(jnp.float32)
    activated, slope = gelu_parts(upward)
    activated_b = activated.astype(jnp.bfloat16)
    down_share = reduce_rows(
        lambda offset, amount: jnp.dot(activated_b, w_shrink, preferred_element_type=jnp.float32),
        share_rows,
    )
    result, normed_two, inverse_two = layer_norm(
        y_one + down_share + biases[1], gain_f[1], biases[3]
    )
    kept_state = (
        inputs_low,
        queries,
        keys_b,
        values_b,
        log_totals,
        context,
        normed_one,
        inverse_one,
        middle_full,
        slope,
        activated_b,
        normed_two,
        inverse_two,
    )
    return (result, kept_state)


def layer_backward(weights, kept_state, grad_result, page_lengths, share_rows):
    w_proj, w_mix, w_grow, w_shrink, bias_heads, bias_grow, gain_pair, bias_set = weights
    (
        inputs_low,
        queries,
        keys_b,
        values_b,
        log_totals,
        context,
        normed_one,
        inverse_one,
        middle_full,
        slope,
        activated_b,
        normed_two,
        inverse_two,
    ) = kept_state
    gain_f = gain_pair.astype(jnp.float32)
    grad_two, grad_gain_two, grad_bias_two = norm_back(
        grad_result, normed_two, inverse_two, gain_f[1]
    )
    grad_down_bias = jnp.sum(grad_two, 0)
    grad_down_full = spread_back(grad_two.astype(jnp.bfloat16))
    grad_shrink = jnp.einsum(
        "tf,td->fd", activated_b, grad_down_full, preferred_element_type=jnp.float32
    )
    grad_act = jnp.einsum("td,fd->tf", grad_down_full, w_shrink, preferred_element_type=jnp.float32)
    grad_up_b = (grad_act * slope).astype(jnp.bfloat16)
    grad_grow = jnp.einsum("td,tf->df", middle_full, grad_up_b, preferred_element_type=jnp.float32)
    grad_grow_bias = jnp.sum(grad_up_b, 0, dtype=jnp.float32).reshape(bias_grow.shape)
    grad_middle = reduce_back(
        lambda offset, amount: jnp.einsum(
            "tf,df->td", grad_up_b, w_grow, preferred_element_type=jnp.float32
        ),
        share_rows,
    )
    grad_one, grad_gain_one, grad_bias_one = norm_back(
        grad_middle + grad_two, normed_one, inverse_one, gain_f[0]
    )
    grad_mix_bias = jnp.sum(grad_one, 0)
    grad_mix_full = spread_back(grad_one.astype(jnp.bfloat16))
    grad_mix = jnp.einsum("tc,td->cd", context, grad_mix_full, preferred_element_type=jnp.float32)
    grad_context = jnp.einsum(
        "td,cd->tc", grad_mix_full, w_mix, preferred_element_type=jnp.float32
    ).astype(jnp.bfloat16)
    grad_q, grad_k, grad_v = attention_backward(
        queries, keys_b, values_b, page_lengths, log_totals, grad_context
    )
    grad_stack = jnp.stack([grad_q, grad_k, grad_v])
    grad_proj = jnp.einsum(
        "td,ktc->kdc", inputs_low, grad_stack, preferred_element_type=jnp.float32
    )
    grad_heads_bias = jnp.stack(
        [jnp.sum(grad_q, 0, dtype=jnp.float32), jnp.sum(grad_v, 0, dtype=jnp.float32)]
    ).reshape(bias_heads.shape)
    grad_input = (
        reduce_back(
            lambda offset, amount: jnp.einsum(
                "ktc,kdc->td", grad_stack, w_proj, preferred_element_type=jnp.float32
            ),
            share_rows,
        )
        + grad_one
    )
    grad_gain_pair = jnp.stack([grad_gain_one, grad_gain_two])
    grad_bias_set = jnp.stack([grad_mix_bias, grad_down_bias, grad_bias_one, grad_bias_two])
    return (
        grad_input,
        (
            grad_proj,
            grad_mix,
            grad_grow,
            grad_shrink,
            grad_heads_bias,
            grad_grow_bias,
            grad_gain_pair,
            grad_bias_set,
        ),
    )


def regroup(grad_array, axis_dim, outer_size, inner_size):
    old_shape = grad_array.shape
    split_shape = (
        old_shape[:axis_dim]
        + (outer_size, inner_size, old_shape[axis_dim] // (outer_size * inner_size))
        + old_shape[axis_dim + 1 :]
    )
    return jnp.swapaxes(grad_array.reshape(split_shape), axis_dim, axis_dim + 1).reshape(old_shape)


def per_device(
    activations,
    cotangent,
    lengths,
    w_qkv,
    w_out,
    w_up,
    w_down,
    b_qv,
    b_up,
    norm_gains,
    layer_biases,
):
    tensor_size = lax.axis_size("tensor")
    share_rows = activations.shape[0] // tensor_size
    first_row = lax.axis_index("tensor") * share_rows
    inputs_share = lax.dynamic_slice_in_dim(activations, first_row, share_rows, 0).astype(
        jnp.float32
    )
    inputs_low = activations
    fetched = []
    kept_all = []
    for layer_index in range(LAYERS):
        weights = fetch_layer(
            w_qkv[layer_index],
            w_out[layer_index],
            w_up[layer_index],
            w_down[layer_index],
            b_qv[layer_index],
            b_up[layer_index],
            norm_gains[layer_index],
            layer_biases[layer_index],
        )
        fetched.append(weights)
        result, kept_state = layer_forward(weights, inputs_low, inputs_share, lengths, share_rows)
        kept_all.append(kept_state)
        inputs_share = result
        if layer_index + 1 < LAYERS:
            inputs_low = spread_rows(result.astype(jnp.bfloat16))
    layer_out = inputs_share.astype(jnp.bfloat16)
    grad_share = cotangent.astype(jnp.float32)
    layer_grads = [None] * LAYERS
    for layer_index in reversed(range(LAYERS)):
        weights = refetch_layer(
            w_qkv[layer_index],
            w_out[layer_index],
            w_up[layer_index],
            w_down[layer_index],
            b_qv[layer_index],
            b_up[layer_index],
            norm_gains[layer_index],
            layer_biases[layer_index],
        )
        grad_share, layer_grads[layer_index] = layer_backward(
            weights, kept_all[layer_index], grad_share, lengths, share_rows
        )
    stacked = [
        jnp.stack([layer_grads[layer_index][member] for layer_index in range(LAYERS)])
        for member in range(8)
    ]
    gain_total, bias_total = (
        lax.psum(stacked[6].astype(jnp.bfloat16), "tensor").astype(jnp.float32),
        lax.psum(stacked[7].astype(jnp.bfloat16), "tensor").astype(jnp.float32),
    )
    fsdp_size = lax.axis_size("fsdp")
    data_size = lax.axis_size("dp")
    scattered = (
        lax.psum_scatter(
            regroup(stacked[0], 2, fsdp_size, data_size),
            ("dp", "fsdp"),
            scatter_dimension=2,
            tiled=True,
        ),
        lax.psum_scatter(
            regroup(stacked[1], 2, fsdp_size, data_size),
            ("dp", "fsdp"),
            scatter_dimension=2,
            tiled=True,
        ),
        lax.psum_scatter(
            regroup(stacked[2], 1, fsdp_size, data_size),
            ("dp", "fsdp"),
            scatter_dimension=1,
            tiled=True,
        ),
        lax.psum_scatter(
            regroup(stacked[3], 2, fsdp_size, data_size),
            ("dp", "fsdp"),
            scatter_dimension=2,
            tiled=True,
        ),
        lax.psum_scatter(
            regroup(stacked[4], 3, fsdp_size, data_size),
            ("dp", "fsdp"),
            scatter_dimension=3,
            tiled=True,
        ),
        lax.psum_scatter(
            regroup(stacked[5], 2, fsdp_size, data_size),
            ("dp", "fsdp"),
            scatter_dimension=2,
            tiled=True,
        ),
        lax.psum_scatter(
            regroup(gain_total, 2, fsdp_size, data_size),
            ("dp", "fsdp"),
            scatter_dimension=2,
            tiled=True,
        ),
        lax.psum_scatter(
            regroup(bias_total, 2, fsdp_size, data_size),
            ("dp", "fsdp"),
            scatter_dimension=2,
            tiled=True,
        ),
    )
    reduced = (
        lax.all_gather(scattered[0].astype(jnp.bfloat16), "dp", axis=2, tiled=True).astype(
            jnp.float32
        ),
        lax.all_gather(scattered[1].astype(jnp.bfloat16), "dp", axis=2, tiled=True).astype(
            jnp.float32
        ),
        lax.all_gather(scattered[2].astype(jnp.bfloat16), "dp", axis=1, tiled=True).astype(
            jnp.float32
        ),
        lax.all_gather(scattered[3].astype(jnp.bfloat16), "dp", axis=2, tiled=True).astype(
            jnp.float32
        ),
        lax.all_gather(scattered[4].astype(jnp.bfloat16), "dp", axis=3, tiled=True).astype(
            jnp.float32
        ),
        lax.all_gather(scattered[5].astype(jnp.bfloat16), "dp", axis=2, tiled=True).astype(
            jnp.float32
        ),
        lax.all_gather(scattered[6].astype(jnp.bfloat16), "dp", axis=2, tiled=True).astype(
            jnp.float32
        ),
        lax.all_gather(scattered[7].astype(jnp.bfloat16), "dp", axis=2, tiled=True).astype(
            jnp.float32
        ),
    )
    return (
        layer_out,
        grad_share,
        reduced[0],
        reduced[1],
        reduced[2],
        reduced[3],
        reduced[4],
        reduced[5],
        reduced[6],
        reduced[7],
    )


def solution(mesh):
    in_specs = (
        P(("dp", "fsdp"), None),
        P(("dp", "fsdp", "tensor"), None),
        P(("dp", "fsdp")),
        P(None, None, "fsdp", "tensor"),
        P(None, "tensor", "fsdp"),
        P(None, "fsdp", "tensor"),
        P(None, "tensor", "fsdp"),
        P(None, None, "tensor", "fsdp"),
        P(None, "tensor", "fsdp"),
        P(None, None, "fsdp"),
        P(None, None, "fsdp"),
    )
    out_specs = (
        P(("dp", "fsdp", "tensor"), None),
        P(("dp", "fsdp", "tensor"), None),
        P(None, None, "fsdp", "tensor"),
        P(None, "tensor", "fsdp"),
        P(None, "fsdp", "tensor"),
        P(None, "tensor", "fsdp"),
        P(None, None, "tensor", "fsdp"),
        P(None, "tensor", "fsdp"),
        P(None, None, "fsdp"),
        P(None, None, "fsdp"),
    )
    return jax.shard_map(
        per_device, mesh=mesh, in_specs=in_specs, out_specs=out_specs, check_vma=False
    )
```

profile of v0, /device:TPU:0, one launch (start us, length us, event | category | flops | bytes accessed | tf_op | source)
XLA Modules:
  0.0 1614.7 jit_solution(6773108793043851923)
XLA Ops:
  12.3 5.3 all-gather.1
  21.0 14.0 all-gather.2
  35.1 10.8 all-gather.53.cloned.1.call-done
  63.2 4.3 all-gather.4
  67.5 4.3 all-gather.3
  71.9 22.8 %reduce-scatter.23.cloned.1.call-done = bf16[288,1024]{1,0:T(8,128)(2,1)} async-done(((bf16[1152,1024]{1,0:T(8,128)(2,1)}), bf16[288,1024]{1,0:T(8,128)(2,1)}) %reduce-scatter.23.cloned.1.call-update) | async-done | bytes 589840 | tf_op jit(solution)/shard_map/reduce_scatter | solution.py:72
  104.1 5.2 all-gather.6
  109.3 21.4 %all-gather.55.cloned.1.call-done = bf16[1,1024,1024]{2,1,0:T(8,128)(2,1)} async-done(((bf16[1,512,1024]{2,1,0:T(8,128)(2,1)}), bf16[1,1024,1024]{2,1,0:T(8,128)(2,1)}) %all-gather.55.cloned.1.call-update) | async-done | bytes 2097168 | tf_op jit(solution)/shard_map/all_gather | solution.py:41
  130.8 26.2 %all-gather.33.cloned.1.call-done = bf16[1152,1024]{1,0:T(8,128)(2,1)} async-done(((bf16[288,1024]{1,0:T(8,128)(2,1)}), bf16[1152,1024]{1,0:T(8,128)(2,1)}) %all-gather.33.cloned.1.call-update) | async-done | bytes 2359312 | tf_op jit(solution)/shard_map/all_gather | solution.py:64
  157.0 8.3 multiply_convert_fusion.1
  165.3 26.9 %all-gather.57.cloned.1.call-done = bf16[1,1024,1024]{2,1,0:T(8,128)(2,1)} async-done(((bf16[1,1024,512]{2,1,0:T(8,128)(2,1)}), bf16[1,1024,1024]{2,1,0:T(8,128)(2,1)}) %all-gather.57.cloned.1.call-update) | async-done | bytes 2097168 | tf_op jit(solution)/shard_map/all_gather | solution.py:42
  192.2 6.3 convolution_convert_fusion.4
  199.8 31.9 %reduce-scatter.25.cloned.1.call-done = bf16[288,1024]{1,0:T(8,128)(2,1)} async-done(((bf16[1152,1024]{1,0:T(8,128)(2,1)}), bf16[288,1024]{1,0:T(8,128)(2,1)}) %reduce-scatter.25.cloned.1.call-update) | async-done | bytes 589840 | tf_op jit(solution)/shard_map/reduce_scatter | solution.py:72
  235.2 4.4 all-gather.9
  240.0 13.6 all-gather.10
  253.5 11.4 all-gather.59.cloned.1.call-done
  264.9 26.2 %all-gather.35.cloned.1.call-done = bf16[1152,1024]{1,0:T(8,128)(2,1)} async-done(((bf16[288,1024]{1,0:T(8,128)(2,1)}), bf16[1152,1024]{1,0:T(8,128)(2,1)}) %all-gather.35.cloned.1.call-update) | async-done | bytes 2359312 | tf_op jit(solution)/shard_map/all_gather | solution.py:64
  291.1 4.4 fusion.171
  308.1 4.3 all-gather.12
  318.0 22.7 %reduce-scatter.27.cloned.1.call-done = bf16[288,1024]{1,0:T(8,128)(2,1)} async-done(((bf16[1152,1024]{1,0:T(8,128)(2,1)}), bf16[288,1024]{1,0:T(8,128)(2,1)}) %reduce-scatter.27.cloned.1.call-update) | async-done | bytes 589840 | tf_op jit(solution)/shard_map/reduce_scatter | solution.py:72
  344.5 5.1 all-gather.14
  349.6 26.3 %all-gather.61.cloned.1.call-done = bf16[1,1024,1024]{2,1,0:T(8,128)(2,1)} async-done(((bf16[1,512,1024]{2,1,0:T(8,128)(2,1)}), bf16[1,1024,1024]{2,1,0:T(8,128)(2,1)}) %all-gather.61.cloned.1.call-update) | async-done | bytes 2097168 | tf_op jit(solution)/shard_map/all_gather | solution.py:41
  375.9 26.3 %all-gather.37.cloned.1.call-done = bf16[1152,1024]{1,0:T(8,128)(2,1)} async-done(((bf16[288,1024]{1,0:T(8,128)(2,1)}), bf16[1152,1024]{1,0:T(8,128)(2,1)}) %all-gather.37.cloned.1.call-update) | async-done | bytes 2359312 | tf_op jit(solution)/shard_map/all_gather | solution.py:64
  402.2 8.3 multiply_convert_fusion
  410.5 26.4 %all-gather.63.cloned.1.call-done = bf16[1,1024,1024]{2,1,0:T(8,128)(2,1)} async-done(((bf16[1,1024,512]{2,1,0:T(8,128)(2,1)}), bf16[1,1024,1024]{2,1,0:T(8,128)(2,1)}) %all-gather.63.cloned.1.call-update) | async-done | bytes 2097168 | tf_op jit(solution)/shard_map/all_gather | solution.py:42
  436.9 6.3 convolution_convert_fusion.2
  443.3 33.2 %reduce-scatter.29.cloned.1.call-done = bf16[288,1024]{1,0:T(8,128)(2,1)} async-done(((bf16[1152,1024]{1,0:T(8,128)(2,1)}), bf16[288,1024]{1,0:T(8,128)(2,1)}) %reduce-scatter.29.cloned.1.call-update) | async-done | bytes 589840 | tf_op jit(solution)/shard_map/reduce_scatter | solution.py:72
  481.5 24.2 %all-gather.39.cloned.1.call-done = bf16[1152,1024]{1,0:T(8,128)(2,1)} async-done(((bf16[288,1024]{1,0:T(8,128)(2,1)}), bf16[1152,1024]{1,0:T(8,128)(2,1)}) %all-gather.39.cloned.1.call-update) | async-done | bytes 2359312 | tf_op jit(solution)/shard_map/all_gather | solution.py:68
  505.6 7.7 convert_reduce_fusion
  518.9 33.2 %reduce-scatter.31.cloned.1.call-done = bf16[288,1024]{1,0:T(8,128)(2,1)} async-done(((bf16[1152,1024]{1,0:T(8,128)(2,1)}), bf16[288,1024]{1,0:T(8,128)(2,1)}) %reduce-scatter.31.cloned.1.call-update) | async-done | bytes 589840 | tf_op jit(solution)/shard_map/reduce_scatter | solution.py:81
  556.9 23.9 %all-gather.41.cloned.1.call-done = bf16[1152,1024]{1,0:T(8,128)(2,1)} async-done(((bf16[288,1024]{1,0:T(8,128)(2,1)}), bf16[1152,1024]{1,0:T(8,128)(2,1)}) %all-gather.41.cloned.1.call-update) | async-done | bytes 2359312 | tf_op jit(solution)/shard_map/all_gather | solution.py:68
  600.9 4.9 bitcast_convert_fusion.1
  605.9 33.1 %reduce-scatter.33.cloned.1.call-done = bf16[288,1024]{1,0:T(8,128)(2,1)} async-done(((bf16[1152,1024]{1,0:T(8,128)(2,1)}), bf16[288,1024]{1,0:T(8,128)(2,1)}) %reduce-scatter.33.cloned.1.call-update) | async-done | bytes 589840 | tf_op jit(solution)/shard_map/reduce_scatter | solution.py:81
  643.8 24.0 %all-gather.43.cloned.1.call-done = bf16[1152,1024]{1,0:T(8,128)(2,1)} async-done(((bf16[288,1024]{1,0:T(8,128)(2,1)}), bf16[1152,1024]{1,0:T(8,128)(2,1)}) %all-gather.43.cloned.1.call-update) | async-done | bytes 2359312 | tf_op jit(solution)/shard_map/all_gather | solution.py:68
  667.7 7.7 convert_reduce_fusion.1
  680.9 33.2 %reduce-scatter.35.cloned.1.call-done = bf16[288,1024]{1,0:T(8,128)(2,1)} async-done(((bf16[1152,1024]{1,0:T(8,128)(2,1)}), bf16[288,1024]{1,0:T(8,128)(2,1)}) %reduce-scatter.35.cloned.1.call-update) | async-done | bytes 589840 | tf_op jit(solution)/shard_map/reduce_scatter | solution.py:81
  721.0 5.5 fusion.176
  737.1 4.9 fusion.178
  749.2 13.4 copy.424
  762.5 11.5 reshape.1080
  775.4 4.5 fusion.39
  808.2 6.1 fusion.36
  814.3 5.5 stack.166
  819.8 6.2 maximum_bitcast_fusion.2
  825.9 7.6 copy.421
  836.5 11.1 all-reduce.1
  863.5 6.4 bitcast_convert_fusion
  870.0 28.4 %reduce-scatter.43.cloned.1.call-done = f32[2,128,1024]{2,1,0:T(8,128)} async-done(((f32[2,1024,1024]{2,1,0:T(8,128)}), f32[2,128,1024]{2,1,0:T(8,128)}) %reduce-scatter.43.cloned.1.call-update) | async-done | bytes 1048592 | tf_op jit(solution)/shard_map/reduce_scatter | solution.py:395
  900.5 149.9 %reduce-scatter.45.cloned.1.call-done = f32[2,1024,128]{2,1,0:T(8,128)} async-done(((f32[2,1024,1024]{2,1,0:T(8,128)}), f32[2,1024,128]{2,1,0:T(8,128)}) %reduce-scatter.45.cloned.1.call-update) | async-done | bytes 1048592 | tf_op jit(solution)/shard_map/reduce_scatter | solution.py:401
  1052.8 119.0 %reduce-scatter.39.cloned.1.call-done = f32[2,3,128,256]{3,2,1,0:T(8,128)} async-done(((f32[2,3,1024,256]{3,2,1,0:T(8,128)}), f32[2,3,128,256]{3,2,1,0:T(8,128)}) %reduce-scatter.39.cloned.1.call-update) | async-done | bytes 786448 | tf_op jit(solution)/shard_map/reduce_scatter | solution.py:383
  1176.0 59.8 %reduce-scatter.47.cloned.1.call-done = f32[16,16]{1,0:T(8,128)} async-done(((f32[128,16]{1,0:T(8,128)}), f32[16,16]{1,0:T(8,128)}) %reduce-scatter.47.cloned.1.call-update) | async-done | bytes 1040
  1236.8 13.1 all_gather.131
  1250.6 50.5 %reduce-scatter.49.cloned.1.call-done = f32[128,4]{1,0:T(8,128)} async-done(((f32[1024,4]{1,0:T(8,128)}), f32[128,4]{1,0:T(8,128)}) %reduce-scatter.49.cloned.1.call-update) | async-done | bytes 2064
  1302.1 9.8 all_gather.132
  1312.6 52.7 %reduce-scatter.51.cloned.1.call-done = f32[128,8]{1,0:T(8,128)} async-done(((f32[1024,8]{1,0:T(8,128)}), f32[128,8]{1,0:T(8,128)}) %reduce-scatter.51.cloned.1.call-update) | async-done | bytes 4112
  1366.2 9.9 all_gather.133
  1378.0 18.3 %all-reduce = bf16[2,2,4,64]{3,2,1,0:T(4,128)(2,1)S(1)} all-reduce(f32[2,2,4,64]{3,2,1,0:T(4,128)S(1)} %reshape.1094), channel_id=30, replica_groups=mesh['dp'=4,'fsdp'=2,'tensor'=4] {'dp','fsdp'}, use_global_device_ids=true, to_apply=%region_50.51.clone | all-reduce | flops 1024 | bytes 6144
  1396.5 13.1 all_gather.130
  1410.3 26.9 %reduce-scatter.41.cloned.1.call-done = f32[2,256,128]{2,1,0:T(8,128)} async-done(((f32[2,256,1024]{2,1,0:T(8,128)}), f32[2,256,128]{2,1,0:T(8,128)}) %reduce-scatter.41.cloned.1.call-update) | async-done | bytes 262160 | tf_op jit(solution)/shard_map/reduce_scatter | solution.py:389
  1438.2 14.6 all_gather.127
  1453.9 18.7 %reduce-scatter.37.cloned.1.call-done = bf16[288,1024]{1,0:T(8,128)(2,1)} async-done(((bf16[1152,1024]{1,0:T(8,128)(2,1)}), bf16[288,1024]{1,0:T(8,128)(2,1)}) %reduce-scatter.37.cloned.1.call-update) | async-done | bytes 589840 | tf_op jit(solution)/shard_map/reduce_scatter | solution.py:81
  1474.9 45.9 %all-gather.49.cloned.1.call-done = bf16[2,512,1024]{2,1,0:T(8,128)(2,1)} async-done(((bf16[2,128,1024]{2,1,0:T(8,128)(2,1)}), bf16[2,512,1024]{2,1,0:T(8,128)(2,1)}) %all-gather.49.cloned.1.call-update) | async-done | bytes 2097168 | tf_op jit(solution)/shard_map/all_gather | solution.py:439
  1524.8 42.3 %all-gather.51.cloned.1.call-done = bf16[2,1024,512]{2,1,0:T(8,128)(2,1)} async-done(((bf16[2,1024,128]{2,1,0:T(8,128)(2,1)}), bf16[2,1024,512]{2,1,0:T(8,128)(2,1)}) %all-gather.51.cloned.1.call-update) | async-done | bytes 2097168 | tf_op jit(solution)/shard_map/all_gather | solution.py:442
  1571.3 32.7 %all-gather.47.cloned.1.call-done = bf16[2,3,512,256]{3,2,1,0:T(8,128)(2,1)} async-done(((bf16[2,3,128,256]{3,2,1,0:T(8,128)(2,1)}), bf16[2,3,512,256]{3,2,1,0:T(8,128)(2,1)}) %all-gather.47.cloned.1.call-update) | async-done | bytes 1572880 | tf_op jit(solution)/shard_map/all_gather | solution.py:433
  (701 shorter events, 209.5 us)
Async XLA Ops:
  7.2 38.8 %all-gather.53.cloned.1.call-start = ((), (), s32[]{:S(2)}) async-start(), calls=%async_computation.37 | async-start | bytes 2359296 | tf_op jit(solution)/shard_map/all_gather | solution.py:39
  9.6 36.4 %copy-start.17 = (bf16[1152,1024]{1,0:T(8,128)(2,1)S(1)}, bf16[1152,1024]{1,0:T(8,128)(2,1)}, u32[]{:S(2)}) copy-start(bf16[1152,1024]{1,0:T(8,128)(2,1)} %param.11) | copy-start | bytes 7077892
  12.1 82.7 %reduce-scatter.23.cloned.1.call-start = ((), (), s32[]{:S(2)}) async-start(), calls=%async_computation.15 | async-start | bytes 2949120 | tf_op jit(solution)/shard_map/reduce_scatter | solution.py:72
  60.0 70.8 %all-gather.55.cloned.1.call-start = ((), (), s32[]{:S(2)}) async-start(), calls=%async_computation.38 | async-start | bytes 3145728 | tf_op jit(solution)/shard_map/all_gather | solution.py:41
  63.1 93.9 %all-gather.33.cloned.1.call-start = ((), (), s32[]{:S(2)}) async-start(), calls=%async_computation.16 | async-start | bytes 2949120 | tf_op jit(solution)/shard_map/all_gather | solution.py:64
  96.3 135.4 %copy-start.109 = (f32[288]{0:T(512)}, f32[288]{0:T(512)S(1)}, u32[]{:S(2)}) copy-start(f32[288]{0:T(512)S(1)} %broadcast_multiply_fusion.11) | copy-start | bytes 3460
  98.0 133.8 %copy-start.114 = (f32[288]{0:T(512)}, f32[288]{0:T(512)S(1)}, u32[]{:S(2)}) copy-start(f32[288]{0:T(512)S(1)} %add_rsqrt_fusion.3) | copy-start | bytes 3460
  100.2 91.9 %all-gather.57.cloned.1.call-start = ((), (), s32[]{:S(2)}) async-start(), calls=%async_computation.39 | async-start | bytes 3145728 | tf_op jit(solution)/shard_map/all_gather | solution.py:42
  103.3 128.4 %reduce-scatter.25.cloned.1.call-start = ((), (), s32[]{:S(2)}) async-start(), calls=%async_computation.17 | async-start | bytes 2949120 | tf_op jit(solution)/shard_map/reduce_scatter | solution.py:72
  198.5 66.4 %all-gather.59.cloned.1.call-start = ((), (), s32[]{:S(2)}) async-start(), calls=%async_computation.40 | async-start | bytes 2359296 | tf_op jit(solution)/shard_map/all_gather | solution.py:39
  199.7 91.4 %all-gather.35.cloned.1.call-start = ((), (), s32[]{:S(2)}) async-start(), calls=%async_computation.18 | async-start | bytes 2949120 | tf_op jit(solution)/shard_map/all_gather | solution.py:64
  233.9 405.2 %copy-start.113 = (f32[288]{0:T(512)}, f32[288]{0:T(512)S(1)}, u32[]{:S(2)}) copy-start(f32[288]{0:T(512)S(1)} %add_rsqrt_fusion.2) | copy-start | bytes 3460
  235.0 105.7 %reduce-scatter.27.cloned.1.call-start = ((), (), s32[]{:S(2)}) async-start(), calls=%async_computation.19 | async-start | bytes 2949120 | tf_op jit(solution)/shard_map/reduce_scatter | solution.py:72
  307.5 68.4 %all-gather.61.cloned.1.call-start = ((), (), s32[]{:S(2)}) async-start(), calls=%async_computation.41 | async-start | bytes 3145728 | tf_op jit(solution)/shard_map/all_gather | solution.py:41
  308.1 94.1 %all-gather.37.cloned.1.call-start = ((), (), s32[]{:S(2)}) async-start(), calls=%async_computation.20 | async-start | bytes 2949120 | tf_op jit(solution)/shard_map/all_gather | solution.py:64
  318.0 25.7 %copy-start.120 = (f32[1,1,1024]{2,1,0:T(1,128)}, f32[1,1,1024]{2,1,0:T(1,128)S(1)}, u32[]{:S(2)}) copy-start(f32[1,1,1024]{2,1,0:T(1,128)S(1)} %get-tuple-element.83) | copy-start | bytes 12292
  343.7 93.1 %all-gather.63.cloned.1.call-start = ((), (), s32[]{:S(2)}) async-start(), calls=%async_computation.42 | async-start | bytes 3145728 | tf_op jit(solution)/shard_map/all_gather | solution.py:42
  344.3 132.1 %reduce-scatter.29.cloned.1.call-start = ((), (), s32[]{:S(2)}) async-start(), calls=%async_computation.21 | async-start | bytes 2949120 | tf_op jit(solution)/shard_map/reduce_scatter | solution.py:72
  443.2 33.3 %copy-start.121 = (f32[1,1,1024]{2,1,0:T(1,128)S(1)}, f32[1,1,1024]{2,1,0:T(1,128)}, u32[]{:S(2)}) copy-start(f32[1,1,1024]{2,1,0:T(1,128)} %copy-done.120) | copy-start | bytes 12292
  443.2 33.3 %copy-start.139 = (f32[1,1,1024]{2,1,0:T(1,128)S(1)}, f32[1,1,1024]{2,1,0:T(1,128)}, u32[]{:S(2)}) copy-start(f32[1,1,1024]{2,1,0:T(1,128)} %get-tuple-element.82) | copy-start | bytes 12292
  443.2 35.2 %copy-start.122 = (f32[1,1,1024]{2,1,0:T(1,128)S(1)}, f32[1,1,1024]{2,1,0:T(1,128)}, u32[]{:S(2)}) copy-start(f32[1,1,1024]{2,1,0:T(1,128)} %get-tuple-element.91) | copy-start | bytes 12292
  443.2 62.4 %all-gather.39.cloned.1.call-start = ((), (), s32[]{:S(2)}) async-start(), calls=%async_computation.22 | async-start | bytes 2949120 | tf_op jit(solution)/shard_map/all_gather | solution.py:68
  481.4 70.6 %reduce-scatter.31.cloned.1.call-start = ((), (), s32[]{:S(2)}) async-start(), calls=%async_computation.23 | async-start | bytes 2949120 | tf_op jit(solution)/shard_map/reduce_scatter | solution.py:81
  505.6 9.2 copy-start.164
  518.8 62.0 %all-gather.41.cloned.1.call-start = ((), (), s32[]{:S(2)}) async-start(), calls=%async_computation.24 | async-start | bytes 2949120 | tf_op jit(solution)/shard_map/all_gather | solution.py:68
  556.6 82.5 %reduce-scatter.33.cloned.1.call-start = ((), (), s32[]{:S(2)}) async-start(), calls=%async_computation.25 | async-start | bytes 2949120 | tf_op jit(solution)/shard_map/reduce_scatter | solution.py:81
  556.9 28.0 %copy-start.12 = (f32[3,4,128,128]{2,3,1,0:T(8,128)S(1)}, f32[3,4,128,128]{2,3,1,0:T(8,128)}, u32[]{:S(2)}) copy-start(f32[3,4,128,128]{2,3,1,0:T(8,128)} %copy-done.11) | copy-start | bytes 2359300
  586.3 11.2 copy-start.38
  588.2 10.3 copy-start.42
  590.2 9.1 copy-start.59
  605.8 33.2 %copy-start.15 = (f32[288,1024]{1,0:T(8,128)S(1)}, f32[288,1024]{1,0:T(8,128)}, u32[]{:S(2)}) copy-start(f32[288,1024]{1,0:T(8,128)} %get-tuple-element.55) | copy-start | bytes 3538948
  605.9 61.9 %all-gather.43.cloned.1.call-start = ((), (), s32[]{:S(2)}) async-start(), calls=%async_computation.26 | async-start | bytes 2949120 | tf_op jit(solution)/shard_map/all_gather | solution.py:68
  643.5 70.6 %reduce-scatter.35.cloned.1.call-start = ((), (), s32[]{:S(2)}) async-start(), calls=%async_computation.27 | async-start | bytes 2949120 | tf_op jit(solution)/shard_map/reduce_scatter | solution.py:81
  667.7 9.2 copy-start.163
  680.8 33.2 %copy-start.7 = (bf16[288,1024]{1,0:T(8,128)(2,1)S(1)}, bf16[288,1024]{1,0:T(8,128)(2,1)}, u32[]{:S(2)}) copy-start(bf16[288,1024]{1,0:T(8,128)(2,1)} %reduce-scatter.23.cloned.1.call-done) | copy-start | bytes 1769476
  680.8 33.2 %copy-start.110 = (f32[288]{0:T(512)S(1)}, f32[288]{0:T(512)}, u32[]{:S(2)}) copy-start(f32[288]{0:T(512)} %copy-done.109) | copy-start | bytes 3460
  680.8 33.2 %copy-start.115 = (f32[288]{0:T(512)S(1)}, f32[288]{0:T(512)}, u32[]{:S(2)}) copy-start(f32[288]{0:T(512)} %copy-done.114) | copy-start | bytes 3460
  680.9 102.0 %all-gather.45.cloned.1.call-start = ((), (), s32[]{:S(2)}) async-start(), calls=%async_computation.28 | async-start | bytes 2949120 | tf_op jit(solution)/shard_map/all_gather | solution.py:68
  721.0 177.4 %reduce-scatter.43.cloned.1.call-start = ((), (), s32[]{:S(2)}) async-start(), calls=%async_computation.33 | async-start | bytes 9437184 | tf_op jit(solution)/shard_map/reduce_scatter | solution.py:395
  735.4 314.9 %reduce-scatter.45.cloned.1.call-start = ((), (), s32[]{:S(2)}) async-start(), calls=%async_computation.35 | async-start | bytes 9437184 | tf_op jit(solution)/shard_map/reduce_scatter | solution.py:401
  774.1 397.7 %reduce-scatter.39.cloned.1.call-start = ((), (), s32[]{:S(2)}) async-start(), calls=%async_computation.30 | async-start | bytes 7077888 | tf_op jit(solution)/shard_map/reduce_scatter | solution.py:383
  833.7 402.2 %reduce-scatter.47.cloned.1.call-start = ((), (), s32[]{:S(2)}) async-start(), calls=%async_computation.43 | async-start | bytes 73728
  834.8 14.7 copy-start.94
  834.8 14.7 copy-start.167
  834.8 14.7 copy-start.170
  836.1 465.0 %reduce-scatter.49.cloned.1.call-start = ((), (), s32[]{:S(2)}) async-start(), calls=%async_computation.44 | async-start | bytes 589824
  849.4 515.8 %reduce-scatter.51.cloned.1.call-start = ((), (), s32[]{:S(2)}) async-start(), calls=%async_computation.45 | async-start | bytes 589824
  854.5 582.7 %reduce-scatter.41.cloned.1.call-start = ((), (), s32[]{:S(2)}) async-start(), calls=%async_computation.32 | async-start | bytes 2359296 | tf_op jit(solution)/shard_map/reduce_scatter | solution.py:389
  862.2 610.4 %reduce-scatter.37.cloned.1.call-start = ((), (), s32[]{:S(2)}) async-start(), calls=%async_computation.29 | async-start | bytes 2949120 | tf_op jit(solution)/shard_map/reduce_scatter | solution.py:81
  869.9 650.8 %all-gather.49.cloned.1.call-start = ((), (), s32[]{:S(2)}) async-start(), calls=%async_computation.34 | async-start | bytes 2621440 | tf_op jit(solution)/shard_map/all_gather | solution.py:439
  900.4 273.4 %copy-start.171 = (u32[32]{0:T(128)S(1)}, u32[32]{0:T(128)}, u32[]{:S(2)}) copy-start(u32[32]{0:T(128)} %constant.57) | copy-start | bytes 388
  900.4 274.6 %copy-start.39 = (bf16[3,128,4,64]{1,3,2,0:T(8,128)(2,1)S(1)}, bf16[3,128,4,64]{1,3,2,0:T(8,128)(2,1)}, u32[]{:S(2)}) copy-start(bf16[3,128,4,64]{1,3,2,0:T(8,128)(2,1)} %copy-done.38) | copy-start | bytes 589828
  900.4 274.8 %copy-start.43 = (bf16[3,128,4,64]{1,3,2,0:T(8,128)(2,1)S(1)}, bf16[3,128,4,64]{1,3,2,0:T(8,128)(2,1)}, u32[]{:S(2)}) copy-start(bf16[3,128,4,64]{1,3,2,0:T(8,128)(2,1)} %copy-done.42) | copy-start | bytes 589828
  900.4 666.7 %all-gather.51.cloned.1.call-start = ((), (), s32[]{:S(2)}) async-start(), calls=%async_computation.36 | async-start | bytes 2621440 | tf_op jit(solution)/shard_map/all_gather | solution.py:442
  1052.4 123.0 %copy-start.29 = (bf16[4,64,512]{2,1,0:T(8,128)(2,1)S(1)}, bf16[4,64,512]{2,1,0:T(8,128)(2,1)}, u32[]{:S(2)}) copy-start(bf16[4,64,512]{2,1,0:T(8,128)(2,1)} %copy-done.28) | copy-start | bytes 786436
  1052.4 123.0 %copy-start.52 = (bf16[4,64,256]{2,1,0:T(8,128)(2,1)S(1)}, bf16[4,64,256]{2,1,0:T(8,128)(2,1)}, u32[]{:S(2)}) copy-start(bf16[4,64,256]{2,1,0:T(8,128)(2,1)} %copy-done.51) | copy-start | bytes 393220
  1052.5 123.3 %copy-start.31 = (bf16[4,64,512]{2,1,0:T(8,128)(2,1)S(1)}, bf16[4,64,512]{2,1,0:T(8,128)(2,1)}, u32[]{:S(2)}) copy-start(bf16[4,64,512]{2,1,0:T(8,128)(2,1)} %copy-done.30) | copy-start | bytes 786436
  1052.5 123.3 %copy-start.60 = (bf16[4,64,256]{2,1,0:T(8,128)(2,1)S(1)}, bf16[4,64,256]{2,1,0:T(8,128)(2,1)}, u32[]{:S(2)}) copy-start(bf16[4,64,256]{2,1,0:T(8,128)(2,1)} %copy-done.59) | copy-start | bytes 393220
  1052.5 551.6 %all-gather.47.cloned.1.call-start = ((), (), s32[]{:S(2)}) async-start(), calls=%async_computation.31 | async-start | bytes 1966080 | tf_op jit(solution)/shard_map/all_gather | solution.py:433
  1173.7 203.0 %copy-start.41 = (bf16[3,128,4,64]{1,3,2,0:T(8,128)(2,1)S(1)}, bf16[3,128,4,64]{1,3,2,0:T(8,128)(2,1)}, u32[]{:S(2)}) copy-start(bf16[3,128,4,64]{1,3,2,0:T(8,128)(2,1)} %copy-done.40) | copy-start | bytes 589828
  1173.8 203.2 %copy-start.45 = (bf16[3,128,4,64]{1,3,2,0:T(8,128)(2,1)S(1)}, bf16[3,128,4,64]{1,3,2,0:T(8,128)(2,1)}, u32[]{:S(2)}) copy-start(bf16[3,128,4,64]{1,3,2,0:T(8,128)(2,1)} %copy-done.44) | copy-start | bytes 589828
  1175.4 201.8 %copy-start.54 = (bf16[4,64,256]{2,1,0:T(8,128)(2,1)S(1)}, bf16[4,64,256]{2,1,0:T(8,128)(2,1)}, u32[]{:S(2)}) copy-start(bf16[4,64,256]{2,1,0:T(8,128)(2,1)} %copy-done.53) | copy-start | bytes 393220
  1175.6 201.8 %copy-start.33 = (bf16[4,64,512]{2,1,0:T(8,128)(2,1)S(1)}, bf16[4,64,512]{2,1,0:T(8,128)(2,1)}, u32[]{:S(2)}) copy-start(bf16[4,64,512]{2,1,0:T(8,128)(2,1)} %copy-done.32) | copy-start | bytes 786436
  1377.3 95.3 %copy-start.14 = (f32[288,1024]{1,0:T(8,128)S(1)}, f32[288,1024]{1,0:T(8,128)}, u32[]{:S(2)}) copy-start(f32[288,1024]{1,0:T(8,128)} %copy-done.13) | copy-start | bytes 3538948
  (143 other events, 318.6 us)
Sparse Core Ops, SparseCore 0:
  12.2 33.7 all-gather.52
  60.1 34.5 reduce-scatter.22
  96.9 33.8 all-gather.54
  132.9 24.0 all-gather.32
  159.0 33.1 all-gather.56
  198.6 33.0 reduce-scatter.24
  233.8 31.0 all-gather.58
  267.0 24.0 all-gather.34
  307.6 33.0 reduce-scatter.26
  342.8 33.1 all-gather.60
  378.1 24.0 all-gather.36
  403.7 33.1 all-gather.62
  443.3 33.0 reduce-scatter.28
  481.5 24.0 all-gather.38
  518.9 33.0 reduce-scatter.30
  556.7 24.0 all-gather.40
  606.0 33.0 reduce-scatter.32
  643.6 24.0 all-gather.42
  681.0 33.0 reduce-scatter.34
  721.1 24.0 all-gather.44
  749.2 149.0 reduce-scatter.42
  901.9 148.3 reduce-scatter.44
  1054.4 117.3 reduce-scatter.38
  1175.4 60.4 reduce-scatter.46
  1240.1 60.8 reduce-scatter.48
  1304.3 60.8 reduce-scatter.50
  1369.6 67.6 reduce-scatter.40
  1440.5 32.0 reduce-scatter.36
  1474.8 45.9 all-gather.48
  1522.2 44.9 all-gather.50
  1568.7 35.3 all-gather.46
where the time goes:
time: 1620 us; the launch traced here: 1610 us
  waiting for transfers between devices  1110 us (69%)
  blocking collectives  155 us (10%)
  matrix products  139 us (9%)
  local copies, waits for them, and re-layouts  112 us (7%)
  other arithmetic  75.3 us (5%)
  between operations  18.4 us (1%)
    unnamed x34, waiting for transfers between devices  165 us
    reduce_scatter x1, waiting for transfers between devices, per_device(): lax.psum_scatter(regroup(stacked[3], 2, fsdp_size, data_size), ('dp', 'fs...  150 us
    reduce_scatter x1, waiting for transfers between devices, per_device(): lax.psum_scatter(regroup(stacked[0], 2, fsdp_size, data_size), ('dp', 'fs...  119 us
    reduce_scatter x4, waiting for transfers between devices, reduce_back(): lax.psum_scatter(term_fn(jnp.int32(0), lax.axis_size('tensor') * share_ro...  118 us
    reduce_scatter x4, waiting for transfers between devices, reduce_rows(): lax.psum_scatter(term_fn(jnp.int32(0), lax.axis_size('tensor') * share_ro...  111 us
    all_gather x3, waiting for transfers between devices, spread_rows(): return lax.all_gather(share_low, 'tensor', axis=0, tiled=True)  78.7 us
    all_gather x4, waiting for transfers between devices, spread_back(): return lax.all_gather(share_low, 'tensor', axis=0, tiled=True)  72 us
    all_gather x2, waiting for transfers between devices, fetch_layer(): lax.all_gather(w_shrink, 'fsdp', axis=1, tiled=True)  53.2 us
  transfers between devices with their start and end apart: 31, of which 30 were waited for; matrix products, arithmetic and copies ran while one was open for 12% of the time, Pallas kernels for 0%

commit v1 on v0

v1 whole, which is shorter than its diff:
```python
import jax
import jax.numpy as jnp
from jax import lax
from jax.sharding import PartitionSpec as P

HEAD = 64
LAYERS = 2
LEN_A = 512
LEN_B = 256
LEN_C = 128
PAGES_A = 1
PAGES_B = 1
PAGES_C = 3
BF = jnp.bfloat16
F32 = jnp.float32
CORE_SWAP = [(0, 1), (1, 0), (2, 3), (3, 2)]
CHIP_SWAP = [(0, 2), (2, 0), (1, 3), (3, 1)]


def to_core(value):
    return lax.ppermute(value, "tensor", CORE_SWAP)


def to_chip(value):
    return lax.ppermute(value, "tensor", CHIP_SWAP)


def from_fsdp(value, step):
    size = lax.axis_size("fsdp")
    return lax.ppermute(value, "fsdp", [((i + step) % size, i) for i in range(size)])


def to_fsdp(value, step):
    size = lax.axis_size("fsdp")
    return lax.ppermute(value, "fsdp", [(i, (i + step) % size) for i in range(size)])


def gather_own_first(shard, axis):
    size = lax.axis_size("fsdp")
    return jnp.concatenate([shard] + [from_fsdp(shard, step) for step in range(1, size)], axis)


def own_first(whole, axis):
    size = lax.axis_size("fsdp")
    here = lax.axis_index("fsdp")
    width = whole.shape[axis] // size
    return jnp.concatenate(
        [lax.dynamic_slice_in_dim(whole, (here + k) % size * width, width, axis) for k in range(size)], axis
    )


def natural(relative, axis):
    size = lax.axis_size("fsdp")
    here = lax.axis_index("fsdp")
    width = relative.shape[axis] // size
    return jnp.concatenate(
        [
            lax.dynamic_slice_in_dim(relative, (k - here + size) % size * width, width, axis)
            for k in range(size)
        ],
        axis,
    )


def swap_slots(rows):
    here = lax.axis_index("tensor")
    share = rows.shape[0] // 4
    return jnp.concatenate(
        [lax.dynamic_slice_in_dim(rows, (here ^ k) * share, share, 0) for k in range(4)], 0
    )


def layer_norm(hidden, gain_row, bias_row):
    center = hidden - jnp.mean(hidden, -1, keepdims=True)
    inverse = lax.rsqrt(jnp.mean(center * center, -1, keepdims=True) + 1e-05)
    normed = center * inverse
    return (normed * gain_row + bias_row, normed, inverse)


def norm_back(grad_result, normed, inverse, gain_row):
    grad_norm = grad_result * gain_row
    mean_one = jnp.mean(grad_norm, -1, keepdims=True)
    mean_two = jnp.mean(grad_norm * normed, -1, keepdims=True)
    grad_in = inverse * (grad_norm - mean_one - normed * mean_two)
    return (grad_in, jnp.sum(grad_result * normed, 0), jnp.sum(grad_result, 0))


def gelu_parts(upward):
    cdf_val = 0.5 * (1.0 + lax.erf(upward * 0.7071067811865476))
    density = jnp.exp(-0.5 * upward * upward) * 0.3989422804014327
    return (upward * cdf_val, cdf_val + upward * density)


def dot(left, right):
    return jnp.dot(left, right, preferred_element_type=F32)


def dot_t(left, right):
    return lax.dot_general(left, right, (((1,), (1,)), ((), ())), preferred_element_type=F32)


def dot_rows(left, right):
    return lax.dot_general(left, right, (((0,), (0,)), ((), ())), preferred_element_type=F32)


def gather_rows(share):
    across = to_chip(share)
    return (
        jnp.concatenate([share, to_core(share)], 0),
        jnp.concatenate([across, to_core(across)], 0),
    )


def reduce_rows(part_here, part_there):
    there = part_there()
    share = there.shape[0] // 2
    from_core = to_core(there[share:].astype(BF))
    from_chip = to_chip((there[:share] + from_core.astype(F32)).astype(BF))
    here = part_here()
    own = to_core(here[share:].astype(BF))
    return here[:share] + own.astype(F32) + from_chip.astype(F32)


def bucket_scores(query_heads, key_heads, page_lengths, length):
    scores = jnp.einsum(
        "plhe,pmhe->phlm", query_heads, key_heads, preferred_element_type=jnp.float32
    ) * HEAD ** (-0.5)
    valid_keys = (
        jnp.arange(length, dtype=jnp.int32)[None, None, None, :] < page_lengths[:, None, None, None]
    )
    return jnp.where(valid_keys, scores, -1000000000.0)


def attention_forward(queries, keys_b, values_b, page_lengths):
    heads_here = queries.shape[1] // HEAD
    outputs = []
    log_totals = []
    row_at = 0
    page_at = 0
    for amount, length in ((PAGES_A, LEN_A), (PAGES_B, LEN_B), (PAGES_C, LEN_C)):
        span_rows = amount * length
        head_shape = (amount, length, heads_here, HEAD)
        query_heads = queries[row_at : row_at + span_rows].reshape(head_shape)
        key_heads = keys_b[row_at : row_at + span_rows].reshape(head_shape)
        value_heads = values_b[row_at : row_at + span_rows].reshape(head_shape)
        scores = bucket_scores(
            query_heads, key_heads, page_lengths[page_at : page_at + amount], length
        )
        row_peak = jnp.max(scores, -1, keepdims=True)
        exponent = jnp.exp(scores - row_peak)
        row_total = jnp.sum(exponent, -1, keepdims=True)
        attn_low = (exponent / row_total).astype(jnp.bfloat16)
        context = jnp.einsum(
            "phlm,pmhe->plhe", attn_low, value_heads, preferred_element_type=jnp.float32
        )
        outputs.append(context.reshape(span_rows, heads_here * HEAD))
        log_totals.append(row_peak + jnp.log(row_total))
        row_at += span_rows
        page_at += amount
    return (jnp.concatenate(outputs, 0).astype(jnp.bfloat16), log_totals)


def attention_backward(queries, keys_b, values_b, page_lengths, log_totals, grad_context):
    heads_here = queries.shape[1] // HEAD
    grad_q_list = []
    grad_k_list = []
    grad_v_list = []
    row_at = 0
    page_at = 0
    bucket_index = 0
    for amount, length in ((PAGES_A, LEN_A), (PAGES_B, LEN_B), (PAGES_C, LEN_C)):
        span_rows = amount * length
        head_shape = (amount, length, heads_here, HEAD)
        query_heads = queries[row_at : row_at + span_rows].reshape(head_shape)
        key_heads = keys_b[row_at : row_at + span_rows].reshape(head_shape)
        value_heads = values_b[row_at : row_at + span_rows].reshape(head_shape)
        grad_heads = grad_context[row_at : row_at + span_rows].reshape(head_shape)
        scores = bucket_scores(
            query_heads, key_heads, page_lengths[page_at : page_at + amount], length
        )
        attn_probs = jnp.exp(scores - log_totals[bucket_index])
        attn_low = attn_probs.astype(jnp.bfloat16)
        grad_values = jnp.einsum(
            "phlm,plhe->pmhe", attn_low, grad_heads, preferred_element_type=jnp.float32
        )
        grad_probs = jnp.einsum(
            "plhe,pmhe->phlm", grad_heads, value_heads, preferred_element_type=jnp.float32
        )
        grad_scores = (
            attn_probs * (grad_probs - jnp.sum(attn_probs * grad_probs, -1, keepdims=True))
        ).astype(jnp.bfloat16)
        grad_queries = jnp.einsum(
            "phlm,pmhe->plhe", grad_scores, key_heads, preferred_element_type=jnp.float32
        ) * HEAD ** (-0.5)
        grad_keys = jnp.einsum(
            "phlm,plhe->pmhe", grad_scores, query_heads, preferred_element_type=jnp.float32
        ) * HEAD ** (-0.5)
        grad_q_list.append(grad_queries.reshape(span_rows, heads_here * HEAD))
        grad_k_list.append(grad_keys.reshape(span_rows, heads_here * HEAD))
        grad_v_list.append(grad_values.reshape(span_rows, heads_here * HEAD))
        row_at += span_rows
        page_at += amount
        bucket_index += 1
    return (
        jnp.concatenate(grad_q_list, 0).astype(jnp.bfloat16),
        jnp.concatenate(grad_k_list, 0).astype(jnp.bfloat16),
        jnp.concatenate(grad_v_list, 0).astype(jnp.bfloat16),
    )


def halves(rows):
    half = rows.shape[0] // 2
    return rows[:half], rows[half:]


def layer_forward(weights, small, inputs, inputs_share, page_lengths):
    w_proj, w_mix, w_grow, w_shrink = weights
    bias_q, bias_v, bias_grow, gains, biases = small
    inputs_here, inputs_there = inputs
    half = inputs_here.shape[0]
    width = w_proj.shape[2]

    def project(rows):
        queries = (dot(rows, w_proj[0]) + bias_q).astype(BF)
        keys_b = dot(rows, w_proj[1]).astype(BF)
        values_b = (dot(rows, w_proj[2]) + bias_v).astype(BF)
        return jnp.concatenate([queries, keys_b, values_b], 1)

    qkv = swap_slots(jnp.concatenate([project(inputs_here), project(inputs_there)], 0))
    queries, keys_b, values_b = qkv[:, :width], qkv[:, width : 2 * width], qkv[:, 2 * width :]
    context, log_totals = attention_forward(queries, keys_b, values_b, page_lengths)
    context_own = swap_slots(context)
    attn_share = reduce_rows(
        lambda: dot(context_own[:half], w_mix), lambda: dot(context_own[half:], w_mix)
    )
    y_one, normed_one, inverse_one = layer_norm(
        inputs_share + attn_share + biases[0], gains[0], biases[2]
    )
    middle = gather_rows(y_one.astype(BF))

    def grow(rows):
        activated, slope = gelu_parts(dot(rows, w_grow) + bias_grow)
        return activated.astype(BF), slope

    act_here, slope_here = grow(middle[0])
    act_there, slope_there = grow(middle[1])
    down_share = reduce_rows(lambda: dot(act_here, w_shrink), lambda: dot(act_there, w_shrink))
    result, normed_two, inverse_two = layer_norm(
        y_one + down_share + biases[1], gains[1], biases[3]
    )
    kept = (
        inputs,
        (queries, keys_b, values_b),
        log_totals,
        context_own,
        normed_one,
        inverse_one,
        middle,
        (slope_here, slope_there),
        (act_here, act_there),
        normed_two,
        inverse_two,
    )
    return result, kept


def layer_backward(weights, small, kept, grad_result, page_lengths):
    w_proj, w_mix, w_grow, w_shrink = weights
    bias_q, bias_v, bias_grow, gains, biases = small
    (
        inputs,
        qkv,
        log_totals,
        context_own,
        normed_one,
        inverse_one,
        middle,
        slopes,
        acts,
        normed_two,
        inverse_two,
    ) = kept
    half = inputs[0].shape[0]
    grad_two, grad_gain_two, grad_bias_two = norm_back(grad_result, normed_two, inverse_two, gains[1])
    grad_down_bias = jnp.sum(grad_two, 0)
    grad_down = gather_rows(grad_two.astype(BF))
    grad_up = [
        (dot_t(grad_down[i], w_shrink) * slopes[i]).astype(BF) for i in range(2)
    ]
    grad_middle = reduce_rows(lambda: dot_t(grad_up[0], w_grow), lambda: dot_t(grad_up[1], w_grow))
    grad_down_all = jnp.concatenate(grad_down, 0)
    grad_up_all = jnp.concatenate(grad_up, 0)
    grad_shrink = dot_rows(jnp.concatenate(acts, 0), grad_down_all).astype(BF)
    grad_grow = dot_rows(jnp.concatenate(middle, 0), grad_up_all).astype(BF)
    grad_grow_bias = jnp.sum(grad_up_all, 0, dtype=F32)
    grad_one, grad_gain_one, grad_bias_one = norm_back(
        grad_middle + grad_two, normed_one, inverse_one, gains[0]
    )
    grad_mix_bias = jnp.sum(grad_one, 0)
    grad_mix_rows = gather_rows(grad_one.astype(BF))
    grad_context = swap_slots(
        jnp.concatenate([dot_t(grad_mix_rows[i], w_mix).astype(BF) for i in range(2)], 0)
    )
    grad_mix = dot_rows(context_own, jnp.concatenate(grad_mix_rows, 0)).astype(BF)
    grads = attention_backward(*qkv, page_lengths, log_totals, grad_context)
    grad_qkv = swap_slots(jnp.concatenate(grads, 1))
    w_flat = jnp.concatenate([w_proj[0], w_proj[1], w_proj[2]], 1)
    grad_input = (
        reduce_rows(lambda: dot_t(grad_qkv[:half], w_flat), lambda: dot_t(grad_qkv[half:], w_flat))
        + grad_one
    )
    inputs_all = jnp.concatenate(inputs, 0)
    grad_proj = jnp.stack([dot_rows(inputs_all, g) for g in jnp.split(grad_qkv, 3, 1)]).astype(BF)
    column_sums = jnp.sum(grad_qkv, 0, dtype=F32)
    width = w_mix.shape[0]
    grad_heads_bias = jnp.stack([column_sums[:width], column_sums[2 * width :]])
    grad_gain_pair = jnp.stack([grad_gain_one, grad_gain_two])
    grad_bias_set = jnp.stack([grad_mix_bias, grad_down_bias, grad_bias_one, grad_bias_two])
    return grad_input, (
        (grad_proj, grad_mix, grad_grow, grad_shrink),
        (grad_heads_bias, grad_grow_bias, grad_gain_pair, grad_bias_set),
    )


def sum_line(value):
    size = lax.axis_size("dp")
    here = lax.axis_index("dp")
    middle = size // 2
    for step in range(middle - 1):
        came = lax.ppermute(value, "dp", [(step, step + 1), (size - 1 - step, size - 2 - step)])
        value = (value.astype(F32) + came.astype(F32)).astype(BF)
    came = lax.ppermute(value, "dp", [(middle - 1, middle), (middle, middle - 1)])
    value = (value.astype(F32) + came.astype(F32)).astype(BF)
    for step in reversed(range(middle - 1)):
        came = lax.ppermute(value, "dp", [(step + 1, step), (size - 2 - step, size - 1 - step)])
        takes = (here == step) | (here == size - 1 - step)
        value = jnp.where(takes, came, value)
    return value


def sum_weight(grad, axis):
    size = lax.axis_size("fsdp")
    width = grad.shape[axis] // size
    total = lax.slice_in_dim(grad, 0, width, axis=axis).astype(F32)
    for step in range(1, size):
        piece = lax.slice_in_dim(grad, step * width, (step + 1) * width, axis=axis)
        total = total + to_fsdp(piece, step).astype(F32)
    return sum_line(total.astype(BF)).astype(F32)


def per_device(
    activations, cotangent, lengths, w_qkv, w_out, w_up, w_down, b_qv, b_up, norm_gains, layer_biases
):
    fsdp_size = lax.axis_size("fsdp")
    fsdp_here = lax.axis_index("fsdp")
    share_rows = activations.shape[0] // lax.axis_size("tensor")
    half = 2 * share_rows

    smalls = (b_qv, b_up, norm_gains, layer_biases)
    flat = jnp.concatenate([value.reshape(-1) for value in smalls])
    pieces = [flat] + [from_fsdp(flat, step) for step in range(1, fsdp_size)]

    def unpack(at):
        found, start = [], 0
        for value in smalls:
            found.append(pieces[at][start : start + value.size].reshape(value.shape))
            start += value.size
        return found

    unpacked = [unpack(at) for at in range(fsdp_size)]
    bias_heads, bias_grow, gains, biases = (
        jnp.concatenate([u[i] for u in unpacked], -1).astype(F32) for i in range(4)
    )
    bias_heads, bias_grow = natural(bias_heads, 3), natural(bias_grow, 2)

    inputs_all = own_first(swap_slots(activations), 1)
    inputs = (inputs_all[:half], inputs_all[half:])
    inputs_share = inputs_all[:share_rows].astype(F32)
    grad_share = own_first(cotangent, 1).astype(F32)

    fetched, small_all, kept_all = [], [], []
    for layer in range(LAYERS):
        weights = (
            gather_own_first(w_qkv[layer], 1),
            gather_own_first(w_out[layer], 1),
            gather_own_first(w_up[layer], 0),
            gather_own_first(w_down[layer], 1),
        )
        small = (
            bias_heads[layer, 0].reshape(-1),
            bias_heads[layer, 1].reshape(-1),
            bias_grow[layer].reshape(-1),
            gains[layer],
            biases[layer],
        )
        result, kept = layer_forward(weights, small, inputs, inputs_share, lengths)
        fetched.append(weights)
        small_all.append(small)
        kept_all.append(kept)
        inputs_share = result
        if layer + 1 < LAYERS:
            inputs = gather_rows(result.astype(BF))
    layer_out = natural(inputs_share.astype(BF), 1)
    big, little = [None] * LAYERS, [None] * LAYERS
    for layer in reversed(range(LAYERS)):
        grad_share, (grads, little[layer]) = layer_backward(
            fetched[layer], small_all[layer], kept_all[layer], grad_share, lengths
        )
        big[layer] = [sum_weight(grad, axis) for grad, axis in zip(grads, (1, 1, 0, 1))]
    stacked = [jnp.stack([big[layer][i] for layer in range(LAYERS)]) for i in range(4)]

    heads_bias = jnp.stack([little[layer][0] for layer in range(LAYERS)]).reshape(bias_heads.shape)
    grow_bias = jnp.stack([little[layer][1] for layer in range(LAYERS)]).reshape(bias_grow.shape)
    gain_pair = jnp.stack([little[layer][2] for layer in range(LAYERS)])
    bias_set = jnp.stack([little[layer][3] for layer in range(LAYERS)])
    norms = jnp.concatenate([gain_pair.reshape(-1, gain_pair.shape[-1]), bias_set.reshape(-1, bias_set.shape[-1])])
    norms = norms + to_core(norms)
    norms = norms + to_chip(norms)
    own_heads, own_grow = own_first(heads_bias, 3), own_first(grow_bias, 2)
    little_all = []
    for step in range(fsdp_size):
        parts = []
        for value in (own_heads, own_grow, norms):
            width = value.shape[-1] // fsdp_size
            parts.append(value[..., step * width : (step + 1) * width].reshape(-1))
        little_all.append(jnp.concatenate(parts))
    total = little_all[0]
    for step in range(1, fsdp_size):
        total = total + to_fsdp(little_all[step], step)
    total = lax.psum(total, "dp")
    count = [v.size // fsdp_size for v in (own_heads, own_grow, gain_pair, bias_set)]
    shapes = [v.shape[:-1] + (v.shape[-1] // fsdp_size,) for v in (own_heads, own_grow, gain_pair, bias_set)]
    finals, start = [], 0
    for amount, shape in zip(count, shapes):
        finals.append(total[start : start + amount].reshape(shape))
        start += amount
    return (layer_out, natural(grad_share, 1), *stacked, *finals)


def solution(mesh):
    in_specs = (
        P(("dp", "fsdp"), None),
        P(("dp", "fsdp", "tensor"), None),
        P(("dp", "fsdp")),
        P(None, None, "fsdp", "tensor"),
        P(None, "tensor", "fsdp"),
        P(None, "fsdp", "tensor"),
        P(None, "tensor", "fsdp"),
        P(None, None, "tensor", "fsdp"),
        P(None, "tensor", "fsdp"),
        P(None, None, "fsdp"),
        P(None, None, "fsdp"),
    )
    out_specs = (
        P(("dp", "fsdp", "tensor"), None),
        P(("dp", "fsdp", "tensor"), None),
        P(None, None, "fsdp", "tensor"),
        P(None, "tensor", "fsdp"),
        P(None, "fsdp", "tensor"),
        P(None, "tensor", "fsdp"),
        P(None, None, "tensor", "fsdp"),
        P(None, "tensor", "fsdp"),
        P(None, None, "fsdp"),
        P(None, None, "fsdp"),
    )
    return jax.shard_map(
        per_device, mesh=mesh, in_specs=in_specs, out_specs=out_specs, check_vma=False
    )
```

time: 1620 us -> 867 us (0.54)
  waiting for transfers between devices: 1110 us -> 361 us
  blocking collectives: 155 us -> 30.6 us
  starting transfers between devices: 2.5 us -> 93.7 us
  other arithmetic: 75.3 us -> 125 us
  local copies, waits for them, and re-layouts: 112 us -> 95.4 us
    reduce_scatter x12 -> x0, waiting for transfers between devices: 553 us -> none  [the longest x1 150 us: per_device(): lax.psum_scatter(regroup(stacked[3], 2, fsdp_size, data_size), ('dp', 'fs...]
    all_gather x16 -> x0, waiting for transfers between devices: 395 us -> none  [the longest x3 78.7 us: spread_rows(): return lax.all_gather(share_low, 'tensor', axis=0, tiled=True)]
    ppermute x0 -> x89, waiting for transfers between devices: none -> 361 us  [the longest x16 122 us: to_chip(): return lax.ppermute(value, 'tensor', CHIP_SWAP)]
    unnamed x34 -> x0, waiting for transfers between devices: 165 us -> none
    all_gather x15 -> x0, blocking collectives: 126 us -> none  [the longest x2 27.6 us: fetch_layer(): lax.all_gather(w_mix, 'fsdp', axis=1, tiled=True)]
    ppermute x0 -> x89, starting transfers between devices: none -> 93.7 us  [the longest x8 32.7 us: sum_line(): lax.ppermute(value, 'dp', [(step, step + 1), (size - 1 - step, size - 2 -...]
    concatenate x0 -> x27, other arithmetic: none -> 41.7 us  [the longest x2 28 us: layer_backward(): grad_qkv = swap_slots(jnp.concatenate(grads, 1))]
    transpose x7 -> x2, local copies, waits for them, and re-layouts: 26.3 us -> 0.34 us  [attention_backward(): jnp.einsum('phlm,plhe->pmhe', attn_low, grad_heads, preferred_element_typ...]
  transfers between devices with their start and end apart: 31 -> 89, of which waited for: 30 -> 31; matrix products, arithmetic and copies ran while one was open for 12% -> 37% of each run, Pallas kernels for 0% -> 0%
where the time goes in v1:
time: 867 us; the launch traced here: 855 us
  waiting for transfers between devices  361 us (42%)
  matrix products  144 us (17%)
  other arithmetic  125 us (14%)
  local copies, waits for them, and re-layouts  95.4 us (11%)
  starting transfers between devices  93.7 us (11%)
  blocking collectives  30.6 us (4%)
    ppermute x16, waiting for transfers between devices, to_chip(): return lax.ppermute(value, 'tensor', CHIP_SWAP)  122 us
    ppermute x9, waiting for transfers between devices, to_fsdp(): lax.ppermute(value, 'fsdp', [(i, (i + step) % size) for i in range(size)])  92.5 us
    ppermute x8, waiting for transfers between devices, sum_line(): lax.ppermute(value, 'dp', [(step + 1, step), (size - 2 - step, size - 1 -...  69.9 us
    ppermute x9, waiting for transfers between devices, from_fsdp(): lax.ppermute(value, 'fsdp', [((i + step) % size, i) for i in range(size)])  62.5 us
    dot_general x16, matrix products, dot_t(): lax.dot_general(left, right, (((1,), (1,)), ((), ())), preferred_element_...  42 us
    dot_general x24, matrix products, dot(): return jnp.dot(left, right, preferred_element_type=F32)  37.3 us
    ppermute x8, starting transfers between devices, sum_line(): lax.ppermute(value, 'dp', [(step, step + 1), (size - 1 - step, size - 2 -...  32.7 us
    psum x1, blocking collectives, per_device(): total = lax.psum(total, 'dp')  30.6 us
  transfers between devices with their start and end apart: 89, of which 31 were waited for; matrix products, arithmetic and copies ran while one was open for 37% of the time, Pallas kernels for 0%

profile of v1, /device:TPU:0, one launch (start us, length us, event | category | flops | bytes accessed | tf_op | source)
XLA Modules:
  0.0 854.9 jit_solution(4931942444640216869)
XLA Ops:
  3.7 3.0 collective-permute-start.1
  6.7 2.6 slice_bitcast_fusion.4
  19.5 10.6 %collective-permute-done = bf16[3,512,256]{2,1,0:T(8,128)(2,1)} collective-permute-done((bf16[3,512,256]{2,1,0:T(8,128)(2,1)}, bf16[3,512,256]{2,1,0:T(8,128)(2,1)}, u32[]{:S(2)}, u32[]{:S(2)}) %collective-permute-start) | collective-permute-done | bytes 786464 | tf_op jit(solution)/shard_map/ppermute | solution.py:30
  62.5 11.9 %collective-permute-done.5 = bf16[288,1024]{1,0:T(8,128)(2,1)S(1)} collective-permute-done((bf16[288,1024]{1,0:T(8,128)(2,1)}, bf16[288,1024]{1,0:T(8,128)(2,1)S(1)}, u32[]{:S(2)}, u32[]{:S(2)}) %collective-permute-start.5) | collective-permute-done | bytes 589856 | tf_op jit(solution)/shard_map/ppermute | solution.py:25
  81.4 11.4 %collective-permute-done.10 = bf16[288,1024]{1,0:T(8,128)(2,1)} collective-permute-done((bf16[288,1024]{1,0:T(8,128)(2,1)}, bf16[288,1024]{1,0:T(8,128)(2,1)}, u32[]{:S(2)}, u32[]{:S(2)}) %collective-permute-start.10) | collective-permute-done | bytes 589856 | tf_op jit(solution)/shard_map/ppermute | solution.py:25
  95.7 11.3 %collective-permute-done.7 = bf16[512,1024]{1,0:T(8,128)(2,1)} collective-permute-done((bf16[512,1024]{1,0:T(8,128)(2,1)S(1)}, bf16[512,1024]{1,0:T(8,128)(2,1)}, u32[]{:S(2)}, u32[]{:S(2)}) %collective-permute-start.7) | collective-permute-done | bytes 1048608 | tf_op jit(solution)/shard_map/ppermute | solution.py:30
  107.0 3.0 fusion.183
  110.0 5.5 multiply_convert_fusion.5
  115.5 11.8 %collective-permute-done.8 = bf16[1024,512]{1,0:T(8,128)(2,1)} collective-permute-done((bf16[1024,512]{1,0:T(8,128)(2,1)S(1)}, bf16[1024,512]{1,0:T(8,128)(2,1)}, u32[]{:S(2)}, u32[]{:S(2)}) %collective-permute-start.8) | collective-permute-done | bytes 1048608 | tf_op jit(solution)/shard_map/ppermute | solution.py:30
  127.3 2.6 fusion.355
  130.1 2.6 fusion.356
  135.1 13.9 %collective-permute-done.13 = bf16[288,1024]{1,0:T(8,128)(2,1)S(1)} collective-permute-done((bf16[288,1024]{1,0:T(8,128)(2,1)S(1)}, bf16[288,1024]{1,0:T(8,128)(2,1)S(1)}, u32[]{:S(2)}, u32[]{:S(2)}) %collective-permute-start.13) | collective-permute-done | bytes 589856 | tf_op jit(solution)/shard_map/ppermute | solution.py:25
  155.2 9.7 %collective-permute-done.16 = bf16[288,1024]{1,0:T(8,128)(2,1)S(1)} collective-permute-done((bf16[288,1024]{1,0:T(8,128)(2,1)S(1)}, bf16[288,1024]{1,0:T(8,128)(2,1)S(1)}, u32[]{:S(2)}, u32[]{:S(2)}) %collective-permute-start.16) | collective-permute-done | bytes 589856 | tf_op jit(solution)/shard_map/ppermute | solution.py:25
  196.9 14.0 %collective-permute-done.21 = bf16[288,1024]{1,0:T(8,128)(2,1)S(1)} collective-permute-done((bf16[288,1024]{1,0:T(8,128)(2,1)S(1)}, bf16[288,1024]{1,0:T(8,128)(2,1)S(1)}, u32[]{:S(2)}, u32[]{:S(2)}) %collective-permute-start.21) | collective-permute-done | bytes 589856 | tf_op jit(solution)/shard_map/ppermute | solution.py:25
  213.6 13.4 %collective-permute-done.26 = bf16[288,1024]{1,0:T(8,128)(2,1)S(1)} collective-permute-done((bf16[288,1024]{1,0:T(8,128)(2,1)S(1)}, bf16[288,1024]{1,0:T(8,128)(2,1)S(1)}, u32[]{:S(2)}, u32[]{:S(2)}) %collective-permute-start.26) | collective-permute-done | bytes 589856 | tf_op jit(solution)/shard_map/ppermute | solution.py:25
  228.1 11.0 %collective-permute-done.23 = bf16[512,1024]{1,0:T(8,128)(2,1)S(1)} collective-permute-done((bf16[512,1024]{1,0:T(8,128)(2,1)S(1)}, bf16[512,1024]{1,0:T(8,128)(2,1)S(1)}, u32[]{:S(2)}, u32[]{:S(2)}) %collective-permute-start.23) | collective-permute-done | bytes 1048608 | tf_op jit(solution)/shard_map/ppermute | solution.py:30
  240.5 3.4 multiply_convert_fusion.3
  244.0 15.8 %collective-permute-done.24 = bf16[1024,512]{1,0:T(8,128)(2,1)S(1)} collective-permute-done((bf16[1024,512]{1,0:T(8,128)(2,1)S(1)}, bf16[1024,512]{1,0:T(8,128)(2,1)S(1)}, u32[]{:S(2)}, u32[]{:S(2)}) %collective-permute-start.24) | collective-permute-done | bytes 1048608 | tf_op jit(solution)/shard_map/ppermute | solution.py:30
  270.5 10.3 %collective-permute-done.29 = bf16[288,1024]{1,0:T(8,128)(2,1)} collective-permute-done((bf16[288,1024]{1,0:T(8,128)(2,1)}, bf16[288,1024]{1,0:T(8,128)(2,1)}, u32[]{:S(2)}, u32[]{:S(2)}) %collective-permute-start.29) | collective-permute-done | bytes 589856 | tf_op jit(solution)/shard_map/ppermute | solution.py:25
  289.9 12.3 %collective-permute-done.32 = bf16[288,1024]{1,0:T(8,128)(2,1)} collective-permute-done((bf16[288,1024]{1,0:T(8,128)(2,1)}, bf16[288,1024]{1,0:T(8,128)(2,1)}, u32[]{:S(2)}, u32[]{:S(2)}) %collective-permute-start.32) | collective-permute-done | bytes 589856 | tf_op jit(solution)/shard_map/ppermute | solution.py:25
  302.2 2.6 concatenate.391
  304.8 4.8 fusion.9
  309.7 3.4 fusion.15
  315.2 3.0 fusion.100
  319.5 4.6 fusion.90
  328.4 16.0 %collective-permute-done.74 = bf16[512,1024]{1,0:T(8,128)(2,1)S(1)} collective-permute-done((bf16[512,1024]{1,0:T(8,128)(2,1)S(1)}, bf16[512,1024]{1,0:T(8,128)(2,1)S(1)}, u32[]{:S(2)}, u32[]{:S(2)}) %collective-permute-start.74) | collective-permute-done | bytes 1048608 | tf_op jit(solution)/shard_map/ppermute | solution.py:35
  344.8 3.7 collective-permute-start.75
  348.5 17.4 %collective-permute-done.82 = bf16[1024,512]{1,0:T(8,128)(2,1)S(1)} collective-permute-done((bf16[1024,512]{1,0:T(8,128)(2,1)S(1)}, bf16[1024,512]{1,0:T(8,128)(2,1)S(1)}, u32[]{:S(2)}, u32[]{:S(2)}) %collective-permute-start.82) | collective-permute-done | bytes 1048608 | tf_op jit(solution)/shard_map/ppermute | solution.py:35
  366.4 3.5 collective-permute-start.83
  376.4 11.9 %collective-permute-done.37 = bf16[288,1024]{1,0:T(8,128)(2,1)S(1)} collective-permute-done((bf16[288,1024]{1,0:T(8,128)(2,1)S(1)}, bf16[288,1024]{1,0:T(8,128)(2,1)S(1)}, u32[]{:S(2)}, u32[]{:S(2)}) %collective-permute-start.37) | collective-permute-done | bytes 589856 | tf_op jit(solution)/shard_map/ppermute | solution.py:25
  403.8 2.7 multiply_reduce_fusion.18
  413.3 3.1 fusion.136
  423.5 14.0 %maximum_maximum_fusion.2 = bf16[1152,768]{0,1:T(8,128)(2,1)S(1)} fusion(bf16[384,256]{0,1:T(8,128)(2,1)S(1)} %bitcast.397, bf16[256,256]{0,1:T(8,128)(2,1)S(1)} %bitcast.403, bf16[512,256]{0,1:T(8,128)(2,1)S(1)} %bitcast.377, bf16[384,256]{0,1:T(8,128)(2,1)S(1)} %bitcast.399, bf16[256,256]{0,1:T(8,128)(2,1)S(1)} %bitcast.405, ...), kind=kLoop, calls=%fused_computation.157 | loop fusion | flops 15925248 | bytes 3538944 | tf_op jit(solution)/shard_map/concatenate | solution.py:306
  438.9 3.0 fusion.242
  441.9 3.0 fusion.238
  444.9 3.4 concatenate.388
  464.3 4.6 collective-permute-start.67
  480.3 11.7 %collective-permute-done.58 = bf16[3,512,256]{2,1,0:T(8,128)(2,1)S(1)} collective-permute-done((bf16[3,512,256]{2,1,0:T(8,128)(2,1)}, bf16[3,512,256]{2,1,0:T(8,128)(2,1)S(1)}, u32[]{:S(2)}, u32[]{:S(2)}) %collective-permute-start.58) | collective-permute-done | bytes 786464 | tf_op jit(solution)/shard_map/ppermute | solution.py:35
  493.5 4.7 collective-permute-start.59
  505.4 20.1 %collective-permute-done.69 = bf16[256,512]{1,0:T(8,128)(2,1)S(1)} collective-permute-done((bf16[256,512]{1,0:T(8,128)(2,1)S(1)}, bf16[256,512]{1,0:T(8,128)(2,1)S(1)}, u32[]{:S(2)}, u32[]{:S(2)}) %collective-permute-start.69) | collective-permute-done | bytes 262176 | tf_op jit(solution)/shard_map/ppermute | solution.py:335
  529.5 3.3 fusion.21
  532.8 2.6 fusion.358
  538.1 6.4 collective-permute-done.85
  545.7 3.2 fusion.27
  548.9 2.6 fusion.357
  551.7 4.7 fusion.103
  558.5 3.4 fusion.95
  571.0 12.8 %collective-permute-done.70 = bf16[512,1024]{1,0:T(8,128)(2,1)} collective-permute-done((bf16[512,1024]{1,0:T(8,128)(2,1)S(1)}, bf16[512,1024]{1,0:T(8,128)(2,1)}, u32[]{:S(2)}, u32[]{:S(2)}) %collective-permute-start.70) | collective-permute-done | bytes 1048608 | tf_op jit(solution)/shard_map/ppermute | solution.py:35
  591.3 14.6 %collective-permute-done.78 = bf16[1024,512]{1,0:T(8,128)(2,1)} collective-permute-done((bf16[1024,512]{1,0:T(8,128)(2,1)}, bf16[1024,512]{1,0:T(8,128)(2,1)}, u32[]{:S(2)}, u32[]{:S(2)}) %collective-permute-start.78) | collective-permute-done | bytes 1048608 | tf_op jit(solution)/shard_map/ppermute | solution.py:35
  615.3 13.1 %collective-permute-done.87 = f32[12,1024]{1,0:T(8,128)S(1)} collective-permute-done((f32[12,1024]{1,0:T(8,128)S(1)}, f32[12,1024]{1,0:T(8,128)S(1)}, u32[]{:S(2)}, u32[]{:S(2)}) %collective-permute-start.87) | collective-permute-done | bytes 49184 | tf_op jit(solution)/shard_map/ppermute | solution.py:25
  631.6 2.6 add_convert_fusion.10
  654.8 3.1 fusion.133
  665.1 14.0 %maximum_maximum_fusion.3 = bf16[1152,768]{0,1:T(8,128)(2,1)S(1)} fusion(bf16[384,256]{0,1:T(8,128)(2,1)S(1)} %bitcast.398, bf16[256,256]{0,1:T(8,128)(2,1)S(1)} %bitcast.404, bf16[512,256]{0,1:T(8,128)(2,1)S(1)} %bitcast.378, bf16[384,256]{0,1:T(8,128)(2,1)S(1)} %bitcast.400, bf16[256,256]{0,1:T(8,128)(2,1)S(1)} %bitcast.406, ...), kind=kLoop, calls=%fused_computation.158 | loop fusion | flops 15925248 | bytes 3538944 | tf_op jit(solution)/shard_map/concatenate | solution.py:306
  681.2 3.0 fusion.250
  684.2 3.3 concatenate.386
  687.5 2.7 fusion.121
  703.6 18.3 %collective-permute-done.62 = bf16[256,512]{1,0:T(8,128)(2,1)} collective-permute-done((bf16[256,512]{1,0:T(8,128)(2,1)}, bf16[256,512]{1,0:T(8,128)(2,1)}, u32[]{:S(2)}, u32[]{:S(2)}) %collective-permute-start.62) | collective-permute-done | bytes 262176 | tf_op jit(solution)/shard_map/ppermute | solution.py:35
  725.7 3.1 fusion.246
  732.8 30.6 %psum.7 = f32[7680]{0:T(1024)S(1)} all-reduce(f32[7680]{0:T(1024)S(1)} %maximum_add_fusion), channel_id=1, replica_groups=mesh['dp'=4,'fsdp'=2,'tensor'=4] {'dp'}, use_global_device_ids=true, to_apply=%region_50.51 | all-reduce | flops 7680 | bytes 61440 | tf_op jit(solution)/shard_map/psum | solution.py:430
  772.0 9.3 %collective-permute-start.55 = (bf16[3,512,256]{2,1,0:T(8,128)(2,1)S(1)}, bf16[3,512,256]{2,1,0:T(8,128)(2,1)S(1)}, u32[]{:S(2)}, u32[]{:S(2)}) collective-permute-start(bf16[3,512,256]{2,1,0:T(8,128)(2,1)S(1)} %add_convert_fusion.17), channel_id=1, source_target_pairs={{0,8},{24,16},{1,9},{25,17},{2,10},{26,18},{3,11},{27,19},{4,12},{... | collective-permute-start | bytes 2359304 | tf_op jit(solution)/shard_map/ppermute | solution.py:330
  787.5 10.4 %collective-permute-done.55 = bf16[3,512,256]{2,1,0:T(8,128)(2,1)S(1)} collective-permute-done((bf16[3,512,256]{2,1,0:T(8,128)(2,1)S(1)}, bf16[3,512,256]{2,1,0:T(8,128)(2,1)S(1)}, u32[]{:S(2)}, u32[]{:S(2)}) %collective-permute-start.55) | collective-permute-done | bytes 786464 | tf_op jit(solution)/shard_map/ppermute | solution.py:330
  804.5 10.5 %collective-permute-done.73 = bf16[512,1024]{1,0:T(8,128)(2,1)S(1)} collective-permute-done((bf16[512,1024]{1,0:T(8,128)(2,1)S(1)}, bf16[512,1024]{1,0:T(8,128)(2,1)S(1)}, u32[]{:S(2)}, u32[]{:S(2)}) %collective-permute-start.73) | collective-permute-done | bytes 1048608 | tf_op jit(solution)/shard_map/ppermute | solution.py:335
  817.4 20.0 %collective-permute-done.81 = bf16[1024,512]{1,0:T(8,128)(2,1)S(1)} collective-permute-done((bf16[1024,512]{1,0:T(8,128)(2,1)S(1)}, bf16[1024,512]{1,0:T(8,128)(2,1)S(1)}, u32[]{:S(2)}, u32[]{:S(2)}) %collective-permute-start.81) | collective-permute-done | bytes 1048608 | tf_op jit(solution)/shard_map/ppermute | solution.py:335
  839.9 12.9 %collective-permute-done.57 = bf16[3,512,256]{2,1,0:T(8,128)(2,1)S(1)} collective-permute-done((bf16[3,512,256]{2,1,0:T(8,128)(2,1)S(1)}, bf16[3,512,256]{2,1,0:T(8,128)(2,1)S(1)}, u32[]{:S(2)}, u32[]{:S(2)}) %collective-permute-start.57) | collective-permute-done | bytes 786464 | tf_op jit(solution)/shard_map/ppermute | solution.py:335
  (921 shorter events, 318.1 us)
Async XLA Ops:
  9.3 20.8 %collective-permute-start = (bf16[3,512,256]{2,1,0:T(8,128)(2,1)}, bf16[3,512,256]{2,1,0:T(8,128)(2,1)}, u32[]{:S(2)}, u32[]{:S(2)}) collective-permute-start(bf16[3,512,256]{2,1,0:T(8,128)(2,1)} %get-tuple-element.75), channel_id=1, source_target_pairs={{4,0},{0,4},{5,1},{1,5},{6,2},{2,6},{7,3},{3,7},{12,8},{8,12},{13,... | collective-permute-start | bytes 2359304 | tf_op jit(solution)/shard_map/ppermute | solution.py:30
  10.3 38.5 %collective-permute-start.2 = (bf16[256,512]{1,0:T(8,128)(2,1)}, bf16[256,512]{1,0:T(8,128)(2,1)}, u32[]{:S(2)}, u32[]{:S(2)}) collective-permute-start(bf16[256,512]{1,0:T(8,128)(2,1)} %get-tuple-element.121), channel_id=1, source_target_pairs={{4,0},{0,4},{5,1},{1,5},{6,2},{2,6},{7,3},{3,7},{12,8},{8,12},{13,... | collective-permute-start | bytes 786440 | tf_op jit(solution)/shard_map/ppermute | solution.py:30
  59.0 15.4 %collective-permute-start.5 = (bf16[288,1024]{1,0:T(8,128)(2,1)}, bf16[288,1024]{1,0:T(8,128)(2,1)S(1)}, u32[]{:S(2)}, u32[]{:S(2)}) collective-permute-start(bf16[288,1024]{1,0:T(8,128)(2,1)} %fusion.175), channel_id=1, source_target_pairs={{0,2},{2,0},{1,3},{3,1},{4,6},{6,4},{5,7},{7,5},{8,10},{10,8},{9,1... | collective-permute-start | bytes 1769480 | tf_op jit(solution)/shard_map/ppermute | solution.py:25
  78.2 14.7 %collective-permute-start.10 = (bf16[288,1024]{1,0:T(8,128)(2,1)}, bf16[288,1024]{1,0:T(8,128)(2,1)}, u32[]{:S(2)}, u32[]{:S(2)}) collective-permute-start(bf16[288,1024]{1,0:T(8,128)(2,1)} %fusion.235), channel_id=1, source_target_pairs={{0,2},{2,0},{1,3},{3,1},{4,6},{6,4},{5,7},{7,5},{8,10},{10,8},{9,1... | collective-permute-start | bytes 1769480 | tf_op jit(solution)/shard_map/ppermute | solution.py:25
  80.8 26.2 %collective-permute-start.7 = (bf16[512,1024]{1,0:T(8,128)(2,1)S(1)}, bf16[512,1024]{1,0:T(8,128)(2,1)}, u32[]{:S(2)}, u32[]{:S(2)}) collective-permute-start(bf16[512,1024]{1,0:T(8,128)(2,1)S(1)} %get-tuple-element.54), channel_id=1, source_target_pairs={{4,0},{0,4},{5,1},{1,5},{6,2},{2,6},{7,3},{3,7},{12,8},{8,12},{13,... | collective-permute-start | bytes 3145736 | tf_op jit(solution)/shard_map/ppermute | solution.py:30
  81.4 28.6 %collective-permute-start.6 = (bf16[288,1024]{1,0:T(8,128)(2,1)}, bf16[288,1024]{1,0:T(8,128)(2,1)}, u32[]{:S(2)}, u32[]{:S(2)}) collective-permute-start(bf16[288,1024]{1,0:T(8,128)(2,1)} %fusion.235), channel_id=1, source_target_pairs={{0,1},{1,0},{2,3},{3,2},{4,5},{5,4},{6,7},{7,6},{8,9},{9,8},{10,11... | collective-permute-start | bytes 1769480 | tf_op jit(solution)/shard_map/ppermute | solution.py:21
  94.0 33.3 %collective-permute-start.8 = (bf16[1024,512]{1,0:T(8,128)(2,1)S(1)}, bf16[1024,512]{1,0:T(8,128)(2,1)}, u32[]{:S(2)}, u32[]{:S(2)}) collective-permute-start(bf16[1024,512]{1,0:T(8,128)(2,1)S(1)} %get-tuple-element.52), channel_id=1, source_target_pairs={{4,0},{0,4},{5,1},{1,5},{6,2},{2,6},{7,3},{3,7},{12,8},{8,12},{13,... | collective-permute-start | bytes 3145736 | tf_op jit(solution)/shard_map/ppermute | solution.py:30
  133.6 15.3 %collective-permute-start.13 = (bf16[288,1024]{1,0:T(8,128)(2,1)S(1)}, bf16[288,1024]{1,0:T(8,128)(2,1)S(1)}, u32[]{:S(2)}, u32[]{:S(2)}) collective-permute-start(bf16[288,1024]{1,0:T(8,128)(2,1)S(1)} %fusion.171), channel_id=1, source_target_pairs={{0,2},{2,0},{1,3},{3,1},{4,6},{6,4},{5,7},{7,5},{8,10},{10,8},{9,1... | collective-permute-start | bytes 1769480 | tf_op jit(solution)/shard_map/ppermute | solution.py:25
  134.4 19.5 %collective-permute-start.15 = (bf16[3,512,256]{2,1,0:T(8,128)(2,1)S(1)}, bf16[3,512,256]{2,1,0:T(8,128)(2,1)}, u32[]{:S(2)}, u32[]{:S(2)}) collective-permute-start(bf16[3,512,256]{2,1,0:T(8,128)(2,1)S(1)} %copy-done.27), channel_id=1, source_target_pairs={{4,0},{0,4},{5,1},{1,5},{6,2},{2,6},{7,3},{3,7},{12,8},{8,12},{13,... | collective-permute-start | bytes 2359304 | tf_op jit(solution)/shard_map/ppermute | solution.py:30
  150.3 14.6 %collective-permute-start.16 = (bf16[288,1024]{1,0:T(8,128)(2,1)S(1)}, bf16[288,1024]{1,0:T(8,128)(2,1)S(1)}, u32[]{:S(2)}, u32[]{:S(2)}) collective-permute-start(bf16[288,1024]{1,0:T(8,128)(2,1)S(1)} %fusion.236), channel_id=1, source_target_pairs={{0,2},{2,0},{1,3},{3,1},{4,6},{6,4},{5,7},{7,5},{8,10},{10,8},{9,1... | collective-permute-start | bytes 1769480 | tf_op jit(solution)/shard_map/ppermute | solution.py:25
  151.1 39.8 %collective-permute-start.18 = (bf16[256,512]{1,0:T(8,128)(2,1)S(1)}, bf16[256,512]{1,0:T(8,128)(2,1)}, u32[]{:S(2)}, u32[]{:S(2)}) collective-permute-start(bf16[256,512]{1,0:T(8,128)(2,1)S(1)} %copy-done.40), channel_id=1, source_target_pairs={{4,0},{0,4},{5,1},{1,5},{6,2},{2,6},{7,3},{3,7},{12,8},{8,12},{13,... | collective-permute-start | bytes 786440 | tf_op jit(solution)/shard_map/ppermute | solution.py:30
  195.3 15.6 %collective-permute-start.21 = (bf16[288,1024]{1,0:T(8,128)(2,1)S(1)}, bf16[288,1024]{1,0:T(8,128)(2,1)S(1)}, u32[]{:S(2)}, u32[]{:S(2)}) collective-permute-start(bf16[288,1024]{1,0:T(8,128)(2,1)S(1)} %fusion.167), channel_id=1, source_target_pairs={{0,2},{2,0},{1,3},{3,1},{4,6},{6,4},{5,7},{7,5},{8,10},{10,8},{9,1... | collective-permute-start | bytes 1769480 | tf_op jit(solution)/shard_map/ppermute | solution.py:25
  212.1 14.8 %collective-permute-start.26 = (bf16[288,1024]{1,0:T(8,128)(2,1)S(1)}, bf16[288,1024]{1,0:T(8,128)(2,1)S(1)}, u32[]{:S(2)}, u32[]{:S(2)}) collective-permute-start(bf16[288,1024]{1,0:T(8,128)(2,1)S(1)} %fusion.237), channel_id=1, source_target_pairs={{0,2},{2,0},{1,3},{3,1},{4,6},{6,4},{5,7},{7,5},{8,10},{10,8},{9,1... | collective-permute-start | bytes 1769480 | tf_op jit(solution)/shard_map/ppermute | solution.py:25
  212.9 26.1 %collective-permute-start.23 = (bf16[512,1024]{1,0:T(8,128)(2,1)S(1)}, bf16[512,1024]{1,0:T(8,128)(2,1)S(1)}, u32[]{:S(2)}, u32[]{:S(2)}) collective-permute-start(bf16[512,1024]{1,0:T(8,128)(2,1)S(1)} %copy-done.89), channel_id=1, source_target_pairs={{4,0},{0,4},{5,1},{1,5},{6,2},{2,6},{7,3},{3,7},{12,8},{8,12},{13,... | collective-permute-start | bytes 3145736 | tf_op jit(solution)/shard_map/ppermute | solution.py:30
  227.4 32.3 %collective-permute-start.24 = (bf16[1024,512]{1,0:T(8,128)(2,1)S(1)}, bf16[1024,512]{1,0:T(8,128)(2,1)S(1)}, u32[]{:S(2)}, u32[]{:S(2)}) collective-permute-start(bf16[1024,512]{1,0:T(8,128)(2,1)S(1)} %copy-done.91), channel_id=1, source_target_pairs={{4,0},{0,4},{5,1},{1,5},{6,2},{2,6},{7,3},{3,7},{12,8},{8,12},{13,... | collective-permute-start | bytes 3145736 | tf_op jit(solution)/shard_map/ppermute | solution.py:30
  265.2 15.6 %collective-permute-start.29 = (bf16[288,1024]{1,0:T(8,128)(2,1)}, bf16[288,1024]{1,0:T(8,128)(2,1)}, u32[]{:S(2)}, u32[]{:S(2)}) collective-permute-start(bf16[288,1024]{1,0:T(8,128)(2,1)} %fusion.163), channel_id=1, source_target_pairs={{0,2},{2,0},{1,3},{3,1},{4,6},{6,4},{5,7},{7,5},{8,10},{10,8},{9,1... | collective-permute-start | bytes 1769480 | tf_op jit(solution)/shard_map/ppermute | solution.py:25
  287.4 14.7 %collective-permute-start.32 = (bf16[288,1024]{1,0:T(8,128)(2,1)}, bf16[288,1024]{1,0:T(8,128)(2,1)}, u32[]{:S(2)}, u32[]{:S(2)}) collective-permute-start(bf16[288,1024]{1,0:T(8,128)(2,1)} %convert_element_type.604), channel_id=1, source_target_pairs={{0,2},{2,0},{1,3},{3,1},{4,6},{6,4},{5,7},{7,5},{8,10},{10,8},{9,1... | collective-permute-start | bytes 1769480 | tf_op jit(solution)/shard_map/ppermute | solution.py:25
  289.2 15.5 %collective-permute-start.30 = (bf16[288,1024]{1,0:T(8,128)(2,1)}, bf16[288,1024]{1,0:T(8,128)(2,1)}, u32[]{:S(2)}, u32[]{:S(2)}) collective-permute-start(bf16[288,1024]{1,0:T(8,128)(2,1)} %convert_element_type.604), channel_id=1, source_target_pairs={{0,1},{1,0},{2,3},{3,2},{4,5},{5,4},{6,7},{7,6},{8,9},{9,8},{10,11... | collective-permute-start | bytes 1769480 | tf_op jit(solution)/shard_map/ppermute | solution.py:21
  318.3 26.1 %collective-permute-start.74 = (bf16[512,1024]{1,0:T(8,128)(2,1)S(1)}, bf16[512,1024]{1,0:T(8,128)(2,1)S(1)}, u32[]{:S(2)}, u32[]{:S(2)}) collective-permute-start(bf16[512,1024]{1,0:T(8,128)(2,1)S(1)} %slice.775), channel_id=1, source_target_pairs={{0,4},{4,0},{1,5},{5,1},{2,6},{6,2},{3,7},{7,3},{8,12},{12,8},{9,1... | collective-permute-start | bytes 3145736 | tf_op jit(solution)/shard_map/ppermute | solution.py:35
  324.2 41.8 %collective-permute-start.82 = (bf16[1024,512]{1,0:T(8,128)(2,1)S(1)}, bf16[1024,512]{1,0:T(8,128)(2,1)S(1)}, u32[]{:S(2)}, u32[]{:S(2)}) collective-permute-start(bf16[1024,512]{1,0:T(8,128)(2,1)S(1)} %slice.779), channel_id=1, source_target_pairs={{0,4},{4,0},{1,5},{5,1},{2,6},{6,2},{3,7},{7,3},{8,12},{12,8},{9,1... | collective-permute-start | bytes 3145736 | tf_op jit(solution)/shard_map/ppermute | solution.py:35
  326.7 43.2 %collective-permute-start.31 = (bf16[288,1024]{1,0:T(8,128)(2,1)S(1)}, bf16[288,1024]{1,0:T(8,128)(2,1)S(1)}, u32[]{:S(2)}, u32[]{:S(2)}) collective-permute-start(bf16[288,1024]{1,0:T(8,128)(2,1)S(1)} %slice.979), channel_id=1, source_target_pairs={{0,1},{1,0},{2,3},{3,2},{4,5},{5,4},{6,7},{7,6},{8,9},{9,8},{10,11... | collective-permute-start | bytes 1769480 | tf_op jit(solution)/shard_map/ppermute | solution.py:21
  327.2 42.8 %collective-permute-start.35 = (bf16[288,1024]{1,0:T(8,128)(2,1)S(1)}, bf16[288,1024]{1,0:T(8,128)(2,1)S(1)}, u32[]{:S(2)}, u32[]{:S(2)}) collective-permute-start(bf16[288,1024]{1,0:T(8,128)(2,1)S(1)} %fusion.160), channel_id=1, source_target_pairs={{0,2},{2,0},{1,3},{3,1},{4,6},{6,4},{5,7},{7,5},{8,10},{10,8},{9,1... | collective-permute-start | bytes 1769480 | tf_op jit(solution)/shard_map/ppermute | solution.py:25
  344.8 45.2 %collective-permute-start.75 = (bf16[512,1024]{1,0:T(8,128)(2,1)S(1)}, bf16[512,1024]{1,0:T(8,128)(2,1)S(1)}, u32[]{:S(2)}, u32[]{:S(2)}) collective-permute-start(bf16[512,1024]{1,0:T(8,128)(2,1)S(1)} %add_convert_fusion.8), channel_id=1, source_target_pairs={{0,8},{24,16},{1,9},{25,17},{2,10},{26,18},{3,11},{27,19},{4,12},{... | collective-permute-start | bytes 3145736 | tf_op jit(solution)/shard_map/ppermute | solution.py:330
  366.4 26.6 %collective-permute-start.83 = (bf16[1024,512]{1,0:T(8,128)(2,1)S(1)}, bf16[1024,512]{1,0:T(8,128)(2,1)S(1)}, u32[]{:S(2)}, u32[]{:S(2)}) collective-permute-start(bf16[1024,512]{1,0:T(8,128)(2,1)S(1)} %add_convert_fusion.2), channel_id=1, source_target_pairs={{0,8},{24,16},{1,9},{25,17},{2,10},{26,18},{3,11},{27,19},{4,12},{... | collective-permute-start | bytes 3145736 | tf_op jit(solution)/shard_map/ppermute | solution.py:330
  372.4 15.8 %collective-permute-start.36 = (bf16[288,1024]{1,0:T(8,128)(2,1)S(1)}, bf16[288,1024]{1,0:T(8,128)(2,1)S(1)}, u32[]{:S(2)}, u32[]{:S(2)}) collective-permute-start(bf16[288,1024]{1,0:T(8,128)(2,1)S(1)} %convert_element_type.611), channel_id=1, source_target_pairs={{0,1},{1,0},{2,3},{3,2},{4,5},{5,4},{6,7},{7,6},{8,9},{9,8},{10,11... | collective-permute-start | bytes 1769480 | tf_op jit(solution)/shard_map/ppermute | solution.py:21
  372.5 15.7 %collective-permute-start.37 = (bf16[288,1024]{1,0:T(8,128)(2,1)S(1)}, bf16[288,1024]{1,0:T(8,128)(2,1)S(1)}, u32[]{:S(2)}, u32[]{:S(2)}) collective-permute-start(bf16[288,1024]{1,0:T(8,128)(2,1)S(1)} %convert_element_type.611), channel_id=1, source_target_pairs={{0,2},{2,0},{1,3},{3,1},{4,6},{6,4},{5,7},{7,5},{8,10},{10,8},{9,1... | collective-permute-start | bytes 1769480 | tf_op jit(solution)/shard_map/ppermute | solution.py:25
  391.4 85.5 %collective-permute-start.76 = (bf16[512,1024]{1,0:T(8,128)(2,1)}, bf16[512,1024]{1,0:T(8,128)(2,1)}, u32[]{:S(2)}, u32[]{:S(2)}) collective-permute-start(bf16[512,1024]{1,0:T(8,128)(2,1)} %add_convert_fusion.7), channel_id=1, source_target_pairs={{8,16},{16,8},{9,17},{17,9},{10,18},{18,10},{11,19},{19,11},{12,20... | collective-permute-start | bytes 3145736 | tf_op jit(solution)/shard_map/ppermute | solution.py:332
  394.3 107.7 %collective-permute-start.84 = (bf16[1024,512]{1,0:T(8,128)(2,1)}, bf16[1024,512]{1,0:T(8,128)(2,1)}, u32[]{:S(2)}, u32[]{:S(2)}) collective-permute-start(bf16[1024,512]{1,0:T(8,128)(2,1)} %add_convert_fusion.1), channel_id=1, source_target_pairs={{8,16},{16,8},{9,17},{17,9},{10,18},{18,10},{11,19},{19,11},{12,20... | collective-permute-start | bytes 3145736 | tf_op jit(solution)/shard_map/ppermute | solution.py:332
  450.7 23.9 %collective-permute-start.40 = (bf16[288,1024]{1,0:T(8,128)(2,1)}, bf16[288,1024]{1,0:T(8,128)(2,1)}, u32[]{:S(2)}, u32[]{:S(2)}) collective-permute-start(bf16[288,1024]{1,0:T(8,128)(2,1)} %slice.976), channel_id=1, source_target_pairs={{0,1},{1,0},{2,3},{3,2},{4,5},{5,4},{6,7},{7,6},{8,9},{9,8},{10,11... | collective-permute-start | bytes 1769480 | tf_op jit(solution)/shard_map/ppermute | solution.py:21
  453.3 44.9 %collective-permute-start.39 = (bf16[288,1024]{1,0:T(8,128)(2,1)}, bf16[288,1024]{1,0:T(8,128)(2,1)}, u32[]{:S(2)}, u32[]{:S(2)}) collective-permute-start(bf16[288,1024]{1,0:T(8,128)(2,1)} %slice.977), channel_id=1, source_target_pairs={{0,1},{1,0},{2,3},{3,2},{4,5},{5,4},{6,7},{7,6},{8,9},{9,8},{10,11... | collective-permute-start | bytes 1769480 | tf_op jit(solution)/shard_map/ppermute | solution.py:21
  473.9 18.0 %collective-permute-start.58 = (bf16[3,512,256]{2,1,0:T(8,128)(2,1)}, bf16[3,512,256]{2,1,0:T(8,128)(2,1)S(1)}, u32[]{:S(2)}, u32[]{:S(2)}) collective-permute-start(bf16[3,512,256]{2,1,0:T(8,128)(2,1)} %slice.767), channel_id=1, source_target_pairs={{0,4},{4,0},{1,5},{5,1},{2,6},{6,2},{3,7},{7,3},{8,12},{12,8},{9,1... | collective-permute-start | bytes 2359304 | tf_op jit(solution)/shard_map/ppermute | solution.py:35
  474.6 18.8 %collective-permute-start.68 = (bf16[256,512]{1,0:T(8,128)(2,1)S(1)}, bf16[256,512]{1,0:T(8,128)(2,1)S(1)}, u32[]{:S(2)}, u32[]{:S(2)}) collective-permute-start(bf16[256,512]{1,0:T(8,128)(2,1)S(1)} %add_convert_fusion.20), channel_id=1, source_target_pairs={{8,16},{16,8},{9,17},{17,9},{10,18},{18,10},{11,19},{19,11},{12,20... | collective-permute-start | bytes 786440 | tf_op jit(solution)/shard_map/ppermute | solution.py:332
  476.9 22.6 %collective-permute-start.41 = (bf16[288,1024]{1,0:T(8,128)(2,1)S(1)}, bf16[288,1024]{1,0:T(8,128)(2,1)S(1)}, u32[]{:S(2)}, u32[]{:S(2)}) collective-permute-start(bf16[288,1024]{1,0:T(8,128)(2,1)S(1)} %fusion.157), channel_id=1, source_target_pairs={{0,2},{2,0},{1,3},{3,1},{4,6},{6,4},{5,7},{7,5},{8,10},{10,8},{9,1... | collective-permute-start | bytes 1769480 | tf_op jit(solution)/shard_map/ppermute | solution.py:25
  491.9 45.1 %collective-permute-start.77 = (bf16[512,1024]{1,0:T(8,128)(2,1)S(1)}, bf16[512,1024]{1,0:T(8,128)(2,1)S(1)}, u32[]{:S(2)}, u32[]{:S(2)}) collective-permute-start(bf16[512,1024]{1,0:T(8,128)(2,1)S(1)} %add_convert_fusion.6), channel_id=1, source_target_pairs={{8,0},{16,24},{9,1},{17,25},{10,2},{18,26},{11,3},{19,27},{12,4},{... | collective-permute-start | bytes 3145736 | tf_op jit(solution)/shard_map/ppermute | solution.py:335
  493.5 34.0 %collective-permute-start.59 = (bf16[3,512,256]{2,1,0:T(8,128)(2,1)S(1)}, bf16[3,512,256]{2,1,0:T(8,128)(2,1)S(1)}, u32[]{:S(2)}, u32[]{:S(2)}) collective-permute-start(bf16[3,512,256]{2,1,0:T(8,128)(2,1)S(1)} %add_convert_fusion.14), channel_id=1, source_target_pairs={{0,8},{24,16},{1,9},{25,17},{2,10},{26,18},{3,11},{27,19},{4,12},{... | collective-permute-start | bytes 2359304 | tf_op jit(solution)/shard_map/ppermute | solution.py:330
  498.2 27.3 %collective-permute-start.69 = (bf16[256,512]{1,0:T(8,128)(2,1)S(1)}, bf16[256,512]{1,0:T(8,128)(2,1)S(1)}, u32[]{:S(2)}, u32[]{:S(2)}) collective-permute-start(bf16[256,512]{1,0:T(8,128)(2,1)S(1)} %add_convert_fusion.19), channel_id=1, source_target_pairs={{8,0},{16,24},{9,1},{17,25},{10,2},{18,26},{11,3},{19,27},{12,4},{... | collective-permute-start | bytes 786440 | tf_op jit(solution)/shard_map/ppermute | solution.py:335
  501.9 27.5 %collective-permute-start.42 = (bf16[288,1024]{1,0:T(8,128)(2,1)S(1)}, bf16[288,1024]{1,0:T(8,128)(2,1)S(1)}, u32[]{:S(2)}, u32[]{:S(2)}) collective-permute-start(bf16[288,1024]{1,0:T(8,128)(2,1)S(1)} %convert_element_type.624), channel_id=1, source_target_pairs={{0,1},{1,0},{2,3},{3,2},{4,5},{5,4},{6,7},{7,6},{8,9},{9,8},{10,11... | collective-permute-start | bytes 1769480 | tf_op jit(solution)/shard_map/ppermute | solution.py:21
  504.0 40.5 %collective-permute-start.85 = (bf16[1024,512]{1,0:T(8,128)(2,1)S(1)}, bf16[1024,512]{1,0:T(8,128)(2,1)S(1)}, u32[]{:S(2)}, u32[]{:S(2)}) collective-permute-start(bf16[1024,512]{1,0:T(8,128)(2,1)S(1)} %add_convert_fusion), channel_id=1, source_target_pairs={{8,0},{16,24},{9,1},{17,25},{10,2},{18,26},{11,3},{19,27},{12,4},{... | collective-permute-start | bytes 3145736 | tf_op jit(solution)/shard_map/ppermute | solution.py:335
  527.7 39.5 %collective-permute-start.60 = (bf16[3,512,256]{2,1,0:T(8,128)(2,1)S(1)}, bf16[3,512,256]{2,1,0:T(8,128)(2,1)}, u32[]{:S(2)}, u32[]{:S(2)}) collective-permute-start(bf16[3,512,256]{2,1,0:T(8,128)(2,1)S(1)} %add_convert_fusion.13), channel_id=1, source_target_pairs={{8,16},{16,8},{9,17},{17,9},{10,18},{18,10},{11,19},{19,11},{12,20... | collective-permute-start | bytes 2359304 | tf_op jit(solution)/shard_map/ppermute | solution.py:332
  536.5 51.4 %collective-permute-start.43 = (bf16[288,1024]{1,0:T(8,128)(2,1)}, bf16[288,1024]{1,0:T(8,128)(2,1)}, u32[]{:S(2)}, u32[]{:S(2)}) collective-permute-start(bf16[288,1024]{1,0:T(8,128)(2,1)} %slice.975), channel_id=1, source_target_pairs={{0,1},{1,0},{2,3},{3,2},{4,5},{5,4},{6,7},{7,6},{8,9},{9,8},{10,11... | collective-permute-start | bytes 1769480 | tf_op jit(solution)/shard_map/ppermute | solution.py:21
  557.7 26.1 %collective-permute-start.70 = (bf16[512,1024]{1,0:T(8,128)(2,1)S(1)}, bf16[512,1024]{1,0:T(8,128)(2,1)}, u32[]{:S(2)}, u32[]{:S(2)}) collective-permute-start(bf16[512,1024]{1,0:T(8,128)(2,1)S(1)} %slice.773), channel_id=1, source_target_pairs={{0,4},{4,0},{1,5},{5,1},{2,6},{6,2},{3,7},{7,3},{8,12},{12,8},{9,1... | collective-permute-start | bytes 3145736 | tf_op jit(solution)/shard_map/ppermute | solution.py:35
  563.1 42.8 %collective-permute-start.78 = (bf16[1024,512]{1,0:T(8,128)(2,1)}, bf16[1024,512]{1,0:T(8,128)(2,1)}, u32[]{:S(2)}, u32[]{:S(2)}) collective-permute-start(bf16[1024,512]{1,0:T(8,128)(2,1)} %slice.777), channel_id=1, source_target_pairs={{0,4},{4,0},{1,5},{5,1},{2,6},{6,2},{3,7},{7,3},{8,12},{12,8},{9,1... | collective-permute-start | bytes 3145736 | tf_op jit(solution)/shard_map/ppermute | solution.py:35
  565.8 22.1 %collective-permute-start.47 = (bf16[288,1024]{1,0:T(8,128)(2,1)}, bf16[288,1024]{1,0:T(8,128)(2,1)}, u32[]{:S(2)}, u32[]{:S(2)}) collective-permute-start(bf16[288,1024]{1,0:T(8,128)(2,1)} %fusion.154), channel_id=1, source_target_pairs={{0,2},{2,0},{1,3},{3,1},{4,6},{6,4},{5,7},{7,5},{8,10},{10,8},{9,1... | collective-permute-start | bytes 1769480 | tf_op jit(solution)/shard_map/ppermute | solution.py:25
  569.5 42.7 %collective-permute-start.61 = (bf16[3,512,256]{2,1,0:T(8,128)(2,1)}, bf16[3,512,256]{2,1,0:T(8,128)(2,1)}, u32[]{:S(2)}, u32[]{:S(2)}) collective-permute-start(bf16[3,512,256]{2,1,0:T(8,128)(2,1)} %add_convert_fusion.12), channel_id=1, source_target_pairs={{8,0},{16,24},{9,1},{17,25},{10,2},{18,26},{11,3},{19,27},{12,4},{... | collective-permute-start | bytes 2359304 | tf_op jit(solution)/shard_map/ppermute | solution.py:335
  585.4 46.2 %collective-permute-start.71 = (bf16[512,1024]{1,0:T(8,128)(2,1)S(1)}, bf16[512,1024]{1,0:T(8,128)(2,1)}, u32[]{:S(2)}, u32[]{:S(2)}) collective-permute-start(bf16[512,1024]{1,0:T(8,128)(2,1)S(1)} %add_convert_fusion.11), channel_id=1, source_target_pairs={{0,8},{24,16},{1,9},{25,17},{2,10},{26,18},{3,11},{27,19},{4,12},{... | collective-permute-start | bytes 3145736 | tf_op jit(solution)/shard_map/ppermute | solution.py:330
  591.2 19.9 %collective-permute-start.86 = (f32[12,1024]{1,0:T(8,128)S(1)}, f32[12,1024]{1,0:T(8,128)S(1)}, u32[]{:S(2)}, u32[]{:S(2)}) collective-permute-start(f32[12,1024]{1,0:T(8,128)S(1)} %pad_maximum_fusion.59), channel_id=1, source_target_pairs={{0,1},{1,0},{2,3},{3,2},{4,5},{5,4},{6,7},{7,6},{8,9},{9,8},{10,11... | collective-permute-start | bytes 147464 | tf_op jit(solution)/shard_map/ppermute | solution.py:21
  607.7 28.2 %collective-permute-start.79 = (bf16[1024,512]{1,0:T(8,128)(2,1)S(1)}, bf16[1024,512]{1,0:T(8,128)(2,1)}, u32[]{:S(2)}, u32[]{:S(2)}) collective-permute-start(bf16[1024,512]{1,0:T(8,128)(2,1)S(1)} %add_convert_fusion.5), channel_id=1, source_target_pairs={{0,8},{24,16},{1,9},{25,17},{2,10},{26,18},{3,11},{27,19},{4,12},{... | collective-permute-start | bytes 3145736 | tf_op jit(solution)/shard_map/ppermute | solution.py:330
  611.1 18.6 %collective-permute-start.48 = (bf16[288,1024]{1,0:T(8,128)(2,1)}, bf16[288,1024]{1,0:T(8,128)(2,1)}, u32[]{:S(2)}, u32[]{:S(2)}) collective-permute-start(bf16[288,1024]{1,0:T(8,128)(2,1)} %convert_element_type.631), channel_id=1, source_target_pairs={{0,1},{1,0},{2,3},{3,2},{4,5},{5,4},{6,7},{7,6},{8,9},{9,8},{10,11... | collective-permute-start | bytes 1769480 | tf_op jit(solution)/shard_map/ppermute | solution.py:21
  611.1 18.6 %collective-permute-start.49 = (bf16[288,1024]{1,0:T(8,128)(2,1)}, bf16[288,1024]{1,0:T(8,128)(2,1)}, u32[]{:S(2)}, u32[]{:S(2)}) collective-permute-start(bf16[288,1024]{1,0:T(8,128)(2,1)} %convert_element_type.631), channel_id=1, source_target_pairs={{0,2},{2,0},{1,3},{3,1},{4,6},{6,4},{5,7},{7,5},{8,10},{10,8},{9,1... | collective-permute-start | bytes 1769480 | tf_op jit(solution)/shard_map/ppermute | solution.py:25
  612.3 16.2 %collective-permute-start.87 = (f32[12,1024]{1,0:T(8,128)S(1)}, f32[12,1024]{1,0:T(8,128)S(1)}, u32[]{:S(2)}, u32[]{:S(2)}) collective-permute-start(f32[12,1024]{1,0:T(8,128)S(1)} %fusion.350), channel_id=1, source_target_pairs={{0,2},{2,0},{1,3},{3,1},{4,6},{6,4},{5,7},{7,5},{8,10},{10,8},{9,1... | collective-permute-start | bytes 147464 | tf_op jit(solution)/shard_map/ppermute | solution.py:25
  634.2 147.2 %collective-permute-start.72 = (bf16[512,1024]{1,0:T(8,128)(2,1)}, bf16[512,1024]{1,0:T(8,128)(2,1)}, u32[]{:S(2)}, u32[]{:S(2)}) collective-permute-start(bf16[512,1024]{1,0:T(8,128)(2,1)} %add_convert_fusion.10), channel_id=1, source_target_pairs={{8,16},{16,8},{9,17},{17,9},{10,18},{18,10},{11,19},{19,11},{12,20... | collective-permute-start | bytes 3145736 | tf_op jit(solution)/shard_map/ppermute | solution.py:332
  694.5 72.6 %collective-permute-start.52 = (bf16[288,1024]{1,0:T(8,128)(2,1)}, bf16[288,1024]{1,0:T(8,128)(2,1)}, u32[]{:S(2)}, u32[]{:S(2)}) collective-permute-start(bf16[288,1024]{1,0:T(8,128)(2,1)} %slice.972), channel_id=1, source_target_pairs={{0,1},{1,0},{2,3},{3,2},{4,5},{5,4},{6,7},{7,6},{8,9},{9,8},{10,11... | collective-permute-start | bytes 1769480 | tf_op jit(solution)/shard_map/ppermute | solution.py:21
  696.2 73.2 %collective-permute-start.54 = (bf16[3,512,256]{2,1,0:T(8,128)(2,1)}, bf16[3,512,256]{2,1,0:T(8,128)(2,1)}, u32[]{:S(2)}, u32[]{:S(2)}) collective-permute-start(bf16[3,512,256]{2,1,0:T(8,128)(2,1)} %slice.765), channel_id=1, source_target_pairs={{0,4},{4,0},{1,5},{5,1},{2,6},{6,2},{3,7},{7,3},{8,12},{12,8},{9,1... | collective-permute-start | bytes 2359304 | tf_op jit(solution)/shard_map/ppermute | solution.py:35
  700.6 21.3 %collective-permute-start.62 = (bf16[256,512]{1,0:T(8,128)(2,1)}, bf16[256,512]{1,0:T(8,128)(2,1)}, u32[]{:S(2)}, u32[]{:S(2)}) collective-permute-start(bf16[256,512]{1,0:T(8,128)(2,1)} %slice.769), channel_id=1, source_target_pairs={{0,4},{4,0},{1,5},{5,1},{2,6},{6,2},{3,7},{7,3},{8,12},{12,8},{9,1... | collective-permute-start | bytes 786440 | tf_op jit(solution)/shard_map/ppermute | solution.py:35
  703.0 27.4 %collective-permute-start.88 = (f32[7680]{0:T(1024)}, f32[7680]{0:T(1024)}, u32[]{:S(2)}, u32[]{:S(2)}) collective-permute-start(f32[7680]{0:T(1024)} %pad_maximum_fusion.61), channel_id=1, source_target_pairs={{0,4},{4,0},{1,5},{5,1},{2,6},{6,2},{3,7},{7,3},{8,12},{12,8},{9,1... | collective-permute-start | bytes 92168 | tf_op jit(solution)/shard_map/ppermute | solution.py:35
  723.7 42.3 %collective-permute-start.63 = (bf16[256,512]{1,0:T(8,128)(2,1)}, bf16[256,512]{1,0:T(8,128)(2,1)}, u32[]{:S(2)}, u32[]{:S(2)}) collective-permute-start(bf16[256,512]{1,0:T(8,128)(2,1)} %add_convert_fusion.24), channel_id=1, source_target_pairs={{0,8},{24,16},{1,9},{25,17},{2,10},{26,18},{3,11},{27,19},{4,12},{... | collective-permute-start | bytes 786440 | tf_op jit(solution)/shard_map/ppermute | solution.py:330
  730.4 54.3 %collective-permute-start.80 = (bf16[1024,512]{1,0:T(8,128)(2,1)}, bf16[1024,512]{1,0:T(8,128)(2,1)}, u32[]{:S(2)}, u32[]{:S(2)}) collective-permute-start(bf16[1024,512]{1,0:T(8,128)(2,1)} %add_convert_fusion.4), channel_id=1, source_target_pairs={{8,16},{16,8},{9,17},{17,9},{10,18},{18,10},{11,19},{19,11},{12,20... | collective-permute-start | bytes 3145736 | tf_op jit(solution)/shard_map/ppermute | solution.py:332
  766.0 35.3 %collective-permute-start.51 = (bf16[288,1024]{1,0:T(8,128)(2,1)S(1)}, bf16[288,1024]{1,0:T(8,128)(2,1)S(1)}, u32[]{:S(2)}, u32[]{:S(2)}) collective-permute-start(bf16[288,1024]{1,0:T(8,128)(2,1)S(1)} %slice.973), channel_id=1, source_target_pairs={{0,1},{1,0},{2,3},{3,2},{4,5},{5,4},{6,7},{7,6},{8,9},{9,8},{10,11... | collective-permute-start | bytes 1769480 | tf_op jit(solution)/shard_map/ppermute | solution.py:21
  769.4 31.9 %collective-permute-start.53 = (bf16[288,1024]{1,0:T(8,128)(2,1)S(1)}, bf16[288,1024]{1,0:T(8,128)(2,1)S(1)}, u32[]{:S(2)}, u32[]{:S(2)}) collective-permute-start(bf16[288,1024]{1,0:T(8,128)(2,1)S(1)} %fusion.151), channel_id=1, source_target_pairs={{0,2},{2,0},{1,3},{3,1},{4,6},{6,4},{5,7},{7,5},{8,10},{10,8},{9,1... | collective-permute-start | bytes 1769480 | tf_op jit(solution)/shard_map/ppermute | solution.py:25
  772.0 26.0 %collective-permute-start.55 = (bf16[3,512,256]{2,1,0:T(8,128)(2,1)S(1)}, bf16[3,512,256]{2,1,0:T(8,128)(2,1)S(1)}, u32[]{:S(2)}, u32[]{:S(2)}) collective-permute-start(bf16[3,512,256]{2,1,0:T(8,128)(2,1)S(1)} %add_convert_fusion.17), channel_id=1, source_target_pairs={{0,8},{24,16},{1,9},{25,17},{2,10},{26,18},{3,11},{27,19},{4,12},{... | collective-permute-start | bytes 2359304 | tf_op jit(solution)/shard_map/ppermute | solution.py:330
  781.4 18.0 %collective-permute-start.65 = (bf16[256,512]{1,0:T(8,128)(2,1)S(1)}, bf16[256,512]{1,0:T(8,128)(2,1)S(1)}, u32[]{:S(2)}, u32[]{:S(2)}) collective-permute-start(bf16[256,512]{1,0:T(8,128)(2,1)S(1)} %add_convert_fusion.22), channel_id=1, source_target_pairs={{8,0},{16,24},{9,1},{17,25},{10,2},{18,26},{11,3},{19,27},{12,4},{... | collective-permute-start | bytes 786440 | tf_op jit(solution)/shard_map/ppermute | solution.py:335
  784.6 30.4 %collective-permute-start.73 = (bf16[512,1024]{1,0:T(8,128)(2,1)S(1)}, bf16[512,1024]{1,0:T(8,128)(2,1)S(1)}, u32[]{:S(2)}, u32[]{:S(2)}) collective-permute-start(bf16[512,1024]{1,0:T(8,128)(2,1)S(1)} %add_convert_fusion.9), channel_id=1, source_target_pairs={{8,0},{16,24},{9,1},{17,25},{10,2},{18,26},{11,3},{19,27},{12,4},{... | collective-permute-start | bytes 3145736 | tf_op jit(solution)/shard_map/ppermute | solution.py:335
  797.9 39.5 %collective-permute-start.81 = (bf16[1024,512]{1,0:T(8,128)(2,1)S(1)}, bf16[1024,512]{1,0:T(8,128)(2,1)S(1)}, u32[]{:S(2)}, u32[]{:S(2)}) collective-permute-start(bf16[1024,512]{1,0:T(8,128)(2,1)S(1)} %add_convert_fusion.3), channel_id=1, source_target_pairs={{8,0},{16,24},{9,1},{17,25},{10,2},{18,26},{11,3},{19,27},{12,4},{... | collective-permute-start | bytes 3145736 | tf_op jit(solution)/shard_map/ppermute | solution.py:335
  803.1 49.6 %collective-permute-start.57 = (bf16[3,512,256]{2,1,0:T(8,128)(2,1)S(1)}, bf16[3,512,256]{2,1,0:T(8,128)(2,1)S(1)}, u32[]{:S(2)}, u32[]{:S(2)}) collective-permute-start(bf16[3,512,256]{2,1,0:T(8,128)(2,1)S(1)} %add_convert_fusion.15), channel_id=1, source_target_pairs={{8,0},{16,24},{9,1},{17,25},{10,2},{18,26},{11,3},{19,27},{12,4},{... | collective-permute-start | bytes 2359304 | tf_op jit(solution)/shard_map/ppermute | solution.py:335
  (237 other events, 1937.2 us)

commit v2 on v1

v2 whole, which is shorter than its diff:
```python
import functools

import jax
import jax.numpy as jnp
from jax import lax
from jax.experimental import pallas as pl
from jax.experimental.pallas import tpu as pltpu
from jax.sharding import PartitionSpec as P

HEAD = 64
PAIR = 2 * HEAD
LAYERS = 2
LENGTHS = (512, 256, 128, 128, 128)
STARTS = (0, 512, 768, 896, 1024)
STREAMS = ((0,), (1, 2, 3, 4))
HALVES = 2
BF = jnp.bfloat16
F32 = jnp.float32
MIB = 1 << 20
CORE_SWAP = [(0, 1), (1, 0), (2, 3), (3, 2)]
CHIP_SWAP = [(0, 2), (2, 0), (1, 3), (3, 1)]


def to_core(value):
    return lax.ppermute(value, "tensor", CORE_SWAP)


def to_chip(value):
    return lax.ppermute(value, "tensor", CHIP_SWAP)


def from_fsdp(value, step):
    size = lax.axis_size("fsdp")
    return lax.ppermute(value, "fsdp", [((i + step) % size, i) for i in range(size)])


def to_fsdp(value, step):
    size = lax.axis_size("fsdp")
    return lax.ppermute(value, "fsdp", [(i, (i + step) % size) for i in range(size)])


def own_first(whole, axis):
    size = lax.axis_size("fsdp")
    here = lax.axis_index("fsdp")
    width = whole.shape[axis] // size
    return jnp.concatenate(
        [lax.dynamic_slice_in_dim(whole, (here + k) % size * width, width, axis) for k in range(size)], axis
    )


def natural(relative, axis):
    size = lax.axis_size("fsdp")
    here = lax.axis_index("fsdp")
    width = relative.shape[axis] // size
    return jnp.concatenate(
        [
            lax.dynamic_slice_in_dim(relative, (k - here + size) % size * width, width, axis)
            for k in range(size)
        ],
        axis,
    )


def dot(left, right):
    return jnp.dot(left, right, preferred_element_type=F32)


def dot_t(left, right):
    return lax.dot_general(left, right, (((1,), (1,)), ((), ())), preferred_element_type=F32)


def dot_rows(left, right):
    return lax.dot_general(left, right, (((0,), (0,)), ((), ())), preferred_element_type=F32)


def share_rows(stream):
    return sum(LENGTHS[page] for page in stream) // HALVES


def page_places(stream):
    places, at = [], 0
    for page in stream:
        places.append((page, LENGTHS[page], at, at // HALVES))
        at += LENGTHS[page]
    return places


class Order:
    def __init__(self):
        self.last = None
        self.pins = []

    def pin(self, arrays):
        self.pins.extend(arrays)

    def hold(self):
        def body(out):
            out[...] = jnp.zeros(out.shape, F32)

        self.call(body, [], [shape_of((8, 128), F32)], name="hold")

    def call(
        self, body, inputs, outputs, scratch=(), grid=(), in_specs=None, out_specs=None, name=None, limit=16, alias=None
    ):
        pins, self.pins = self.pins, []
        count = len(inputs)
        in_specs = in_specs or [None] * count
        out_specs = out_specs or [None] * len(outputs)
        in_specs = [whole_of(v.shape, grid) if s is None else s for s, v in zip(in_specs, inputs)]
        out_specs = [whole_of(v.shape, grid) if s is None else s for s, v in zip(out_specs, outputs)]
        inputs = list(inputs)
        unread = pins + ([] if self.last is None else [self.last])
        extra = len(unread)
        inputs += unread
        in_specs += [pl.BlockSpec(memory_space=pl.ANY)] * extra

        def kernel(*refs):
            body(*refs[:count], *refs[count + extra :])

        result = pl.pallas_call(
            kernel,
            grid=grid,
            in_specs=in_specs,
            out_specs=out_specs,
            out_shape=outputs,
            scratch_shapes=list(scratch),
            input_output_aliases=alias or {},
            name=name,
            cost_estimate=pl.CostEstimate(flops=0, bytes_accessed=0, transcendentals=0),
            compiler_params=pltpu.CompilerParams(vmem_limit_bytes=limit * MIB),
        )(*inputs)
        self.last = result[0]
        return result


def whole_of(shape, grid):
    if not grid:
        return pl.BlockSpec(memory_space=pltpu.VMEM)
    return pl.BlockSpec(shape, lambda *at: (0,) * len(shape))


def shape_of(shape, dtype):
    return jax.ShapeDtypeStruct(tuple(shape), dtype)


SMEM = pl.BlockSpec(memory_space=pltpu.SMEM)
ANY = pl.BlockSpec(memory_space=pl.ANY)


def core_index():
    return lax.rem(lax.axis_index("tensor"), 2)


class Weight:
    def __init__(self, arrays, axis):
        self.arrays = arrays
        self.axis = axis
        self.widths = [v.shape[axis] for v in arrays]
        self.starts = [sum(self.widths[:i]) for i in range(len(arrays))]
        self.shape = arrays[0].shape

    def specs(self, block=None):
        if block is None:
            return [None] * len(self.arrays)
        found = []
        for v in self.arrays:
            shape = [block, block]
            shape[self.axis] = v.shape[self.axis]
            found.append(pl.BlockSpec(tuple(shape), (lambda i: (0, i)) if self.axis == 0 else (lambda i: (i, 0))))
        return found

    def take(self, refs):
        count = len(self.arrays)
        places = [slice(a, a + w) for a, w in zip(self.starts, self.widths)]
        return list(zip(refs[:count], places)), refs[count:]


def deal_rows(order, activations):
    features = activations.shape[1]
    size = lax.axis_size("fsdp")
    width = features // size

    def body(whole, *outs):
        here = core_index()
        mine = lax.axis_index("fsdp")
        for at, stream in enumerate(STREAMS):
            for slot in range(HALVES):
                out = outs[at * HALVES + slot]
                for page, length, _, offset in page_places(stream):
                    part = length // HALVES
                    row = pl.multiple_of(STARTS[page] + (here ^ slot) * part, 32)
                    for k in range(size):
                        column = pl.multiple_of(lax.rem(mine + k, size) * width, 128)
                        out[offset : offset + part, k * width : (k + 1) * width] = whole[
                            pl.ds(row, part), pl.ds(column, width)
                        ]

    outs = order.call(
        body,
        [activations],
        [shape_of((share_rows(stream), features), BF) for stream in STREAMS for _ in range(HALVES)],
        name="deal_rows",
    )
    return [outs[at * HALVES : (at + 1) * HALVES] for at in range(len(STREAMS))]


def deal_share(order, slots):
    rows, features = slots[0].shape
    size = lax.axis_size("fsdp")
    width = features // size

    def body(a, b, c, d, *outs):
        whole = outs[-1]
        here = lax.axis_index("tensor")
        core = core_index()
        mine = lax.axis_index("fsdp")
        for slot, ref in enumerate((a, b, c, d)):
            whole[pl.ds(pl.multiple_of((here ^ slot) * rows, 32), rows), :] = ref[...]
        for at, stream in enumerate(STREAMS):
            for page, length, _, offset in page_places(stream):
                part = length // HALVES
                row = pl.multiple_of(STARTS[page] + core * part, 32)
                for k in range(size):
                    column = pl.multiple_of(lax.rem(mine + k, size) * width, 128)
                    outs[at][offset : offset + part, k * width : (k + 1) * width] = whole[
                        pl.ds(row, part), pl.ds(column, width)
                    ]

    return order.call(
        body,
        slots,
        [shape_of((share_rows(stream), features), BF) for stream in STREAMS],
        scratch=[pltpu.VMEM((rows * 4, features), BF)],
        name="deal_share",
    )


def natural_share(order, slots, dtype):
    rows, features = slots[0].shape
    share = rows // 2
    size = lax.axis_size("fsdp")
    width = features // size

    def body(a, b, out, whole):
        here = lax.axis_index("tensor")
        core = core_index()
        mine = lax.axis_index("fsdp")
        for slot, ref in enumerate((a, b)):
            first = 0
            for stream in STREAMS:
                for page, length, _, offset in page_places(stream):
                    part = length // HALVES
                    row = pl.multiple_of(STARTS[page] + (core ^ slot) * part, 32)
                    whole[pl.ds(row, part), :] = ref[first + offset : first + offset + part, :]
                first += share_rows(stream)
        own = pl.multiple_of(here * share, 32)
        for k in range(size):
            column = pl.multiple_of(lax.rem(mine + k, size) * width, 128)
            out[:, pl.ds(column, width)] = whole[pl.ds(own, share), k * width : (k + 1) * width].astype(dtype)

    return order.call(
        body,
        slots,
        [shape_of((share, features), dtype)],
        scratch=[pltpu.VMEM((rows * 2, features), BF)],
        name="natural_share",
    )[0]


def add_send(order, kept, came):
    half = kept.shape[0] // 2

    def body(a, b, c, low, wide):
        for at, came_ref in ((0, b), (half, c)):
            total = a[at : at + half, :] + came_ref[...].astype(F32)
            wide[at : at + half, :] = total
            low[at : at + half, :] = total.astype(BF)

    return order.call(body, [kept, *came], [shape_of(kept.shape, BF), shape_of(kept.shape, F32)], name="add_send")


def row_of(ref, at):
    return ref[at : at + 1, :]


def norm_forward(order, terms, residual, vectors, rows_of_vectors):
    rows, features = terms[0].shape
    bias_at, gain_at, shift_at = rows_of_vectors

    def body(a, b, before, vec, low, normed, inverse):
        value = before[...].astype(F32)
        if residual[1] is not None:
            value = value * row_of(vec, residual[1]) + row_of(vec, residual[2])
        value = value + a[...] + b[...].astype(F32) + row_of(vec, bias_at)
        center = value - jnp.mean(value, -1, keepdims=True)
        scale = lax.rsqrt(jnp.mean(center * center, -1, keepdims=True) + 1e-05)
        unit = center * scale
        normed[...] = unit
        inverse[...] = scale
        low[...] = (unit * row_of(vec, gain_at) + row_of(vec, shift_at)).astype(BF)

    return order.call(
        body,
        [*terms, residual[0], vectors],
        [shape_of((rows, features), BF), shape_of((rows, features), F32), shape_of((rows, 1), F32)],
        name="norm_forward",
    )


def norm_backward(order, terms, normed, inverse, vectors, gain_at):
    rows, features = normed.shape
    count = len(terms)

    def body(*refs):
        unit, scale, vec, low, sums, wide = refs[count:]
        total = refs[0][...].astype(F32)
        for ref in refs[1:count]:
            total = total + ref[...].astype(F32)
        n = unit[...]
        grad = total * row_of(vec, gain_at)
        mean_one = jnp.mean(grad, -1, keepdims=True)
        mean_two = jnp.mean(grad * n, -1, keepdims=True)
        result = scale[...] * (grad - mean_one - n * mean_two)
        wide[...] = result
        low[...] = result.astype(BF)
        sums[0:1, :] = jnp.sum(total * n, 0, keepdims=True)
        sums[1:2, :] = jnp.sum(total, 0, keepdims=True)
        sums[2:3, :] = jnp.sum(result, 0, keepdims=True)

    return order.call(
        body,
        [*terms, normed, inverse, vectors],
        [shape_of((rows, features), BF), shape_of((3, features), F32), shape_of((rows, features), F32)],
        name="norm_backward",
    )


def last_sum(order, terms):
    def body(*refs):
        total = refs[0][...]
        for ref in refs[1:-1]:
            total = total + ref[...].astype(F32)
        refs[-1][...] = total.astype(BF)

    return order.call(body, terms, [shape_of(terms[0].shape, BF)], name="last_sum")[0]


def head_mask(which):
    lane = lax.broadcasted_iota(jnp.int32, (1, PAIR), 1)
    return (lane < HEAD) if which == 0 else (lane >= HEAD)


def key_bias(length, limit):
    part = length // HALVES
    place = lax.broadcasted_iota(jnp.int32, (1, length), 1)
    half = (place // part) ^ core_index()
    return jnp.where(half * part + place % part < limit, 0.0, -1000000000.0).astype(F32)


def put_rows(ref, lanes, value, row, part, share, offset):
    done = 0
    while done < value.shape[0]:
        at = row + done
        count = min(part - at % part, value.shape[0] - done)
        first = (at // part) * share + offset + at % part
        ref[first : first + count, lanes] = value[done : done + count]
        done += count


def attention_forward(order, stream, slots, weights, lengths):
    w_proj, w_mix, bias_rows = weights
    share, features = slots[0].shape
    span = w_mix.shape[0]
    heads = span // HEAD
    places = page_places(stream)

    def body(*refs):
        xs, refs = refs[:HALVES], refs[HALVES:]
        wp, refs = w_proj.take(refs)
        wm, refs = w_mix.take(refs)
        bias, limits, refs = refs[0], refs[1], refs[2:]
        others, part_own, qkv, ctx, probs = refs[:2], refs[2], refs[3], refs[4], refs[5:]
        for kind in range(3):
            value = None
            for w, at in wp:
                rows = jnp.concatenate([x[:, at] for x in xs], 0)
                term = dot(rows, w[kind])
                value = term if value is None else value + term
            if kind == 0:
                value = value + bias[0:1, :]
            elif kind == 2:
                value = value + bias[1:2, :]
            value = value.astype(BF)
            if kind == 0:
                value = value * jnp.asarray(HEAD ** (-0.5), BF)
            for _, length, base, offset in places:
                part = length // HALVES
                for slot in range(HALVES):
                    qkv[base + slot * part : base + (slot + 1) * part, kind * span : (kind + 1) * span] = value[
                        slot * share + offset : slot * share + offset + part, :
                    ]
        for index, (page, length, base, offset) in enumerate(places):
            part = length // HALVES
            shut = key_bias(length, limits[page])
            step = min(length, 256)
            for pair in range(heads // 2):
                lanes = slice(pair * PAIR, (pair + 1) * PAIR)
                keys = qkv[base : base + length, span + pair * PAIR : span + (pair + 1) * PAIR]
                values = qkv[base : base + length, 2 * span + pair * PAIR : 2 * span + (pair + 1) * PAIR]
                for row in range(0, length, step):
                    queries = qkv[base + row : base + row + step, lanes]
                    found = []
                    for which in range(2):
                        masked = queries * head_mask(which).astype(BF)
                        scores = dot_t(masked, keys) + shut
                        peak = jnp.max(scores, -1, keepdims=True)
                        raised = jnp.exp(scores - peak)
                        chance = raised * (1.0 / jnp.sum(raised, -1, keepdims=True))
                        chance = chance.astype(BF)
                        probs[index][2 * pair + which, row : row + step, :] = chance
                        found.append(dot(chance, values))
                    both = jnp.where(head_mask(0), found[0], found[1]).astype(BF)
                    put_rows(ctx, lanes, both, row, part, share, offset)
        for w, at in wm:
            value = dot(ctx[...], w[...])
            part_own[:, at] = value[:share]
            split_rows(others, at, value[share:])

    outs = order.call(
        body,
        [*slots, *w_proj.arrays, *w_mix.arrays, bias_rows, lengths],
        [
            *[shape_of((share // 2, features), BF)] * 2,
            shape_of((share, features), F32),
            shape_of((2 * share, 3 * span), BF),
            shape_of((2 * share, span), BF),
        ]
        + [shape_of((heads, length, length), BF) for _, length, _, _ in places],
        in_specs=[None] * HALVES + w_proj.specs() + w_mix.specs() + [None, SMEM],
        name="attention_forward",
    )
    return {"other": outs[:2], "own": outs[2], "qkv": outs[3], "ctx": outs[4], "probs": outs[5:]}


def attention_backward(order, stream, slots, weights, state):
    w_proj, w_mix = weights
    probs, qkv = state["probs"], state["qkv"]
    share, features = slots[0].shape
    span = w_mix.shape[0]
    heads = span // HEAD
    places = page_places(stream)

    def body(*refs):
        ds, refs = refs[:HALVES], refs[HALVES:]
        wp, refs = w_proj.take(refs)
        wm, refs = w_mix.take(refs)
        chances, refs = refs[: len(places)], refs[len(places) :]
        qkv_ref, *others, part_own, grad, sums, low = refs
        value = None
        for w, at in wm:
            rows = jnp.concatenate([d[:, at] for d in ds], 0)
            term = dot_t(rows, w[...])
            value = term if value is None else value + term
        value = value.astype(BF)
        for _, length, base, offset in places:
            part = length // HALVES
            for slot in range(HALVES):
                low[base + slot * part : base + (slot + 1) * part, :] = value[
                    slot * share + offset : slot * share + offset + part, :
                ]
        for index, (page, length, base, offset) in enumerate(places):
            part = length // HALVES
            step = min(length, 256)
            for pair in range(heads // 2):
                lanes = slice(pair * PAIR, (pair + 1) * PAIR)
                keys = qkv_ref[base : base + length, span + pair * PAIR : span + (pair + 1) * PAIR]
                values = qkv_ref[base : base + length, 2 * span + pair * PAIR : 2 * span + (pair + 1) * PAIR]
                grad_keys, grad_values = [None, None], [None, None]
                for row in range(0, length, step):
                    queries = qkv_ref[base + row : base + row + step, lanes]
                    grad_rows = low[base + row : base + row + step, lanes]
                    found = []
                    for which in range(2):
                        chance = chances[index][2 * pair + which, row : row + step, :]
                        wide = chance.astype(F32)
                        back = dot_t(grad_rows * head_mask(which).astype(BF), values)
                        inner = jnp.sum(wide * back, -1, keepdims=True)
                        grad_scores = (wide * (back - inner)).astype(BF)
                        found.append(dot(grad_scores, keys))
                        of_keys = dot_rows(grad_scores, queries)
                        of_values = dot_rows(chance, grad_rows)
                        first = grad_keys[which] is None
                        grad_keys[which] = of_keys if first else grad_keys[which] + of_keys
                        grad_values[which] = of_values if first else grad_values[which] + of_values
                    both = (jnp.where(head_mask(0), found[0], found[1]) * HEAD ** (-0.5)).astype(BF)
                    put_rows(grad, lanes, both, row, part, share, offset)
                for kind, parts in ((1, grad_keys), (2, grad_values)):
                    both = jnp.where(head_mask(0), parts[0], parts[1]).astype(BF)
                    for slot in range(HALVES):
                        grad[
                            slot * share + offset : slot * share + offset + part,
                            kind * span + pair * PAIR : kind * span + (pair + 1) * PAIR,
                        ] = both[slot * part : (slot + 1) * part, :]
        for w, at in wp:
            value = None
            for kind in range(3):
                term = dot_t(grad[:, kind * span : (kind + 1) * span], w[kind])
                value = term if value is None else value + term
            part_own[:, at] = value[:share]
            split_rows(others, at, value[share:])
        sums[...] = jnp.sum(grad[...].astype(F32), 0, keepdims=True)

    outs = order.call(
        body,
        [*slots, *w_proj.arrays, *w_mix.arrays, *probs, qkv],
        [
            *[shape_of((share // 2, features), BF)] * 2,
            shape_of((share, features), F32),
            shape_of((2 * share, 3 * span), BF),
            shape_of((1, 3 * span), F32),
        ],
        scratch=[pltpu.VMEM((2 * share, span), BF)],
        in_specs=[None] * HALVES + w_proj.specs() + w_mix.specs() + [None] * (len(places) + 1),
        name="attention_backward",
    )
    return {"other": outs[:2], "own": outs[2], "grad": outs[3], "sums": outs[4]}


FF_BLOCK = 256


def feed_forward(order, slots, weights):
    w_grow, w_shrink, bias = weights
    share, features = slots[0].shape
    hidden = w_shrink.shape[0]
    block = min(FF_BLOCK, hidden)
    steps = hidden // block

    def body(*refs):
        xs, refs = refs[:HALVES], refs[HALVES:]
        wg, refs = w_grow.take(refs)
        ws, refs = w_shrink.take(refs)
        b, *others, act, slope, part_own, total = refs
        step = pl.program_id(0)
        value = None
        for w, at in wg:
            rows = jnp.concatenate([x[:, at] for x in xs], 0)
            term = dot(rows, w[...])
            value = term if value is None else value + term
        up = value + b[...]
        cdf = 0.5 * (1.0 + lax.erf(up * 0.7071067811865476))
        density = jnp.exp(-0.5 * up * up) * 0.3989422804014327
        low = (up * cdf).astype(BF)
        act[...] = low
        slope[...] = (cdf + up * density).astype(BF)
        accumulate(step, steps, low, ws, dot, total, share, others, part_own)

    outs = order.call(
        body,
        [*slots, *w_grow.arrays, *w_shrink.arrays, bias],
        [
            *[shape_of((share // 2, features), BF)] * 2,
            shape_of((2 * share, hidden), BF),
            shape_of((2 * share, hidden), BF),
            shape_of((share, features), F32),
        ],
        scratch=[pltpu.VMEM((2 * share, features), F32)],
        grid=(steps,),
        in_specs=[None] * HALVES
        + w_grow.specs(block)
        + w_shrink.specs(block)
        + [pl.BlockSpec((1, block), lambda i: (0, i))],
        out_specs=[None] * 2 + [pl.BlockSpec((2 * share, block), lambda i: (0, i))] * 2 + [None],
        name="feed_forward",
    )
    return {"other": outs[:2], "act": outs[2], "slope": outs[3], "own": outs[4]}


def split_rows(refs, at, value):
    half = value.shape[0] // 2
    refs[0][:, at] = value[:half].astype(BF)
    refs[1][:, at] = value[half:].astype(BF)


def accumulate(step, steps, low, weight, product, total, share, others, part_own):
    for w, at in weight:
        term = product(low, w[...])

        @pl.when(step == 0)
        def _():
            total[:, at] = term

        @pl.when((step > 0) & (step < steps - 1))
        def _():
            total[:, at] += term

        @pl.when(step == steps - 1)
        def _():
            done = term if steps == 1 else total[:, at] + term
            part_own[:, at] = done[:share, :]
            split_rows(others, at, done[share:, :])


def feed_backward(order, slots, slope, weights):
    w_grow, w_shrink = weights
    share, features = slots[0].shape
    hidden = w_shrink.shape[0]
    block = min(FF_BLOCK, hidden)
    steps = hidden // block

    def body(*refs):
        ds, refs = refs[:HALVES], refs[HALVES:]
        wg, refs = w_grow.take(refs)
        ws, refs = w_shrink.take(refs)
        tilt, *others, grad, sums, part_own, total = refs
        step = pl.program_id(0)
        value = None
        for w, at in ws:
            rows = jnp.concatenate([d[:, at] for d in ds], 0)
            term = dot_t(rows, w[...])
            value = term if value is None else value + term
        low = (value * tilt[...].astype(F32)).astype(BF)
        grad[...] = low
        sums[...] = jnp.sum(low.astype(F32), 0, keepdims=True)
        accumulate(step, steps, low, wg, dot_t, total, share, others, part_own)

    outs = order.call(
        body,
        [*slots, *w_grow.arrays, *w_shrink.arrays, slope],
        [
            *[shape_of((share // 2, features), BF)] * 2,
            shape_of((2 * share, hidden), BF),
            shape_of((1, hidden), F32),
            shape_of((share, features), F32),
        ],
        scratch=[pltpu.VMEM((2 * share, features), F32)],
        grid=(steps,),
        in_specs=[None] * HALVES
        + w_grow.specs(block)
        + w_shrink.specs(block)
        + [pl.BlockSpec((2 * share, block), lambda i: (0, i))],
        out_specs=[
            None,
            None,
            pl.BlockSpec((2 * share, block), lambda i: (0, i)),
            pl.BlockSpec((1, block), lambda i: (0, i)),
            None,
        ],
        name="feed_backward",
    )
    return {"other": outs[:2], "grad": outs[2], "sums": outs[3], "own": outs[4]}


def weight_grad(order, pairs, part, parts, first=0, count=None):
    features = pairs[0][0][0].shape[1]
    width = features // parts
    count = count or width
    block = min(256, count)
    per, skip, wide = count // block, first // block, width // block
    start, shards = (0, 1) if part == 0 else (1, parts - 1)
    spans = [right[0].shape[1] for _, right in pairs]
    flat, specs = [], []
    for left, right in pairs:
        flat += [*left, *right]
        specs += [
            pl.BlockSpec((v.shape[0], block), lambda i: (0, (start + i // per) * wide + skip + i % per)) for v in left
        ]
        specs += [None] * len(right)

    def body(*refs):
        out, at, column = refs[-1], 0, 0
        for (left, right), span in zip(pairs, spans):
            a = jnp.concatenate([r[...] for r in refs[at : at + len(left)]], 0)
            at += len(left)
            b = jnp.concatenate([r[...] for r in refs[at : at + len(right)]], 0)
            at += len(right)
            out[0, :, column : column + span] = dot_rows(a, b).astype(BF)
            column += span

    return order.call(
        body,
        flat,
        [shape_of((shards, count, sum(spans)), BF)],
        grid=(shards * per,),
        in_specs=specs,
        out_specs=[pl.BlockSpec((1, block, sum(spans)), lambda i: (i // per, i % per, 0))],
        name="weight_grad",
    )[0]


class Pipeline:
    def __init__(self, order):
        self.order = order
        self.line = lax.axis_size("dp") == 4
        self.waiting, self.pieces, self.at = [], [], 0

    def offer(self, others, own, finish):
        self.waiting.append({"others": others, "own": own, "finish": finish})

    def piece(self, at):
        return self.pieces[at] if 0 <= at < len(self.pieces) else None

    def step(self):
        size = lax.axis_size("fsdp")
        now = self.at
        self.at += 1
        oldest, older, old, new = (self.piece(now - 1 - back) for back in (3, 2, 1, 0))
        if not self.line:
            if new is not None:
                total = lax.psum(combine(self.order, [new["own"], *new["came"]]), "dp")
                new["finish"](total, total)
        else:
            if old is not None:
                old["inner"] = combine(self.order, [old["sum"], old["swapped"]])
                old["met"] = lax.ppermute(old["inner"], "dp", [(1, 2), (2, 1)])
            if older is not None:
                older["total"] = combine(self.order, [older["inner"], older["met"]])
            if new is not None and older is not None and new["own"].shape == older["total"].shape:
                new["sum"], send = combine(self.order, [new["own"], *new["came"]], older["total"])
                new["swapped"] = older["back"] = lax.ppermute(send, "dp", [(0, 1), (1, 0), (2, 3), (3, 2)])
            else:
                if new is not None:
                    new["sum"] = combine(self.order, [new["own"], *new["came"]])
                    new["swapped"] = lax.ppermute(new["sum"], "dp", [(0, 1), (3, 2)])
                if older is not None:
                    older["back"] = lax.ppermute(older["total"], "dp", [(1, 0), (2, 3)])
            if oldest is not None:
                oldest["finish"](oldest["total"], oldest["back"])
        if self.waiting:
            piece = self.waiting.pop(0)
            piece["came"] = [to_fsdp(piece["others"][k], k + 1) for k in range(size - 1)]
            self.pieces.append(piece)
        else:
            self.pieces.append(None)

    def drain(self):
        while self.waiting or any(p is not None for p in self.pieces[self.at - 4 :]):
            self.step()


def at_end():
    here = lax.axis_index("dp")
    return (here == 0) | (here == lax.axis_size("dp") - 1)


def combine(order, terms, other=None):
    rows, width = terms[0].shape
    dtype = terms[0].dtype
    count = len(terms)
    block = max(rows // 2, 16)
    spec = pl.BlockSpec((block, width), lambda i: (i, 0))
    given = [*terms] + ([] if other is None else [other])

    def body(*refs):
        total = refs[0][...].astype(F32)
        for ref in refs[1:count]:
            total = total + ref[...].astype(F32)
        total = total.astype(dtype)
        refs[len(given)][...] = total
        if other is not None:
            refs[-1][...] = jnp.where(at_end(), total.astype(F32), refs[count][...].astype(F32)).astype(dtype)

    found = order.call(
        body,
        given,
        [shape_of((rows, width), dtype)] * (1 if other is None else 2),
        grid=(rows // block,),
        in_specs=[spec] * len(given),
        out_specs=[spec] * (1 if other is None else 2),
        name="combine",
    )
    return found[0] if other is None else found


def finish_piece(order, total, back, layer, first, held, parts, name):
    rows, width = total.shape
    given = [] if held is None else list(held)
    blocks = []
    for shape, axis, _, _ in parts:
        block, place = [1, *shape[1:]], [layer] + [0] * (len(shape) - 1)
        block[axis], place[axis] = rows, first // rows
        blocks.append(pl.BlockSpec(tuple(block), lambda i, place=tuple(place): place))

    def body(*refs):
        outs = refs[2 + len(given) :]
        value = jnp.where(at_end(), refs[1][...].astype(F32), refs[0][...].astype(F32))
        for out, (shape, axis, start, count) in zip(outs, parts):
            if len(shape) == 4:
                span = count // shape[1]
                for g in range(shape[1]):
                    out[0, g] = value[:, start + g * span : start + (g + 1) * span]
            elif axis == 2:
                out[0] = value[:, start : start + count].T
            else:
                out[0] = value[:, start : start + count]

    return order.call(
        body,
        [total, back, *given],
        [shape_of(shape, F32) for shape, *_ in parts],
        grid=(1,),
        in_specs=[None, None] + [ANY] * len(given),
        out_specs=blocks,
        alias={2 + i: i for i in range(len(given))},
        name=name,
        limit=24,
    )


STEPS = (0, 1, 0, 1, 0, 1, 0, 1)
MORE_STEPS = (0, 0, 1, 0, 1, 0, 1, 0)
LAST_CUT = 2


def gather_halves(share):
    return [share, to_core(share)]


def per_device(
    activations, cotangent, lengths, w_qkv, w_out, w_up, w_down, b_qv, b_up, norm_gains, layer_biases
):
    size = lax.axis_size("fsdp")
    order = Order()
    kinds = range(len(STREAMS))

    smalls = (b_qv, b_up, norm_gains, layer_biases)
    flat = jnp.concatenate([value.reshape(-1) for value in smalls])
    pieces = [flat] + [from_fsdp(flat, step) for step in range(1, size)]

    def unpack(at):
        found, start = [], 0
        for value in smalls:
            found.append(pieces[at][start : start + value.size].reshape(value.shape))
            start += value.size
        return found

    unpacked = [unpack(at) for at in range(size)]
    bias_heads, bias_grow, gains, biases = (
        jnp.concatenate([u[i] for u in unpacked], -1).astype(F32) for i in range(4)
    )
    bias_heads, bias_grow = natural(bias_heads, 3), natural(bias_grow, 2)
    features = gains.shape[-1]
    vectors = jnp.concatenate([gains.reshape(-1, features), biases.reshape(-1, features)], 0)
    head_rows = [bias_heads[layer].reshape(2, -1) for layer in range(LAYERS)]
    grow_rows = [bias_grow[layer].reshape(1, -1) for layer in range(LAYERS)]

    def fetch(whole, layer, axis, cut):
        shard = whole[layer]
        count = shard.shape[axis] // cut
        if count < 128:
            cut, count = 1, shard.shape[axis]
        came = []
        for step in range(1, size):
            for at in range(cut):
                piece = lax.slice_in_dim(shard, at * count, (at + 1) * count, axis=axis)
                came.append(from_fsdp(piece, step))
        return Weight([shard] + came, axis)

    weights = [
        [fetch(w_qkv, layer, 1, 1), fetch(w_out, layer, 1, 1), fetch(w_up, layer, 0, 2), fetch(w_down, layer, 1, 2)]
        for layer in range(LAYERS)
    ]

    def halves_of(weight):
        came = weight.arrays[1:]
        middle = (len(came) + 1) // 2
        return came[:middle], came[middle:]

    up_zero, down_zero = halves_of(weights[0][2]), halves_of(weights[0][3])
    up_one, down_one = halves_of(weights[1][2]), halves_of(weights[1][3])
    ahead = {
        1: up_zero[0],
        2: [*up_zero[1], *down_zero[0], *down_zero[1]],
        3: weights[1][0].arrays[1:],
        4: [*weights[1][1].arrays[1:], *up_one[0]],
        5: up_one[1],
        6: [*down_one[0], *down_one[1]],
    }

    slots = deal_rows(order, activations)
    residual = [(slots[s][0], None, None) for s in kinds]
    across = to_chip(cotangent)
    shares = deal_share(order, [cotangent, to_core(cotangent), across, to_core(across)])

    streams = len(STREAMS)
    kept = [{k: [None] * streams for k in ("x", "attended", "grown", "one", "two", "middle")} for _ in range(LAYERS)]
    terms = [None] * streams
    back_two, slots_two, fed = ([[None] * streams for _ in range(LAYERS)] for _ in range(3))
    back_one, slots_one, went = ([[None] * streams for _ in range(LAYERS)] for _ in range(3))

    def gain_at(layer, which):
        return 2 * layer + which

    def bias_at(layer, which):
        return 2 * LAYERS + 4 * layer + which

    def second_norm(layer, s):
        one = kept[layer]["one"][s]
        kept[layer]["two"][s] = norm_forward(
            order,
            terms[s],
            (one[1], gain_at(layer, 0), bias_at(layer, 2)),
            vectors,
            (bias_at(layer, 1), gain_at(layer, 1), bias_at(layer, 3)),
        )

    def attend(layer, s):
        def before():
            if layer > 0:
                second_norm(layer - 1, s)
                two = kept[layer - 1]["two"][s]
                slots[s] = gather_halves(two[0])
                residual[s] = (two[1], gain_at(layer - 1, 1), bias_at(layer - 1, 3))
            kept[layer]["x"][s] = slots[s]

        def products():
            w_proj, w_mix = weights[layer][:2]
            found = attention_forward(order, STREAMS[s], slots[s], (w_proj, w_mix, head_rows[layer]), lengths)
            kept[layer]["attended"][s] = found
            return found, []

        return before, products

    def feed(layer, s):
        def before():
            one = norm_forward(
                order, terms[s], residual[s], vectors, (bias_at(layer, 0), gain_at(layer, 0), bias_at(layer, 2))
            )
            kept[layer]["one"][s] = one
            kept[layer]["middle"][s] = gather_halves(one[0])

        def products():
            w_grow, w_shrink = weights[layer][2:]
            found = feed_forward(order, kept[layer]["middle"][s], (w_grow, w_shrink, grow_rows[layer]))
            kept[layer]["grown"][s] = found
            return found, []

        return before, products

    def feed_back(layer, s):
        def before():
            if layer + 1 == LAYERS:
                second_norm(layer, s)
                terms[s] = [shares[s]]
            two = kept[layer]["two"][s]
            back_two[layer][s] = norm_backward(order, terms[s], two[1], two[2], vectors, gain_at(layer, 1))
            slots_two[layer][s] = gather_halves(back_two[layer][s][0])

        def products():
            w_grow, w_shrink = weights[layer][2:]
            found = feed_backward(order, slots_two[layer][s], kept[layer]["grown"][s]["slope"], (w_grow, w_shrink))
            fed[layer][s] = found
            if s + 1 == streams:
                state = kept[layer]
                queue(layer, "down", [([v for t in kinds for v in slots_two[layer][t]], [state["grown"][t]["act"] for t in kinds])])
                queue(layer, "up", [([v for t in kinds for v in state["middle"][t]], [fed[layer][t]["grad"] for t in kinds])])
            return found, [back_two[layer][s][2]]

        return before, products

    def attend_back(layer, s):
        def before():
            one = kept[layer]["one"][s]
            back_one[layer][s] = norm_backward(order, terms[s], one[1], one[2], vectors, gain_at(layer, 0))
            slots_one[layer][s] = gather_halves(back_one[layer][s][0])

        def products():
            w_proj, w_mix = weights[layer][:2]
            state = kept[layer]
            found = attention_backward(order, STREAMS[s], slots_one[layer][s], (w_proj, w_mix), state["attended"][s])
            went[layer][s] = found
            if s + 1 == streams:
                queue(
                    layer,
                    "att",
                    [
                        ([v for t in kinds for v in state["x"][t]], [went[layer][t]["grad"] for t in kinds]),
                        ([v for t in kinds for v in slots_one[layer][t]], [state["attended"][t]["ctx"] for t in kinds]),
                    ],
                    1 if layer > 0 else LAST_CUT,
                )
            return found, [back_one[layer][s][2]]

        return before, products

    pipeline = Pipeline(order)
    fillers = []
    outputs = {}
    span, hidden = w_out.shape[1], w_down.shape[1]
    width = features // size
    forms = {
        "down": [((LAYERS, hidden, width), 2, 0, hidden)],
        "up": [((LAYERS, width, hidden), 1, 0, hidden)],
        "att": [((LAYERS, 3, width, span), 2, 0, 3 * span), ((LAYERS, span, width), 2, 3 * span, span)],
    }

    def queue(layer, name, pairs, cut=1):
        count = width // cut if width // cut >= 128 else width
        for first in range(0, width, count):
            queue_rows(layer, name, pairs, first, count)

    def queue_rows(layer, name, pairs, first, count):
        def finish(total, back):
            outputs[name] = finish_piece(
                order, total, back, layer, first, outputs.get(name), forms[name], "finish_" + name
            )

        found = {}

        def others():
            found["others"] = weight_grad(order, pairs, 1, size, first, count)

        def own():
            found["own"] = weight_grad(order, pairs, 0, size, first, count)[0]
            pipeline.offer(found["others"], found["own"], finish)

        fillers.extend([others, own])

    def fill(count):
        for _ in range(count):
            if fillers:
                fillers.pop(0)()

    items = []
    for layer in range(LAYERS):
        items += [attend(layer, s) for s in kinds] + [feed(layer, s) for s in kinds]
    forward_items = len(items)
    for layer in reversed(range(LAYERS)):
        items += [feed_back(layer, s) for s in kinds] + [attend_back(layer, s) for s in kinds]
    items[0][0]()
    for at, (_, products) in enumerate(items):
        s = at % streams
        found, more = products()
        beside = [to_core(part) for part in found["other"]]
        if at >= forward_items:
            fill(2)
            if STEPS[at - forward_items]:
                pipeline.step()
        order.pin(ahead.get(at + 1, []))
        if at == 0:
            order.hold()
        if at + 1 < len(items):
            items[at + 1][0]()
        if at == forward_items + 1:
            out_rows = gather_halves(jnp.concatenate([kept[-1]["two"][t][0] for t in kinds], 0))
        low, wide = add_send(order, found["own"], beside)
        terms[s] = [wide, to_chip(low), *more]
        if at >= forward_items and MORE_STEPS[at - forward_items]:
            pipeline.step()
    fill(len(fillers))
    pipeline.step()
    layer_out = natural_share(order, out_rows, BF)
    ends = [last_sum(order, terms[s]) for s in kinds]
    end_rows = gather_halves(jnp.concatenate(ends, 0))
    pipeline.step()
    input_grad = natural_share(order, end_rows, F32)
    pipeline.drain()

    sums, head_sums, grow_sums = {}, {}, {}
    for layer in range(LAYERS):
        sums[layer] = [sum(back_one[layer][s][1] for s in kinds), sum(back_two[layer][s][1] for s in kinds)]
        head_sums[layer] = sum(went[layer][s]["sums"] for s in kinds)
        grow_sums[layer] = sum(fed[layer][s]["sums"] for s in kinds)
    heads_bias = jnp.stack(
        [
            jnp.stack([head_sums[layer][0, :span], head_sums[layer][0, 2 * span :]])
            for layer in range(LAYERS)
        ]
    ).reshape(bias_heads.shape)
    grow_bias = jnp.stack([grow_sums[layer] for layer in range(LAYERS)]).reshape(bias_grow.shape)
    gain_pair = jnp.stack([jnp.stack([sums[layer][i][0] for i in range(2)]) for layer in range(LAYERS)])
    bias_set = jnp.stack(
        [
            jnp.stack([sums[layer][0][2], sums[layer][1][2], sums[layer][0][1], sums[layer][1][1]])
            for layer in range(LAYERS)
        ]
    )
    norms = jnp.concatenate([gain_pair.reshape(-1, features), bias_set.reshape(-1, features)])
    norms = norms + to_core(norms)
    own_heads, own_grow = own_first(heads_bias, 3), own_first(grow_bias, 2)
    little = []
    for step in range(size):
        parts = []
        for value in (own_heads, own_grow, norms):
            part = value.shape[-1] // size
            parts.append(value[..., step * part : (step + 1) * part].reshape(-1))
        little.append(jnp.concatenate(parts))
    total = little[0]
    for step in range(1, size):
        total = total + to_fsdp(little[step], step)
    dp_size = lax.axis_size("dp")
    reach = 1
    while reach < dp_size:
        total = total + lax.ppermute(total, "dp", [(i, i ^ reach) for i in range(dp_size)])
        reach *= 2
    finals, start = [], 0
    for value in (own_heads, own_grow, gain_pair, bias_set):
        amount = value.size // size
        finals.append(total[start : start + amount].reshape(value.shape[:-1] + (value.shape[-1] // size,)))
        start += amount
    return (layer_out, input_grad, *outputs["att"], *outputs["up"], *outputs["down"], *finals)


def solution(mesh):
    in_specs = (
        P(("dp", "fsdp"), None),
        P(("dp", "fsdp", "tensor"), None),
        P(("dp", "fsdp")),
        P(None, None, "fsdp", "tensor"),
        P(None, "tensor", "fsdp"),
        P(None, "fsdp", "tensor"),
        P(None, "tensor", "fsdp"),
        P(None, None, "tensor", "fsdp"),
        P(None, "tensor", "fsdp"),
        P(None, None, "fsdp"),
        P(None, None, "fsdp"),
    )
    out_specs = (
        P(("dp", "fsdp", "tensor"), None),
        P(("dp", "fsdp", "tensor"), None),
        P(None, None, "fsdp", "tensor"),
        P(None, "tensor", "fsdp"),
        P(None, "fsdp", "tensor"),
        P(None, "tensor", "fsdp"),
        P(None, None, "tensor", "fsdp"),
        P(None, "tensor", "fsdp"),
        P(None, None, "fsdp"),
        P(None, None, "fsdp"),
    )
    return jax.shard_map(
        per_device, mesh=mesh, in_specs=in_specs, out_specs=out_specs, check_vma=False
    )
```

time: 867 us -> 591 us (0.68)
  Pallas kernels: 0 us -> 250 us
  waiting for transfers between devices: 361 us -> 160 us
  matrix products: 144 us -> 0 us
  other arithmetic: 125 us -> 3 us
  blocking collectives: 30.6 us -> 0 us
  local copies, waits for them, and re-layouts: 95.4 us -> 70.9 us
    pallas_call x0 -> x97, Pallas kernels: none -> 250 us  [call(): pl.pallas_call(kernel, grid=grid, in_specs=in_specs, out_specs=out_specs,...]
    dot_general x88 -> x0, matrix products: 144 us -> none  [the longest x16 42 us: dot_t(): lax.dot_general(left, right, (((1,), (1,)), ((), ())), preferred_element_...]
    ppermute x16 -> x17, waiting for transfers between devices: 122 us -> 18 us  [to_chip(): return lax.ppermute(value, 'tensor', CHIP_SWAP)]
    ppermute x9 -> x8, waiting for transfers between devices: 92.5 us -> 9.66 us  [to_fsdp(): lax.ppermute(value, 'fsdp', [(i, (i + step) % size) for i in range(size)])]
    convert_element_type x45 -> x0, other arithmetic: 41.9 us -> none  [the longest x16 19.6 us: sum_line(): value = (value.astype(F32) + came.astype(F32)).astype(BF)]
    concatenate x23 -> x4, other arithmetic: 39.1 us -> 1.13 us  [the longest x1 1.1 us: per_device(): end_rows = gather_halves(jnp.concatenate(ends, 0))]
    unnamed x435 -> x339, local copies, waits for them, and re-layouts: 18.6 us -> 52.5 us
    psum x1 -> x0, blocking collectives: 30.6 us -> none  [per_device(): total = lax.psum(total, 'dp')]
  transfers between devices with their start and end apart: 89 -> 110, of which waited for: 31 -> 50; matrix products, arithmetic and copies ran while one was open for 37% -> 4% of each run, Pallas kernels for 0% -> 41%
where the time goes in v2:
time: 591 us; the launch traced here: 580 us
  Pallas kernels  250 us (42%)
  waiting for transfers between devices  160 us (27%)
  starting transfers between devices  92.9 us (16%)
  local copies, waits for them, and re-layouts  70.9 us (12%)
    pallas_call x97, Pallas kernels, call(): pl.pallas_call(kernel, grid=grid, in_specs=in_specs, out_specs=out_specs,...  250 us
    unnamed x339, local copies, waits for them, and re-layouts  52.5 us
    ppermute x13, waiting for transfers between devices, from_fsdp(): lax.ppermute(value, 'fsdp', [((i + step) % size, i) for i in range(size)])  47 us
    ppermute x5, waiting for transfers between devices, step(): new['swapped'] = lax.ppermute(new['sum'], 'dp', [(0, 1), (3, 2)])  24.8 us
    ppermute x5, waiting for transfers between devices, step(): older['back'] = lax.ppermute(older['total'], 'dp', [(1, 0), (2, 3)])  22 us
    ppermute x5, starting transfers between devices, step(): new['swapped'] = lax.ppermute(new['sum'], 'dp', [(0, 1), (3, 2)])  20.2 us
    ppermute x51, waiting for transfers between devices, to_core(): return lax.ppermute(value, 'tensor', CORE_SWAP)  19.2 us
    ppermute x17, waiting for transfers between devices, to_chip(): return lax.ppermute(value, 'tensor', CHIP_SWAP)  18 us
  transfers between devices with their start and end apart: 110, of which 50 were waited for; matrix products, arithmetic and copies ran while one was open for 4% of the time, Pallas kernels for 41%

profile of v2, /device:TPU:0, one launch (start us, length us, event | category | flops | bytes accessed | tf_op | source)
XLA Modules:
  0.0 579.9 jit_solution(11602773903783716612)
XLA Ops:
  0.6 3.0 collective-permute-start.4
  8.2 2.8 slice_bitcast_fusion.4
  29.9 7.5 %collective-permute-done.1.refs_5_ = bf16[256,512]{1,0:T(8,128)(2,1)} collective-permute-done((bf16[256,512]{1,0:T(8,128)(2,1)S(1)}, bf16[256,512]{1,0:T(8,128)(2,1)}, u32[]{:S(2)}, u32[]{:S(2)}) %collective-permute-start.1) | collective-permute-done | bytes 262176 | tf_op jit(solution)/shard_map/ppermute | solution.py:34
  37.3 6.4 %attention_forward.4 = (bf16[128,1024]{1,0:T(8,128)(2,1)S(1)}, bf16[128,1024]{1,0:T(8,128)(2,1)S(1)}, f32[256,1024]{1,0:T(8,128)S(1)}, bf16[512,768]{1,0:T(8,128...) custom-call(bf16[256,1024]{1,0:T(8,128)(2,1)S(1)} %get-tuple-element.196.refs_4_.refs_0_.refs_2_, ...), custom_call_target="tpu_custom_call" | custom-call | tf_op jit(solution)/shard_map/attention_forward/pallas_call | solution.py:120
  51.2 8.8 %attention_forward.5 = (bf16[160,1024]{1,0:T(8,128)(2,1)}, bf16[160,1024]{1,0:T(8,128)(2,1)}, f32[320,1024]{1,0:T(8,128)S(1)}, bf16[640,768]{1,0:T(8,128)(2,1)S(...) custom-call(bf16[320,1024]{1,0:T(8,128)(2,1)S(1)} %get-tuple-element, ...), custom_call_target="tpu_custom_call" | custom-call | tf_op jit(solution)/shard_map/attention_forward/pallas_call | solution.py:120
  66.0 4.9 collective-permute-done.12.refs_6_.refs_7_
  74.4 7.8 %collective-permute-done.10.refs_4_ = bf16[256,1024]{1,0:T(8,128)(2,1)} collective-permute-done((bf16[256,1024]{1,0:T(8,128)(2,1)}, bf16[256,1024]{1,0:T(8,128)(2,1)}, u32[]{:S(2)}, u32[]{:S(2)}) %collective-permute-start.10) | collective-permute-done | bytes 524320 | tf_op jit(solution)/shard_map/ppermute | solution.py:34
  84.5 2.4 norm_forward.8
  91.5 2.7 slice_bitcast_fusion
  96.3 9.6 %feed_forward.4 = (bf16[128,1024]{1,0:T(8,128)(2,1)S(1)}, bf16[128,1024]{1,0:T(8,128)(2,1)S(1)}, bf16[512,1024]{1,0:T(8,128)(2,1)S(1)}, bf16[512,1024]{1,0:T(8,128)(2,1)S(1)}, f32[256,1024]{1,0:T(8,128)S(1)}) custom-call(bf16[256,1024]{1,0:T(8,128)(2,1)} %get-tuple-element.207.refs_3_.refs_0_, bf16[256,1024]{1,0:T(8,128)(2,1)} %collective-permute-done.13.refs_1_, ...), custom_call_target="tpu_custom_call" | custom-call | tf_op jit(solution)/shard_map/feed_forward/pallas_call | solution.py:120
  114.0 10.4 %feed_forward.5 = (bf16[160,1024]{1,0:T(8,128)(2,1)S(1)}, bf16[160,1024]{1,0:T(8,128)(2,1)S(1)}, bf16[640,1024]{1,0:T(8,128)(2,1)S(1)}, bf16[640,1024]{1,0:T(8,128)(2,1)S(1)}, f32[320,1024]{1,0:T(8,128)S(1)}) custom-call(bf16[320,1024]{1,0:T(8,128)(2,1)S(1)} %get-tuple-element.215.refs_3_.refs_0_.refs_2_, ...), custom_call_target="tpu_custom_call" | custom-call | tf_op jit(solution)/shard_map/feed_forward/pallas_call | solution.py:120
  125.6 7.8 %collective-permute-done.21.refs_4_.refs_5_ = bf16[256,512]{1,0:T(8,128)(2,1)S(1)} collective-permute-done((bf16[256,512]{1,0:T(8,128)(2,1)S(1)}, bf16[256,512]{1,0:T(8,128)(2,1)S(1)}, u32[]{:S(2)}, u32[]{:S(2)}) %collective-permute-start.21) | collective-permute-done | bytes 262176 | tf_op jit(solution)/shard_map/ppermute | solution.py:34
  142.6 6.8 %attention_forward.6 = (bf16[128,1024]{1,0:T(8,128)(2,1)S(1)}, bf16[128,1024]{1,0:T(8,128)(2,1)S(1)}, f32[256,1024]{1,0:T(8,128)S(1)}, bf16[512,768]{1,0:T(8,128...) custom-call(bf16[256,1024]{1,0:T(8,128)(2,1)} %get-tuple-element.220.refs_3_.refs_0_, ...), custom_call_target="tpu_custom_call" | custom-call | tf_op jit(solution)/shard_map/attention_forward/pallas_call | solution.py:120
  149.3 3.7 collective-permute-done.30.refs_4_
  159.6 8.0 %attention_forward.7 = (bf16[160,1024]{1,0:T(8,128)(2,1)S(1)}, bf16[160,1024]{1,0:T(8,128)(2,1)S(1)}, f32[320,1024]{1,0:T(8,128)S(1)}, bf16[640,768]{1,0:T(8,128...) custom-call(bf16[320,1024]{1,0:T(8,128)(2,1)S(1)} %get-tuple-element, ...), custom_call_target="tpu_custom_call" | custom-call | tf_op jit(solution)/shard_map/attention_forward/pallas_call | solution.py:120
  168.1 3.2 collective-permute-done.32.refs_4_.refs_6_
  171.3 10.8 %collective-permute-done.33.refs_5_.refs_7_ = bf16[1024,256]{1,0:T(8,128)(2,1)S(1)} collective-permute-done((bf16[1024,256]{1,0:T(8,128)(2,1)S(1)}, bf16[1024,256]{1,0:T(8,128)(2,1)S(1)}, u32[]{:S(2)}, u32[]{:S(2)}) %collective-permute-start.33) | collective-permute-done | bytes 524320 | tf_op jit(solution)/shard_map/ppermute | solution.py:34
  185.5 17.0 %feed_forward.6 = (bf16[128,1024]{1,0:T(8,128)(2,1)S(1)}, bf16[128,1024]{1,0:T(8,128)(2,1)S(1)}, bf16[512,1024]{1,0:T(8,128)(2,1)S(1)}, bf16[512,1024]{1,0:T(8,128)(2,1)S(1)}, f32[256,1024]{1,0:T(8,128)S(1)}) custom-call(bf16[256,1024]{1,0:T(8,128)(2,1)S(1)} %get-tuple-element.234.refs_3_.refs_0_, bf16[256,1024]{1,0:T(8,128)(2,1)S(1)} %collective-permute-done.35.refs_1_, ...), custom_call_target="tpu_custom_call" | custom-call | tf_op jit(solution)/shard_map/feed_forward/pallas_call | solution.py:120
  207.7 10.1 %feed_forward.7 = (bf16[160,1024]{1,0:T(8,128)(2,1)S(1)}, bf16[160,1024]{1,0:T(8,128)(2,1)S(1)}, bf16[640,1024]{1,0:T(8,128)(2,1)S(1)}, bf16[640,1024]{1,0:T(8,128)(2,1)S(1)}, f32[320,1024]{1,0:T(8,128)S(1)}) custom-call(bf16[320,1024]{1,0:T(8,128)(2,1)S(1)} %get-tuple-element.243.refs_3_.refs_0_.refs_2_, ...), custom_call_target="tpu_custom_call" | custom-call | tf_op jit(solution)/shard_map/feed_forward/pallas_call | solution.py:120
  225.6 8.6 %feed_backward.4 = (bf16[128,1024]{1,0:T(8,128)(2,1)S(1)}, bf16[128,1024]{1,0:T(8,128)(2,1)S(1)}, bf16[512,1024]{1,0:T(8,128)(2,1)S(1)}, f32[1,1024]{1,0:T(1,128)S(1)}, f32[256,1024]{1,0:T(8,128)S(1)}) custom-call(bf16[256,1024]{1,0:T(8,128)(2,1)S(1)} %get-tuple-element.253.refs_3_.refs_0_, bf16[256,1024]{1,0:T(8,128)(2,1)S(1)} %collective-permute-done.46.refs_1_, ...), custom_call_target="tpu_custom_call" | custom-call | tf_op jit(solution)/shard_map/feed_backward/pallas_call | solution.py:120
  234.3 4.0 collective-permute-done.45.refs_1_
  244.7 9.9 %feed_backward.5 = (bf16[160,1024]{1,0:T(8,128)(2,1)S(1)}, bf16[160,1024]{1,0:T(8,128)(2,1)S(1)}, bf16[640,1024]{1,0:T(8,128)(2,1)S(1)}, f32[1,1024]{1,0:T(1,128)S(1)}, f32[320,1024]{1,0:T(8,128)S(1)}) custom-call(bf16[320,1024]{1,0:T(8,128)(2,1)S(1)} %get-tuple-element.265.refs_3_.refs_0_.refs_2_, ...), custom_call_target="tpu_custom_call" | custom-call | tf_op jit(solution)/shard_map/feed_backward/pallas_call | solution.py:120
  254.6 2.3 weight_grad.14.refs_6_
  262.7 7.0 %attention_backward.4 = (bf16[128,1024]{1,0:T(8,128)(2,1)S(1)}, bf16[128,1024]{1,0:T(8,128)(2,1)S(1)}, f32[256,1024]{1,0:T(8,128)S(1)}, bf16[512,768]{1,0:T(8,128)(2,1)S(1)}, f32[1,768]{1,0:T(1,128)S(1)}) custom-call(bf16[256,1024]{1,0:T(8,128)(2,1)S(1)} %get-tuple-element.274.refs_3_.refs_0_.refs_6_, ...), custom_call_target="tpu_custom_call" | custom-call | tf_op jit(solution)/shard_map/attention_backward/pallas_call | solution.py:120
  274.4 3.9 collective-permute-done.57.refs_1_
  279.4 2.4 collective-permute-done.60.refs_1_
  282.1 4.0 collective-permute-start.61
  288.8 8.5 %attention_backward.5 = (bf16[160,1024]{1,0:T(8,128)(2,1)S(1)}, bf16[160,1024]{1,0:T(8,128)(2,1)S(1)}, f32[320,1024]{1,0:T(8,128)S(1)}, bf16[640,768]{1,0:T(8,128)(2,1)S(1)}, f32[1,768]{1,0:T(1,128)S(1)}) custom-call(bf16[320,1024]{1,0:T(8,128)(2,1)S(1)} %get-tuple-element.288.refs_3_.refs_0_.refs_8_, ...), custom_call_target="tpu_custom_call" | custom-call | tf_op jit(solution)/shard_map/attention_backward/pallas_call | solution.py:120
  297.8 2.8 weight_grad.18.refs_12_
  300.6 2.8 weight_grad.19.refs_2_
  303.5 3.7 collective-permute-done.61.refs_1_
  307.5 2.5 collective-permute-done.59.refs_1_
  317.2 8.7 %feed_backward.6 = (bf16[128,1024]{1,0:T(8,128)(2,1)S(1)}, bf16[128,1024]{1,0:T(8,128)(2,1)S(1)}, bf16[512,1024]{1,0:T(8,128)(2,1)S(1)}, f32[1,1024]{1,0:T(1,128)S(1)}, f32[256,1024]{1,0:T(8,128)S(1)}) custom-call(bf16[256,1024]{1,0:T(8,128)(2,1)S(1)} %get-tuple-element.303.refs_3_.refs_0_, bf16[256,1024]{1,0:T(8,128)(2,1)S(1)} %collective-permute-done.63.refs_1_, ...), custom_call_target="tpu_custom_call" | custom-call | tf_op jit(solution)/shard_map/feed_backward/pallas_call | solution.py:120
  326.1 2.7 collective-permute-done.68.refs_1_
  330.5 2.3 collective-permute-done.71.refs_1_
  333.4 2.5 collective-permute-done.72.refs_1_
  341.6 10.1 %feed_backward.7 = (bf16[160,1024]{1,0:T(8,128)(2,1)S(1)}, bf16[160,1024]{1,0:T(8,128)(2,1)S(1)}, bf16[640,1024]{1,0:T(8,128)(2,1)S(1)}, f32[1,1024]{1,0:T(1,128)S(1)}, f32[320,1024]{1,0:T(8,128)S(1)}) custom-call(bf16[320,1024]{1,0:T(8,128)(2,1)S(1)} %get-tuple-element.314.refs_3_.refs_0_.refs_2_, ...), custom_call_target="tpu_custom_call" | custom-call | tf_op jit(solution)/shard_map/feed_backward/pallas_call | solution.py:120
  355.7 2.9 collective-permute-done.73.refs_1_
  368.1 7.1 %attention_backward.6 = (bf16[128,1024]{1,0:T(8,128)(2,1)S(1)}, bf16[128,1024]{1,0:T(8,128)(2,1)S(1)}, f32[256,1024]{1,0:T(8,128)S(1)}, bf16[512,768]{1,0:T(8,128)(2,1)S(1)}, f32[1,768]{1,0:T(1,128)S(1)}) custom-call(bf16[256,1024]{1,0:T(8,128)(2,1)S(1)} %get-tuple-element.325.refs_3_.refs_0_.refs_6_, ...), custom_call_target="tpu_custom_call" | custom-call | tf_op jit(solution)/shard_map/attention_backward/pallas_call | solution.py:120
  376.3 2.8 weight_grad.22.refs_6_
  379.1 2.9 weight_grad.23.refs_6_
  389.9 3.8 collective-permute-start.87
  395.2 17.1 %collective-permute-done.81.refs_1_ = bf16[512,1024]{1,0:T(8,128)(2,1)S(1)} collective-permute-done((bf16[512,1024]{1,0:T(8,128)(2,1)S(1)}, bf16[512,1024]{1,0:T(8,128)(2,1)S(1)}, u32[]{:S(2)}, u32[]{:S(2)}) %collective-permute-start.81) | collective-permute-done | bytes 1048608 | tf_op jit(solution)/shard_map/ppermute | solution.py:726
  416.6 9.5 %attention_backward.7 = (bf16[160,1024]{1,0:T(8,128)(2,1)}, bf16[160,1024]{1,0:T(8,128)(2,1)}, f32[320,1024]{1,0:T(8,128)S(1)}, bf16[640,768]{1,0:T(8,128)(2,1)S(1)}, f32[1,768]{1,0:T(1,128)S(1)}) custom-call(bf16[320,1024]{1,0:T(8,128)(2,1)S(1)} %get-tuple-element.338.refs_3_.refs_0_.refs_8_, bf16[320,1024]{1,0:T(8,128)(2,1)S(1)} %collective-permute-done.80.refs_1_.refs_9_, ...), custom_call_target="tpu_custom_call" | custom-call | tf_op jit(solution)/shard_map/attention_backward/pallas_call | solution.py:120
  428.8 5.0 collective-permute-done.87.refs_1_
  436.3 2.6 collective-permute-start.90
  446.8 2.2 add_send.31
  451.1 8.9 %collective-permute-done.90.refs_1_ = bf16[512,1024]{1,0:T(8,128)(2,1)} collective-permute-done((bf16[512,1024]{1,0:T(8,128)(2,1)}, bf16[512,1024]{1,0:T(8,128)(2,1)}, u32[]{:S(2)}, u32[]{:S(2)}) %collective-permute-start.90) | collective-permute-done | bytes 1048608 | tf_op jit(solution)/shard_map/ppermute | solution.py:724
  465.3 2.7 combine.33.refs_2_.refs_0_
  470.0 2.6 combine.34.refs_2_.refs_0_
  474.4 2.8 natural_share.2.refs_3_
  485.4 5.3 collective-permute-start.99
  492.1 9.6 %collective-permute-done.99.refs_1_ = bf16[256,1024]{1,0:T(8,128)(2,1)} collective-permute-done((bf16[256,1024]{1,0:T(8,128)(2,1)}, bf16[256,1024]{1,0:T(8,128)(2,1)}, u32[]{:S(2)}, u32[]{:S(2)}) %collective-permute-start.99) | collective-permute-done | bytes 524320 | tf_op jit(solution)/shard_map/ppermute | solution.py:724
  504.1 2.6 combine.37.refs_2_.refs_0_
  509.9 6.4 %collective-permute-start.100 = (bf16[256,1024]{1,0:T(8,128)(2,1)}, bf16[256,1024]{1,0:T(8,128)(2,1)}, u32[]{:S(2)}, u32[]{:S(2)}) collective-permute-start(bf16[256,1024]{1,0:T(8,128)(2,1)} %combine.38.refs_3_.refs_0_), channel_id=1, source_target_pairs={{0,8},{24,16},{1,9},{25,17},{2,10},{26,18},{3,11},{27,19},{4,12},{... | collective-permute-start | bytes 1572872 | tf_op jit(solution)/shard_map/ppermute | solution.py:724
  518.9 3.3 finish_down.3.refs_2_
  524.4 2.9 natural_share.3.refs_2_
  536.4 3.9 collective-permute-done.102.refs_1_
  540.4 3.1 finish_up.3.refs_2_
  550.8 2.2 collective-permute-done.107
  553.0 6.2 %collective-permute-start.108 = (f32[7680]{0:T(1024)S(1)}, f32[7680]{0:T(1024)S(1)}, u32[]{:S(2)}, u32[]{:S(2)}) collective-permute-start(f32[7680]{0:T(1024)S(1)} %maximum_add_fusion), channel_id=1, source_target_pairs={{0,8},{8,0},{16,24},{24,16},{1,9},{9,1},{17,25},{25,17},{2,10},{10... | collective-permute-start | bytes 92168 | tf_op jit(solution)/shard_map/ppermute | solution.py:1094
  559.2 6.6 %collective-permute-done.108 = f32[7680]{0:T(1024)S(1)} collective-permute-done((f32[7680]{0:T(1024)S(1)}, f32[7680]{0:T(1024)S(1)}, u32[]{:S(2)}, u32[]{:S(2)}) %collective-permute-start.108) | collective-permute-done | bytes 30752 | tf_op jit(solution)/shard_map/ppermute | solution.py:1094
  565.8 4.8 collective-permute-done.109
  577.1 2.4 finish_att.5
  (671 shorter events, 222.4 us)
Async XLA Ops:
  0.6 16.7 %collective-permute-start.4 = (bf16[288,1024]{1,0:T(8,128)(2,1)}, bf16[288,1024]{1,0:T(8,128)(2,1)}, u32[]{:S(2)}, u32[]{:S(2)}) collective-permute-start(bf16[288,1024]{1,0:T(8,128)(2,1)} %refs_0_.3), channel_id=1, source_target_pairs={{0,2},{2,0},{1,3},{3,1},{4,6},{6,4},{5,7},{7,5},{8,10},{10,8},{9,1... | collective-permute-start | bytes 1769480 | tf_op jit(solution)/shard_map/ppermute | solution.py:29
  3.6 21.5 %collective-permute-start.3 = (bf16[288,1024]{1,0:T(8,128)(2,1)}, bf16[288,1024]{1,0:T(8,128)(2,1)}, u32[]{:S(2)}, u32[]{:S(2)}) collective-permute-start(bf16[288,1024]{1,0:T(8,128)(2,1)} %refs_0_.3), channel_id=1, source_target_pairs={{0,1},{1,0},{2,3},{3,2},{4,5},{5,4},{6,7},{7,6},{8,9},{9,8},{10,11... | collective-permute-start | bytes 1769480 | tf_op jit(solution)/shard_map/ppermute | solution.py:25
  6.6 15.2 %collective-permute-start.2 = (bf16[7680]{0:T(1024)(128)(2,1)S(1)}, bf16[7680]{0:T(1024)(128)(2,1)}, u32[]{:S(2)}, u32[]{:S(2)}) collective-permute-start(bf16[7680]{0:T(1024)(128)(2,1)S(1)} %pad_maximum_fusion.4), channel_id=1, source_target_pairs={{4,0},{0,4},{5,1},{1,5},{6,2},{2,6},{7,3},{3,7},{12,8},{8,12},{13,... | collective-permute-start | bytes 46088 | tf_op jit(solution)/shard_map/ppermute | solution.py:34
  11.0 26.3 %collective-permute-start = (bf16[3,512,256]{2,1,0:T(8,128)(2,1)}, bf16[3,512,256]{2,1,0:T(8,128)(2,1)}, u32[]{:S(2)}, u32[]{:S(2)}) collective-permute-start(bf16[3,512,256]{2,1,0:T(8,128)(2,1)} %get-tuple-element.391.refs_2_), channel_id=1, source_target_pairs={{4,0},{0,4},{5,1},{1,5},{6,2},{2,6},{7,3},{3,7},{12,8},{8,12},{13,... | collective-permute-start | bytes 2359304 | tf_op jit(solution)/shard_map/ppermute | solution.py:34
  12.2 25.1 %collective-permute-start.1 = (bf16[256,512]{1,0:T(8,128)(2,1)S(1)}, bf16[256,512]{1,0:T(8,128)(2,1)}, u32[]{:S(2)}, u32[]{:S(2)}) collective-permute-start(bf16[256,512]{1,0:T(8,128)(2,1)S(1)} %get-tuple-element.397.refs_4_), channel_id=1, source_target_pairs={{4,0},{0,4},{5,1},{1,5},{6,2},{2,6},{7,3},{3,7},{12,8},{8,12},{13,... | collective-permute-start | bytes 786440 | tf_op jit(solution)/shard_map/ppermute | solution.py:34
  21.8 26.7 %collective-permute-start.8 = (bf16[256,1024]{1,0:T(8,128)(2,1)}, bf16[256,1024]{1,0:T(8,128)(2,1)}, u32[]{:S(2)}, u32[]{:S(2)}) collective-permute-start(bf16[256,1024]{1,0:T(8,128)(2,1)} %get-tuple-element.389), channel_id=1, source_target_pairs={{4,0},{0,4},{5,1},{1,5},{6,2},{2,6},{7,3},{3,7},{12,8},{8,12},{13,... | collective-permute-start | bytes 1572872 | tf_op jit(solution)/shard_map/ppermute | solution.py:34
  25.2 40.3 %collective-permute-start.11 = (bf16[1024,256]{1,0:T(8,128)(2,1)}, bf16[1024,256]{1,0:T(8,128)(2,1)}, u32[]{:S(2)}, u32[]{:S(2)}) collective-permute-start(bf16[1024,256]{1,0:T(8,128)(2,1)} %get-tuple-element.395), channel_id=1, source_target_pairs={{4,0},{0,4},{5,1},{1,5},{6,2},{2,6},{7,3},{3,7},{12,8},{8,12},{13,... | collective-permute-start | bytes 1572872 | tf_op jit(solution)/shard_map/ppermute | solution.py:34
  46.7 24.2 %collective-permute-start.12 = (bf16[1024,256]{1,0:T(8,128)(2,1)S(1)}, bf16[1024,256]{1,0:T(8,128)(2,1)S(1)}, u32[]{:S(2)}, u32[]{:S(2)}) collective-permute-start(bf16[1024,256]{1,0:T(8,128)(2,1)S(1)} %copy-done.162), channel_id=1, source_target_pairs={{4,0},{0,4},{5,1},{1,5},{6,2},{2,6},{7,3},{3,7},{12,8},{8,12},{13,... | collective-permute-start | bytes 1572872 | tf_op jit(solution)/shard_map/ppermute | solution.py:34
  48.6 33.7 %collective-permute-start.10 = (bf16[256,1024]{1,0:T(8,128)(2,1)}, bf16[256,1024]{1,0:T(8,128)(2,1)}, u32[]{:S(2)}, u32[]{:S(2)}) collective-permute-start(bf16[256,1024]{1,0:T(8,128)(2,1)} %get-tuple-element.388), channel_id=1, source_target_pairs={{4,0},{0,4},{5,1},{1,5},{6,2},{2,6},{7,3},{3,7},{12,8},{8,12},{13,... | collective-permute-start | bytes 1572872 | tf_op jit(solution)/shard_map/ppermute | solution.py:34
  51.0 31.3 %collective-permute-start.9 = (bf16[256,1024]{1,0:T(8,128)(2,1)}, bf16[256,1024]{1,0:T(8,128)(2,1)}, u32[]{:S(2)}, u32[]{:S(2)}) collective-permute-start(bf16[256,1024]{1,0:T(8,128)(2,1)} %get-tuple-element.203.refs_8_), channel_id=1, source_target_pairs={{0,2},{2,0},{1,3},{3,1},{4,6},{6,4},{5,7},{7,5},{8,10},{10,8},{9,1... | collective-permute-start | bytes 1572872 | tf_op jit(solution)/shard_map/ppermute | solution.py:29
  65.5 22.5 %collective-permute-start.14 = (bf16[160,1024]{1,0:T(8,128)(2,1)}, bf16[160,1024]{1,0:T(8,128)(2,1)S(1)}, u32[]{:S(2)}, u32[]{:S(2)}) collective-permute-start(bf16[160,1024]{1,0:T(8,128)(2,1)} %get-tuple-element.206.refs_7_), channel_id=1, source_target_pairs={{0,1},{1,0},{2,3},{3,2},{4,5},{5,4},{6,7},{7,6},{8,9},{9,8},{10,11... | collective-permute-start | bytes 983048 | tf_op jit(solution)/shard_map/ppermute | solution.py:25
  65.5 22.5 %collective-permute-start.15 = (bf16[160,1024]{1,0:T(8,128)(2,1)}, bf16[160,1024]{1,0:T(8,128)(2,1)}, u32[]{:S(2)}, u32[]{:S(2)}) collective-permute-start(bf16[160,1024]{1,0:T(8,128)(2,1)} %get-tuple-element.209), channel_id=1, source_target_pairs={{0,1},{1,0},{2,3},{3,2},{4,5},{5,4},{6,7},{7,6},{8,9},{9,8},{10,11... | collective-permute-start | bytes 983048 | tf_op jit(solution)/shard_map/ppermute | solution.py:25
  71.8 34.1 %collective-permute-start.19 = (bf16[3,512,256]{2,1,0:T(8,128)(2,1)}, bf16[3,512,256]{2,1,0:T(8,128)(2,1)}, u32[]{:S(2)}, u32[]{:S(2)}) collective-permute-start(bf16[3,512,256]{2,1,0:T(8,128)(2,1)} %get-tuple-element.390.refs_2_), channel_id=1, source_target_pairs={{4,0},{0,4},{5,1},{1,5},{6,2},{2,6},{7,3},{3,7},{12,8},{8,12},{13,... | collective-permute-start | bytes 2359304 | tf_op jit(solution)/shard_map/ppermute | solution.py:34
  91.0 15.7 %collective-permute-start.18 = (bf16[320,1024]{1,0:T(8,128)(2,1)}, bf16[320,1024]{1,0:T(8,128)(2,1)}, u32[]{:S(2)}, u32[]{:S(2)}) collective-permute-start(bf16[320,1024]{1,0:T(8,128)(2,1)} %get-tuple-element.210.refs_9_), channel_id=1, source_target_pairs={{0,2},{2,0},{1,3},{3,1},{4,6},{6,4},{5,7},{7,5},{8,10},{10,8},{9,1... | collective-permute-start | bytes 1966088 | tf_op jit(solution)/shard_map/ppermute | solution.py:29
  110.3 23.0 %collective-permute-start.22 = (bf16[256,1024]{1,0:T(8,128)(2,1)S(1)}, bf16[256,1024]{1,0:T(8,128)(2,1)S(1)}, u32[]{:S(2)}, u32[]{:S(2)}) collective-permute-start(bf16[256,1024]{1,0:T(8,128)(2,1)S(1)} %copy-done.163), channel_id=1, source_target_pairs={{4,0},{0,4},{5,1},{1,5},{6,2},{2,6},{7,3},{3,7},{12,8},{8,12},{13,... | collective-permute-start | bytes 1572872 | tf_op jit(solution)/shard_map/ppermute | solution.py:34
  112.6 20.8 %collective-permute-start.20 = (bf16[256,1024]{1,0:T(8,128)(2,1)S(1)}, bf16[256,1024]{1,0:T(8,128)(2,1)S(1)}, u32[]{:S(2)}, u32[]{:S(2)}) collective-permute-start(bf16[256,1024]{1,0:T(8,128)(2,1)S(1)} %get-tuple-element.217.refs_9_), channel_id=1, source_target_pairs={{0,2},{2,0},{1,3},{3,1},{4,6},{6,4},{5,7},{7,5},{8,10},{10,8},{9,1... | collective-permute-start | bytes 1572872 | tf_op jit(solution)/shard_map/ppermute | solution.py:29
  137.8 16.2 %collective-permute-start.29 = (bf16[320,1024]{1,0:T(8,128)(2,1)}, bf16[320,1024]{1,0:T(8,128)(2,1)}, u32[]{:S(2)}, u32[]{:S(2)}) collective-permute-start(bf16[320,1024]{1,0:T(8,128)(2,1)} %get-tuple-element.223.refs_8_), channel_id=1, source_target_pairs={{0,2},{2,0},{1,3},{3,1},{4,6},{6,4},{5,7},{7,5},{8,10},{10,8},{9,1... | collective-permute-start | bytes 1966088 | tf_op jit(solution)/shard_map/ppermute | solution.py:29
  138.4 14.7 %collective-permute-start.30 = (bf16[256,1024]{1,0:T(8,128)(2,1)}, bf16[256,1024]{1,0:T(8,128)(2,1)}, u32[]{:S(2)}, u32[]{:S(2)}) collective-permute-start(bf16[256,1024]{1,0:T(8,128)(2,1)} %get-tuple-element.386), channel_id=1, source_target_pairs={{4,0},{0,4},{5,1},{1,5},{6,2},{2,6},{7,3},{3,7},{12,8},{8,12},{13,... | collective-permute-start | bytes 1572872 | tf_op jit(solution)/shard_map/ppermute | solution.py:34
  156.5 14.8 %collective-permute-start.32 = (bf16[1024,256]{1,0:T(8,128)(2,1)S(1)}, bf16[1024,256]{1,0:T(8,128)(2,1)S(1)}, u32[]{:S(2)}, u32[]{:S(2)}) collective-permute-start(bf16[1024,256]{1,0:T(8,128)(2,1)S(1)} %get-tuple-element.393), channel_id=1, source_target_pairs={{4,0},{0,4},{5,1},{1,5},{6,2},{2,6},{7,3},{3,7},{12,8},{8,12},{13,... | collective-permute-start | bytes 1572872 | tf_op jit(solution)/shard_map/ppermute | solution.py:34
  157.1 25.0 %collective-permute-start.33 = (bf16[1024,256]{1,0:T(8,128)(2,1)S(1)}, bf16[1024,256]{1,0:T(8,128)(2,1)S(1)}, u32[]{:S(2)}, u32[]{:S(2)}) collective-permute-start(bf16[1024,256]{1,0:T(8,128)(2,1)S(1)} %get-tuple-element.392), channel_id=1, source_target_pairs={{4,0},{0,4},{5,1},{1,5},{6,2},{2,6},{7,3},{3,7},{12,8},{8,12},{13,... | collective-permute-start | bytes 1572872 | tf_op jit(solution)/shard_map/ppermute | solution.py:34
  158.8 23.2 %collective-permute-start.31 = (bf16[256,1024]{1,0:T(8,128)(2,1)S(1)}, bf16[256,1024]{1,0:T(8,128)(2,1)S(1)}, u32[]{:S(2)}, u32[]{:S(2)}) collective-permute-start(bf16[256,1024]{1,0:T(8,128)(2,1)S(1)} %get-tuple-element.231.refs_8_), channel_id=1, source_target_pairs={{0,2},{2,0},{1,3},{3,1},{4,6},{6,4},{5,7},{7,5},{8,10},{10,8},{9,1... | collective-permute-start | bytes 1572872 | tf_op jit(solution)/shard_map/ppermute | solution.py:29
  167.5 15.1 %collective-permute-start.36 = (bf16[160,1024]{1,0:T(8,128)(2,1)S(1)}, bf16[160,1024]{1,0:T(8,128)(2,1)S(1)}, u32[]{:S(2)}, u32[]{:S(2)}) collective-permute-start(bf16[160,1024]{1,0:T(8,128)(2,1)S(1)} %get-tuple-element.233.refs_6_), channel_id=1, source_target_pairs={{0,1},{1,0},{2,3},{3,2},{4,5},{5,4},{6,7},{7,6},{8,9},{9,8},{10,11... | collective-permute-start | bytes 983048 | tf_op jit(solution)/shard_map/ppermute | solution.py:25
  167.6 15.0 %collective-permute-start.37 = (bf16[160,1024]{1,0:T(8,128)(2,1)S(1)}, bf16[160,1024]{1,0:T(8,128)(2,1)S(1)}, u32[]{:S(2)}, u32[]{:S(2)}) collective-permute-start(bf16[160,1024]{1,0:T(8,128)(2,1)S(1)} %get-tuple-element.236), channel_id=1, source_target_pairs={{0,1},{1,0},{2,3},{3,2},{4,5},{5,4},{6,7},{7,6},{8,9},{9,8},{10,11... | collective-permute-start | bytes 983048 | tf_op jit(solution)/shard_map/ppermute | solution.py:25
  182.9 19.7 %collective-permute-start.40 = (bf16[320,1024]{1,0:T(8,128)(2,1)S(1)}, bf16[320,1024]{1,0:T(8,128)(2,1)S(1)}, u32[]{:S(2)}, u32[]{:S(2)}) collective-permute-start(bf16[320,1024]{1,0:T(8,128)(2,1)S(1)} %get-tuple-element.237.refs_9_), channel_id=1, source_target_pairs={{0,2},{2,0},{1,3},{3,1},{4,6},{6,4},{5,7},{7,5},{8,10},{10,8},{9,1... | collective-permute-start | bytes 1966088 | tf_op jit(solution)/shard_map/ppermute | solution.py:29
  206.3 14.0 %collective-permute-start.41 = (bf16[256,1024]{1,0:T(8,128)(2,1)S(1)}, bf16[256,1024]{1,0:T(8,128)(2,1)S(1)}, u32[]{:S(2)}, u32[]{:S(2)}) collective-permute-start(bf16[256,1024]{1,0:T(8,128)(2,1)S(1)} %get-tuple-element.245.refs_9_), channel_id=1, source_target_pairs={{0,2},{2,0},{1,3},{3,1},{4,6},{6,4},{5,7},{7,5},{8,10},{10,8},{9,1... | collective-permute-start | bytes 1572872 | tf_op jit(solution)/shard_map/ppermute | solution.py:29
  222.3 16.0 %collective-permute-start.45 = (bf16[320,1024]{1,0:T(8,128)(2,1)S(1)}, bf16[320,1024]{1,0:T(8,128)(2,1)S(1)}, u32[]{:S(2)}, u32[]{:S(2)}) collective-permute-start(bf16[320,1024]{1,0:T(8,128)(2,1)S(1)} %get-tuple-element.255.refs_9_), channel_id=1, source_target_pairs={{0,2},{2,0},{1,3},{3,1},{4,6},{6,4},{5,7},{7,5},{8,10},{10,8},{9,1... | collective-permute-start | bytes 1966088 | tf_op jit(solution)/shard_map/ppermute | solution.py:29
  243.3 16.7 %collective-permute-start.50 = (bf16[256,1024]{1,0:T(8,128)(2,1)S(1)}, bf16[256,1024]{1,0:T(8,128)(2,1)S(1)}, u32[]{:S(2)}, u32[]{:S(2)}) collective-permute-start(bf16[256,1024]{1,0:T(8,128)(2,1)S(1)} %get-tuple-element.267.refs_9_), channel_id=1, source_target_pairs={{0,2},{2,0},{1,3},{3,1},{4,6},{6,4},{5,7},{7,5},{8,10},{10,8},{9,1... | collective-permute-start | bytes 1572872 | tf_op jit(solution)/shard_map/ppermute | solution.py:29
  256.9 25.0 %collective-permute-start.60 = (bf16[512,1024]{1,0:T(8,128)(2,1)S(1)}, bf16[512,1024]{1,0:T(8,128)(2,1)S(1)}, u32[]{:S(2)}, u32[]{:S(2)}) collective-permute-start(bf16[512,1024]{1,0:T(8,128)(2,1)S(1)} %bitcast.63), channel_id=1, source_target_pairs={{0,4},{4,0},{1,5},{5,1},{2,6},{6,2},{3,7},{7,3},{8,12},{12,8},{9,1... | collective-permute-start | bytes 3145736 | tf_op jit(solution)/shard_map/ppermute | solution.py:39
  261.1 17.2 %collective-permute-start.57 = (bf16[320,1024]{1,0:T(8,128)(2,1)S(1)}, bf16[320,1024]{1,0:T(8,128)(2,1)S(1)}, u32[]{:S(2)}, u32[]{:S(2)}) collective-permute-start(bf16[320,1024]{1,0:T(8,128)(2,1)S(1)} %get-tuple-element.279.refs_8_), channel_id=1, source_target_pairs={{0,2},{2,0},{1,3},{3,1},{4,6},{6,4},{5,7},{7,5},{8,10},{10,8},{9,1... | collective-permute-start | bytes 1966088 | tf_op jit(solution)/shard_map/ppermute | solution.py:29
  282.1 25.0 %collective-permute-start.61 = (bf16[512,1024]{1,0:T(8,128)(2,1)S(1)}, bf16[512,1024]{1,0:T(8,128)(2,1)S(1)}, u32[]{:S(2)}, u32[]{:S(2)}) collective-permute-start(bf16[512,1024]{1,0:T(8,128)(2,1)S(1)} %combine.21.refs_11_.refs_0_), channel_id=1, source_target_pairs={{0,8},{24,16},{1,9},{25,17},{2,10},{26,18},{3,11},{27,19},{4,12},{... | collective-permute-start | bytes 3145736 | tf_op jit(solution)/shard_map/ppermute | solution.py:724
  286.1 23.8 %collective-permute-start.59 = (bf16[512,1024]{1,0:T(8,128)(2,1)S(1)}, bf16[512,1024]{1,0:T(8,128)(2,1)S(1)}, u32[]{:S(2)}, u32[]{:S(2)}) collective-permute-start(bf16[512,1024]{1,0:T(8,128)(2,1)S(1)} %bitcast.64), channel_id=1, source_target_pairs={{0,4},{4,0},{1,5},{5,1},{2,6},{6,2},{3,7},{7,3},{8,12},{12,8},{9,1... | collective-permute-start | bytes 3145736 | tf_op jit(solution)/shard_map/ppermute | solution.py:39
  286.7 26.3 %collective-permute-start.58 = (bf16[256,1024]{1,0:T(8,128)(2,1)S(1)}, bf16[256,1024]{1,0:T(8,128)(2,1)S(1)}, u32[]{:S(2)}, u32[]{:S(2)}) collective-permute-start(bf16[256,1024]{1,0:T(8,128)(2,1)S(1)} %get-tuple-element.290.refs_2_), channel_id=1, source_target_pairs={{0,2},{2,0},{1,3},{3,1},{4,6},{6,4},{5,7},{7,5},{8,10},{10,8},{9,1... | collective-permute-start | bytes 1572872 | tf_op jit(solution)/shard_map/ppermute | solution.py:29
  297.3 17.1 %collective-permute-start.64 = (bf16[160,1024]{1,0:T(8,128)(2,1)S(1)}, bf16[160,1024]{1,0:T(8,128)(2,1)S(1)}, u32[]{:S(2)}, u32[]{:S(2)}) collective-permute-start(bf16[160,1024]{1,0:T(8,128)(2,1)S(1)} %get-tuple-element.302.refs_12_), channel_id=1, source_target_pairs={{0,1},{1,0},{2,3},{3,2},{4,5},{5,4},{6,7},{7,6},{8,9},{9,8},{10,11... | collective-permute-start | bytes 983048 | tf_op jit(solution)/shard_map/ppermute | solution.py:25
  297.5 16.9 %collective-permute-start.65 = (bf16[160,1024]{1,0:T(8,128)(2,1)S(1)}, bf16[160,1024]{1,0:T(8,128)(2,1)S(1)}, u32[]{:S(2)}, u32[]{:S(2)}) collective-permute-start(bf16[160,1024]{1,0:T(8,128)(2,1)S(1)} %get-tuple-element.306), channel_id=1, source_target_pairs={{0,1},{1,0},{2,3},{3,2},{4,5},{5,4},{6,7},{7,6},{8,9},{9,8},{10,11... | collective-permute-start | bytes 983048 | tf_op jit(solution)/shard_map/ppermute | solution.py:25
  310.2 22.6 %collective-permute-start.71 = (bf16[512,1024]{1,0:T(8,128)(2,1)S(1)}, bf16[512,1024]{1,0:T(8,128)(2,1)S(1)}, u32[]{:S(2)}, u32[]{:S(2)}) collective-permute-start(bf16[512,1024]{1,0:T(8,128)(2,1)S(1)} %combine.23.refs_6_.refs_0_), channel_id=1, source_target_pairs={{0,8},{24,16},{1,9},{25,17},{2,10},{26,18},{3,11},{27,19},{4,12},{... | collective-permute-start | bytes 3145736 | tf_op jit(solution)/shard_map/ppermute | solution.py:724
  312.2 20.9 %collective-permute-start.70 = (bf16[512,1024]{1,0:T(8,128)(2,1)S(1)}, bf16[512,1024]{1,0:T(8,128)(2,1)S(1)}, u32[]{:S(2)}, u32[]{:S(2)}) collective-permute-start(bf16[512,1024]{1,0:T(8,128)(2,1)S(1)} %combine.22.refs_2_.refs_0_), channel_id=1, source_target_pairs={{8,16},{16,8},{9,17},{17,9},{10,18},{18,10},{11,19},{19,11},{12,20... | collective-permute-start | bytes 3145736 | tf_op jit(solution)/shard_map/ppermute | solution.py:715
  313.0 22.9 %collective-permute-start.72 = (bf16[512,1024]{1,0:T(8,128)(2,1)S(1)}, bf16[512,1024]{1,0:T(8,128)(2,1)S(1)}, u32[]{:S(2)}, u32[]{:S(2)}) collective-permute-start(bf16[512,1024]{1,0:T(8,128)(2,1)S(1)} %bitcast.62), channel_id=1, source_target_pairs={{0,4},{4,0},{1,5},{5,1},{2,6},{6,2},{3,7},{7,3},{8,12},{12,8},{9,1... | collective-permute-start | bytes 3145736 | tf_op jit(solution)/shard_map/ppermute | solution.py:39
  314.6 14.2 %collective-permute-start.68 = (bf16[320,1024]{1,0:T(8,128)(2,1)S(1)}, bf16[320,1024]{1,0:T(8,128)(2,1)S(1)}, u32[]{:S(2)}, u32[]{:S(2)}) collective-permute-start(bf16[320,1024]{1,0:T(8,128)(2,1)S(1)} %get-tuple-element.307.refs_9_), channel_id=1, source_target_pairs={{0,2},{2,0},{1,3},{3,1},{4,6},{6,4},{5,7},{7,5},{8,10},{10,8},{9,1... | collective-permute-start | bytes 1966088 | tf_op jit(solution)/shard_map/ppermute | solution.py:29
  336.3 22.3 %collective-permute-start.73 = (bf16[512,1024]{1,0:T(8,128)(2,1)S(1)}, bf16[512,1024]{1,0:T(8,128)(2,1)S(1)}, u32[]{:S(2)}, u32[]{:S(2)}) collective-permute-start(bf16[512,1024]{1,0:T(8,128)(2,1)S(1)} %get-tuple-element.319), channel_id=1, source_target_pairs={{0,8},{8,0},{16,24},{24,16},{1,9},{9,1},{17,25},{25,17},{2,10},{10... | collective-permute-start | bytes 3145736 | tf_op jit(solution)/shard_map/ppermute | solution.py:720
  338.5 21.8 %collective-permute-start.74 = (bf16[512,1024]{1,0:T(8,128)(2,1)S(1)}, bf16[512,1024]{1,0:T(8,128)(2,1)S(1)}, u32[]{:S(2)}, u32[]{:S(2)}) collective-permute-start(bf16[512,1024]{1,0:T(8,128)(2,1)S(1)} %combine.24.refs_2_.refs_0_), channel_id=1, source_target_pairs={{8,16},{16,8},{9,17},{17,9},{10,18},{18,10},{11,19},{19,11},{12,20... | collective-permute-start | bytes 3145736 | tf_op jit(solution)/shard_map/ppermute | solution.py:715
  339.5 23.4 %collective-permute-start.69 = (bf16[256,1024]{1,0:T(8,128)(2,1)S(1)}, bf16[256,1024]{1,0:T(8,128)(2,1)S(1)}, u32[]{:S(2)}, u32[]{:S(2)}) collective-permute-start(bf16[256,1024]{1,0:T(8,128)(2,1)S(1)} %get-tuple-element.316.refs_2_), channel_id=1, source_target_pairs={{0,2},{2,0},{1,3},{3,1},{4,6},{6,4},{5,7},{7,5},{8,10},{10,8},{9,1... | collective-permute-start | bytes 1572872 | tf_op jit(solution)/shard_map/ppermute | solution.py:29
  359.0 29.0 %collective-permute-start.83 = (bf16[512,1024]{1,0:T(8,128)(2,1)S(1)}, bf16[512,1024]{1,0:T(8,128)(2,1)S(1)}, u32[]{:S(2)}, u32[]{:S(2)}) collective-permute-start(bf16[512,1024]{1,0:T(8,128)(2,1)S(1)} %combine.27.refs_2_.refs_0_), channel_id=1, source_target_pairs={{8,16},{16,8},{9,17},{17,9},{10,18},{18,10},{11,19},{19,11},{12,20... | collective-permute-start | bytes 3145736 | tf_op jit(solution)/shard_map/ppermute | solution.py:715
  359.7 29.2 %collective-permute-start.82 = (bf16[512,1024]{1,0:T(8,128)(2,1)S(1)}, bf16[512,1024]{1,0:T(8,128)(2,1)S(1)}, u32[]{:S(2)}, u32[]{:S(2)}) collective-permute-start(bf16[512,1024]{1,0:T(8,128)(2,1)S(1)} %bitcast.61), channel_id=1, source_target_pairs={{0,4},{4,0},{1,5},{5,1},{2,6},{6,2},{3,7},{7,3},{8,12},{12,8},{9,1... | collective-permute-start | bytes 3145736 | tf_op jit(solution)/shard_map/ppermute | solution.py:39
  366.2 17.2 %collective-permute-start.79 = (bf16[320,1024]{1,0:T(8,128)(2,1)S(1)}, bf16[320,1024]{1,0:T(8,128)(2,1)S(1)}, u32[]{:S(2)}, u32[]{:S(2)}) collective-permute-start(bf16[320,1024]{1,0:T(8,128)(2,1)S(1)} %get-tuple-element.330.refs_8_), channel_id=1, source_target_pairs={{0,2},{2,0},{1,3},{3,1},{4,6},{6,4},{5,7},{7,5},{8,10},{10,8},{9,1... | collective-permute-start | bytes 1966088 | tf_op jit(solution)/shard_map/ppermute | solution.py:29
  383.3 29.0 %collective-permute-start.81 = (bf16[512,1024]{1,0:T(8,128)(2,1)S(1)}, bf16[512,1024]{1,0:T(8,128)(2,1)S(1)}, u32[]{:S(2)}, u32[]{:S(2)}) collective-permute-start(bf16[512,1024]{1,0:T(8,128)(2,1)S(1)} %combine.28.refs_2_.refs_0_), channel_id=1, source_target_pairs={{8,0},{16,24},{9,1},{17,25},{10,2},{18,26},{11,3},{19,27},{12,4},{... | collective-permute-start | bytes 3145736 | tf_op jit(solution)/shard_map/ppermute | solution.py:726
  389.9 43.9 %collective-permute-start.87 = (bf16[512,1024]{1,0:T(8,128)(2,1)S(1)}, bf16[512,1024]{1,0:T(8,128)(2,1)S(1)}, u32[]{:S(2)}, u32[]{:S(2)}) collective-permute-start(bf16[512,1024]{1,0:T(8,128)(2,1)S(1)} %get-tuple-element.352), channel_id=1, source_target_pairs={{0,8},{8,0},{16,24},{24,16},{1,9},{9,1},{17,25},{25,17},{2,10},{10... | collective-permute-start | bytes 3145736 | tf_op jit(solution)/shard_map/ppermute | solution.py:720
  393.6 41.4 %collective-permute-start.89 = (bf16[512,1024]{1,0:T(8,128)(2,1)S(1)}, bf16[512,1024]{1,0:T(8,128)(2,1)S(1)}, u32[]{:S(2)}, u32[]{:S(2)}) collective-permute-start(bf16[512,1024]{1,0:T(8,128)(2,1)S(1)} %bitcast.65), channel_id=1, source_target_pairs={{0,4},{4,0},{1,5},{5,1},{2,6},{6,2},{3,7},{7,3},{8,12},{12,8},{9,1... | collective-permute-start | bytes 3145736 | tf_op jit(solution)/shard_map/ppermute | solution.py:39
  395.2 18.8 %collective-permute-start.80 = (bf16[320,1024]{1,0:T(8,128)(2,1)S(1)}, bf16[320,1024]{1,0:T(8,128)(2,1)S(1)}, u32[]{:S(2)}, u32[]{:S(2)}) collective-permute-start(bf16[320,1024]{1,0:T(8,128)(2,1)S(1)} %get-tuple-element.338.refs_3_.refs_0_.refs_8_), channel_id=1, source_target_pairs={{0,1},{1,0},{2,3},{3,2},{4,5},{5,4},{6,7},{7,6},{8,9},{9,8},{10,11... | collective-permute-start | bytes 1966088 | tf_op jit(solution)/shard_map/ppermute | solution.py:25
  436.3 23.7 %collective-permute-start.90 = (bf16[512,1024]{1,0:T(8,128)(2,1)}, bf16[512,1024]{1,0:T(8,128)(2,1)}, u32[]{:S(2)}, u32[]{:S(2)}) collective-permute-start(bf16[512,1024]{1,0:T(8,128)(2,1)} %combine.32.refs_2_.refs_0_), channel_id=1, source_target_pairs={{0,8},{24,16},{1,9},{25,17},{2,10},{26,18},{3,11},{27,19},{4,12},{... | collective-permute-start | bytes 3145736 | tf_op jit(solution)/shard_map/ppermute | solution.py:724
  438.8 29.1 %collective-permute-start.88 = (bf16[512,1024]{1,0:T(8,128)(2,1)}, bf16[512,1024]{1,0:T(8,128)(2,1)}, u32[]{:S(2)}, u32[]{:S(2)}) collective-permute-start(bf16[512,1024]{1,0:T(8,128)(2,1)} %combine.31.refs_2_.refs_0_), channel_id=1, source_target_pairs={{8,16},{16,8},{9,17},{17,9},{10,18},{18,10},{11,19},{19,11},{12,20... | collective-permute-start | bytes 3145736 | tf_op jit(solution)/shard_map/ppermute | solution.py:715
  442.2 32.3 %collective-permute-start.47 = (bf16[576,1024]{1,0:T(8,128)(2,1)}, bf16[576,1024]{1,0:T(8,128)(2,1)}, u32[]{:S(2)}, u32[]{:S(2)}) collective-permute-start(bf16[576,1024]{1,0:T(8,128)(2,1)} %constant_dynamic-update-slice_fusion.refs_0_), channel_id=1, source_target_pairs={{0,1},{1,0},{2,3},{3,2},{4,5},{5,4},{6,7},{7,6},{8,9},{9,8},{10,11... | collective-permute-start | bytes 3538952 | tf_op jit(solution)/shard_map/ppermute | solution.py:25
  449.0 31.1 %collective-permute-start.94 = (bf16[320,1024]{1,0:T(8,128)(2,1)}, bf16[320,1024]{1,0:T(8,128)(2,1)}, u32[]{:S(2)}, u32[]{:S(2)}) collective-permute-start(bf16[320,1024]{1,0:T(8,128)(2,1)} %get-tuple-element.356.refs_12_), channel_id=1, source_target_pairs={{0,2},{2,0},{1,3},{3,1},{4,6},{6,4},{5,7},{7,5},{8,10},{10,8},{9,1... | collective-permute-start | bytes 1966088 | tf_op jit(solution)/shard_map/ppermute | solution.py:29
  449.6 28.1 %collective-permute-start.93 = (bf16[256,1024]{1,0:T(8,128)(2,1)}, bf16[256,1024]{1,0:T(8,128)(2,1)}, u32[]{:S(2)}, u32[]{:S(2)}) collective-permute-start(bf16[256,1024]{1,0:T(8,128)(2,1)} %get-tuple-element.346.refs_2_), channel_id=1, source_target_pairs={{0,2},{2,0},{1,3},{3,1},{4,6},{6,4},{5,7},{7,5},{8,10},{10,8},{9,1... | collective-permute-start | bytes 1572872 | tf_op jit(solution)/shard_map/ppermute | solution.py:29
  468.0 36.2 %collective-permute-start.98 = (bf16[512,1024]{1,0:T(8,128)(2,1)}, bf16[512,1024]{1,0:T(8,128)(2,1)}, u32[]{:S(2)}, u32[]{:S(2)}) collective-permute-start(bf16[512,1024]{1,0:T(8,128)(2,1)} %combine.33.refs_2_.refs_0_), channel_id=1, source_target_pairs={{8,16},{16,8},{9,17},{17,9},{10,18},{18,10},{11,19},{19,11},{12,20... | collective-permute-start | bytes 3145736 | tf_op jit(solution)/shard_map/ppermute | solution.py:715
  483.8 38.4 %collective-permute-start.95 = (bf16[576,1024]{1,0:T(8,128)(2,1)}, bf16[576,1024]{1,0:T(8,128)(2,1)}, u32[]{:S(2)}, u32[]{:S(2)}) collective-permute-start(bf16[576,1024]{1,0:T(8,128)(2,1)} %pad_maximum_fusion.refs_0_), channel_id=1, source_target_pairs={{0,1},{1,0},{2,3},{3,2},{4,5},{5,4},{6,7},{7,6},{8,9},{9,8},{10,11... | collective-permute-start | bytes 3538952 | tf_op jit(solution)/shard_map/ppermute | solution.py:25
  483.8 24.2 %collective-permute-start.97 = (bf16[256,1024]{1,0:T(8,128)(2,1)}, bf16[256,1024]{1,0:T(8,128)(2,1)}, u32[]{:S(2)}, u32[]{:S(2)}) collective-permute-start(bf16[256,1024]{1,0:T(8,128)(2,1)} %bitcast.27), channel_id=1, source_target_pairs={{0,4},{4,0},{1,5},{5,1},{2,6},{6,2},{3,7},{7,3},{8,12},{12,8},{9,1... | collective-permute-start | bytes 1572872 | tf_op jit(solution)/shard_map/ppermute | solution.py:39
  485.4 16.3 %collective-permute-start.99 = (bf16[256,1024]{1,0:T(8,128)(2,1)}, bf16[256,1024]{1,0:T(8,128)(2,1)}, u32[]{:S(2)}, u32[]{:S(2)}) collective-permute-start(bf16[256,1024]{1,0:T(8,128)(2,1)} %combine.35.refs_2_.refs_0_), channel_id=1, source_target_pairs={{0,8},{24,16},{1,9},{25,17},{2,10},{26,18},{3,11},{27,19},{4,12},{... | collective-permute-start | bytes 1572872 | tf_op jit(solution)/shard_map/ppermute | solution.py:724
  490.7 28.2 %collective-permute-start.96 = (bf16[512,1024]{1,0:T(8,128)(2,1)}, bf16[512,1024]{1,0:T(8,128)(2,1)}, u32[]{:S(2)}, u32[]{:S(2)}) collective-permute-start(bf16[512,1024]{1,0:T(8,128)(2,1)} %combine.34.refs_2_.refs_0_), channel_id=1, source_target_pairs={{8,0},{16,24},{9,1},{17,25},{10,2},{18,26},{11,3},{19,27},{12,4},{... | collective-permute-start | bytes 3145736 | tf_op jit(solution)/shard_map/ppermute | solution.py:726
  501.7 14.7 %collective-permute-start.106 = (f32[12,1024]{1,0:T(8,128)S(1)}, f32[12,1024]{1,0:T(8,128)S(1)}, u32[]{:S(2)}, u32[]{:S(2)}) collective-permute-start(f32[12,1024]{1,0:T(8,128)S(1)} %pad_maximum_fusion.1), channel_id=1, source_target_pairs={{0,1},{1,0},{2,3},{3,2},{4,5},{5,4},{6,7},{7,6},{8,9},{9,8},{10,11... | collective-permute-start | bytes 147464 | tf_op jit(solution)/shard_map/ppermute | solution.py:25
  506.8 33.6 %collective-permute-start.102 = (bf16[512,1024]{1,0:T(8,128)(2,1)}, bf16[512,1024]{1,0:T(8,128)(2,1)}, u32[]{:S(2)}, u32[]{:S(2)}) collective-permute-start(bf16[512,1024]{1,0:T(8,128)(2,1)} %combine.37.refs_2_.refs_0_), channel_id=1, source_target_pairs={{8,0},{16,24},{9,1},{17,25},{10,2},{18,26},{11,3},{19,27},{12,4},{... | collective-permute-start | bytes 3145736 | tf_op jit(solution)/shard_map/ppermute | solution.py:726
  509.9 17.6 %collective-permute-start.100 = (bf16[256,1024]{1,0:T(8,128)(2,1)}, bf16[256,1024]{1,0:T(8,128)(2,1)}, u32[]{:S(2)}, u32[]{:S(2)}) collective-permute-start(bf16[256,1024]{1,0:T(8,128)(2,1)} %combine.38.refs_3_.refs_0_), channel_id=1, source_target_pairs={{0,8},{24,16},{1,9},{25,17},{2,10},{26,18},{3,11},{27,19},{4,12},{... | collective-permute-start | bytes 1572872 | tf_op jit(solution)/shard_map/ppermute | solution.py:724
  516.5 15.8 %collective-permute-start.103 = (bf16[256,1024]{1,0:T(8,128)(2,1)}, bf16[256,1024]{1,0:T(8,128)(2,1)}, u32[]{:S(2)}, u32[]{:S(2)}) collective-permute-start(bf16[256,1024]{1,0:T(8,128)(2,1)} %copy-done.64), channel_id=1, source_target_pairs={{8,16},{16,8},{9,17},{17,9},{10,18},{18,10},{11,19},{19,11},{12,20... | collective-permute-start | bytes 1572872 | tf_op jit(solution)/shard_map/ppermute | solution.py:715
  535.2 38.1 %collective-permute-start.105 = (bf16[256,1024]{1,0:T(8,128)(2,1)}, bf16[256,1024]{1,0:T(8,128)(2,1)}, u32[]{:S(2)}, u32[]{:S(2)}) collective-permute-start(bf16[256,1024]{1,0:T(8,128)(2,1)} %combine.40.refs_3_.refs_0_), channel_id=1, source_target_pairs={{8,0},{16,24},{9,1},{17,25},{10,2},{18,26},{11,3},{19,27},{12,4},{... | collective-permute-start | bytes 1572872 | tf_op jit(solution)/shard_map/ppermute | solution.py:726
  547.6 29.5 %collective-permute-start.104 = (bf16[256,1024]{1,0:T(8,128)(2,1)}, bf16[256,1024]{1,0:T(8,128)(2,1)}, u32[]{:S(2)}, u32[]{:S(2)}) collective-permute-start(bf16[256,1024]{1,0:T(8,128)(2,1)} %combine.41.refs_4_.refs_0_), channel_id=1, source_target_pairs={{8,0},{16,24},{9,1},{17,25},{10,2},{18,26},{11,3},{19,27},{12,4},{... | collective-permute-start | bytes 1572872 | tf_op jit(solution)/shard_map/ppermute | solution.py:726
  (213 other events, 1423.4 us)

commit v3 on v2

--- a/solution.py
+++ b/solution.py
@@ -85,22 +85,29 @@
     return places
 
 
+SCOPED = 8
+
+
 class Order:
     def __init__(self):
         self.last = None
         self.pins = []
 
     def pin(self, arrays):
-        self.pins.extend(arrays)
-
-    def hold(self):
-        def body(out):
-            out[...] = jnp.zeros(out.shape, F32)
-
-        self.call(body, [], [shape_of((8, 128), F32)], name="hold")
+        self.pins.extend(v for v in arrays)
 
     def call(
-        self, body, inputs, outputs, scratch=(), grid=(), in_specs=None, out_specs=None, name=None, limit=16, alias=None
+        self,
+        body,
+        inputs,
+        outputs,
+        scratch=(),
+        grid=(),
+        in_specs=None,
+        out_specs=None,
+        name=None,
+        limit=SCOPED,
+        alias=None,
     ):
         pins, self.pins = self.pins, []
         count = len(inputs)
@@ -108,28 +115,29 @@
         out_specs = out_specs or [None] * len(outputs)
         in_specs = [whole_of(v.shape, grid) if s is None else s for s, v in zip(in_specs, inputs)]
         out_specs = [whole_of(v.shape, grid) if s is None else s for s, v in zip(out_specs, outputs)]
-        inputs = list(inputs)
-        unread = pins + ([] if self.last is None else [self.last])
-        extra = len(unread)
-        inputs += unread
-        in_specs += [pl.BlockSpec(memory_space=pl.ANY)] * extra
+        token = shape_of((8, 128), F32)
+        inputs = list(inputs) + pins + ([] if self.last is None else [self.last])
+        in_specs += [ANY] * (len(inputs) - count)
+        extra = len(inputs) - count
 
         def kernel(*refs):
-            body(*refs[:count], *refs[count + extra :])
-
-        result = pl.pallas_call(
+            given, refs = refs[:count], refs[count + extra :]
+            outs, mark, own = refs[: len(outputs)], refs[len(outputs)], refs[len(outputs) + 1 :]
+            mark[...] = jnp.zeros(mark.shape, F32)
+            body(*given, *outs, *own)
+
+        *result, self.last = pl.pallas_call(
             kernel,
             grid=grid,
             in_specs=in_specs,
-            out_specs=out_specs,
-            out_shape=outputs,
+            out_specs=[*out_specs, whole_of(token.shape, grid)],
+            out_shape=[*outputs, token],
             scratch_shapes=list(scratch),
             input_output_aliases=alias or {},
             name=name,
             cost_estimate=pl.CostEstimate(flops=0, bytes_accessed=0, transcendentals=0),
             compiler_params=pltpu.CompilerParams(vmem_limit_bytes=limit * MIB),
         )(*inputs)
-        self.last = result[0]
         return result
 
 
@@ -145,6 +153,7 @@
 
 SMEM = pl.BlockSpec(memory_space=pltpu.SMEM)
 ANY = pl.BlockSpec(memory_space=pl.ANY)
+HELD = pl.BlockSpec(memory_space=pltpu.HBM)
 
 
 def core_index():
@@ -152,27 +161,83 @@
 
 
 class Weight:
-    def __init__(self, arrays, axis):
-        self.arrays = arrays
-        self.axis = axis
-        self.widths = [v.shape[axis] for v in arrays]
-        self.starts = [sum(self.widths[:i]) for i in range(len(arrays))]
-        self.shape = arrays[0].shape
-
-    def specs(self, block=None):
-        if block is None:
-            return [None] * len(self.arrays)
-        found = []
-        for v in self.arrays:
-            shape = [block, block]
-            shape[self.axis] = v.shape[self.axis]
-            found.append(pl.BlockSpec(tuple(shape), (lambda i: (0, i)) if self.axis == 0 else (lambda i: (i, 0))))
-        return found
+    def __init__(self, order, whole, layer, axis):
+        self.order, self.whole, self.layer, self.axis = order, whole, layer, axis
+        self.size = lax.axis_size("fsdp")
+        shape = whole.shape[1:]
+        width = shape[axis]
+        self.halved = self.size == 2 and lax.axis_size("dp") % 2 == 0 and width % 256 == 0
+        self.widths = [width] + ([width // 2] * 2 if self.halved else [width] * (self.size - 1))
+        self.shape = shape
+
+    def places(self):
+        width = self.widths[0]
+        if not self.halved:
+            return [pl.ds(k * width, width) for k in range(self.size)]
+        parity = lax.rem(lax.axis_index("dp"), 2)
+        half = width // 2
+        return [
+            pl.ds(0, width),
+            pl.ds(pl.multiple_of(width + parity * half, 128), half),
+            pl.ds(pl.multiple_of(width + (1 - parity) * half, 128), half),
+        ]
+
+    def start(self, own, half):
+        if self.halved:
+            self.early = [from_fsdp(half, 1)]
+            size = lax.axis_size("dp")
+            self.late = [lax.ppermute(self.early[0], "dp", [(i, i ^ 1) for i in range(size)])]
+        else:
+            self.early = [from_fsdp(own, step) for step in range(1, self.size)]
+            self.late = []
+        self.arrays = [own, *self.early, *self.late]
+
+    def specs(self):
+        return [None] * len(self.arrays)
 
     def take(self, refs):
         count = len(self.arrays)
-        places = [slice(a, a + w) for a, w in zip(self.starts, self.widths)]
-        return list(zip(refs[:count], places)), refs[count:]
+        return list(zip(refs[:count], self.places())), refs[count:]
+
+
+def fetch(order, weights):
+    outputs = []
+    for w in weights:
+        outputs.append(shape_of(w.shape, BF))
+        if w.halved:
+            shape = list(w.shape)
+            shape[w.axis] //= 2
+            outputs.append(shape_of(shape, BF))
+
+    def body(*refs):
+        outs, sems = list(refs[len(weights) : -1]), refs[-1]
+        parity = lax.rem(lax.axis_index("dp"), 2)
+        copies = []
+        for w, ref in zip(weights, refs):
+            sources = [ref.at[w.layer]]
+            if w.halved:
+                half = w.widths[1]
+                place = [slice(None)] * len(w.shape)
+                place[w.axis] = pl.ds(pl.multiple_of(parity * half, 128), half)
+                sources.append(ref.at[(w.layer, *place)])
+            for source in sources:
+                copy = pltpu.make_async_copy(source, outs.pop(0), sems.at[len(copies)])
+                copy.start()
+                copies.append(copy)
+        for copy in copies:
+            copy.wait()
+
+    found = order.call(
+        body,
+        [w.whole for w in weights],
+        outputs,
+        scratch=[pltpu.SemaphoreType.DMA((len(outputs),))],
+        in_specs=[HELD] * len(weights),
+        name="fetch",
+    )
+    for w in weights:
+        own = found.pop(0)
+        w.start(own, found.pop(0) if w.halved else None)
 
 
 def deal_rows(order, activations):
@@ -202,6 +267,13 @@
         name="deal_rows",
     )
     return [outs[at * HALVES : (at + 1) * HALVES] for at in range(len(STREAMS))]
+
+
+def copy_rows(order, rows):
+    def body(a, out):
+        out[...] = a[...]
+
+    return order.call(body, [rows], [shape_of(rows.shape, rows.dtype)], name="copy_rows")[0]
 
 
 def deal_share(order, slots):
@@ -270,13 +342,16 @@
 def add_send(order, kept, came):
     half = kept.shape[0] // 2
 
-    def body(a, b, c, low, wide):
+    def body(a, b, c, low):
         for at, came_ref in ((0, b), (half, c)):
-            total = a[at : at + half, :] + came_ref[...].astype(F32)
-            wide[at : at + half, :] = total
-            low[at : at + half, :] = total.astype(BF)
-
-    return order.call(body, [kept, *came], [shape_of(kept.shape, BF), shape_of(kept.shape, F32)], name="add_send")
+            low[at : at + half, :] = (a[at : at + half, :].astype(F32) + came_ref[...].astype(F32)).astype(BF)
+
+    return order.call(body, [kept, *came], [shape_of(kept.shape, BF)], name="add_send")[0]
+
+
+def sum_terms(own, first, second, across):
+    beside = jnp.concatenate([first[...], second[...]], 0)
+    return own[...].astype(F32) + beside.astype(F32) + across[...].astype(F32)
 
 
 def row_of(ref, at):
@@ -287,22 +362,28 @@
     rows, features = terms[0].shape
     bias_at, gain_at, shift_at = rows_of_vectors
 
-    def body(a, b, before, vec, low, normed, inverse):
+    def body(a, b, c, d, before, vec, low, normed, inverse, kept):
         value = before[...].astype(F32)
         if residual[1] is not None:
             value = value * row_of(vec, residual[1]) + row_of(vec, residual[2])
-        value = value + a[...] + b[...].astype(F32) + row_of(vec, bias_at)
+        value = value + sum_terms(a, b, c, d) + row_of(vec, bias_at)
         center = value - jnp.mean(value, -1, keepdims=True)
         scale = lax.rsqrt(jnp.mean(center * center, -1, keepdims=True) + 1e-05)
         unit = center * scale
         normed[...] = unit
+        kept[...] = unit.astype(BF)
         inverse[...] = scale
         low[...] = (unit * row_of(vec, gain_at) + row_of(vec, shift_at)).astype(BF)
 
     return order.call(
         body,
         [*terms, residual[0], vectors],
-        [shape_of((rows, features), BF), shape_of((rows, features), F32), shape_of((rows, 1), F32)],
+        [
+            shape_of((rows, features), BF),
+            shape_of((rows, features), F32),
+            shape_of((rows, 1), F32),
+            shape_of((rows, features), BF),
+        ],
         name="norm_forward",
     )
 
@@ -313,10 +394,10 @@
 
     def body(*refs):
         unit, scale, vec, low, sums, wide = refs[count:]
-        total = refs[0][...].astype(F32)
-        for ref in refs[1:count]:
-            total = total + ref[...].astype(F32)
-        n = unit[...]
+        total = refs[count - 1][...].astype(F32)
+        if count > 1:
+            total = total + sum_terms(*refs[: count - 1])
+        n = unit[...].astype(F32)
         grad = total * row_of(vec, gain_at)
         mean_one = jnp.mean(grad, -1, keepdims=True)
         mean_two = jnp.mean(grad * n, -1, keepdims=True)
@@ -337,10 +418,7 @@
 
 def last_sum(order, terms):
     def body(*refs):
-        total = refs[0][...]
-        for ref in refs[1:-1]:
-            total = total + ref[...].astype(F32)
-        refs[-1][...] = total.astype(BF)
+        refs[-1][...] = (refs[4][...] + sum_terms(*refs[:4])).astype(BF)
 
     return order.call(body, terms, [shape_of(terms[0].shape, BF)], name="last_sum")[0]
 
@@ -423,7 +501,7 @@
                     put_rows(ctx, lanes, both, row, part, share, offset)
         for w, at in wm:
             value = dot(ctx[...], w[...])
-            part_own[:, at] = value[:share]
+            part_own[:, at] = value[:share].astype(BF)
             split_rows(others, at, value[share:])
 
     outs = order.call(
@@ -431,7 +509,7 @@
         [*slots, *w_proj.arrays, *w_mix.arrays, bias_rows, lengths],
         [
             *[shape_of((share // 2, features), BF)] * 2,
-            shape_of((share, features), F32),
+            shape_of((share, features), BF),
             shape_of((2 * share, 3 * span), BF),
             shape_of((2 * share, span), BF),
         ]
@@ -506,7 +584,7 @@
             for kind in range(3):
                 term = dot_t(grad[:, kind * span : (kind + 1) * span], w[kind])
                 value = term if value is None else value + term
-            part_own[:, at] = value[:share]
+            part_own[:, at] = value[:share].astype(BF)
             split_rows(others, at, value[share:])
         sums[...] = jnp.sum(grad[...].astype(F32), 0, keepdims=True)
 
@@ -515,7 +593,7 @@
         [*slots, *w_proj.arrays, *w_mix.arrays, *probs, qkv],
         [
             *[shape_of((share // 2, features), BF)] * 2,
-            shape_of((share, features), F32),
+            shape_of((share, features), BF),
             shape_of((2 * share, 3 * span), BF),
             shape_of((1, 3 * span), F32),
         ],
@@ -526,22 +604,29 @@
     return {"other": outs[:2], "own": outs[2], "grad": outs[3], "sums": outs[4]}
 
 
-FF_BLOCK = 256
+def split_rows(refs, at, value):
+    half = value.shape[0] // 2
+    refs[0][:, at] = value[:half].astype(BF)
+    refs[1][:, at] = value[half:].astype(BF)
+
+
+def leave_terms(low, weight, product, share, others, part_own):
+    for w, at in weight:
+        done = product(low, w[...])
+        part_own[:, at] = done[:share, :].astype(BF)
+        split_rows(others, at, done[share:, :])
 
 
 def feed_forward(order, slots, weights):
     w_grow, w_shrink, bias = weights
     share, features = slots[0].shape
     hidden = w_shrink.shape[0]
-    block = min(FF_BLOCK, hidden)
-    steps = hidden // block
 
     def body(*refs):
         xs, refs = refs[:HALVES], refs[HALVES:]
         wg, refs = w_grow.take(refs)
         ws, refs = w_shrink.take(refs)
-        b, *others, act, slope, part_own, total = refs
-        step = pl.program_id(0)
+        b, *others, act, slope, part_own = refs
         value = None
         for w, at in wg:
             rows = jnp.concatenate([x[:, at] for x in xs], 0)
@@ -553,7 +638,7 @@
         low = (up * cdf).astype(BF)
         act[...] = low
         slope[...] = (cdf + up * density).astype(BF)
-        accumulate(step, steps, low, ws, dot, total, share, others, part_own)
+        leave_terms(low, ws, dot, share, others, part_own)
 
     outs = order.call(
         body,
@@ -562,58 +647,24 @@
             *[shape_of((share // 2, features), BF)] * 2,
             shape_of((2 * share, hidden), BF),
             shape_of((2 * share, hidden), BF),
-            shape_of((share, features), F32),
+            shape_of((share, features), BF),
         ],
-        scratch=[pltpu.VMEM((2 * share, features), F32)],
-        grid=(steps,),
-        in_specs=[None] * HALVES
-        + w_grow.specs(block)
-        + w_shrink.specs(block)
-        + [pl.BlockSpec((1, block), lambda i: (0, i))],
-        out_specs=[None] * 2 + [pl.BlockSpec((2 * share, block), lambda i: (0, i))] * 2 + [None],
         name="feed_forward",
+        limit=FEED_LIMIT,
     )
     return {"other": outs[:2], "act": outs[2], "slope": outs[3], "own": outs[4]}
-
-
-def split_rows(refs, at, value):
-    half = value.shape[0] // 2
-    refs[0][:, at] = value[:half].astype(BF)
-    refs[1][:, at] = value[half:].astype(BF)
-
-
-def accumulate(step, steps, low, weight, product, total, share, others, part_own):
-    for w, at in weight:
-        term = product(low, w[...])
-
-        @pl.when(step == 0)
-        def _():
-            total[:, at] = term
-
-        @pl.when((step > 0) & (step < steps - 1))
-        def _():
-            total[:, at] += term
-
-        @pl.when(step == steps - 1)
-        def _():
-            done = term if steps == 1 else total[:, at] + term
-            part_own[:, at] = done[:share, :]
-            split_rows(others, at, done[share:, :])
 
 
 def feed_backward(order, slots, slope, weights):
     w_grow, w_shrink = weights
     share, features = slots[0].shape
     hidden = w_shrink.shape[0]
-    block = min(FF_BLOCK, hidden)
-    steps = hidden // block
 
     def body(*refs):
         ds, refs = refs[:HALVES], refs[HALVES:]
         wg, refs = w_grow.take(refs)
         ws, refs = w_shrink.take(refs)
-        tilt, *others, grad, sums, part_own, total = refs
-        step = pl.program_id(0)
+        tilt, *others, grad, sums, part_own = refs
         value = None
         for w, at in ws:
             rows = jnp.concatenate([d[:, at] for d in ds], 0)
@@ -622,7 +673,7 @@
         low = (value * tilt[...].astype(F32)).astype(BF)
         grad[...] = low
         sums[...] = jnp.sum(low.astype(F32), 0, keepdims=True)
-        accumulate(step, steps, low, wg, dot_t, total, share, others, part_own)
+        leave_terms(low, wg, dot_t, share, others, part_own)
 
     outs = order.call(
         body,
@@ -631,60 +682,50 @@
             *[shape_of((share // 2, features), BF)] * 2,
             shape_of((2 * share, hidden), BF),
             shape_of((1, hidden), F32),
-            shape_of((share, features), F32),
-        ],
-        scratch=[pltpu.VMEM((2 * share, features), F32)],
-        grid=(steps,),
-        in_specs=[None] * HALVES
-        + w_grow.specs(block)
-        + w_shrink.specs(block)
-        + [pl.BlockSpec((2 * share, block), lambda i: (0, i))],
-        out_specs=[
-            None,
-            None,
-            pl.BlockSpec((2 * share, block), lambda i: (0, i)),
-            pl.BlockSpec((1, block), lambda i: (0, i)),
-            None,
+            shape_of((share, features), BF),
         ],
         name="feed_backward",
+        limit=FEED_LIMIT,
     )
     return {"other": outs[:2], "grad": outs[2], "sums": outs[3], "own": outs[4]}
 
 
-def weight_grad(order, pairs, part, parts, first=0, count=None):
+def weight_grad(order, pairs, part, parts, extra=None):
     features = pairs[0][0][0].shape[1]
     width = features // parts
-    count = count or width
-    block = min(256, count)
-    per, skip, wide = count // block, first // block, width // block
     start, shards = (0, 1) if part == 0 else (1, parts - 1)
-    spans = [right[0].shape[1] for _, right in pairs]
-    flat, specs = [], []
-    for left, right in pairs:
+    flat, specs, total = [], [], 0
+    for left, right, first, count in pairs:
         flat += [*left, *right]
-        specs += [
-            pl.BlockSpec((v.shape[0], block), lambda i: (0, (start + i // per) * wide + skip + i % per)) for v in left
-        ]
-        specs += [None] * len(right)
+        specs += [pl.BlockSpec((v.shape[0], width), lambda i: (0, start + i)) for v in left]
+        specs += [pl.BlockSpec((v.shape[0], count), lambda i, at=first // count: (0, at)) for v in right]
+        total += count
+    more = 0 if extra is None else extra.shape[1]
+    if more:
+        flat.append(extra)
+        specs.append(pl.BlockSpec((1, *extra.shape[1:]), lambda i: (start + i, 0, 0)))
 
     def body(*refs):
         out, at, column = refs[-1], 0, 0
-        for (left, right), span in zip(pairs, spans):
+        if more:
+            out[0, width:, :] = refs[len(flat) - 1][0].astype(BF)
+        for left, right, _, count in pairs:
             a = jnp.concatenate([r[...] for r in refs[at : at + len(left)]], 0)
             at += len(left)
             b = jnp.concatenate([r[...] for r in refs[at : at + len(right)]], 0)
             at += len(right)
-            out[0, :, column : column + span] = dot_rows(a, b).astype(BF)
-            column += span
+            out[0, :width, column : column + count] = dot_rows(a, b).astype(BF)
+            column += count
 
     return order.call(
         body,
         flat,
-        [shape_of((shards, count, sum(spans)), BF)],
-        grid=(shards * per,),
+        [shape_of((shards, width + more, total), BF)],
+        grid=(shards,),
         in_specs=specs,
-        out_specs=[pl.BlockSpec((1, block, sum(spans)), lambda i: (i // per, i % per, 0))],
+        out_specs=[pl.BlockSpec((1, width + more, total), lambda i: (i, 0, 0))],
         name="weight_grad",
+        limit=GRAD_LIMIT,
     )[0]
 
 
@@ -700,42 +741,50 @@
     def piece(self, at):
         return self.pieces[at] if 0 <= at < len(self.pieces) else None
 
-    def step(self):
+    def step(self, last=False):
         size = lax.axis_size("fsdp")
         now = self.at
         self.at += 1
         oldest, older, old, new = (self.piece(now - 1 - back) for back in (3, 2, 1, 0))
-        if not self.line:
-            if new is not None:
-                total = lax.psum(combine(self.order, [new["own"], *new["came"]]), "dp")
-                new["finish"](total, total)
-        else:
+        if last and self.line and oldest is not None:
+            oldest["finish"](oldest["total"], oldest["back"])
+            oldest = None
+        sums = []
+        if new is not None:
+            sums.append(("sum", new, [new["own"], *new["came"]]))
+        if self.line and old is not None:
+            sums.append(("inner", old, [old["sum"], old["swapped"]]))
+        if self.line and older is not None:
+            sums.append(("total", older, [older["inner"], older["met"]]))
+        if sums:
+            send = [piece[0] for piece in sums] if self.line else []
+            found = combine(self.order, [terms for *_, terms in sums], send)
+            for (name, piece, _), value in zip(sums, found):
+                piece[name] = value
+        if not self.line and new is not None:
+            total = lax.psum(new["sum"], "dp")
+            new["finish"](total, total)
+        elif self.line:
             if old is not None:
-                old["inner"] = combine(self.order, [old["sum"], old["swapped"]])
                 old["met"] = lax.ppermute(old["inner"], "dp", [(1, 2), (2, 1)])
-            if older is not None:
-                older["total"] = combine(self.order, [older["inner"], older["met"]])
-            if new is not None and older is not None and new["own"].shape == older["total"].shape:
-                new["sum"], send = combine(self.order, [new["own"], *new["came"]], older["total"])
-                new["swapped"] = older["back"] = lax.ppermute(send, "dp", [(0, 1), (1, 0), (2, 3), (3, 2)])
-            else:
-                if new is not None:
-                    new["sum"] = combine(self.order, [new["own"], *new["came"]])
-                    new["swapped"] = lax.ppermute(new["sum"], "dp", [(0, 1), (3, 2)])
-                if older is not None:
-                    older["back"] = lax.ppermute(older["total"], "dp", [(1, 0), (2, 3)])
-            if oldest is not None:
-                oldest["finish"](oldest["total"], oldest["back"])
+            if new is not None and older is not None:
+                new["swapped"] = older["back"] = lax.ppermute(found[-1], "dp", [(0, 1), (1, 0), (2, 3), (3, 2)])
+            elif new is not None:
+                new["swapped"] = lax.ppermute(new["sum"], "dp", [(0, 1), (3, 2)])
+            elif older is not None:
+                older["back"] = lax.ppermute(older["total"], "dp", [(1, 0), (2, 3)])
         if self.waiting:
             piece = self.waiting.pop(0)
             piece["came"] = [to_fsdp(piece["others"][k], k + 1) for k in range(size - 1)]
             self.pieces.append(piece)
         else:
             self.pieces.append(None)
+        if self.line and oldest is not None:
+            oldest["finish"](oldest["total"], oldest["back"])
 
     def drain(self):
-        while self.waiting or any(p is not None for p in self.pieces[self.at - 4 :]):
-            self.step()
+        while self.waiting or any(p is not None for p in self.pieces[max(self.at - 4, 0) :]):
+            self.step(True)
 
 
 def at_end():
@@ -743,73 +792,163 @@
     return (here == 0) | (here == lax.axis_size("dp") - 1)
 
 
-def combine(order, terms, other=None):
-    rows, width = terms[0].shape
-    dtype = terms[0].dtype
-    count = len(terms)
-    block = max(rows // 2, 16)
-    spec = pl.BlockSpec((block, width), lambda i: (i, 0))
-    given = [*terms] + ([] if other is None else [other])
+def combine(order, groups, names):
+    width = groups[0][0].shape[1]
+    rows = [terms[0].shape[0] for terms in groups]
+    both = "sum" in names and "total" in names
+    given = [v for terms in groups for v in terms]
+    outputs = [shape_of((count, width), BF) for count in rows]
+    if both:
+        ends, inside = names.index("sum"), names.index("total")
+        outputs.append(shape_of((max(rows[ends], rows[inside]), width), BF))
 
     def body(*refs):
-        total = refs[0][...].astype(F32)
-        for ref in refs[1:count]:
-            total = total + ref[...].astype(F32)
-        total = total.astype(dtype)
-        refs[len(given)][...] = total
-        if other is not None:
-            refs[-1][...] = jnp.where(at_end(), total.astype(F32), refs[count][...].astype(F32)).astype(dtype)
-
-    found = order.call(
-        body,
-        given,
-        [shape_of((rows, width), dtype)] * (1 if other is None else 2),
-        grid=(rows // block,),
-        in_specs=[spec] * len(given),
-        out_specs=[spec] * (1 if other is None else 2),
-        name="combine",
-    )
-    return found[0] if other is None else found
-
-
-def finish_piece(order, total, back, layer, first, held, parts, name):
-    rows, width = total.shape
-    given = [] if held is None else list(held)
-    blocks = []
-    for shape, axis, _, _ in parts:
-        block, place = [1, *shape[1:]], [layer] + [0] * (len(shape) - 1)
-        block[axis], place[axis] = rows, first // rows
-        blocks.append(pl.BlockSpec(tuple(block), lambda i, place=tuple(place): place))
+        at, sums = 0, []
+        for index, (terms, count) in enumerate(zip(groups, rows)):
+            total = refs[at][...].astype(F32)
+            for ref in refs[at + 1 : at + len(terms)]:
+                total = total + ref[:count, :].astype(F32)
+            at += len(terms)
+            sums.append(total)
+            refs[len(given) + index][...] = total.astype(BF)
+        if both:
+            a, b, send = sums[ends], sums[inside], refs[-1]
+            short = min(rows[ends], rows[inside])
+            send[:short, :] = jnp.where(at_end(), a[:short], b[:short]).astype(BF)
+            if send.shape[0] > short:
+                send[short:, :] = (a if rows[ends] > short else b)[short:].astype(BF)
+
+    return order.call(body, given, outputs, name="combine")
+
+
+def finish_piece(order, total, back, layer, rows, held, parts, name):
+    more = total.shape[0] - rows
+    width = total.shape[1]
+    given = [v for v in held if v is not None]
+    both = [total, back]
+    scratch = []
+    for shape, form, _, _, count in parts:
+        if form == "kinds":
+            scratch.append(pltpu.VMEM((shape[1], rows, count // shape[1]), F32))
+        else:
+            scratch.append(pltpu.VMEM((rows, count) if form == "columns" else (count, rows), F32))
 
     def body(*refs):
-        outs = refs[2 + len(given) :]
-        value = jnp.where(at_end(), refs[1][...].astype(F32), refs[0][...].astype(F32))
-        for out, (shape, axis, start, count) in zip(outs, parts):
-            if len(shape) == 4:
+        outs = refs[len(both) + len(given) : len(both) + len(given) + len(parts)]
+        rest = refs[len(both) + len(given) + len(parts) :]
+        if more:
+            extra, rest = rest[0], rest[1:]
+        blocks, sems = rest[:-1], rest[-1]
+        value = jnp.where(at_end(), refs[1][: total.shape[0], :].astype(F32), refs[0][...].astype(F32))
+        if more:
+            extra[...] = value[rows:]
+            value = value[:rows]
+        copies = []
+        for at, (out, block, (shape, form, place, first, count)) in enumerate(zip(outs, blocks, parts)):
+            if form == "kinds":
                 span = count // shape[1]
                 for g in range(shape[1]):
-                    out[0, g] = value[:, start + g * span : start + (g + 1) * span]
-            elif axis == 2:
-                out[0] = value[:, start : start + count].T
+                    block[g] = value[:, first + g * span : first + (g + 1) * span]
+                there = out.at[layer]
+            elif form == "turned":
+                block[...] = value[:, first : first + count].T
+                there = out.at[layer, pl.ds(place, count), :]
             else:
-                out[0] = value[:, start : start + count]
-
+                block[...] = value[:, first : first + count]
+                there = out.at[layer, :, pl.ds(place, count)]
+            copy = pltpu.make_async_copy(block, there, sems.at[at])
+            copy.start()
+            copies.append(copy)
+        for copy in copies:
+            copy.wait()
+
+    alias, at = {}, 0
+    for index, v in enumerate(held):
+        if v is not None:
+            alias[len(both) + at] = index
+            at += 1
     return order.call(
         body,
-        [total, back, *given],
-        [shape_of(shape, F32) for shape, *_ in parts],
-        grid=(1,),
-        in_specs=[None, None] + [ANY] * len(given),
-        out_specs=blocks,
-        alias={2 + i: i for i in range(len(given))},
+        [*both, *given],
+        [shape_of(shape, F32) for shape, *_ in parts] + ([shape_of((more, width), F32)] if more else []),
+        scratch=[*scratch, pltpu.SemaphoreType.DMA((len(parts),))],
+        in_specs=[None] * len(both) + [HELD] * len(given),
+        out_specs=[HELD] * len(parts) + ([None] if more else []),
+        alias=alias,
         name=name,
-        limit=24,
-    )
-
-
-STEPS = (0, 1, 0, 1, 0, 1, 0, 1)
-MORE_STEPS = (0, 0, 1, 0, 1, 0, 1, 0)
-LAST_CUT = 2
+        limit=12,
+    )
+
+
+def sum_norm_rows(order, sums):
+    streams = len(sums[0])
+    features = sums[0][0].shape[1]
+
+    def body(*refs):
+        out = refs[-1]
+        found = []
+        for at in range(len(sums)):
+            total = refs[at * streams][...]
+            for ref in refs[at * streams + 1 : (at + 1) * streams]:
+                total = total + ref[...]
+            found.append(total)
+        rows = [found[at][0:1] for at in range(2 * LAYERS)]
+        for layer in range(LAYERS):
+            one, two = found[2 * layer], found[2 * layer + 1]
+            rows += [one[2:3], two[2:3], one[1:2], two[1:2]]
+        for at, row in enumerate(rows):
+            out[at : at + 1, :] = row
+
+    return order.call(
+        body,
+        [v for group in sums for v in group],
+        [shape_of((6 * LAYERS, features), F32)],
+        name="sum_norm_rows",
+    )[0]
+
+
+def little_gradients(order, norms, grow, heads, span):
+    size = lax.axis_size("fsdp")
+    features = norms[0].shape[1]
+    width = features // size
+    columns = 3 * span
+    hidden = grow[0][0].shape[1]
+    streams = len(grow[0])
+
+    def body(a, b, *refs):
+        out = refs[-1]
+        out[...] = jnp.zeros(out.shape, F32)
+        total = a[...] + b[...]
+        rows = 6 * LAYERS
+        for k in range(size):
+            out[k, :rows, :width] = total[:, k * width : (k + 1) * width]
+        for layer in range(LAYERS):
+            at = layer * streams
+            up = sum(ref[...] for ref in refs[at : at + streams])
+            at += LAYERS * streams
+            qkv = sum(ref[...] for ref in refs[at : at + streams])
+            for k in range(size):
+                row = rows + 2 * layer
+                rest = hidden - columns
+                out[k, row : row + 1, :] = up[:, :columns]
+                out[k, row + 1 : row + 2, :rest] = up[:, columns:]
+                out[k, row + 1 : row + 2, rest : rest + span] = qkv[:, :span]
+                out[k, row + 1 : row + 2, rest + span : rest + 2 * span] = qkv[:, 2 * span :]
+
+    return order.call(
+        body,
+        [*norms, *[v for group in grow for v in group], *[v for group in heads for v in group]],
+        [shape_of((size, 8 * LAYERS, columns), F32)],
+        name="little_gradients",
+    )[0]
+
+
+FILLS = (0, 2, 2, 2, 2, 2, 2, 2)
+STEPS = (0, 1, 1, 1, 1, 1, 1, 1)
+MORE_STEPS = (0, 0, 0, 0, 0, 0, 0, 0)
+GRAD_LIMIT = 12
+ADD_FIRST = (0,) * 16
+FEED_LIMIT = 12
 
 
 def gather_halves(share):
@@ -844,43 +983,38 @@
     head_rows = [bias_heads[layer].reshape(2, -1) for layer in range(LAYERS)]
     grow_rows = [bias_grow[layer].reshape(1, -1) for layer in range(LAYERS)]
 
-    def fetch(whole, layer, axis, cut):
-        shard = whole[layer]
-        count = shard.shape[axis] // cut
-        if count < 128:
-            cut, count = 1, shard.shape[axis]
-        came = []
-        for step in range(1, size):
-            for at in range(cut):
-                piece = lax.slice_in_dim(shard, at * count, (at + 1) * count, axis=axis)
-                came.append(from_fsdp(piece, step))
-        return Weight([shard] + came, axis)
-
     weights = [
-        [fetch(w_qkv, layer, 1, 1), fetch(w_out, layer, 1, 1), fetch(w_up, layer, 0, 2), fetch(w_down, layer, 1, 2)]
+        [
+            Weight(order, w_qkv, layer, 1),
+            Weight(order, w_out, layer, 1),
+            Weight(order, w_up, layer, 0),
+            Weight(order, w_down, layer, 1),
+        ]
         for layer in range(LAYERS)
     ]
-
-    def halves_of(weight):
-        came = weight.arrays[1:]
-        middle = (len(came) + 1) // 2
-        return came[:middle], came[middle:]
-
-    up_zero, down_zero = halves_of(weights[0][2]), halves_of(weights[0][3])
-    up_one, down_one = halves_of(weights[1][2]), halves_of(weights[1][3])
-    ahead = {
-        1: up_zero[0],
-        2: [*up_zero[1], *down_zero[0], *down_zero[1]],
-        3: weights[1][0].arrays[1:],
-        4: [*weights[1][1].arrays[1:], *up_one[0]],
-        5: up_one[1],
-        6: [*down_one[0], *down_one[1]],
-    }
+    fetch(order, weights[0][:2])
 
     slots = deal_rows(order, activations)
+    fetch(order, weights[1])
     residual = [(slots[s][0], None, None) for s in kinds]
+    cotangent = copy_rows(order, cotangent)
     across = to_chip(cotangent)
-    shares = deal_share(order, [cotangent, to_core(cotangent), across, to_core(across)])
+    cotangents = [cotangent, to_core(cotangent), across, to_core(across)]
+
+    order.pin([*pieces[1:], *weights[0][0].early, *weights[0][0].late, *weights[0][1].early, *weights[0][1].late])
+    fetch(order, weights[0][2:3])
+
+    def ahead(at):
+        zero, one = weights
+        waits = {
+            1: lambda: zero[2].early,
+            2: lambda: [*zero[3].early, *zero[2].late],
+            3: lambda: [*one[0].early, *one[1].early],
+            4: lambda: [*one[0].late, *one[1].late, *one[2].early],
+            5: lambda: [*one[2].late, *one[3].early],
+            6: lambda: one[3].late,
+        }
+        return waits[at]() if at in waits else []
 
     streams = len(STREAMS)
     kept = [{k: [None] * streams for k in ("x", "attended", "grown", "one", "two", "middle")} for _ in range(LAYERS)]
@@ -943,7 +1077,7 @@
                 second_norm(layer, s)
                 terms[s] = [shares[s]]
             two = kept[layer]["two"][s]
-            back_two[layer][s] = norm_backward(order, terms[s], two[1], two[2], vectors, gain_at(layer, 1))
+            back_two[layer][s] = norm_backward(order, terms[s], two[3], two[2], vectors, gain_at(layer, 1))
             slots_two[layer][s] = gather_halves(back_two[layer][s][0])
 
         def products():
@@ -951,9 +1085,7 @@
             found = feed_backward(order, slots_two[layer][s], kept[layer]["grown"][s]["slope"], (w_grow, w_shrink))
             fed[layer][s] = found
             if s + 1 == streams:
-                state = kept[layer]
-                queue(layer, "down", [([v for t in kinds for v in slots_two[layer][t]], [state["grown"][t]["act"] for t in kinds])])
-                queue(layer, "up", [([v for t in kinds for v in state["middle"][t]], [fed[layer][t]["grad"] for t in kinds])])
+                queue_feed(layer)
             return found, [back_two[layer][s][2]]
 
         return before, products
@@ -961,7 +1093,7 @@
     def attend_back(layer, s):
         def before():
             one = kept[layer]["one"][s]
-            back_one[layer][s] = norm_backward(order, terms[s], one[1], one[2], vectors, gain_at(layer, 0))
+            back_one[layer][s] = norm_backward(order, terms[s], one[3], one[2], vectors, gain_at(layer, 0))
             slots_one[layer][s] = gather_halves(back_one[layer][s][0])
 
         def products():
@@ -970,15 +1102,7 @@
             found = attention_backward(order, STREAMS[s], slots_one[layer][s], (w_proj, w_mix), state["attended"][s])
             went[layer][s] = found
             if s + 1 == streams:
-                queue(
-                    layer,
-                    "att",
-                    [
-                        ([v for t in kinds for v in state["x"][t]], [went[layer][t]["grad"] for t in kinds]),
-                        ([v for t in kinds for v in slots_one[layer][t]], [state["attended"][t]["ctx"] for t in kinds]),
-                    ],
-                    1 if layer > 0 else LAST_CUT,
-                )
+                queue_attend(layer)
             return found, [back_one[layer][s][2]]
 
         return before, products
@@ -988,38 +1112,83 @@
     outputs = {}
     span, hidden = w_out.shape[1], w_down.shape[1]
     width = features // size
-    forms = {
-        "down": [((LAYERS, hidden, width), 2, 0, hidden)],
-        "up": [((LAYERS, width, hidden), 1, 0, hidden)],
-        "att": [((LAYERS, 3, width, span), 2, 0, 3 * span), ((LAYERS, span, width), 2, 3 * span, span)],
+    shapes = {
+        "proj": (LAYERS, 3, width, span),
+        "mix": (LAYERS, span, width),
+        "up": (LAYERS, width, hidden),
+        "down": (LAYERS, hidden, width),
     }
-
-    def queue(layer, name, pairs, cut=1):
-        count = width // cut if width // cut >= 128 else width
-        for first in range(0, width, count):
-            queue_rows(layer, name, pairs, first, count)
-
-    def queue_rows(layer, name, pairs, first, count):
+    forms = {"proj": "kinds", "mix": "turned", "up": "columns", "down": "turned"}
+
+    def queue(layer, sources, extra=None):
+        pairs = [source[1:] for source in sources]
+        starts = [sum(source[4] for source in sources[:i]) for i in range(len(sources))]
+        parts = [
+            (shapes[name], forms[name], first, start, count)
+            for (name, _, _, first, count), start in zip(sources, starts)
+        ]
+
         def finish(total, back):
-            outputs[name] = finish_piece(
-                order, total, back, layer, first, outputs.get(name), forms[name], "finish_" + name
+            names = [source[0] for source in sources]
+            found = finish_piece(
+                order, total, back, layer, width, [outputs.get(n) for n in names], parts, "finish_" + names[0]
             )
+            outputs.update(zip(names, found))
+            if extra is not None:
+                outputs["little"] = found[-1]
 
         found = {}
 
         def others():
-            found["others"] = weight_grad(order, pairs, 1, size, first, count)
+            found["rows"] = None if extra is None else extra()
+            rows = found["rows"]
+            found["others"] = weight_grad(order, pairs, 1, size, rows)
 
         def own():
-            found["own"] = weight_grad(order, pairs, 0, size, first, count)[0]
+            rows = found["rows"]
+            found["own"] = weight_grad(order, pairs, 0, size, rows)[0]
             pipeline.offer(found["others"], found["own"], finish)
 
         fillers.extend([others, own])
+
+    def queue_feed(layer):
+        state = kept[layer]
+        down = [v for t in kinds for v in slots_two[layer][t]], [state["grown"][t]["act"] for t in kinds]
+        up = [v for t in kinds for v in state["middle"][t]], [fed[layer][t]["grad"] for t in kinds]
+        most, half = 3 * hidden // 4, hidden // 2
+        queue(layer, [("down", *down, 0, most)])
+        queue(layer, [("down", *down, most, hidden - most), ("up", *up, 0, half)])
+
+    def queue_attend(layer):
+        state = kept[layer]
+        up = [v for t in kinds for v in state["middle"][t]], [fed[layer][t]["grad"] for t in kinds]
+        mix = [v for t in kinds for v in slots_one[layer][t]], [state["attended"][t]["ctx"] for t in kinds]
+        proj = [v for t in kinds for v in state["x"][t]], [went[layer][t]["grad"] for t in kinds]
+        half = hidden // 2
+        queue(layer, [("up", *up, half, half), ("mix", *mix, 0, span)])
+        queue(layer, [("proj", *proj, 0, 3 * span)], None if layer > 0 else little_rows)
 
     def fill(count):
         for _ in range(count):
             if fillers:
                 fillers.pop(0)()
+
+    norm_sums = []
+
+    def sum_norms():
+        found = sum_norm_rows(
+            order, [[back[layer][s][1] for s in kinds] for layer in range(LAYERS) for back in (back_one, back_two)]
+        )
+        norm_sums.extend([found, to_core(found)])
+
+    def little_rows():
+        return little_gradients(
+            order,
+            norm_sums,
+            [[fed[layer][s]["sums"] for s in kinds] for layer in range(LAYERS)],
+            [[went[layer][s]["sums"] for s in kinds] for layer in range(LAYERS)],
+            span,
+        )
 
     items = []
     for layer in range(LAYERS):
@@ -1033,72 +1202,61 @@
         found, more = products()
         beside = [to_core(part) for part in found["other"]]
         if at >= forward_items:
-            fill(2)
-            if STEPS[at - forward_items]:
+            fill(FILLS[at - forward_items])
+            for _ in range(STEPS[at - forward_items]):
                 pipeline.step()
-        order.pin(ahead.get(at + 1, []))
+        early = ADD_FIRST[at]
+        if early:
+            low = add_send(order, found["own"], beside)
+        order.pin(ahead(at + 1))
         if at == 0:
-            order.hold()
+            fetch(order, weights[0][3:])
+            shares = deal_share(order, cotangents)
         if at + 1 < len(items):
             items[at + 1][0]()
         if at == forward_items + 1:
             out_rows = gather_halves(jnp.concatenate([kept[-1]["two"][t][0] for t in kinds], 0))
-        low, wide = add_send(order, found["own"], beside)
-        terms[s] = [wide, to_chip(low), *more]
-        if at >= forward_items and MORE_STEPS[at - forward_items]:
+        if at + 2 == len(items):
+            sum_norms()
+        if not early:
+            low = add_send(order, found["own"], beside)
+        terms[s] = [found["own"], *beside, to_chip(low), *more]
+        for _ in range(MORE_STEPS[at - forward_items] if at >= forward_items else 0):
             pipeline.step()
-    fill(len(fillers))
-    pipeline.step()
+    while fillers:
+        fill(2)
+        pipeline.step(True)
     layer_out = natural_share(order, out_rows, BF)
+    pipeline.step(True)
     ends = [last_sum(order, terms[s]) for s in kinds]
     end_rows = gather_halves(jnp.concatenate(ends, 0))
-    pipeline.step()
+    pipeline.step(True)
     input_grad = natural_share(order, end_rows, F32)
     pipeline.drain()
 
-    sums, head_sums, grow_sums = {}, {}, {}
-    for layer in range(LAYERS):
-        sums[layer] = [sum(back_one[layer][s][1] for s in kinds), sum(back_two[layer][s][1] for s in kinds)]
-        head_sums[layer] = sum(went[layer][s]["sums"] for s in kinds)
-        grow_sums[layer] = sum(fed[layer][s]["sums"] for s in kinds)
-    heads_bias = jnp.stack(
-        [
-            jnp.stack([head_sums[layer][0, :span], head_sums[layer][0, 2 * span :]])
-            for layer in range(LAYERS)
-        ]
-    ).reshape(bias_heads.shape)
-    grow_bias = jnp.stack([grow_sums[layer] for layer in range(LAYERS)]).reshape(bias_grow.shape)
-    gain_pair = jnp.stack([jnp.stack([sums[layer][i][0] for i in range(2)]) for layer in range(LAYERS)])
-    bias_set = jnp.stack(
-        [
-            jnp.stack([sums[layer][0][2], sums[layer][1][2], sums[layer][0][1], sums[layer][1][1]])
-            for layer in range(LAYERS)
-        ]
-    )
-    norms = jnp.concatenate([gain_pair.reshape(-1, features), bias_set.reshape(-1, features)])
-    norms = norms + to_core(norms)
-    own_heads, own_grow = own_first(heads_bias, 3), own_first(grow_bias, 2)
-    little = []
-    for step in range(size):
-        parts = []
-        for value in (own_heads, own_grow, norms):
-            part = value.shape[-1] // size
-            parts.append(value[..., step * part : (step + 1) * part].reshape(-1))
-        little.append(jnp.concatenate(parts))
-    total = little[0]
-    for step in range(1, size):
-        total = total + to_fsdp(little[step], step)
-    dp_size = lax.axis_size("dp")
-    reach = 1
-    while reach < dp_size:
-        total = total + lax.ppermute(total, "dp", [(i, i ^ reach) for i in range(dp_size)])
-        reach *= 2
-    finals, start = [], 0
-    for value in (own_heads, own_grow, gain_pair, bias_set):
-        amount = value.size // size
-        finals.append(total[start : start + amount].reshape(value.shape[:-1] + (value.shape[-1] // size,)))
-        start += amount
-    return (layer_out, input_grad, *outputs["att"], *outputs["up"], *outputs["down"], *finals)
+    little = outputs["little"]
+    grad_gains = little[: 2 * LAYERS, :width].reshape(LAYERS, 2, width)
+    grad_biases = little[2 * LAYERS : 6 * LAYERS, :width].reshape(LAYERS, 4, width)
+    rest = little[6 * LAYERS : 8 * LAYERS].reshape(LAYERS, -1)
+    here = lax.axis_index("fsdp")
+    grow = rest[:, :hidden].reshape(bias_grow.shape)
+    heads = rest[:, hidden : hidden + 2 * span].reshape(bias_heads.shape)
+    part = grow.shape[-1] // size
+    grow = lax.dynamic_slice_in_dim(grow, here * part, part, grow.ndim - 1)
+    part = heads.shape[-1] // size
+    heads = lax.dynamic_slice_in_dim(heads, here * part, part, heads.ndim - 1)
+    return (
+        layer_out,
+        input_grad,
+        outputs["proj"],
+        outputs["mix"],
+        outputs["up"],
+        outputs["down"],
+        heads,
+        grow,
+        grad_gains,
+        grad_biases,
+    )
 
 
 def solution(mesh):

time: 591 us -> 490 us (0.83)
  Pallas kernels: 250 us -> 165 us
  local copies, waits for them, and re-layouts: 70.9 us -> 51.3 us
  waiting for transfers between devices: 160 us -> 168 us
    pallas_call x97 -> x95, Pallas kernels: 250 us -> 165 us  [call(): pl.pallas_call(kernel, grid=grid, in_specs=in_specs, out_specs=[*out_spec...]
    ppermute x13 -> x9, waiting for transfers between devices: 47 us -> 11.9 us  [from_fsdp(): lax.ppermute(value, 'fsdp', [((i + step) % size, i) for i in range(size)])]
    ppermute x4 -> x14, waiting for transfers between devices: 19.3 us -> 44.5 us  [the longest x6 28.8 us: step(): lax.ppermute(found[-1], 'dp', [(0, 1), (1, 0), (2, 3), (3, 2)])]
    ppermute x17, waiting for transfers between devices: 18 us -> 41.2 us  [to_chip(): return lax.ppermute(value, 'tensor', CHIP_SWAP)]
    ppermute x5 -> x2, waiting for transfers between devices: 24.8 us -> 5.54 us  [step(): new['swapped'] = lax.ppermute(new['sum'], 'dp', [(0, 1), (3, 2)])]
    ppermute x5 -> x2, starting transfers between devices: 20.2 us -> 6.81 us  [step(): new['swapped'] = lax.ppermute(new['sum'], 'dp', [(0, 1), (3, 2)])]
    ppermute x4 -> x14, starting transfers between devices: 12.1 us -> 24 us  [the longest x6 17.3 us: step(): lax.ppermute(found[-1], 'dp', [(0, 1), (1, 0), (2, 3), (3, 2)])]
    ppermute x5 -> x2, waiting for transfers between devices: 22 us -> 32.1 us  [step(): older['back'] = lax.ppermute(older['total'], 'dp', [(1, 0), (2, 3)])]
  transfers between devices with their start and end apart: 110 -> 111, of which waited for: 50 -> 50; matrix products, arithmetic and copies ran while one was open for 4% -> 1% of each run, Pallas kernels for 41% -> 31%
where the time goes in v3:
time: 490 us; the launch traced here: 484 us
  waiting for transfers between devices  168 us (34%)
  Pallas kernels  165 us (34%)
  starting transfers between devices  94.6 us (19%)
  local copies, waits for them, and re-layouts  51.3 us (10%)
    pallas_call x95, Pallas kernels, call(): pl.pallas_call(kernel, grid=grid, in_specs=in_specs, out_specs=[*out_spec...  165 us
    unnamed x302, local copies, waits for them, and re-layouts  46.5 us
    ppermute x17, waiting for transfers between devices, to_chip(): return lax.ppermute(value, 'tensor', CHIP_SWAP)  41.2 us
    ppermute x2, waiting for transfers between devices, step(): older['back'] = lax.ppermute(older['total'], 'dp', [(1, 0), (2, 3)])  32.1 us
    ppermute x6, waiting for transfers between devices, step(): lax.ppermute(found[-1], 'dp', [(0, 1), (1, 0), (2, 3), (3, 2)])  28.8 us
    ppermute x17, starting transfers between devices, to_chip(): return lax.ppermute(value, 'tensor', CHIP_SWAP)  23.5 us
    ppermute x51, waiting for transfers between devices, to_core(): return lax.ppermute(value, 'tensor', CORE_SWAP)  21.6 us
    ppermute x6, starting transfers between devices, step(): lax.ppermute(found[-1], 'dp', [(0, 1), (1, 0), (2, 3), (3, 2)])  17.3 us
  transfers between devices with their start and end apart: 111, of which 50 were waited for; matrix products, arithmetic and copies ran while one was open for 1% of the time, Pallas kernels for 31%

profile of v3, /device:TPU:0, one launch (start us, length us, event | category | flops | bytes accessed | tf_op | source)
XLA Modules:
  0.0 484.1 jit_solution(13027864821820131858)
XLA Ops:
  3.3 3.0 collective-permute-start
  9.9 1.8 copy-done.49
  23.2 3.7 collective-permute-done.2.refs_4_.refs_6_
  28.9 2.5 collective-permute-done.4.refs_1_
  31.4 2.4 collective-permute-done.8.refs_2_
  33.9 1.8 copy-done.47
  42.4 5.5 %attention_forward.4 = (bf16[128,1024]{1,0:T(8,128)(2,1)S(1)}, bf16[128,1024]{1,0:T(8,128)(2,1)S(1)}, bf16[256,1024]{1,0:T(8,128)(2,1)S(1)}, bf16[512,768]{1,0:T...) custom-call(bf16[256,1024]{1,0:T(8,128)(2,1)S(1)} %copy-done.41, ...), custom_call_target="tpu_custom_call" | custom-call | tf_op jit(solution)/shard_map/attention_forward/pallas_call | solution.py:129
  52.8 2.2 deal_share.1
  61.3 7.9 %attention_forward.5 = (bf16[160,1024]{1,0:T(8,128)(2,1)}, bf16[160,1024]{1,0:T(8,128)(2,1)}, bf16[320,1024]{1,0:T(8,128)(2,1)S(1)}, bf16[640,768]{1,0:T(8,128)(...) custom-call(bf16[320,1024]{1,0:T(8,128)(2,1)S(1)} %copy-done.28, ...), custom_call_target="tpu_custom_call" | custom-call | tf_op jit(solution)/shard_map/attention_forward/pallas_call | solution.py:129
  83.3 2.2 add_send.17
  92.0 9.3 %collective-permute-done.15.refs_7_ = bf16[1024,256]{1,0:T(8,128)(2,1)} collective-permute-done((bf16[1024,256]{1,0:T(8,128)(2,1)}, bf16[1024,256]{1,0:T(8,128)(2,1)}, u32[]{:S(2)}, u32[]{:S(2)}) %collective-permute-start.15) | collective-permute-done | bytes 524320 | tf_op jit(solution)/shard_map/ppermute | solution.py:189
  105.1 4.1 feed_forward.4
  110.4 2.1 norm_forward.9
  120.9 5.2 %feed_forward.5 = (bf16[160,1024]{1,0:T(8,128)(2,1)S(1)}, bf16[160,1024]{1,0:T(8,128)(2,1)S(1)}, bf16[640,1024]{1,0:T(8,128)(2,1)S(1)}, bf16[640,1024]{1,0:T(8,1...) custom-call(bf16[320,1024]{1,0:T(8,128)(2,1)S(1)} %get-tuple-element.396.refs_0_.refs_8_.refs_2_, ...), custom_call_target="tpu_custom_call" | custom-call | tf_op jit(solution)/shard_map/feed_forward/pallas_call | solution.py:129
  126.8 2.5 collective-permute-done.26.refs_8_.refs_3_
  129.3 3.5 collective-permute-done.24.refs_6_.refs_4_
  143.2 6.5 %attention_forward.6 = (bf16[128,1024]{1,0:T(8,128)(2,1)S(1)}, bf16[128,1024]{1,0:T(8,128)(2,1)S(1)}, bf16[256,1024]{1,0:T(8,128)(2,1)S(1)}, bf16[512,768]{1,0:T...) custom-call(bf16[256,1024]{1,0:T(8,128)(2,1)} %get-tuple-element.399.refs_0_,, ...), custom_call_target="tpu_custom_call" | custom-call | tf_op jit(solution)/shard_map/attention_forward/pallas_call | solution.py:129
  149.7 1.9 collective-permute-done.35.refs_7_.refs_6_
  152.4 2.0 norm_forward.11
  159.0 7.8 %attention_forward.7 = (bf16[160,1024]{1,0:T(8,128)(2,1)S(1)}, bf16[160,1024]{1,0:T(8,128)(2,1)S(1)}, bf16[320,1024]{1,0:T(8,128)(2,1)S(1)}, bf16[640,768]{1,0:T...) custom-call(bf16[320,1024]{1,0:T(8,128)(2,1)S(1)} %get-tuple-element, ...), custom_call_target="tpu_custom_call" | custom-call | tf_op jit(solution)/shard_map/attention_forward/pallas_call | solution.py:129
  167.4 2.2 collective-permute-done.37.refs_6_.refs_7_
  169.6 1.9 collective-permute-done.36.refs_3_
  172.4 1.8 collective-permute-start.44
  174.2 1.9 collective-permute-done.39.refs_1_.refs_7_
  176.1 4.0 feed_forward.6
  180.1 8.5 %collective-permute-done.44.refs_3_ = bf16[320,1024]{1,0:T(8,128)(2,1)S(1)} collective-permute-done((bf16[320,1024]{1,0:T(8,128)(2,1)S(1)}, bf16[320,1024]{1,0:T(8,128)(2,1)S(1)}, u32[]{:S(2)}, u32[]{:S(2)}) %collective-permute-start.44) | collective-permute-done | bytes 655392 | tf_op jit(solution)/shard_map/ppermute | solution.py:29
  190.2 1.9 collective-permute-done.42.refs_1_
  194.1 4.7 feed_forward.7
  199.4 7.2 %collective-permute-done.45.refs_3_ = bf16[256,1024]{1,0:T(8,128)(2,1)S(1)} collective-permute-done((bf16[256,1024]{1,0:T(8,128)(2,1)S(1)}, bf16[256,1024]{1,0:T(8,128)(2,1)S(1)}, u32[]{:S(2)}, u32[]{:S(2)}) %collective-permute-start.45) | collective-permute-done | bytes 524320 | tf_op jit(solution)/shard_map/ppermute | solution.py:29
  210.7 1.9 collective-permute-done.50.refs_1_
  212.6 3.8 feed_backward.4
  216.4 8.7 %collective-permute-done.49.refs_3_ = bf16[320,1024]{1,0:T(8,128)(2,1)S(1)} collective-permute-done((bf16[320,1024]{1,0:T(8,128)(2,1)S(1)}, bf16[320,1024]{1,0:T(8,128)(2,1)S(1)}, u32[]{:S(2)}, u32[]{:S(2)}) %collective-permute-start.49) | collective-permute-done | bytes 655392 | tf_op jit(solution)/shard_map/ppermute | solution.py:29
  225.2 1.9 norm_forward.15
  232.5 4.5 feed_backward.5
  241.1 3.8 collective-permute-done.54.refs_3_
  247.6 1.9 collective-permute-done.56.refs_1_.refs_7_
  249.5 6.6 %attention_backward.4 = (bf16[128,1024]{1,0:T(8,128)(2,1)S(1)}, bf16[128,1024]{1,0:T(8,128)(2,1)S(1)}, bf16[256,1024]{1,0:T(8,128)(2,1)S(1)}, bf16[512,768]{1,0:...) custom-call(bf16[256,1024]{1,0:T(8,128)(2,1)S(1)} %get-tuple-element.476.refs_0_.refs_6_, ...), custom_call_target="tpu_custom_call" | custom-call | tf_op jit(solution)/shard_map/attention_backward/pallas_call | solution.py:129
  259.0 3.0 collective-permute-done.61.refs_3_
  264.3 2.4 collective-permute-start.65
  270.4 8.2 %attention_backward.5 = (bf16[160,1024]{1,0:T(8,128)(2,1)S(1)}, bf16[160,1024]{1,0:T(8,128)(2,1)S(1)}, bf16[320,1024]{1,0:T(8,128)(2,1)S(1)}, bf16[640,768]{1,0:...) custom-call(bf16[320,1024]{1,0:T(8,128)(2,1)S(1)} %get-tuple-element.507.refs_0_.refs_8_, ...), custom_call_target="tpu_custom_call" | custom-call | tf_op jit(solution)/shard_map/attention_backward/pallas_call | solution.py:129
  284.1 4.4 collective-permute-start.72
  293.5 3.8 feed_backward.6
  297.6 2.3 weight_grad.22
  299.8 5.0 %collective-permute-done.72.refs_3_ = bf16[512,768]{1,0:T(8,128)(2,1)S(1)} collective-permute-done((bf16[512,768]{1,0:T(8,128)(2,1)S(1)}, bf16[512,768]{1,0:T(8,128)(2,1)S(1)}, u32[]{:S(2)}, u32[]{:S(2)}) %collective-permute-start.72) | collective-permute-done | bytes 786464 | tf_op jit(solution)/shard_map/ppermute | solution.py:773
  305.8 2.3 weight_grad.23
  308.1 2.0 collective-permute-done.71.refs_1_
  310.7 3.3 collective-permute-start.78
  318.5 4.5 feed_backward.7
  328.6 4.0 collective-permute-start.85
  339.4 5.6 %attention_backward.6 = (bf16[128,1024]{1,0:T(8,128)(2,1)S(1)}, bf16[128,1024]{1,0:T(8,128)(2,1)S(1)}, bf16[256,1024]{1,0:T(8,128)(2,1)S(1)}, bf16[512,768]{1,0:...) custom-call(bf16[256,1024]{1,0:T(8,128)(2,1)S(1)} %get-tuple-element.567.refs_0_.refs_6_, ...), custom_call_target="tpu_custom_call" | custom-call | tf_op jit(solution)/shard_map/attention_backward/pallas_call | solution.py:129
  349.7 4.5 collective-permute-done.86.refs_1_
  355.0 3.2 collective-permute-start.93
  362.1 2.0 collective-permute-done.89.refs_1_
  365.8 7.1 %attention_backward.7 = (bf16[160,1024]{1,0:T(8,128)(2,1)S(1)}, bf16[160,1024]{1,0:T(8,128)(2,1)S(1)}, bf16[320,1024]{1,0:T(8,128)(2,1)S(1)}, bf16[640,768]{1,0:...) custom-call(bf16[320,1024]{1,0:T(8,128)(2,1)S(1)} %get-tuple-element.591.refs_0_.refs_8_, ...), custom_call_target="tpu_custom_call" | custom-call | tf_op jit(solution)/shard_map/attention_backward/pallas_call | solution.py:129
  380.6 2.8 collective-permute-done.99.refs_2_
  389.8 6.4 %collective-permute-done.95.refs_1_.refs_3_ = bf16[512,768]{1,0:T(8,128)(2,1)S(1)} collective-permute-done((bf16[512,768]{1,0:T(8,128)(2,1)S(1)}, bf16[512,768]{1,0:T(8,128)(2,1)S(1)}, u32[]{:S(2)}, u32[]{:S(2)}) %collective-permute-start.95) | collective-permute-done | bytes 786464 | tf_op jit(solution)/shard_map/ppermute | solution.py:771
  400.0 3.0 collective-permute-start.102
  406.9 12.2 %collective-permute-done.102.refs_1_.refs_3_ = bf16[512,768]{1,0:T(8,128)(2,1)S(1)} collective-permute-done((bf16[512,768]{1,0:T(8,128)(2,1)S(1)}, bf16[512,768]{1,0:T(8,128)(2,1)S(1)}, u32[]{:S(2)}, u32[]{:S(2)}) %collective-permute-start.102) | collective-permute-done | bytes 786464 | tf_op jit(solution)/shard_map/ppermute | solution.py:771
  421.3 2.2 collective-permute-start.106
  424.3 5.5 %collective-permute-done.100.refs_3_ = bf16[256,1024]{1,0:T(8,128)(2,1)S(1)} collective-permute-done((bf16[256,1024]{1,0:T(8,128)(2,1)S(1)}, bf16[256,1024]{1,0:T(8,128)(2,1)S(1)}, u32[]{:S(2)}, u32[]{:S(2)}) %collective-permute-start.100) | collective-permute-done | bytes 524320 | tf_op jit(solution)/shard_map/ppermute | solution.py:29
  430.6 8.7 %collective-permute-done.106.refs_1_ = bf16[528,768]{1,0:T(8,128)(2,1)S(1)} collective-permute-done((bf16[528,768]{1,0:T(8,128)(2,1)S(1)}, bf16[528,768]{1,0:T(8,128)(2,1)S(1)}, u32[]{:S(2)}, u32[]{:S(2)}) %collective-permute-start.106) | collective-permute-done | bytes 811040 | tf_op jit(solution)/shard_map/ppermute | solution.py:771
  444.2 15.9 %collective-permute-done.109.refs_1_ = bf16[512,768]{1,0:T(8,128)(2,1)S(1)} collective-permute-done((bf16[512,768]{1,0:T(8,128)(2,1)S(1)}, bf16[512,768]{1,0:T(8,128)(2,1)S(1)}, u32[]{:S(2)}, u32[]{:S(2)}) %collective-permute-start.109) | collective-permute-done | bytes 786464 | tf_op jit(solution)/shard_map/ppermute | solution.py:775
  463.1 16.2 %collective-permute-done.110.refs_1_ = bf16[528,768]{1,0:T(8,128)(2,1)S(1)} collective-permute-done((bf16[528,768]{1,0:T(8,128)(2,1)S(1)}, bf16[528,768]{1,0:T(8,128)(2,1)S(1)}, u32[]{:S(2)}, u32[]{:S(2)}) %collective-permute-start.110) | collective-permute-done | bytes 811040 | tf_op jit(solution)/shard_map/ppermute | solution.py:775
  479.2 1.9 finish_proj.3
  (589 shorter events, 193.4 us)
Async XLA Ops:
  3.3 16.9 %collective-permute-start = (bf16[3,256,256]{2,1,0:T(8,128)(2,1)S(1)}, bf16[3,256,256]{2,1,0:T(8,128)(2,1)S(1)}, u32[]{:S(2)}, u32[]{:S(2)}) collective-permute-start(bf16[3,256,256]{2,1,0:T(8,128)(2,1)S(1)} %get-tuple-element.356), channel_id=1, source_target_pairs={{4,0},{0,4},{5,1},{1,5},{6,2},{2,6},{7,3},{3,7},{12,8},{8,12},{13,... | collective-permute-start | bytes 1179656 | tf_op jit(solution)/shard_map/ppermute | solution.py:34
  18.8 15.1 %collective-permute-start.8 = (bf16[288,1024]{1,0:T(8,128)(2,1)}, bf16[288,1024]{1,0:T(8,128)(2,1)}, u32[]{:S(2)}, u32[]{:S(2)}) collective-permute-start(bf16[288,1024]{1,0:T(8,128)(2,1)} %get-tuple-element.366.refs_0_), channel_id=1, source_target_pairs={{0,2},{2,0},{1,3},{3,1},{4,6},{6,4},{5,7},{7,5},{8,10},{10,8},{9,1... | collective-permute-start | bytes 1769480 | tf_op jit(solution)/shard_map/ppermute | solution.py:29
  20.3 13.6 %collective-permute-start.1 = (bf16[3,256,256]{2,1,0:T(8,128)(2,1)S(1)}, bf16[3,256,256]{2,1,0:T(8,128)(2,1)S(1)}, u32[]{:S(2)}, u32[]{:S(2)}) collective-permute-start(bf16[3,256,256]{2,1,0:T(8,128)(2,1)S(1)} %collective-permute-done.refs_2_.refs_3_), channel_id=1, source_target_pairs={{0,8},{8,0},{16,24},{24,16},{1,9},{9,1},{17,25},{25,17},{2,10},{10... | collective-permute-start | bytes 1179656 | tf_op jit(solution)/shard_map/ppermute | solution.py:189
  28.9 23.8 %collective-permute-start.7 = (bf16[288,1024]{1,0:T(8,128)(2,1)}, bf16[288,1024]{1,0:T(8,128)(2,1)}, u32[]{:S(2)}, u32[]{:S(2)}) collective-permute-start(bf16[288,1024]{1,0:T(8,128)(2,1)} %get-tuple-element.366.refs_0_), channel_id=1, source_target_pairs={{0,1},{1,0},{2,3},{3,2},{4,5},{5,4},{6,7},{7,6},{8,9},{9,8},{10,11... | collective-permute-start | bytes 1769480 | tf_op jit(solution)/shard_map/ppermute | solution.py:25
  33.9 18.9 %collective-permute-start.9 = (bf16[288,1024]{1,0:T(8,128)(2,1)}, bf16[288,1024]{1,0:T(8,128)(2,1)}, u32[]{:S(2)}, u32[]{:S(2)}) collective-permute-start(bf16[288,1024]{1,0:T(8,128)(2,1)} %collective-permute-done.8.refs_2_), channel_id=1, source_target_pairs={{0,1},{1,0},{2,3},{3,2},{4,5},{5,4},{6,7},{7,6},{8,9},{9,8},{10,11... | collective-permute-start | bytes 1769480 | tf_op jit(solution)/shard_map/ppermute | solution.py:25
  36.6 14.6 %collective-permute-start.10 = (bf16[256,1024]{1,0:T(8,128)(2,1)}, bf16[256,1024]{1,0:T(8,128)(2,1)S(1)}, u32[]{:S(2)}, u32[]{:S(2)}) collective-permute-start(bf16[256,1024]{1,0:T(8,128)(2,1)} %get-tuple-element.367), channel_id=1, source_target_pairs={{4,0},{0,4},{5,1},{1,5},{6,2},{2,6},{7,3},{3,7},{12,8},{8,12},{13,... | collective-permute-start | bytes 1572872 | tf_op jit(solution)/shard_map/ppermute | solution.py:34
  57.1 18.7 %collective-permute-start.11 = (bf16[256,1024]{1,0:T(8,128)(2,1)}, bf16[256,1024]{1,0:T(8,128)(2,1)}, u32[]{:S(2)}, u32[]{:S(2)}) collective-permute-start(bf16[256,1024]{1,0:T(8,128)(2,1)} %get-tuple-element.371), channel_id=1, source_target_pairs={{0,2},{2,0},{1,3},{3,1},{4,6},{6,4},{5,7},{7,5},{8,10},{10,8},{9,1... | collective-permute-start | bytes 1572872 | tf_op jit(solution)/shard_map/ppermute | solution.py:29
  58.7 17.2 %collective-permute-start.12 = (bf16[1024,256]{1,0:T(8,128)(2,1)}, bf16[1024,256]{1,0:T(8,128)(2,1)}, u32[]{:S(2)}, u32[]{:S(2)}) collective-permute-start(bf16[1024,256]{1,0:T(8,128)(2,1)} %get-tuple-element.372), channel_id=1, source_target_pairs={{4,0},{0,4},{5,1},{1,5},{6,2},{2,6},{7,3},{3,7},{12,8},{8,12},{13,... | collective-permute-start | bytes 1572872 | tf_op jit(solution)/shard_map/ppermute | solution.py:34
  59.7 16.1 %collective-permute-start.13 = (bf16[256,1024]{1,0:T(8,128)(2,1)S(1)}, bf16[256,1024]{1,0:T(8,128)(2,1)}, u32[]{:S(2)}, u32[]{:S(2)}) collective-permute-start(bf16[256,1024]{1,0:T(8,128)(2,1)S(1)} %collective-permute-done.10.refs_1_.refs_3_), channel_id=1, source_target_pairs={{0,8},{8,0},{16,24},{24,16},{1,9},{9,1},{17,25},{25,17},{2,10},{10... | collective-permute-start | bytes 1572872 | tf_op jit(solution)/shard_map/ppermute | solution.py:189
  86.1 24.2 %collective-permute-start.20 = (bf16[320,1024]{1,0:T(8,128)(2,1)}, bf16[320,1024]{1,0:T(8,128)(2,1)}, u32[]{:S(2)}, u32[]{:S(2)}) collective-permute-start(bf16[320,1024]{1,0:T(8,128)(2,1)} %get-tuple-element.388), channel_id=1, source_target_pairs={{0,2},{2,0},{1,3},{3,1},{4,6},{6,4},{5,7},{7,5},{8,10},{10,8},{9,1... | collective-permute-start | bytes 1966088 | tf_op jit(solution)/shard_map/ppermute | solution.py:29
  86.6 14.7 %collective-permute-start.15 = (bf16[1024,256]{1,0:T(8,128)(2,1)}, bf16[1024,256]{1,0:T(8,128)(2,1)}, u32[]{:S(2)}, u32[]{:S(2)}) collective-permute-start(bf16[1024,256]{1,0:T(8,128)(2,1)} %collective-permute-done.12.refs_6_), channel_id=1, source_target_pairs={{0,8},{8,0},{16,24},{24,16},{1,9},{9,1},{17,25},{25,17},{2,10},{10... | collective-permute-start | bytes 1572872 | tf_op jit(solution)/shard_map/ppermute | solution.py:189
  86.9 23.4 %collective-permute-start.21 = (bf16[3,256,256]{2,1,0:T(8,128)(2,1)}, bf16[3,256,256]{2,1,0:T(8,128)(2,1)}, u32[]{:S(2)}, u32[]{:S(2)}) collective-permute-start(bf16[3,256,256]{2,1,0:T(8,128)(2,1)} %get-tuple-element.389), channel_id=1, source_target_pairs={{4,0},{0,4},{5,1},{1,5},{6,2},{2,6},{7,3},{3,7},{12,8},{8,12},{13,... | collective-permute-start | bytes 1179656 | tf_op jit(solution)/shard_map/ppermute | solution.py:34
  88.0 22.3 %collective-permute-start.22 = (bf16[256,256]{1,0:T(8,128)(2,1)}, bf16[256,256]{1,0:T(8,128)(2,1)}, u32[]{:S(2)}, u32[]{:S(2)}) collective-permute-start(bf16[256,256]{1,0:T(8,128)(2,1)} %get-tuple-element.390), channel_id=1, source_target_pairs={{4,0},{0,4},{5,1},{1,5},{6,2},{2,6},{7,3},{3,7},{12,8},{8,12},{13,... | collective-permute-start | bytes 393224 | tf_op jit(solution)/shard_map/ppermute | solution.py:34
  114.9 14.4 %collective-permute-start.26 = (bf16[256,1024]{1,0:T(8,128)(2,1)S(1)}, bf16[256,1024]{1,0:T(8,128)(2,1)}, u32[]{:S(2)}, u32[]{:S(2)}) collective-permute-start(bf16[256,1024]{1,0:T(8,128)(2,1)S(1)} %copy-done.142), channel_id=1, source_target_pairs={{4,0},{0,4},{5,1},{1,5},{6,2},{2,6},{7,3},{3,7},{12,8},{8,12},{13,... | collective-permute-start | bytes 1572872 | tf_op jit(solution)/shard_map/ppermute | solution.py:34
  117.3 15.5 %collective-permute-start.23 = (bf16[256,1024]{1,0:T(8,128)(2,1)S(1)}, bf16[256,1024]{1,0:T(8,128)(2,1)S(1)}, u32[]{:S(2)}, u32[]{:S(2)}) collective-permute-start(bf16[256,1024]{1,0:T(8,128)(2,1)S(1)} %get-tuple-element.393), channel_id=1, source_target_pairs={{0,2},{2,0},{1,3},{3,1},{4,6},{6,4},{5,7},{7,5},{8,10},{10,8},{9,1... | collective-permute-start | bytes 1572872 | tf_op jit(solution)/shard_map/ppermute | solution.py:29
  119.3 13.5 %collective-permute-start.24 = (bf16[3,256,256]{2,1,0:T(8,128)(2,1)}, bf16[3,256,256]{2,1,0:T(8,128)(2,1)S(1)}, u32[]{:S(2)}, u32[]{:S(2)}) collective-permute-start(bf16[3,256,256]{2,1,0:T(8,128)(2,1)} %collective-permute-done.21.refs_6_.refs_3_), channel_id=1, source_target_pairs={{0,8},{8,0},{16,24},{24,16},{1,9},{9,1},{17,25},{25,17},{2,10},{10... | collective-permute-start | bytes 1179656 | tf_op jit(solution)/shard_map/ppermute | solution.py:189
  136.4 15.9 %collective-permute-start.33 = (bf16[320,1024]{1,0:T(8,128)(2,1)}, bf16[320,1024]{1,0:T(8,128)(2,1)}, u32[]{:S(2)}, u32[]{:S(2)}) collective-permute-start(bf16[320,1024]{1,0:T(8,128)(2,1)} %get-tuple-element.410), channel_id=1, source_target_pairs={{0,2},{2,0},{1,3},{3,1},{4,6},{6,4},{5,7},{7,5},{8,10},{10,8},{9,1... | collective-permute-start | bytes 1966088 | tf_op jit(solution)/shard_map/ppermute | solution.py:29
  136.9 14.7 %collective-permute-start.35 = (bf16[1024,256]{1,0:T(8,128)(2,1)}, bf16[1024,256]{1,0:T(8,128)(2,1)}, u32[]{:S(2)}, u32[]{:S(2)}) collective-permute-start(bf16[1024,256]{1,0:T(8,128)(2,1)} %get-tuple-element.412), channel_id=1, source_target_pairs={{4,0},{0,4},{5,1},{1,5},{6,2},{2,6},{7,3},{3,7},{12,8},{8,12},{13,... | collective-permute-start | bytes 1572872 | tf_op jit(solution)/shard_map/ppermute | solution.py:34
  138.0 14.3 %collective-permute-start.34 = (bf16[256,1024]{1,0:T(8,128)(2,1)}, bf16[256,1024]{1,0:T(8,128)(2,1)}, u32[]{:S(2)}, u32[]{:S(2)}) collective-permute-start(bf16[256,1024]{1,0:T(8,128)(2,1)} %collective-permute-done.26.refs_8_.refs_3_), channel_id=1, source_target_pairs={{0,8},{8,0},{16,24},{24,16},{1,9},{9,1},{17,25},{25,17},{2,10},{10... | collective-permute-start | bytes 1572872 | tf_op jit(solution)/shard_map/ppermute | solution.py:189
  155.1 14.5 %collective-permute-start.37 = (bf16[1024,256]{1,0:T(8,128)(2,1)}, bf16[1024,256]{1,0:T(8,128)(2,1)S(1)}, u32[]{:S(2)}, u32[]{:S(2)}) collective-permute-start(bf16[1024,256]{1,0:T(8,128)(2,1)} %collective-permute-done.35.refs_7_.refs_6_), channel_id=1, source_target_pairs={{0,8},{8,0},{16,24},{24,16},{1,9},{9,1},{17,25},{25,17},{2,10},{10... | collective-permute-start | bytes 1572872 | tf_op jit(solution)/shard_map/ppermute | solution.py:189
  157.5 14.0 %collective-permute-start.36 = (bf16[256,1024]{1,0:T(8,128)(2,1)S(1)}, bf16[256,1024]{1,0:T(8,128)(2,1)S(1)}, u32[]{:S(2)}, u32[]{:S(2)}) collective-permute-start(bf16[256,1024]{1,0:T(8,128)(2,1)S(1)} %get-tuple-element.415), channel_id=1, source_target_pairs={{0,2},{2,0},{1,3},{3,1},{4,6},{6,4},{5,7},{7,5},{8,10},{10,8},{9,1... | collective-permute-start | bytes 1572872 | tf_op jit(solution)/shard_map/ppermute | solution.py:29
  172.4 16.2 %collective-permute-start.44 = (bf16[320,1024]{1,0:T(8,128)(2,1)S(1)}, bf16[320,1024]{1,0:T(8,128)(2,1)S(1)}, u32[]{:S(2)}, u32[]{:S(2)}) collective-permute-start(bf16[320,1024]{1,0:T(8,128)(2,1)S(1)} %get-tuple-element.431), channel_id=1, source_target_pairs={{0,2},{2,0},{1,3},{3,1},{4,6},{6,4},{5,7},{7,5},{8,10},{10,8},{9,1... | collective-permute-start | bytes 1966088 | tf_op jit(solution)/shard_map/ppermute | solution.py:29
  192.6 14.0 %collective-permute-start.45 = (bf16[256,1024]{1,0:T(8,128)(2,1)S(1)}, bf16[256,1024]{1,0:T(8,128)(2,1)S(1)}, u32[]{:S(2)}, u32[]{:S(2)}) collective-permute-start(bf16[256,1024]{1,0:T(8,128)(2,1)S(1)} %get-tuple-element.435), channel_id=1, source_target_pairs={{0,2},{2,0},{1,3},{3,1},{4,6},{6,4},{5,7},{7,5},{8,10},{10,8},{9,1... | collective-permute-start | bytes 1572872 | tf_op jit(solution)/shard_map/ppermute | solution.py:29
  209.1 16.0 %collective-permute-start.49 = (bf16[320,1024]{1,0:T(8,128)(2,1)S(1)}, bf16[320,1024]{1,0:T(8,128)(2,1)S(1)}, u32[]{:S(2)}, u32[]{:S(2)}) collective-permute-start(bf16[320,1024]{1,0:T(8,128)(2,1)S(1)} %get-tuple-element.449), channel_id=1, source_target_pairs={{0,2},{2,0},{1,3},{3,1},{4,6},{6,4},{5,7},{7,5},{8,10},{10,8},{9,1... | collective-permute-start | bytes 1966088 | tf_op jit(solution)/shard_map/ppermute | solution.py:29
  230.9 14.0 %collective-permute-start.54 = (bf16[256,1024]{1,0:T(8,128)(2,1)S(1)}, bf16[256,1024]{1,0:T(8,128)(2,1)S(1)}, u32[]{:S(2)}, u32[]{:S(2)}) collective-permute-start(bf16[256,1024]{1,0:T(8,128)(2,1)S(1)} %get-tuple-element.464), channel_id=1, source_target_pairs={{0,2},{2,0},{1,3},{3,1},{4,6},{6,4},{5,7},{7,5},{8,10},{10,8},{9,1... | collective-permute-start | bytes 1572872 | tf_op jit(solution)/shard_map/ppermute | solution.py:29
  238.8 20.0 %collective-permute-start.62 = (bf16[512,768]{1,0:T(8,128)(2,1)S(1)}, bf16[512,768]{1,0:T(8,128)(2,1)S(1)}, u32[]{:S(2)}, u32[]{:S(2)}) collective-permute-start(bf16[512,768]{1,0:T(8,128)(2,1)S(1)} %bitcast.46), channel_id=1, source_target_pairs={{0,4},{4,0},{1,5},{5,1},{2,6},{6,2},{3,7},{7,3},{8,12},{12,8},{9,1... | collective-permute-start | bytes 2359304 | tf_op jit(solution)/shard_map/ppermute | solution.py:39
  246.0 16.0 %collective-permute-start.61 = (bf16[320,1024]{1,0:T(8,128)(2,1)S(1)}, bf16[320,1024]{1,0:T(8,128)(2,1)S(1)}, u32[]{:S(2)}, u32[]{:S(2)}) collective-permute-start(bf16[320,1024]{1,0:T(8,128)(2,1)S(1)} %get-tuple-element.487), channel_id=1, source_target_pairs={{0,2},{2,0},{1,3},{3,1},{4,6},{6,4},{5,7},{7,5},{8,10},{10,8},{9,1... | collective-permute-start | bytes 1966088 | tf_op jit(solution)/shard_map/ppermute | solution.py:29
  263.2 20.0 %collective-permute-start.64 = (bf16[512,768]{1,0:T(8,128)(2,1)S(1)}, bf16[512,768]{1,0:T(8,128)(2,1)S(1)}, u32[]{:S(2)}, u32[]{:S(2)}) collective-permute-start(bf16[512,768]{1,0:T(8,128)(2,1)S(1)} %bitcast.42), channel_id=1, source_target_pairs={{0,4},{4,0},{1,5},{5,1},{2,6},{6,2},{3,7},{7,3},{8,12},{12,8},{9,1... | collective-permute-start | bytes 2359304 | tf_op jit(solution)/shard_map/ppermute | solution.py:39
  264.3 19.4 %collective-permute-start.65 = (bf16[512,768]{1,0:T(8,128)(2,1)S(1)}, bf16[512,768]{1,0:T(8,128)(2,1)S(1)}, u32[]{:S(2)}, u32[]{:S(2)}) collective-permute-start(bf16[512,768]{1,0:T(8,128)(2,1)S(1)} %get-tuple-element.506.refs_2_), channel_id=1, source_target_pairs={{0,8},{24,16},{1,9},{25,17},{2,10},{26,18},{3,11},{27,19},{4,12},{... | collective-permute-start | bytes 2359304 | tf_op jit(solution)/shard_map/ppermute | solution.py:773
  268.8 20.7 %collective-permute-start.63 = (bf16[256,1024]{1,0:T(8,128)(2,1)S(1)}, bf16[256,1024]{1,0:T(8,128)(2,1)S(1)}, u32[]{:S(2)}, u32[]{:S(2)}) collective-permute-start(bf16[256,1024]{1,0:T(8,128)(2,1)S(1)} %get-tuple-element.500), channel_id=1, source_target_pairs={{0,2},{2,0},{1,3},{3,1},{4,6},{6,4},{5,7},{7,5},{8,10},{10,8},{9,1... | collective-permute-start | bytes 1572872 | tf_op jit(solution)/shard_map/ppermute | solution.py:29
  278.5 13.0 %collective-permute-start.68 = (bf16[160,1024]{1,0:T(8,128)(2,1)S(1)}, bf16[160,1024]{1,0:T(8,128)(2,1)S(1)}, u32[]{:S(2)}, u32[]{:S(2)}) collective-permute-start(bf16[160,1024]{1,0:T(8,128)(2,1)S(1)} %get-tuple-element.523), channel_id=1, source_target_pairs={{0,1},{1,0},{2,3},{3,2},{4,5},{5,4},{6,7},{7,6},{8,9},{9,8},{10,11... | collective-permute-start | bytes 983048 | tf_op jit(solution)/shard_map/ppermute | solution.py:25
  278.6 13.0 %collective-permute-start.69 = (bf16[160,1024]{1,0:T(8,128)(2,1)S(1)}, bf16[160,1024]{1,0:T(8,128)(2,1)S(1)}, u32[]{:S(2)}, u32[]{:S(2)}) collective-permute-start(bf16[160,1024]{1,0:T(8,128)(2,1)S(1)} %get-tuple-element.524), channel_id=1, source_target_pairs={{0,1},{1,0},{2,3},{3,2},{4,5},{5,4},{6,7},{7,6},{8,9},{9,8},{10,11... | collective-permute-start | bytes 983048 | tf_op jit(solution)/shard_map/ppermute | solution.py:25
  284.1 20.7 %collective-permute-start.72 = (bf16[512,768]{1,0:T(8,128)(2,1)S(1)}, bf16[512,768]{1,0:T(8,128)(2,1)S(1)}, u32[]{:S(2)}, u32[]{:S(2)}) collective-permute-start(bf16[512,768]{1,0:T(8,128)(2,1)S(1)} %get-tuple-element.534.refs_2_), channel_id=1, source_target_pairs={{0,8},{24,16},{1,9},{25,17},{2,10},{26,18},{3,11},{27,19},{4,12},{... | collective-permute-start | bytes 2359304 | tf_op jit(solution)/shard_map/ppermute | solution.py:773
  288.6 19.5 %collective-permute-start.73 = (bf16[512,768]{1,0:T(8,128)(2,1)S(1)}, bf16[512,768]{1,0:T(8,128)(2,1)S(1)}, u32[]{:S(2)}, u32[]{:S(2)}) collective-permute-start(bf16[512,768]{1,0:T(8,128)(2,1)S(1)} %get-tuple-element.535.refs_4_), channel_id=1, source_target_pairs={{8,16},{16,8},{9,17},{17,9},{10,18},{18,10},{11,19},{19,11},{12,20... | collective-permute-start | bytes 2359304 | tf_op jit(solution)/shard_map/ppermute | solution.py:769
  289.5 20.5 %collective-permute-start.71 = (bf16[512,768]{1,0:T(8,128)(2,1)S(1)}, bf16[512,768]{1,0:T(8,128)(2,1)S(1)}, u32[]{:S(2)}, u32[]{:S(2)}) collective-permute-start(bf16[512,768]{1,0:T(8,128)(2,1)S(1)} %bitcast.43), channel_id=1, source_target_pairs={{0,4},{4,0},{1,5},{5,1},{2,6},{6,2},{3,7},{7,3},{8,12},{12,8},{9,1... | collective-permute-start | bytes 2359304 | tf_op jit(solution)/shard_map/ppermute | solution.py:39
  291.8 23.2 %collective-permute-start.70 = (bf16[320,1024]{1,0:T(8,128)(2,1)S(1)}, bf16[320,1024]{1,0:T(8,128)(2,1)S(1)}, u32[]{:S(2)}, u32[]{:S(2)}) collective-permute-start(bf16[320,1024]{1,0:T(8,128)(2,1)S(1)} %get-tuple-element.528), channel_id=1, source_target_pairs={{0,2},{2,0},{1,3},{3,1},{4,6},{6,4},{5,7},{7,5},{8,10},{10,8},{9,1... | collective-permute-start | bytes 1966088 | tf_op jit(solution)/shard_map/ppermute | solution.py:29
  297.4 18.8 %collective-permute-start.75 = (bf16[128,1024]{1,0:T(8,128)(2,1)S(1)}, bf16[128,1024]{1,0:T(8,128)(2,1)S(1)}, u32[]{:S(2)}, u32[]{:S(2)}) collective-permute-start(bf16[128,1024]{1,0:T(8,128)(2,1)S(1)} %get-tuple-element.545), channel_id=1, source_target_pairs={{0,1},{1,0},{2,3},{3,2},{4,5},{5,4},{6,7},{7,6},{8,9},{9,8},{10,11... | collective-permute-start | bytes 786440 | tf_op jit(solution)/shard_map/ppermute | solution.py:25
  304.8 20.1 %collective-permute-start.79 = (bf16[512,768]{1,0:T(8,128)(2,1)S(1)}, bf16[512,768]{1,0:T(8,128)(2,1)S(1)}, u32[]{:S(2)}, u32[]{:S(2)}) collective-permute-start(bf16[512,768]{1,0:T(8,128)(2,1)S(1)} %bitcast.45), channel_id=1, source_target_pairs={{0,4},{4,0},{1,5},{5,1},{2,6},{6,2},{3,7},{7,3},{8,12},{12,8},{9,1... | collective-permute-start | bytes 2359304 | tf_op jit(solution)/shard_map/ppermute | solution.py:39
  310.7 17.2 %collective-permute-start.78 = (bf16[512,768]{1,0:T(8,128)(2,1)S(1)}, bf16[512,768]{1,0:T(8,128)(2,1)S(1)}, u32[]{:S(2)}, u32[]{:S(2)}) collective-permute-start(bf16[512,768]{1,0:T(8,128)(2,1)S(1)} %get-tuple-element.555), channel_id=1, source_target_pairs={{0,8},{8,0},{16,24},{24,16},{1,9},{9,1},{17,25},{25,17},{2,10},{10... | collective-permute-start | bytes 2359304 | tf_op jit(solution)/shard_map/ppermute | solution.py:771
  314.1 13.9 %collective-permute-start.80 = (bf16[512,768]{1,0:T(8,128)(2,1)S(1)}, bf16[512,768]{1,0:T(8,128)(2,1)S(1)}, u32[]{:S(2)}, u32[]{:S(2)}) collective-permute-start(bf16[512,768]{1,0:T(8,128)(2,1)S(1)} %get-tuple-element.559.refs_4_), channel_id=1, source_target_pairs={{8,16},{16,8},{9,17},{17,9},{10,18},{18,10},{11,19},{19,11},{12,20... | collective-permute-start | bytes 2359304 | tf_op jit(solution)/shard_map/ppermute | solution.py:769
  316.9 16.8 %collective-permute-start.77 = (bf16[256,1024]{1,0:T(8,128)(2,1)S(1)}, bf16[256,1024]{1,0:T(8,128)(2,1)S(1)}, u32[]{:S(2)}, u32[]{:S(2)}) collective-permute-start(bf16[256,1024]{1,0:T(8,128)(2,1)S(1)} %get-tuple-element.550), channel_id=1, source_target_pairs={{0,2},{2,0},{1,3},{3,1},{4,6},{6,4},{5,7},{7,5},{8,10},{10,8},{9,1... | collective-permute-start | bytes 1572872 | tf_op jit(solution)/shard_map/ppermute | solution.py:29
  323.0 14.3 %collective-permute-start.82 = (bf16[160,1024]{1,0:T(8,128)(2,1)S(1)}, bf16[160,1024]{1,0:T(8,128)(2,1)S(1)}, u32[]{:S(2)}, u32[]{:S(2)}) collective-permute-start(bf16[160,1024]{1,0:T(8,128)(2,1)S(1)} %get-tuple-element.569), channel_id=1, source_target_pairs={{0,1},{1,0},{2,3},{3,2},{4,5},{5,4},{6,7},{7,6},{8,9},{9,8},{10,11... | collective-permute-start | bytes 983048 | tf_op jit(solution)/shard_map/ppermute | solution.py:25
  328.6 21.1 %collective-permute-start.85 = (bf16[512,768]{1,0:T(8,128)(2,1)S(1)}, bf16[512,768]{1,0:T(8,128)(2,1)S(1)}, u32[]{:S(2)}, u32[]{:S(2)}) collective-permute-start(bf16[512,768]{1,0:T(8,128)(2,1)S(1)} %get-tuple-element.577), channel_id=1, source_target_pairs={{0,8},{8,0},{16,24},{24,16},{1,9},{9,1},{17,25},{25,17},{2,10},{10... | collective-permute-start | bytes 2359304 | tf_op jit(solution)/shard_map/ppermute | solution.py:771
  332.6 17.2 %collective-permute-start.87 = (bf16[512,768]{1,0:T(8,128)(2,1)S(1)}, bf16[512,768]{1,0:T(8,128)(2,1)S(1)}, u32[]{:S(2)}, u32[]{:S(2)}) collective-permute-start(bf16[512,768]{1,0:T(8,128)(2,1)S(1)} %get-tuple-element.582.refs_4_), channel_id=1, source_target_pairs={{8,16},{16,8},{9,17},{17,9},{10,18},{18,10},{11,19},{19,11},{12,20... | collective-permute-start | bytes 2359304 | tf_op jit(solution)/shard_map/ppermute | solution.py:769
  333.8 20.5 %collective-permute-start.86 = (bf16[512,768]{1,0:T(8,128)(2,1)S(1)}, bf16[512,768]{1,0:T(8,128)(2,1)S(1)}, u32[]{:S(2)}, u32[]{:S(2)}) collective-permute-start(bf16[512,768]{1,0:T(8,128)(2,1)S(1)} %bitcast.44), channel_id=1, source_target_pairs={{0,4},{4,0},{1,5},{5,1},{2,6},{6,2},{3,7},{7,3},{8,12},{12,8},{9,1... | collective-permute-start | bytes 2359304 | tf_op jit(solution)/shard_map/ppermute | solution.py:39
  337.5 22.8 %collective-permute-start.84 = (bf16[320,1024]{1,0:T(8,128)(2,1)S(1)}, bf16[320,1024]{1,0:T(8,128)(2,1)S(1)}, u32[]{:S(2)}, u32[]{:S(2)}) collective-permute-start(bf16[320,1024]{1,0:T(8,128)(2,1)S(1)} %get-tuple-element.572), channel_id=1, source_target_pairs={{0,2},{2,0},{1,3},{3,1},{4,6},{6,4},{5,7},{7,5},{8,10},{10,8},{9,1... | collective-permute-start | bytes 1966088 | tf_op jit(solution)/shard_map/ppermute | solution.py:29
  346.3 29.3 %collective-permute-start.92 = (bf16[512,768]{1,0:T(8,128)(2,1)S(1)}, bf16[512,768]{1,0:T(8,128)(2,1)S(1)}, u32[]{:S(2)}, u32[]{:S(2)}) collective-permute-start(bf16[512,768]{1,0:T(8,128)(2,1)S(1)} %bitcast.40), channel_id=1, source_target_pairs={{0,4},{4,0},{1,5},{5,1},{2,6},{6,2},{3,7},{7,3},{8,12},{12,8},{9,1... | collective-permute-start | bytes 2359304 | tf_op jit(solution)/shard_map/ppermute | solution.py:39
  355.0 20.7 %collective-permute-start.93 = (bf16[512,768]{1,0:T(8,128)(2,1)S(1)}, bf16[512,768]{1,0:T(8,128)(2,1)S(1)}, u32[]{:S(2)}, u32[]{:S(2)}) collective-permute-start(bf16[512,768]{1,0:T(8,128)(2,1)S(1)} %get-tuple-element.620), channel_id=1, source_target_pairs={{0,8},{8,0},{16,24},{24,16},{1,9},{9,1},{17,25},{25,17},{2,10},{10... | collective-permute-start | bytes 2359304 | tf_op jit(solution)/shard_map/ppermute | solution.py:771
  358.1 17.6 %collective-permute-start.94 = (bf16[512,768]{1,0:T(8,128)(2,1)S(1)}, bf16[512,768]{1,0:T(8,128)(2,1)S(1)}, u32[]{:S(2)}, u32[]{:S(2)}) collective-permute-start(bf16[512,768]{1,0:T(8,128)(2,1)S(1)} %get-tuple-element.621.refs_4_), channel_id=1, source_target_pairs={{8,16},{16,8},{9,17},{17,9},{10,18},{18,10},{11,19},{19,11},{12,20... | collective-permute-start | bytes 2359304 | tf_op jit(solution)/shard_map/ppermute | solution.py:769
  376.4 19.9 %collective-permute-start.95 = (bf16[512,768]{1,0:T(8,128)(2,1)S(1)}, bf16[512,768]{1,0:T(8,128)(2,1)S(1)}, u32[]{:S(2)}, u32[]{:S(2)}) collective-permute-start(bf16[512,768]{1,0:T(8,128)(2,1)S(1)} %get-tuple-element.624), channel_id=1, source_target_pairs={{0,8},{8,0},{16,24},{24,16},{1,9},{9,1},{17,25},{25,17},{2,10},{10... | collective-permute-start | bytes 2359304 | tf_op jit(solution)/shard_map/ppermute | solution.py:771
  378.0 19.6 %collective-permute-start.96 = (bf16[512,768]{1,0:T(8,128)(2,1)S(1)}, bf16[512,768]{1,0:T(8,128)(2,1)S(1)}, u32[]{:S(2)}, u32[]{:S(2)}) collective-permute-start(bf16[512,768]{1,0:T(8,128)(2,1)S(1)} %get-tuple-element.625.refs_4_), channel_id=1, source_target_pairs={{8,16},{16,8},{9,17},{17,9},{10,18},{18,10},{11,19},{19,11},{12,20... | collective-permute-start | bytes 2359304 | tf_op jit(solution)/shard_map/ppermute | solution.py:769
  378.9 20.5 %collective-permute-start.91 = (bf16[512,768]{1,0:T(8,128)(2,1)S(1)}, bf16[512,768]{1,0:T(8,128)(2,1)S(1)}, u32[]{:S(2)}, u32[]{:S(2)}) collective-permute-start(bf16[512,768]{1,0:T(8,128)(2,1)S(1)} %bitcast.41), channel_id=1, source_target_pairs={{0,4},{4,0},{1,5},{5,1},{2,6},{6,2},{3,7},{7,3},{8,12},{12,8},{9,1... | collective-permute-start | bytes 2359304 | tf_op jit(solution)/shard_map/ppermute | solution.py:39
  380.0 25.3 %collective-permute-start.51 = (bf16[576,1024]{1,0:T(8,128)(2,1)S(1)}, bf16[576,1024]{1,0:T(8,128)(2,1)S(1)}, u32[]{:S(2)}, u32[]{:S(2)}) collective-permute-start(bf16[576,1024]{1,0:T(8,128)(2,1)S(1)} %constant_dynamic-update-slice_fusion.refs_0_), channel_id=1, source_target_pairs={{0,1},{1,0},{2,3},{3,2},{4,5},{5,4},{6,7},{7,6},{8,9},{9,8},{10,11... | collective-permute-start | bytes 3538952 | tf_op jit(solution)/shard_map/ppermute | solution.py:25
  387.5 33.1 %collective-permute-start.101 = (bf16[528,768]{1,0:T(8,128)(2,1)S(1)}, bf16[528,768]{1,0:T(8,128)(2,1)S(1)}, u32[]{:S(2)}, u32[]{:S(2)}) collective-permute-start(bf16[528,768]{1,0:T(8,128)(2,1)S(1)} %bitcast.39), channel_id=1, source_target_pairs={{0,4},{4,0},{1,5},{5,1},{2,6},{6,2},{3,7},{7,3},{8,12},{12,8},{9,1... | collective-permute-start | bytes 2433032 | tf_op jit(solution)/shard_map/ppermute | solution.py:39
  400.0 19.1 %collective-permute-start.102 = (bf16[512,768]{1,0:T(8,128)(2,1)S(1)}, bf16[512,768]{1,0:T(8,128)(2,1)S(1)}, u32[]{:S(2)}, u32[]{:S(2)}) collective-permute-start(bf16[512,768]{1,0:T(8,128)(2,1)S(1)} %get-tuple-element.658), channel_id=1, source_target_pairs={{0,8},{8,0},{16,24},{24,16},{1,9},{9,1},{17,25},{25,17},{2,10},{10... | collective-permute-start | bytes 2359304 | tf_op jit(solution)/shard_map/ppermute | solution.py:771
  403.1 17.6 %collective-permute-start.103 = (bf16[512,768]{1,0:T(8,128)(2,1)S(1)}, bf16[512,768]{1,0:T(8,128)(2,1)S(1)}, u32[]{:S(2)}, u32[]{:S(2)}) collective-permute-start(bf16[512,768]{1,0:T(8,128)(2,1)S(1)} %get-tuple-element.659.refs_4_), channel_id=1, source_target_pairs={{8,16},{16,8},{9,17},{17,9},{10,18},{18,10},{11,19},{19,11},{12,20... | collective-permute-start | bytes 2359304 | tf_op jit(solution)/shard_map/ppermute | solution.py:769
  403.8 26.3 %collective-permute-start.104 = (bf16[320,1024]{1,0:T(8,128)(2,1)S(1)}, bf16[320,1024]{1,0:T(8,128)(2,1)S(1)}, u32[]{:S(2)}, u32[]{:S(2)}) collective-permute-start(bf16[320,1024]{1,0:T(8,128)(2,1)S(1)} %get-tuple-element.666), channel_id=1, source_target_pairs={{0,2},{2,0},{1,3},{3,1},{4,6},{6,4},{5,7},{7,5},{8,10},{10,8},{9,1... | collective-permute-start | bytes 1966088 | tf_op jit(solution)/shard_map/ppermute | solution.py:29
  405.3 24.5 %collective-permute-start.100 = (bf16[256,1024]{1,0:T(8,128)(2,1)S(1)}, bf16[256,1024]{1,0:T(8,128)(2,1)S(1)}, u32[]{:S(2)}, u32[]{:S(2)}) collective-permute-start(bf16[256,1024]{1,0:T(8,128)(2,1)S(1)} %get-tuple-element.653), channel_id=1, source_target_pairs={{0,2},{2,0},{1,3},{3,1},{4,6},{6,4},{5,7},{7,5},{8,10},{10,8},{9,1... | collective-permute-start | bytes 1572872 | tf_op jit(solution)/shard_map/ppermute | solution.py:29
  421.3 17.9 %collective-permute-start.106 = (bf16[528,768]{1,0:T(8,128)(2,1)S(1)}, bf16[528,768]{1,0:T(8,128)(2,1)S(1)}, u32[]{:S(2)}, u32[]{:S(2)}) collective-permute-start(bf16[528,768]{1,0:T(8,128)(2,1)S(1)} %get-tuple-element.671), channel_id=1, source_target_pairs={{0,8},{8,0},{16,24},{24,16},{1,9},{9,1},{17,25},{25,17},{2,10},{10... | collective-permute-start | bytes 2433032 | tf_op jit(solution)/shard_map/ppermute | solution.py:771
  423.5 17.0 %collective-permute-start.107 = (bf16[512,768]{1,0:T(8,128)(2,1)S(1)}, bf16[512,768]{1,0:T(8,128)(2,1)S(1)}, u32[]{:S(2)}, u32[]{:S(2)}) collective-permute-start(bf16[512,768]{1,0:T(8,128)(2,1)S(1)} %get-tuple-element.672.refs_2_), channel_id=1, source_target_pairs={{8,16},{16,8},{9,17},{17,9},{10,18},{18,10},{11,19},{19,11},{12,20... | collective-permute-start | bytes 2359304 | tf_op jit(solution)/shard_map/ppermute | solution.py:769
  430.5 12.5 %collective-permute-start.105 = (bf16[576,1024]{1,0:T(8,128)(2,1)S(1)}, bf16[576,1024]{1,0:T(8,128)(2,1)S(1)}, u32[]{:S(2)}, u32[]{:S(2)}) collective-permute-start(bf16[576,1024]{1,0:T(8,128)(2,1)S(1)} %constant_dynamic-update-slice_fusion.2.refs_0_), channel_id=1, source_target_pairs={{0,1},{1,0},{2,3},{3,2},{4,5},{5,4},{6,7},{7,6},{8,9},{9,8},{10,11... | collective-permute-start | bytes 3538952 | tf_op jit(solution)/shard_map/ppermute | solution.py:25
  440.9 20.6 %collective-permute-start.108 = (bf16[528,768]{1,0:T(8,128)(2,1)S(1)}, bf16[528,768]{1,0:T(8,128)(2,1)S(1)}, u32[]{:S(2)}, u32[]{:S(2)}) collective-permute-start(bf16[528,768]{1,0:T(8,128)(2,1)S(1)} %get-tuple-element.680.refs_0_), channel_id=1, source_target_pairs={{8,16},{16,8},{9,17},{17,9},{10,18},{18,10},{11,19},{19,11},{12,20... | collective-permute-start | bytes 2433032 | tf_op jit(solution)/shard_map/ppermute | solution.py:769
  441.6 18.5 %collective-permute-start.109 = (bf16[512,768]{1,0:T(8,128)(2,1)S(1)}, bf16[512,768]{1,0:T(8,128)(2,1)S(1)}, u32[]{:S(2)}, u32[]{:S(2)}) collective-permute-start(bf16[512,768]{1,0:T(8,128)(2,1)S(1)} %get-tuple-element.681.refs_0_), channel_id=1, source_target_pairs={{8,0},{16,24},{9,1},{17,25},{10,2},{18,26},{11,3},{19,27},{12,4},{... | collective-permute-start | bytes 2359304 | tf_op jit(solution)/shard_map/ppermute | solution.py:775
  461.8 17.5 %collective-permute-start.110 = (bf16[528,768]{1,0:T(8,128)(2,1)S(1)}, bf16[528,768]{1,0:T(8,128)(2,1)S(1)}, u32[]{:S(2)}, u32[]{:S(2)}) collective-permute-start(bf16[528,768]{1,0:T(8,128)(2,1)S(1)} %get-tuple-element.686.refs_0_), channel_id=1, source_target_pairs={{8,0},{16,24},{9,1},{17,25},{10,2},{18,26},{11,3},{19,27},{12,4},{... | collective-permute-start | bytes 2433032 | tf_op jit(solution)/shard_map/ppermute | solution.py:775
  (195 other events, 1001.1 us)

commit v4 on v3

--- a/solution.py
+++ b/solution.py
@@ -13,8 +13,10 @@
 LENGTHS = (512, 256, 128, 128, 128)
 STARTS = (0, 512, 768, 896, 1024)
 STREAMS = ((0,), (1, 2, 3, 4))
+CUT = 2
 HALVES = 2
 BF = jnp.bfloat16
+DP, FSDP, TENSOR = "dp", "fsdp", "tensor"
 F32 = jnp.float32
 MIB = 1 << 20
 CORE_SWAP = [(0, 1), (1, 0), (2, 3), (3, 2)]
@@ -22,26 +24,26 @@
 
 
 def to_core(value):
-    return lax.ppermute(value, "tensor", CORE_SWAP)
+    return lax.ppermute(value, TENSOR, CORE_SWAP)
 
 
 def to_chip(value):
-    return lax.ppermute(value, "tensor", CHIP_SWAP)
+    return lax.ppermute(value, TENSOR, CHIP_SWAP)
 
 
 def from_fsdp(value, step):
-    size = lax.axis_size("fsdp")
-    return lax.ppermute(value, "fsdp", [((i + step) % size, i) for i in range(size)])
+    size = lax.axis_size(FSDP)
+    return lax.ppermute(value, FSDP, [((i + step) % size, i) for i in range(size)])
 
 
 def to_fsdp(value, step):
-    size = lax.axis_size("fsdp")
-    return lax.ppermute(value, "fsdp", [(i, (i + step) % size) for i in range(size)])
+    size = lax.axis_size(FSDP)
+    return lax.ppermute(value, FSDP, [(i, (i + step) % size) for i in range(size)])
 
 
 def own_first(whole, axis):
-    size = lax.axis_size("fsdp")
-    here = lax.axis_index("fsdp")
+    size = lax.axis_size(FSDP)
+    here = lax.axis_index(FSDP)
     width = whole.shape[axis] // size
     return jnp.concatenate(
         [lax.dynamic_slice_in_dim(whole, (here + k) % size * width, width, axis) for k in range(size)], axis
@@ -49,8 +51,8 @@
 
 
 def natural(relative, axis):
-    size = lax.axis_size("fsdp")
-    here = lax.axis_index("fsdp")
+    size = lax.axis_size(FSDP)
+    here = lax.axis_index(FSDP)
     width = relative.shape[axis] // size
     return jnp.concatenate(
         [
@@ -157,16 +159,16 @@
 
 
 def core_index():
-    return lax.rem(lax.axis_index("tensor"), 2)
+    return lax.rem(lax.axis_index(TENSOR), 2)
 
 
 class Weight:
     def __init__(self, order, whole, layer, axis):
         self.order, self.whole, self.layer, self.axis = order, whole, layer, axis
-        self.size = lax.axis_size("fsdp")
+        self.size = lax.axis_size(FSDP)
         shape = whole.shape[1:]
         width = shape[axis]
-        self.halved = self.size == 2 and lax.axis_size("dp") % 2 == 0 and width % 256 == 0
+        self.halved = self.size == 2 and lax.axis_size(DP) % 2 == 0 and width % 256 == 0
         self.widths = [width] + ([width // 2] * 2 if self.halved else [width] * (self.size - 1))
         self.shape = shape
 
@@ -174,7 +176,7 @@
         width = self.widths[0]
         if not self.halved:
             return [pl.ds(k * width, width) for k in range(self.size)]
-        parity = lax.rem(lax.axis_index("dp"), 2)
+        parity = lax.rem(lax.axis_index(DP), 2)
         half = width // 2
         return [
             pl.ds(0, width),
@@ -185,8 +187,8 @@
     def start(self, own, half):
         if self.halved:
             self.early = [from_fsdp(half, 1)]
-            size = lax.axis_size("dp")
-            self.late = [lax.ppermute(self.early[0], "dp", [(i, i ^ 1) for i in range(size)])]
+            size = lax.axis_size(DP)
+            self.late = [lax.ppermute(self.early[0], DP, [(i, i ^ 1) for i in range(size)])]
         else:
             self.early = [from_fsdp(own, step) for step in range(1, self.size)]
             self.late = []
@@ -211,7 +213,7 @@
 
     def body(*refs):
         outs, sems = list(refs[len(weights) : -1]), refs[-1]
-        parity = lax.rem(lax.axis_index("dp"), 2)
+        parity = lax.rem(lax.axis_index(DP), 2)
         copies = []
         for w, ref in zip(weights, refs):
             sources = [ref.at[w.layer]]
@@ -242,12 +244,12 @@
 
 def deal_rows(order, activations):
     features = activations.shape[1]
-    size = lax.axis_size("fsdp")
+    size = lax.axis_size(FSDP)
     width = features // size
 
     def body(whole, *outs):
         here = core_index()
-        mine = lax.axis_index("fsdp")
+        mine = lax.axis_index(FSDP)
         for at, stream in enumerate(STREAMS):
             for slot in range(HALVES):
                 out = outs[at * HALVES + slot]
@@ -278,14 +280,14 @@
 
 def deal_share(order, slots):
     rows, features = slots[0].shape
-    size = lax.axis_size("fsdp")
+    size = lax.axis_size(FSDP)
     width = features // size
 
     def body(a, b, c, d, *outs):
         whole = outs[-1]
-        here = lax.axis_index("tensor")
+        here = lax.axis_index(TENSOR)
         core = core_index()
-        mine = lax.axis_index("fsdp")
+        mine = lax.axis_index(FSDP)
         for slot, ref in enumerate((a, b, c, d)):
             whole[pl.ds(pl.multiple_of((here ^ slot) * rows, 32), rows), :] = ref[...]
         for at, stream in enumerate(STREAMS):
@@ -310,13 +312,13 @@
 def natural_share(order, slots, dtype):
     rows, features = slots[0].shape
     share = rows // 2
-    size = lax.axis_size("fsdp")
+    size = lax.axis_size(FSDP)
     width = features // size
 
     def body(a, b, out, whole):
-        here = lax.axis_index("tensor")
+        here = lax.axis_index(TENSOR)
         core = core_index()
-        mine = lax.axis_index("fsdp")
+        mine = lax.axis_index(FSDP)
         for slot, ref in enumerate((a, b)):
             first = 0
             for stream in STREAMS:
@@ -340,17 +342,19 @@
 
 
 def add_send(order, kept, came):
-    half = kept.shape[0] // 2
-
-    def body(a, b, c, low):
-        for at, came_ref in ((0, b), (half, c)):
-            low[at : at + half, :] = (a[at : at + half, :].astype(F32) + came_ref[...].astype(F32)).astype(BF)
+    def body(a, *refs):
+        low, at = refs[-1], 0
+        for ref in refs[:-1]:
+            rows = slice(at, at + ref.shape[0])
+            low[rows, :] = (a[rows, :].astype(F32) + ref[...].astype(F32)).astype(BF)
+            at += ref.shape[0]
 
     return order.call(body, [kept, *came], [shape_of(kept.shape, BF)], name="add_send")[0]
 
 
-def sum_terms(own, first, second, across):
-    beside = jnp.concatenate([first[...], second[...]], 0)
+def sum_terms(own, *refs):
+    *pieces, across = refs
+    beside = jnp.concatenate([ref[...] for ref in pieces], 0)
     return own[...].astype(F32) + beside.astype(F32) + across[...].astype(F32)
 
 
@@ -362,30 +366,32 @@
     rows, features = terms[0].shape
     bias_at, gain_at, shift_at = rows_of_vectors
 
-    def body(a, b, c, d, before, vec, low, normed, inverse, kept):
+    def body(*refs):
+        parts, (before, vec, *lows, normed, inverse, kept) = refs[: len(terms)], refs[len(terms) :]
         value = before[...].astype(F32)
         if residual[1] is not None:
             value = value * row_of(vec, residual[1]) + row_of(vec, residual[2])
-        value = value + sum_terms(a, b, c, d) + row_of(vec, bias_at)
+        value = value + sum_terms(*parts) + row_of(vec, bias_at)
         center = value - jnp.mean(value, -1, keepdims=True)
         scale = lax.rsqrt(jnp.mean(center * center, -1, keepdims=True) + 1e-05)
         unit = center * scale
         normed[...] = unit
         kept[...] = unit.astype(BF)
         inverse[...] = scale
-        low[...] = (unit * row_of(vec, gain_at) + row_of(vec, shift_at)).astype(BF)
-
-    return order.call(
+        split_rows(lows, slice(None), unit * row_of(vec, gain_at) + row_of(vec, shift_at))
+
+    outs = order.call(
         body,
         [*terms, residual[0], vectors],
         [
-            shape_of((rows, features), BF),
+            *[shape_of((rows // CUT, features), BF)] * CUT,
             shape_of((rows, features), F32),
             shape_of((rows, 1), F32),
             shape_of((rows, features), BF),
         ],
         name="norm_forward",
     )
+    return [outs[:CUT], *outs[CUT:]]
 
 
 def norm_backward(order, terms, normed, inverse, vectors, gain_at):
@@ -393,7 +399,7 @@
     count = len(terms)
 
     def body(*refs):
-        unit, scale, vec, low, sums, wide = refs[count:]
+        unit, scale, vec, *lows, sums, wide = refs[count:]
         total = refs[count - 1][...].astype(F32)
         if count > 1:
             total = total + sum_terms(*refs[: count - 1])
@@ -403,22 +409,27 @@
         mean_two = jnp.mean(grad * n, -1, keepdims=True)
         result = scale[...] * (grad - mean_one - n * mean_two)
         wide[...] = result
-        low[...] = result.astype(BF)
+        split_rows(lows, slice(None), result)
         sums[0:1, :] = jnp.sum(total * n, 0, keepdims=True)
         sums[1:2, :] = jnp.sum(total, 0, keepdims=True)
         sums[2:3, :] = jnp.sum(result, 0, keepdims=True)
 
-    return order.call(
+    outs = order.call(
         body,
         [*terms, normed, inverse, vectors],
-        [shape_of((rows, features), BF), shape_of((3, features), F32), shape_of((rows, features), F32)],
+        [
+            *[shape_of((rows // CUT, features), BF)] * CUT,
+            shape_of((3, features), F32),
+            shape_of((rows, features), F32),
+        ],
         name="norm_backward",
     )
+    return [outs[:CUT], *outs[CUT:]]
 
 
 def last_sum(order, terms):
     def body(*refs):
-        refs[-1][...] = (refs[4][...] + sum_terms(*refs[:4])).astype(BF)
+        refs[-1][...] = (refs[-2][...] + sum_terms(*refs[:-2])).astype(BF)
 
     return order.call(body, terms, [shape_of(terms[0].shape, BF)], name="last_sum")[0]
 
@@ -447,17 +458,17 @@
 
 def attention_forward(order, stream, slots, weights, lengths):
     w_proj, w_mix, bias_rows = weights
-    share, features = slots[0].shape
+    share, features = slots_shape(slots)
     span = w_mix.shape[0]
     heads = span // HEAD
     places = page_places(stream)
 
     def body(*refs):
-        xs, refs = refs[:HALVES], refs[HALVES:]
+        xs, refs = refs[: len(slots)], refs[len(slots) :]
         wp, refs = w_proj.take(refs)
         wm, refs = w_mix.take(refs)
         bias, limits, refs = refs[0], refs[1], refs[2:]
-        others, part_own, qkv, ctx, probs = refs[:2], refs[2], refs[3], refs[4], refs[5:]
+        others, (part_own, qkv, ctx), probs = refs[:CUT], refs[CUT : CUT + 3], refs[CUT + 3 :]
         for kind in range(3):
             value = None
             for w, at in wp:
@@ -508,28 +519,28 @@
         body,
         [*slots, *w_proj.arrays, *w_mix.arrays, bias_rows, lengths],
         [
-            *[shape_of((share // 2, features), BF)] * 2,
+            *[shape_of((share // CUT, features), BF)] * CUT,
             shape_of((share, features), BF),
             shape_of((2 * share, 3 * span), BF),
             shape_of((2 * share, span), BF),
         ]
         + [shape_of((heads, length, length), BF) for _, length, _, _ in places],
-        in_specs=[None] * HALVES + w_proj.specs() + w_mix.specs() + [None, SMEM],
+        in_specs=[None] * len(slots) + w_proj.specs() + w_mix.specs() + [None, SMEM],
         name="attention_forward",
     )
-    return {"other": outs[:2], "own": outs[2], "qkv": outs[3], "ctx": outs[4], "probs": outs[5:]}
+    return {"other": outs[:CUT], "own": outs[CUT], "qkv": outs[CUT + 1], "ctx": outs[CUT + 2], "probs": outs[CUT + 3 :]}
 
 
 def attention_backward(order, stream, slots, weights, state):
     w_proj, w_mix = weights
     probs, qkv = state["probs"], state["qkv"]
-    share, features = slots[0].shape
+    share, features = slots_shape(slots)
     span = w_mix.shape[0]
     heads = span // HEAD
     places = page_places(stream)
 
     def body(*refs):
-        ds, refs = refs[:HALVES], refs[HALVES:]
+        ds, refs = refs[: len(slots)], refs[len(slots) :]
         wp, refs = w_proj.take(refs)
         wm, refs = w_mix.take(refs)
         chances, refs = refs[: len(places)], refs[len(places) :]
@@ -592,22 +603,26 @@
         body,
         [*slots, *w_proj.arrays, *w_mix.arrays, *probs, qkv],
         [
-            *[shape_of((share // 2, features), BF)] * 2,
+            *[shape_of((share // CUT, features), BF)] * CUT,
             shape_of((share, features), BF),
             shape_of((2 * share, 3 * span), BF),
             shape_of((1, 3 * span), F32),
         ],
         scratch=[pltpu.VMEM((2 * share, span), BF)],
-        in_specs=[None] * HALVES + w_proj.specs() + w_mix.specs() + [None] * (len(places) + 1),
+        in_specs=[None] * len(slots) + w_proj.specs() + w_mix.specs() + [None] * (len(places) + 1),
         name="attention_backward",
     )
-    return {"other": outs[:2], "own": outs[2], "grad": outs[3], "sums": outs[4]}
+    return {"other": outs[:CUT], "own": outs[CUT], "grad": outs[CUT + 1], "sums": outs[CUT + 2]}
+
+
+def slots_shape(slots):
+    return sum(v.shape[0] for v in slots) // 2, slots[0].shape[1]
 
 
 def split_rows(refs, at, value):
-    half = value.shape[0] // 2
-    refs[0][:, at] = value[:half].astype(BF)
-    refs[1][:, at] = value[half:].astype(BF)
+    count = value.shape[0] // CUT
+    for i, ref in enumerate(refs):
+        ref[:, at] = value[i * count : (i + 1) * count].astype(BF)
 
 
 def leave_terms(low, weight, product, share, others, part_own):
@@ -619,11 +634,11 @@
 
 def feed_forward(order, slots, weights):
     w_grow, w_shrink, bias = weights
-    share, features = slots[0].shape
+    share, features = slots_shape(slots)
     hidden = w_shrink.shape[0]
 
     def body(*refs):
-        xs, refs = refs[:HALVES], refs[HALVES:]
+        xs, refs = refs[: len(slots)], refs[len(slots) :]
         wg, refs = w_grow.take(refs)
         ws, refs = w_shrink.take(refs)
         b, *others, act, slope, part_own = refs
@@ -644,7 +659,7 @@
         body,
         [*slots, *w_grow.arrays, *w_shrink.arrays, bias],
         [
-            *[shape_of((share // 2, features), BF)] * 2,
+            *[shape_of((share // CUT, features), BF)] * CUT,
             shape_of((2 * share, hidden), BF),
             shape_of((2 * share, hidden), BF),
             shape_of((share, features), BF),
@@ -652,16 +667,16 @@
         name="feed_forward",
         limit=FEED_LIMIT,
     )
-    return {"other": outs[:2], "act": outs[2], "slope": outs[3], "own": outs[4]}
+    return {"other": outs[:CUT], "act": outs[CUT], "slope": outs[CUT + 1], "own": outs[CUT + 2]}
 
 
 def feed_backward(order, slots, slope, weights):
     w_grow, w_shrink = weights
-    share, features = slots[0].shape
+    share, features = slots_shape(slots)
     hidden = w_shrink.shape[0]
 
     def body(*refs):
-        ds, refs = refs[:HALVES], refs[HALVES:]
+        ds, refs = refs[: len(slots)], refs[len(slots) :]
         wg, refs = w_grow.take(refs)
         ws, refs = w_shrink.take(refs)
         tilt, *others, grad, sums, part_own = refs
@@ -679,7 +694,7 @@
         body,
         [*slots, *w_grow.arrays, *w_shrink.arrays, slope],
         [
-            *[shape_of((share // 2, features), BF)] * 2,
+            *[shape_of((share // CUT, features), BF)] * CUT,
             shape_of((2 * share, hidden), BF),
             shape_of((1, hidden), F32),
             shape_of((share, features), BF),
@@ -687,7 +702,7 @@
         name="feed_backward",
         limit=FEED_LIMIT,
     )
-    return {"other": outs[:2], "grad": outs[2], "sums": outs[3], "own": outs[4]}
+    return {"other": outs[:CUT], "grad": outs[CUT], "sums": outs[CUT + 1], "own": outs[CUT + 2]}
 
 
 def weight_grad(order, pairs, part, parts, extra=None):
@@ -732,7 +747,7 @@
 class Pipeline:
     def __init__(self, order):
         self.order = order
-        self.line = lax.axis_size("dp") == 4
+        self.line = lax.axis_size(DP) == 4
         self.waiting, self.pieces, self.at = [], [], 0
 
     def offer(self, others, own, finish):
@@ -742,7 +757,7 @@
         return self.pieces[at] if 0 <= at < len(self.pieces) else None
 
     def step(self, last=False):
-        size = lax.axis_size("fsdp")
+        size = lax.axis_size(FSDP)
         now = self.at
         self.at += 1
         oldest, older, old, new = (self.piece(now - 1 - back) for back in (3, 2, 1, 0))
@@ -762,17 +777,17 @@
             for (name, piece, _), value in zip(sums, found):
                 piece[name] = value
         if not self.line and new is not None:
-            total = lax.psum(new["sum"], "dp")
+            total = lax.psum(new["sum"], DP)
             new["finish"](total, total)
         elif self.line:
             if old is not None:
-                old["met"] = lax.ppermute(old["inner"], "dp", [(1, 2), (2, 1)])
+                old["met"] = lax.ppermute(old["inner"], DP, [(1, 2), (2, 1)])
             if new is not None and older is not None:
-                new["swapped"] = older["back"] = lax.ppermute(found[-1], "dp", [(0, 1), (1, 0), (2, 3), (3, 2)])
+                new["swapped"] = older["back"] = lax.ppermute(found[-1], DP, [(0, 1), (1, 0), (2, 3), (3, 2)])
             elif new is not None:
-                new["swapped"] = lax.ppermute(new["sum"], "dp", [(0, 1), (3, 2)])
+                new["swapped"] = lax.ppermute(new["sum"], DP, [(0, 1), (3, 2)])
             elif older is not None:
-                older["back"] = lax.ppermute(older["total"], "dp", [(1, 0), (2, 3)])
+                older["back"] = lax.ppermute(older["total"], DP, [(1, 0), (2, 3)])
         if self.waiting:
             piece = self.waiting.pop(0)
             piece["came"] = [to_fsdp(piece["others"][k], k + 1) for k in range(size - 1)]
@@ -788,8 +803,8 @@
 
 
 def at_end():
-    here = lax.axis_index("dp")
-    return (here == 0) | (here == lax.axis_size("dp") - 1)
+    here = lax.axis_index(DP)
+    return (here == 0) | (here == lax.axis_size(DP) - 1)
 
 
 def combine(order, groups, names):
@@ -908,7 +923,7 @@
 
 
 def little_gradients(order, norms, grow, heads, span):
-    size = lax.axis_size("fsdp")
+    size = lax.axis_size(FSDP)
     features = norms[0].shape[1]
     width = features // size
     columns = 3 * span
@@ -947,18 +962,18 @@
 STEPS = (0, 1, 1, 1, 1, 1, 1, 1)
 MORE_STEPS = (0, 0, 0, 0, 0, 0, 0, 0)
 GRAD_LIMIT = 12
-ADD_FIRST = (0,) * 16
+ADD_FIRST = (1,) * 16
 FEED_LIMIT = 12
 
 
-def gather_halves(share):
-    return [share, to_core(share)]
+def gather_halves(pieces):
+    return [*pieces, *[to_core(piece) for piece in pieces]]
 
 
 def per_device(
     activations, cotangent, lengths, w_qkv, w_out, w_up, w_down, b_qv, b_up, norm_gains, layer_biases
 ):
-    size = lax.axis_size("fsdp")
+    size = lax.axis_size(FSDP)
     order = Order()
     kinds = range(len(STREAMS))
 
@@ -995,22 +1010,23 @@
     fetch(order, weights[0][:2])
 
     slots = deal_rows(order, activations)
+    order.pin([*weights[0][0].early, *weights[0][1].early])
     fetch(order, weights[1])
     residual = [(slots[s][0], None, None) for s in kinds]
     cotangent = copy_rows(order, cotangent)
     across = to_chip(cotangent)
     cotangents = [cotangent, to_core(cotangent), across, to_core(across)]
 
-    order.pin([*pieces[1:], *weights[0][0].early, *weights[0][0].late, *weights[0][1].early, *weights[0][1].late])
+    order.pin([*weights[0][0].early, *weights[0][0].late, *weights[0][1].early, *weights[0][1].late])
     fetch(order, weights[0][2:3])
 
     def ahead(at):
         zero, one = weights
         waits = {
             1: lambda: zero[2].early,
-            2: lambda: [*zero[3].early, *zero[2].late],
-            3: lambda: [*one[0].early, *one[1].early],
-            4: lambda: [*one[0].late, *one[1].late, *one[2].early],
+            2: lambda: [*zero[3].early, *zero[2].late, *one[0].early, *one[1].early],
+            3: lambda: [*one[0].late, *one[1].late],
+            4: lambda: one[2].early,
             5: lambda: [*one[2].late, *one[3].early],
             6: lambda: one[3].late,
         }
@@ -1215,7 +1231,7 @@
         if at + 1 < len(items):
             items[at + 1][0]()
         if at == forward_items + 1:
-            out_rows = gather_halves(jnp.concatenate([kept[-1]["two"][t][0] for t in kinds], 0))
+            out_rows = gather_halves([jnp.concatenate([v for t in kinds for v in kept[-1]["two"][t][0]], 0)])
         if at + 2 == len(items):
             sum_norms()
         if not early:
@@ -1229,7 +1245,7 @@
     layer_out = natural_share(order, out_rows, BF)
     pipeline.step(True)
     ends = [last_sum(order, terms[s]) for s in kinds]
-    end_rows = gather_halves(jnp.concatenate(ends, 0))
+    end_rows = gather_halves([jnp.concatenate(ends, 0)])
     pipeline.step(True)
     input_grad = natural_share(order, end_rows, F32)
     pipeline.drain()
@@ -1238,7 +1254,7 @@
     grad_gains = little[: 2 * LAYERS, :width].reshape(LAYERS, 2, width)
     grad_biases = little[2 * LAYERS : 6 * LAYERS, :width].reshape(LAYERS, 4, width)
     rest = little[6 * LAYERS : 8 * LAYERS].reshape(LAYERS, -1)
-    here = lax.axis_index("fsdp")
+    here = lax.axis_index(FSDP)
     grow = rest[:, :hidden].reshape(bias_grow.shape)
     heads = rest[:, hidden : hidden + 2 * span].reshape(bias_heads.shape)
     part = grow.shape[-1] // size
@@ -1261,29 +1277,29 @@
 
 def solution(mesh):
     in_specs = (
-        P(("dp", "fsdp"), None),
-        P(("dp", "fsdp", "tensor"), None),
-        P(("dp", "fsdp")),
-        P(None, None, "fsdp", "tensor"),
-        P(None, "tensor", "fsdp"),
-        P(None, "fsdp", "tensor"),
-        P(None, "tensor", "fsdp"),
-        P(None, None, "tensor", "fsdp"),
-        P(None, "tensor", "fsdp"),
-        P(None, None, "fsdp"),
-        P(None, None, "fsdp"),
+        P((DP, FSDP), None),
+        P((DP, FSDP, TENSOR), None),
+        P((DP, FSDP)),
+        P(None, None, FSDP, TENSOR),
+        P(None, TENSOR, FSDP),
+        P(None, FSDP, TENSOR),
+        P(None, TENSOR, FSDP),
+        P(None, None, TENSOR, FSDP),
+        P(None, TENSOR, FSDP),
+        P(None, None, FSDP),
+        P(None, None, FSDP),
     )
     out_specs = (
-        P(("dp", "fsdp", "tensor"), None),
-        P(("dp", "fsdp", "tensor"), None),
-        P(None, None, "fsdp", "tensor"),
-        P(None, "tensor", "fsdp"),
-        P(None, "fsdp", "tensor"),
-        P(None, "tensor", "fsdp"),
-        P(None, None, "tensor", "fsdp"),
-        P(None, "tensor", "fsdp"),
-        P(None, None, "fsdp"),
-        P(None, None, "fsdp"),
+        P((DP, FSDP, TENSOR), None),
+        P((DP, FSDP, TENSOR), None),
+        P(None, None, FSDP, TENSOR),
+        P(None, TENSOR, FSDP),
+        P(None, FSDP, TENSOR),
+        P(None, TENSOR, FSDP),
+        P(None, None, TENSOR, FSDP),
+        P(None, TENSOR, FSDP),
+        P(None, None, FSDP),
+        P(None, None, FSDP),
     )
     return jax.shard_map(
         per_device, mesh=mesh, in_specs=in_specs, out_specs=out_specs, check_vma=False

time: 490 us -> 464 us (0.947)
  waiting for transfers between devices: 168 us -> 146 us
    ppermute x111 -> x125, waiting for transfers between devices: 168 us -> 146 us  [the longest x2 32.3 us: step(): older['back'] = lax.ppermute(older['total'], DP, [(1, 0), (2, 3)])]
    ppermute x111 -> x125, starting transfers between devices: 94.6 us -> 98.5 us  [the longest x17 19.2 us: to_chip(): return lax.ppermute(value, TENSOR, CHIP_SWAP)]
    unnamed x302 -> x310, local copies, waits for them, and re-layouts: 46.5 us -> 43.6 us
  transfers between devices with their start and end apart: 111 -> 125, of which waited for: 50 -> 61; matrix products, arithmetic and copies ran while one was open for 1% -> 0% of each run, Pallas kernels for 31% -> 33%
where the time goes in v4:
time: 464 us; the launch traced here: 457 us
  Pallas kernels  163 us (35%)
  waiting for transfers between devices  146 us (31%)
  starting transfers between devices  98.5 us (21%)
  local copies, waits for them, and re-layouts  47.1 us (10%)
    pallas_call x95, Pallas kernels, call(): pl.pallas_call(kernel, grid=grid, in_specs=in_specs, out_specs=[*out_spec...  163 us
    unnamed x310, local copies, waits for them, and re-layouts  43.6 us
    ppermute x2, waiting for transfers between devices, step(): older['back'] = lax.ppermute(older['total'], DP, [(1, 0), (2, 3)])  32.3 us
    ppermute x6, waiting for transfers between devices, step(): lax.ppermute(found[-1], DP, [(0, 1), (1, 0), (2, 3), (3, 2)])  29 us
    ppermute x65, waiting for transfers between devices, to_core(): return lax.ppermute(value, TENSOR, CORE_SWAP)  24.5 us
    ppermute x17, waiting for transfers between devices, to_chip(): return lax.ppermute(value, TENSOR, CHIP_SWAP)  22.8 us
    ppermute x9, waiting for transfers between devices, from_fsdp(): lax.ppermute(value, FSDP, [((i + step) % size, i) for i in range(size)])  22.5 us
    ppermute x17, starting transfers between devices, to_chip(): return lax.ppermute(value, TENSOR, CHIP_SWAP)  19.2 us
  transfers between devices with their start and end apart: 125, of which 61 were waited for; matrix products, arithmetic and copies ran while one was open for 0% of the time, Pallas kernels for 33%

profile of v4, /device:TPU:0, one launch (start us, length us, event | category | flops | bytes accessed | tf_op | source)
XLA Modules:
  0.0 457.3 jit_solution(7269997382212981700)
XLA Ops:
  4.0 3.0 collective-permute-start
  7.0 9.1 %collective-permute-done.refs_4_.refs_1_.refs_3_.refs_5_ = bf16[3,256,256]{2,1,0:T(8,128)(2,1)S(1)} collective-permute-done((bf16[3,256,256]{2,1,0:T(8,128)(2,1)S(1)}, bf16[3,256,256]{2,1,0:T(8,128)(2,1)S(1)}, u32[]{:S(2)}, u32[]{:S(2)}) %collective-permute-start) | collective-permute-done | bytes 393248 | tf_op jit(solution)/shard_map/ppermute | solution.py:36
  16.1 1.8 collective-permute-start.1
  17.9 1.5 collective-permute-start.2
  19.4 1.7 copy-done.84
  31.4 1.5 collective-permute-start.14
  33.6 1.6 collective-permute-start.4
  35.2 2.2 collective-permute-done.4
  37.9 1.8 copy-done.30
  40.6 1.6 collective-permute-start.8
  45.6 5.5 %attention_forward.4 = (bf16[128,1024]{1,0:T(8,128)(2,1)S(1)}, bf16[128,1024]{1,0:T(8,128)(2,1)S(1)}, bf16[256,1024]{1,0:T(8,128)(2,1)S(1)}, bf16[512,768]{1,0:T...) custom-call(bf16[256,1024]{1,0:T(8,128)(2,1)S(1)} %copy-done.32, ...), custom_call_target="tpu_custom_call" | custom-call | tf_op jit(solution)/shard_map/attention_forward/pallas_call | solution.py:131
  57.4 1.9 deal_share.1
  60.2 7.2 %attention_forward.5 = (bf16[160,1024]{1,0:T(8,128)(2,1)S(1)}, bf16[160,1024]{1,0:T(8,128)(2,1)S(1)}, bf16[320,1024]{1,0:T(8,128)(2,1)S(1)}, bf16[640,768]{1,0:T...) custom-call(bf16[320,1024]{1,0:T(8,128)(2,1)S(1)} %copy-done.19, ...), custom_call_target="tpu_custom_call" | custom-call | tf_op jit(solution)/shard_map/attention_forward/pallas_call | solution.py:131
  79.7 9.5 %collective-permute-done.12.refs_9_.refs_8_ = bf16[256,256]{1,0:T(8,128)(2,1)S(1)} collective-permute-done((bf16[256,256]{1,0:T(8,128)(2,1)}, bf16[256,256]{1,0:T(8,128)(2,1)S(1)}, u32[]{:S(2)}, u32[]{:S(2)}) %collective-permute-start.12) | collective-permute-done | bytes 131104 | tf_op jit(solution)/shard_map/ppermute | solution.py:36
  89.2 1.5 collective-permute-start.25
  94.8 1.7 norm_forward.8
  99.2 4.2 feed_forward.4
  105.5 6.4 %collective-permute-done.27.refs_7_.refs_9_ = bf16[256,256]{1,0:T(8,128)(2,1)S(1)} collective-permute-done((bf16[256,256]{1,0:T(8,128)(2,1)S(1)}, bf16[256,256]{1,0:T(8,128)(2,1)S(1)}, u32[]{:S(2)}, u32[]{:S(2)}) %collective-permute-start.27) | collective-permute-done | bytes 131104 | tf_op jit(solution)/shard_map/ppermute | solution.py:191
  112.0 2.1 norm_forward.9
  117.9 5.1 %feed_forward.5 = (bf16[160,1024]{1,0:T(8,128)(2,1)S(1)}, bf16[160,1024]{1,0:T(8,128)(2,1)S(1)}, bf16[640,1024]{1,0:T(8,128)(2,1)S(1)}, bf16[640,1024]{1,0:T(8,1...) custom-call(bf16[160,1024]{1,0:T(8,128)(2,1)S(1)} %get-tuple-element.413.refs_0_.refs_14_.refs_4_, ...), custom_call_target="tpu_custom_call" | custom-call | tf_op jit(solution)/shard_map/feed_forward/pallas_call | solution.py:131
  127.9 1.5 collective-permute-start.39
  130.9 1.5 norm_forward.10
  142.2 6.4 %attention_forward.6 = (bf16[128,1024]{1,0:T(8,128)(2,1)S(1)}, bf16[128,1024]{1,0:T(8,128)(2,1)S(1)}, bf16[256,1024]{1,0:T(8,128)(2,1)S(1)}, bf16[512,768]{1,0:T...) custom-call(bf16[128,1024]{1,0:T(8,128)(2,1)} %get-tuple-element.421.refs_0_,, ...), custom_call_target="tpu_custom_call" | custom-call | tf_op jit(solution)/shard_map/attention_forward/pallas_call | solution.py:131
  150.8 2.1 norm_forward.11
  155.3 7.6 %attention_forward.7 = (bf16[160,1024]{1,0:T(8,128)(2,1)S(1)}, bf16[160,1024]{1,0:T(8,128)(2,1)S(1)}, bf16[320,1024]{1,0:T(8,128)(2,1)S(1)}, bf16[640,768]{1,0:T...) custom-call(bf16[160,1024]{1,0:T(8,128)(2,1)S(1)} %get-tuple-element, ...), custom_call_target="tpu_custom_call" | custom-call | tf_op jit(solution)/shard_map/attention_forward/pallas_call | solution.py:131
  165.3 1.6 collective-permute-start.50
  171.6 4.0 feed_forward.6
  177.7 4.7 %collective-permute-done.50.refs_3_ = bf16[320,1024]{1,0:T(8,128)(2,1)S(1)} collective-permute-done((bf16[320,1024]{1,0:T(8,128)(2,1)S(1)}, bf16[320,1024]{1,0:T(8,128)(2,1)S(1)}, u32[]{:S(2)}, u32[]{:S(2)}) %collective-permute-start.50) | collective-permute-done | bytes 655392 | tf_op jit(solution)/shard_map/ppermute | solution.py:31
  185.5 4.7 %feed_forward.7 = (bf16[160,1024]{1,0:T(8,128)(2,1)S(1)}, bf16[160,1024]{1,0:T(8,128)(2,1)S(1)}, bf16[640,1024]{1,0:T(8,128)(2,1)S(1)}, bf16[640,1024]{1,0:T(8,1...) custom-call(bf16[160,1024]{1,0:T(8,128)(2,1)S(1)} %get-tuple-element.458.refs_0_.refs_14_.refs_4_, ...), custom_call_target="tpu_custom_call" | custom-call | tf_op jit(solution)/shard_map/feed_forward/pallas_call | solution.py:131
  193.8 4.9 %collective-permute-done.49.refs_3_ = bf16[256,1024]{1,0:T(8,128)(2,1)S(1)} collective-permute-done((bf16[256,1024]{1,0:T(8,128)(2,1)S(1)}, bf16[256,1024]{1,0:T(8,128)(2,1)S(1)}, u32[]{:S(2)}, u32[]{:S(2)}) %collective-permute-start.49) | collective-permute-done | bytes 524320 | tf_op jit(solution)/shard_map/ppermute | solution.py:31
  198.7 1.7 norm_forward.14
  203.0 3.8 feed_backward.4
  209.0 2.9 collective-permute-done.55.refs_3_
  211.9 1.9 norm_forward.15
  217.2 4.5 feed_backward.5
  227.3 3.2 collective-permute-done.61.refs_3_
  233.3 6.6 %attention_backward.4 = (bf16[128,1024]{1,0:T(8,128)(2,1)S(1)}, bf16[128,1024]{1,0:T(8,128)(2,1)S(1)}, bf16[256,1024]{1,0:T(8,128)(2,1)S(1)}, bf16[512,768]{1,0:...) custom-call(bf16[128,1024]{1,0:T(8,128)(2,1)S(1)} %get-tuple-element.506.refs_0_.refs_10_, ...), custom_call_target="tpu_custom_call" | custom-call | tf_op jit(solution)/shard_map/attention_backward/pallas_call | solution.py:131
  244.4 2.8 collective-permute-start.78
  250.6 8.1 %attention_backward.5 = (bf16[160,1024]{1,0:T(8,128)(2,1)S(1)}, bf16[160,1024]{1,0:T(8,128)(2,1)S(1)}, bf16[320,1024]{1,0:T(8,128)(2,1)S(1)}, bf16[640,768]{1,0:...) custom-call(bf16[160,1024]{1,0:T(8,128)(2,1)S(1)} %get-tuple-element.531.refs_0_.refs_14_, ...), custom_call_target="tpu_custom_call" | custom-call | tf_op jit(solution)/shard_map/attention_backward/pallas_call | solution.py:131
  264.3 4.6 collective-permute-start.85
  273.8 3.9 feed_backward.6
  277.7 2.6 collective-permute-done.84.refs_1_
  280.3 2.3 weight_grad.22
  282.6 2.2 collective-permute-done.85.refs_3_
  285.8 2.3 weight_grad.23
  288.9 2.6 collective-permute-start.92
  295.8 4.5 feed_backward.7
  305.2 1.7 collective-permute-done.92.refs_3_.refs_1_
  308.5 3.3 collective-permute-start.100
  318.6 5.6 %attention_backward.6 = (bf16[128,1024]{1,0:T(8,128)(2,1)S(1)}, bf16[128,1024]{1,0:T(8,128)(2,1)S(1)}, bf16[256,1024]{1,0:T(8,128)(2,1)S(1)}, bf16[512,768]{1,0:...) custom-call(bf16[128,1024]{1,0:T(8,128)(2,1)S(1)} %get-tuple-element.601.refs_0_.refs_10_, ...), custom_call_target="tpu_custom_call" | custom-call | tf_op jit(solution)/shard_map/attention_backward/pallas_call | solution.py:131
  328.7 3.5 collective-permute-start.107
  339.0 7.1 %attention_backward.7 = (bf16[160,1024]{1,0:T(8,128)(2,1)S(1)}, bf16[160,1024]{1,0:T(8,128)(2,1)S(1)}, bf16[320,1024]{1,0:T(8,128)(2,1)S(1)}, bf16[640,768]{1,0:...) custom-call(bf16[160,1024]{1,0:T(8,128)(2,1)S(1)} %get-tuple-element.626.refs_0_.refs_14_, ...), custom_call_target="tpu_custom_call" | custom-call | tf_op jit(solution)/shard_map/attention_backward/pallas_call | solution.py:131
  351.0 3.5 collective-permute-start.109
  356.0 2.8 collective-permute-done.113.refs_2_
  365.3 6.2 %collective-permute-done.109.refs_1_.refs_3_ = bf16[512,768]{1,0:T(8,128)(2,1)S(1)} collective-permute-done((bf16[512,768]{1,0:T(8,128)(2,1)S(1)}, bf16[512,768]{1,0:T(8,128)(2,1)S(1)}, u32[]{:S(2)}, u32[]{:S(2)}) %collective-permute-start.109) | collective-permute-done | bytes 786464 | tf_op jit(solution)/shard_map/ppermute | solution.py:786
  373.6 2.4 collective-permute-start.116
  379.8 12.3 %collective-permute-done.116.refs_1_.refs_3_ = bf16[512,768]{1,0:T(8,128)(2,1)S(1)} collective-permute-done((bf16[512,768]{1,0:T(8,128)(2,1)S(1)}, bf16[512,768]{1,0:T(8,128)(2,1)S(1)}, u32[]{:S(2)}, u32[]{:S(2)}) %collective-permute-start.116) | collective-permute-done | bytes 786464 | tf_op jit(solution)/shard_map/ppermute | solution.py:786
  392.1 1.5 finish_down.6
  394.3 2.2 collective-permute-start.120
  397.2 5.6 %collective-permute-done.114.refs_3_ = bf16[256,1024]{1,0:T(8,128)(2,1)S(1)} collective-permute-done((bf16[256,1024]{1,0:T(8,128)(2,1)S(1)}, bf16[256,1024]{1,0:T(8,128)(2,1)S(1)}, u32[]{:S(2)}, u32[]{:S(2)}) %collective-permute-start.114) | collective-permute-done | bytes 524320 | tf_op jit(solution)/shard_map/ppermute | solution.py:31
  403.5 8.7 %collective-permute-done.120.refs_1_ = bf16[528,768]{1,0:T(8,128)(2,1)S(1)} collective-permute-done((bf16[528,768]{1,0:T(8,128)(2,1)S(1)}, bf16[528,768]{1,0:T(8,128)(2,1)S(1)}, u32[]{:S(2)}, u32[]{:S(2)}) %collective-permute-start.120) | collective-permute-done | bytes 811040 | tf_op jit(solution)/shard_map/ppermute | solution.py:786
  417.3 16.0 %collective-permute-done.123.refs_1_ = bf16[512,768]{1,0:T(8,128)(2,1)S(1)} collective-permute-done((bf16[512,768]{1,0:T(8,128)(2,1)S(1)}, bf16[512,768]{1,0:T(8,128)(2,1)S(1)}, u32[]{:S(2)}, u32[]{:S(2)}) %collective-permute-start.123) | collective-permute-done | bytes 786464 | tf_op jit(solution)/shard_map/ppermute | solution.py:790
  436.2 16.2 %collective-permute-done.124.refs_1_ = bf16[528,768]{1,0:T(8,128)(2,1)S(1)} collective-permute-done((bf16[528,768]{1,0:T(8,128)(2,1)S(1)}, bf16[528,768]{1,0:T(8,128)(2,1)S(1)}, u32[]{:S(2)}, u32[]{:S(2)}) %collective-permute-start.124) | collective-permute-done | bytes 811040 | tf_op jit(solution)/shard_map/ppermute | solution.py:790
  452.4 1.9 finish_proj.3
  (625 shorter events, 183.4 us)
Async XLA Ops:
  4.0 12.1 %collective-permute-start = (bf16[3,256,256]{2,1,0:T(8,128)(2,1)S(1)}, bf16[3,256,256]{2,1,0:T(8,128)(2,1)S(1)}, u32[]{:S(2)}, u32[]{:S(2)}) collective-permute-start(bf16[3,256,256]{2,1,0:T(8,128)(2,1)S(1)} %get-tuple-element.372), channel_id=1, source_target_pairs={{4,0},{0,4},{5,1},{1,5},{6,2},{2,6},{7,3},{3,7},{12,8},{8,12},{13,... | collective-permute-start | bytes 1179656 | tf_op jit(solution)/shard_map/ppermute | solution.py:36
  16.1 21.8 %collective-permute-start.1 = (bf16[3,256,256]{2,1,0:T(8,128)(2,1)S(1)}, bf16[3,256,256]{2,1,0:T(8,128)(2,1)S(1)}, u32[]{:S(2)}, u32[]{:S(2)}) collective-permute-start(bf16[3,256,256]{2,1,0:T(8,128)(2,1)S(1)} %collective-permute-done.refs_4_.refs_1_.refs_3_.refs_5_), channel_id=1, source_target_pairs={{0,8},{8,0},{16,24},{24,16},{1,9},{9,1},{17,25},{25,17},{2,10},{10... | collective-permute-start | bytes 1179656 | tf_op jit(solution)/shard_map/ppermute | solution.py:191
  31.4 22.2 %collective-permute-start.14 = (bf16[288,1024]{1,0:T(8,128)(2,1)}, bf16[288,1024]{1,0:T(8,128)(2,1)}, u32[]{:S(2)}, u32[]{:S(2)}) collective-permute-start(bf16[288,1024]{1,0:T(8,128)(2,1)} %get-tuple-element.391.refs_0_), channel_id=1, source_target_pairs={{0,2},{2,0},{1,3},{3,1},{4,6},{6,4},{5,7},{7,5},{8,10},{10,8},{9,1... | collective-permute-start | bytes 1769480 | tf_op jit(solution)/shard_map/ppermute | solution.py:31
  40.6 15.4 %collective-permute-start.8 = (bf16[256,1024]{1,0:T(8,128)(2,1)}, bf16[256,1024]{1,0:T(8,128)(2,1)S(1)}, u32[]{:S(2)}, u32[]{:S(2)}) collective-permute-start(bf16[256,1024]{1,0:T(8,128)(2,1)} %get-tuple-element.384), channel_id=1, source_target_pairs={{4,0},{0,4},{5,1},{1,5},{6,2},{2,6},{7,3},{3,7},{12,8},{8,12},{13,... | collective-permute-start | bytes 1572872 | tf_op jit(solution)/shard_map/ppermute | solution.py:36
  56.8 17.8 %collective-permute-start.9 = (bf16[1024,256]{1,0:T(8,128)(2,1)S(1)}, bf16[1024,256]{1,0:T(8,128)(2,1)}, u32[]{:S(2)}, u32[]{:S(2)}) collective-permute-start(bf16[1024,256]{1,0:T(8,128)(2,1)S(1)} %get-tuple-element.386), channel_id=1, source_target_pairs={{4,0},{0,4},{5,1},{1,5},{6,2},{2,6},{7,3},{3,7},{12,8},{8,12},{13,... | collective-permute-start | bytes 1572872 | tf_op jit(solution)/shard_map/ppermute | solution.py:36
  72.9 17.9 %collective-permute-start.7 = (bf16[256,1024]{1,0:T(8,128)(2,1)}, bf16[256,1024]{1,0:T(8,128)(2,1)}, u32[]{:S(2)}, u32[]{:S(2)}) collective-permute-start(bf16[256,1024]{1,0:T(8,128)(2,1)} %get-tuple-element.383), channel_id=1, source_target_pairs={{0,2},{2,0},{1,3},{3,1},{4,6},{6,4},{5,7},{7,5},{8,10},{10,8},{9,1... | collective-permute-start | bytes 1572872 | tf_op jit(solution)/shard_map/ppermute | solution.py:31
  73.4 17.4 %collective-permute-start.10 = (bf16[256,1024]{1,0:T(8,128)(2,1)S(1)}, bf16[256,1024]{1,0:T(8,128)(2,1)}, u32[]{:S(2)}, u32[]{:S(2)}) collective-permute-start(bf16[256,1024]{1,0:T(8,128)(2,1)S(1)} %collective-permute-done.8.refs_1_.refs_5_), channel_id=1, source_target_pairs={{0,8},{8,0},{16,24},{24,16},{1,9},{9,1},{17,25},{25,17},{2,10},{10... | collective-permute-start | bytes 1572872 | tf_op jit(solution)/shard_map/ppermute | solution.py:191
  74.6 16.2 %collective-permute-start.11 = (bf16[3,256,256]{2,1,0:T(8,128)(2,1)}, bf16[3,256,256]{2,1,0:T(8,128)(2,1)}, u32[]{:S(2)}, u32[]{:S(2)}) collective-permute-start(bf16[3,256,256]{2,1,0:T(8,128)(2,1)} %get-tuple-element.387), channel_id=1, source_target_pairs={{4,0},{0,4},{5,1},{1,5},{6,2},{2,6},{7,3},{3,7},{12,8},{8,12},{13,... | collective-permute-start | bytes 1179656 | tf_op jit(solution)/shard_map/ppermute | solution.py:36
  75.6 13.6 %collective-permute-start.12 = (bf16[256,256]{1,0:T(8,128)(2,1)}, bf16[256,256]{1,0:T(8,128)(2,1)S(1)}, u32[]{:S(2)}, u32[]{:S(2)}) collective-permute-start(bf16[256,256]{1,0:T(8,128)(2,1)} %get-tuple-element.388), channel_id=1, source_target_pairs={{4,0},{0,4},{5,1},{1,5},{6,2},{2,6},{7,3},{3,7},{12,8},{8,12},{13,... | collective-permute-start | bytes 393224 | tf_op jit(solution)/shard_map/ppermute | solution.py:36
  76.7 22.5 %collective-permute-start.20 = (bf16[1024,256]{1,0:T(8,128)(2,1)}, bf16[1024,256]{1,0:T(8,128)(2,1)}, u32[]{:S(2)}, u32[]{:S(2)}) collective-permute-start(bf16[1024,256]{1,0:T(8,128)(2,1)} %collective-permute-done.9.refs_6_.refs_8_), channel_id=1, source_target_pairs={{0,8},{8,0},{16,24},{24,16},{1,9},{9,1},{17,25},{25,17},{2,10},{10... | collective-permute-start | bytes 1572872 | tf_op jit(solution)/shard_map/ppermute | solution.py:191
  89.2 22.7 %collective-permute-start.25 = (bf16[320,1024]{1,0:T(8,128)(2,1)}, bf16[320,1024]{1,0:T(8,128)(2,1)}, u32[]{:S(2)}, u32[]{:S(2)}) collective-permute-start(bf16[320,1024]{1,0:T(8,128)(2,1)} %get-tuple-element.411), channel_id=1, source_target_pairs={{0,2},{2,0},{1,3},{3,1},{4,6},{6,4},{5,7},{7,5},{8,10},{10,8},{9,1... | collective-permute-start | bytes 1966088 | tf_op jit(solution)/shard_map/ppermute | solution.py:31
  97.8 14.1 %collective-permute-start.26 = (bf16[3,256,256]{2,1,0:T(8,128)(2,1)}, bf16[3,256,256]{2,1,0:T(8,128)(2,1)S(1)}, u32[]{:S(2)}, u32[]{:S(2)}) collective-permute-start(bf16[3,256,256]{2,1,0:T(8,128)(2,1)} %collective-permute-done.11.refs_8_.refs_5_), channel_id=1, source_target_pairs={{0,8},{8,0},{16,24},{24,16},{1,9},{9,1},{17,25},{25,17},{2,10},{10... | collective-permute-start | bytes 1179656 | tf_op jit(solution)/shard_map/ppermute | solution.py:191
  116.3 14.0 %collective-permute-start.24 = (bf16[256,1024]{1,0:T(8,128)(2,1)S(1)}, bf16[256,1024]{1,0:T(8,128)(2,1)}, u32[]{:S(2)}, u32[]{:S(2)}) collective-permute-start(bf16[256,1024]{1,0:T(8,128)(2,1)S(1)} %copy-done.146), channel_id=1, source_target_pairs={{4,0},{0,4},{5,1},{1,5},{6,2},{2,6},{7,3},{3,7},{12,8},{8,12},{13,... | collective-permute-start | bytes 1572872 | tf_op jit(solution)/shard_map/ppermute | solution.py:36
  117.3 13.6 %collective-permute-start.23 = (bf16[256,1024]{1,0:T(8,128)(2,1)S(1)}, bf16[256,1024]{1,0:T(8,128)(2,1)S(1)}, u32[]{:S(2)}, u32[]{:S(2)}) collective-permute-start(bf16[256,1024]{1,0:T(8,128)(2,1)S(1)} %get-tuple-element.408), channel_id=1, source_target_pairs={{0,2},{2,0},{1,3},{3,1},{4,6},{6,4},{5,7},{7,5},{8,10},{10,8},{9,1... | collective-permute-start | bytes 1572872 | tf_op jit(solution)/shard_map/ppermute | solution.py:31
  127.9 22.8 %collective-permute-start.39 = (bf16[320,1024]{1,0:T(8,128)(2,1)}, bf16[320,1024]{1,0:T(8,128)(2,1)}, u32[]{:S(2)}, u32[]{:S(2)}) collective-permute-start(bf16[320,1024]{1,0:T(8,128)(2,1)} %get-tuple-element.433), channel_id=1, source_target_pairs={{0,2},{2,0},{1,3},{3,1},{4,6},{6,4},{5,7},{7,5},{8,10},{10,8},{9,1... | collective-permute-start | bytes 1966088 | tf_op jit(solution)/shard_map/ppermute | solution.py:31
  135.3 15.4 %collective-permute-start.37 = (bf16[1024,256]{1,0:T(8,128)(2,1)}, bf16[1024,256]{1,0:T(8,128)(2,1)}, u32[]{:S(2)}, u32[]{:S(2)}) collective-permute-start(bf16[1024,256]{1,0:T(8,128)(2,1)} %get-tuple-element.432), channel_id=1, source_target_pairs={{4,0},{0,4},{5,1},{1,5},{6,2},{2,6},{7,3},{3,7},{12,8},{8,12},{13,... | collective-permute-start | bytes 1572872 | tf_op jit(solution)/shard_map/ppermute | solution.py:36
  136.4 14.4 %collective-permute-start.40 = (bf16[256,1024]{1,0:T(8,128)(2,1)}, bf16[256,1024]{1,0:T(8,128)(2,1)}, u32[]{:S(2)}, u32[]{:S(2)}) collective-permute-start(bf16[256,1024]{1,0:T(8,128)(2,1)} %collective-permute-done.24.refs_6_.refs_5_), channel_id=1, source_target_pairs={{0,8},{8,0},{16,24},{24,16},{1,9},{9,1},{17,25},{25,17},{2,10},{10... | collective-permute-start | bytes 1572872 | tf_op jit(solution)/shard_map/ppermute | solution.py:191
  153.5 14.2 %collective-permute-start.38 = (bf16[1024,256]{1,0:T(8,128)(2,1)}, bf16[1024,256]{1,0:T(8,128)(2,1)S(1)}, u32[]{:S(2)}, u32[]{:S(2)}) collective-permute-start(bf16[1024,256]{1,0:T(8,128)(2,1)} %collective-permute-done.37.refs_7_.refs_8_), channel_id=1, source_target_pairs={{0,8},{8,0},{16,24},{24,16},{1,9},{9,1},{17,25},{25,17},{2,10},{10... | collective-permute-start | bytes 1572872 | tf_op jit(solution)/shard_map/ppermute | solution.py:191
  154.7 14.0 %collective-permute-start.36 = (bf16[256,1024]{1,0:T(8,128)(2,1)S(1)}, bf16[256,1024]{1,0:T(8,128)(2,1)S(1)}, u32[]{:S(2)}, u32[]{:S(2)}) collective-permute-start(bf16[256,1024]{1,0:T(8,128)(2,1)S(1)} %get-tuple-element.430), channel_id=1, source_target_pairs={{0,2},{2,0},{1,3},{3,1},{4,6},{6,4},{5,7},{7,5},{8,10},{10,8},{9,1... | collective-permute-start | bytes 1572872 | tf_op jit(solution)/shard_map/ppermute | solution.py:31
  165.3 17.2 %collective-permute-start.50 = (bf16[320,1024]{1,0:T(8,128)(2,1)S(1)}, bf16[320,1024]{1,0:T(8,128)(2,1)S(1)}, u32[]{:S(2)}, u32[]{:S(2)}) collective-permute-start(bf16[320,1024]{1,0:T(8,128)(2,1)S(1)} %get-tuple-element.455), channel_id=1, source_target_pairs={{0,2},{2,0},{1,3},{3,1},{4,6},{6,4},{5,7},{7,5},{8,10},{10,8},{9,1... | collective-permute-start | bytes 1966088 | tf_op jit(solution)/shard_map/ppermute | solution.py:31
  183.9 14.8 %collective-permute-start.49 = (bf16[256,1024]{1,0:T(8,128)(2,1)S(1)}, bf16[256,1024]{1,0:T(8,128)(2,1)S(1)}, u32[]{:S(2)}, u32[]{:S(2)}) collective-permute-start(bf16[256,1024]{1,0:T(8,128)(2,1)S(1)} %get-tuple-element.453), channel_id=1, source_target_pairs={{0,2},{2,0},{1,3},{3,1},{4,6},{6,4},{5,7},{7,5},{8,10},{10,8},{9,1... | collective-permute-start | bytes 1572872 | tf_op jit(solution)/shard_map/ppermute | solution.py:31
  192.6 19.3 %collective-permute-start.55 = (bf16[320,1024]{1,0:T(8,128)(2,1)S(1)}, bf16[320,1024]{1,0:T(8,128)(2,1)S(1)}, u32[]{:S(2)}, u32[]{:S(2)}) collective-permute-start(bf16[320,1024]{1,0:T(8,128)(2,1)S(1)} %get-tuple-element.468), channel_id=1, source_target_pairs={{0,2},{2,0},{1,3},{3,1},{4,6},{6,4},{5,7},{7,5},{8,10},{10,8},{9,1... | collective-permute-start | bytes 1966088 | tf_op jit(solution)/shard_map/ppermute | solution.py:31
  215.6 14.8 %collective-permute-start.61 = (bf16[256,1024]{1,0:T(8,128)(2,1)S(1)}, bf16[256,1024]{1,0:T(8,128)(2,1)S(1)}, u32[]{:S(2)}, u32[]{:S(2)}) collective-permute-start(bf16[256,1024]{1,0:T(8,128)(2,1)S(1)} %get-tuple-element.485), channel_id=1, source_target_pairs={{0,2},{2,0},{1,3},{3,1},{4,6},{6,4},{5,7},{7,5},{8,10},{10,8},{9,1... | collective-permute-start | bytes 1572872 | tf_op jit(solution)/shard_map/ppermute | solution.py:31
  223.5 20.7 %collective-permute-start.70 = (bf16[512,768]{1,0:T(8,128)(2,1)S(1)}, bf16[512,768]{1,0:T(8,128)(2,1)S(1)}, u32[]{:S(2)}, u32[]{:S(2)}) collective-permute-start(bf16[512,768]{1,0:T(8,128)(2,1)S(1)} %bitcast.46), channel_id=1, source_target_pairs={{0,4},{4,0},{1,5},{5,1},{2,6},{6,2},{3,7},{7,3},{8,12},{12,8},{9,1... | collective-permute-start | bytes 2359304 | tf_op jit(solution)/shard_map/ppermute | solution.py:41
  226.0 21.3 %collective-permute-start.72 = (bf16[320,1024]{1,0:T(8,128)(2,1)S(1)}, bf16[320,1024]{1,0:T(8,128)(2,1)S(1)}, u32[]{:S(2)}, u32[]{:S(2)}) collective-permute-start(bf16[320,1024]{1,0:T(8,128)(2,1)S(1)} %get-tuple-element.526), channel_id=1, source_target_pairs={{0,2},{2,0},{1,3},{3,1},{4,6},{6,4},{5,7},{7,5},{8,10},{10,8},{9,1... | collective-permute-start | bytes 1966088 | tf_op jit(solution)/shard_map/ppermute | solution.py:31
  241.7 19.6 %collective-permute-start.77 = (bf16[512,768]{1,0:T(8,128)(2,1)S(1)}, bf16[512,768]{1,0:T(8,128)(2,1)S(1)}, u32[]{:S(2)}, u32[]{:S(2)}) collective-permute-start(bf16[512,768]{1,0:T(8,128)(2,1)S(1)} %bitcast.43), channel_id=1, source_target_pairs={{0,4},{4,0},{1,5},{5,1},{2,6},{6,2},{3,7},{7,3},{8,12},{12,8},{9,1... | collective-permute-start | bytes 2359304 | tf_op jit(solution)/shard_map/ppermute | solution.py:41
  244.4 19.6 %collective-permute-start.78 = (bf16[512,768]{1,0:T(8,128)(2,1)S(1)}, bf16[512,768]{1,0:T(8,128)(2,1)S(1)}, u32[]{:S(2)}, u32[]{:S(2)}) collective-permute-start(bf16[512,768]{1,0:T(8,128)(2,1)S(1)} %get-tuple-element.544.refs_2_), channel_id=1, source_target_pairs={{0,8},{24,16},{1,9},{25,17},{2,10},{26,18},{3,11},{27,19},{4,12},{... | collective-permute-start | bytes 2359304 | tf_op jit(solution)/shard_map/ppermute | solution.py:788
  249.0 21.0 %collective-permute-start.71 = (bf16[256,1024]{1,0:T(8,128)(2,1)S(1)}, bf16[256,1024]{1,0:T(8,128)(2,1)S(1)}, u32[]{:S(2)}, u32[]{:S(2)}) collective-permute-start(bf16[256,1024]{1,0:T(8,128)(2,1)S(1)} %get-tuple-element.522), channel_id=1, source_target_pairs={{0,2},{2,0},{1,3},{3,1},{4,6},{6,4},{5,7},{7,5},{8,10},{10,8},{9,1... | collective-permute-start | bytes 1572872 | tf_op jit(solution)/shard_map/ppermute | solution.py:31
  258.7 10.2 %collective-permute-start.75 = (bf16[160,1024]{1,0:T(8,128)(2,1)S(1)}, bf16[160,1024]{1,0:T(8,128)(2,1)S(1)}, u32[]{:S(2)}, u32[]{:S(2)}) collective-permute-start(bf16[160,1024]{1,0:T(8,128)(2,1)S(1)} %get-tuple-element.540), channel_id=1, source_target_pairs={{0,1},{1,0},{2,3},{3,2},{4,5},{5,4},{6,7},{7,6},{8,9},{9,8},{10,11... | collective-permute-start | bytes 983048 | tf_op jit(solution)/shard_map/ppermute | solution.py:27
  258.9 10.9 %collective-permute-start.76 = (bf16[160,1024]{1,0:T(8,128)(2,1)S(1)}, bf16[160,1024]{1,0:T(8,128)(2,1)S(1)}, u32[]{:S(2)}, u32[]{:S(2)}) collective-permute-start(bf16[160,1024]{1,0:T(8,128)(2,1)S(1)} %get-tuple-element.541), channel_id=1, source_target_pairs={{0,1},{1,0},{2,3},{3,2},{4,5},{5,4},{6,7},{7,6},{8,9},{9,8},{10,11... | collective-permute-start | bytes 983048 | tf_op jit(solution)/shard_map/ppermute | solution.py:27
  261.4 18.9 %collective-permute-start.84 = (bf16[512,768]{1,0:T(8,128)(2,1)S(1)}, bf16[512,768]{1,0:T(8,128)(2,1)S(1)}, u32[]{:S(2)}, u32[]{:S(2)}) collective-permute-start(bf16[512,768]{1,0:T(8,128)(2,1)S(1)} %bitcast.44), channel_id=1, source_target_pairs={{0,4},{4,0},{1,5},{5,1},{2,6},{6,2},{3,7},{7,3},{8,12},{12,8},{9,1... | collective-permute-start | bytes 2359304 | tf_op jit(solution)/shard_map/ppermute | solution.py:41
  264.3 20.5 %collective-permute-start.85 = (bf16[512,768]{1,0:T(8,128)(2,1)S(1)}, bf16[512,768]{1,0:T(8,128)(2,1)S(1)}, u32[]{:S(2)}, u32[]{:S(2)}) collective-permute-start(bf16[512,768]{1,0:T(8,128)(2,1)S(1)} %get-tuple-element.566.refs_2_), channel_id=1, source_target_pairs={{0,8},{24,16},{1,9},{25,17},{2,10},{26,18},{3,11},{27,19},{4,12},{... | collective-permute-start | bytes 2359304 | tf_op jit(solution)/shard_map/ppermute | solution.py:788
  268.9 19.3 %collective-permute-start.86 = (bf16[512,768]{1,0:T(8,128)(2,1)S(1)}, bf16[512,768]{1,0:T(8,128)(2,1)S(1)}, u32[]{:S(2)}, u32[]{:S(2)}) collective-permute-start(bf16[512,768]{1,0:T(8,128)(2,1)S(1)} %get-tuple-element.567.refs_4_), channel_id=1, source_target_pairs={{8,16},{16,8},{9,17},{17,9},{10,18},{18,10},{11,19},{19,11},{12,20... | collective-permute-start | bytes 2359304 | tf_op jit(solution)/shard_map/ppermute | solution.py:784
  272.6 19.9 %collective-permute-start.81 = (bf16[320,1024]{1,0:T(8,128)(2,1)S(1)}, bf16[320,1024]{1,0:T(8,128)(2,1)S(1)}, u32[]{:S(2)}, u32[]{:S(2)}) collective-permute-start(bf16[320,1024]{1,0:T(8,128)(2,1)S(1)} %get-tuple-element.557), channel_id=1, source_target_pairs={{0,2},{2,0},{1,3},{3,1},{4,6},{6,4},{5,7},{7,5},{8,10},{10,8},{9,1... | collective-permute-start | bytes 1966088 | tf_op jit(solution)/shard_map/ppermute | solution.py:31
  277.6 13.8 %collective-permute-start.82 = (bf16[128,1024]{1,0:T(8,128)(2,1)S(1)}, bf16[128,1024]{1,0:T(8,128)(2,1)S(1)}, u32[]{:S(2)}, u32[]{:S(2)}) collective-permute-start(bf16[128,1024]{1,0:T(8,128)(2,1)S(1)} %get-tuple-element.562), channel_id=1, source_target_pairs={{0,1},{1,0},{2,3},{3,2},{4,5},{5,4},{6,7},{7,6},{8,9},{9,8},{10,11... | collective-permute-start | bytes 786440 | tf_op jit(solution)/shard_map/ppermute | solution.py:27
  280.3 12.1 %collective-permute-start.83 = (bf16[128,1024]{1,0:T(8,128)(2,1)S(1)}, bf16[128,1024]{1,0:T(8,128)(2,1)S(1)}, u32[]{:S(2)}, u32[]{:S(2)}) collective-permute-start(bf16[128,1024]{1,0:T(8,128)(2,1)S(1)} %get-tuple-element.563), channel_id=1, source_target_pairs={{0,1},{1,0},{2,3},{3,2},{4,5},{5,4},{6,7},{7,6},{8,9},{9,8},{10,11... | collective-permute-start | bytes 786440 | tf_op jit(solution)/shard_map/ppermute | solution.py:27
  284.8 17.8 %collective-permute-start.93 = (bf16[512,768]{1,0:T(8,128)(2,1)S(1)}, bf16[512,768]{1,0:T(8,128)(2,1)S(1)}, u32[]{:S(2)}, u32[]{:S(2)}) collective-permute-start(bf16[512,768]{1,0:T(8,128)(2,1)S(1)} %bitcast.45), channel_id=1, source_target_pairs={{0,4},{4,0},{1,5},{5,1},{2,6},{6,2},{3,7},{7,3},{8,12},{12,8},{9,1... | collective-permute-start | bytes 2359304 | tf_op jit(solution)/shard_map/ppermute | solution.py:41
  288.9 18.0 %collective-permute-start.92 = (bf16[512,768]{1,0:T(8,128)(2,1)S(1)}, bf16[512,768]{1,0:T(8,128)(2,1)S(1)}, u32[]{:S(2)}, u32[]{:S(2)}) collective-permute-start(bf16[512,768]{1,0:T(8,128)(2,1)S(1)} %get-tuple-element.588), channel_id=1, source_target_pairs={{0,8},{8,0},{16,24},{24,16},{1,9},{9,1},{17,25},{25,17},{2,10},{10... | collective-permute-start | bytes 2359304 | tf_op jit(solution)/shard_map/ppermute | solution.py:786
  291.4 16.5 %collective-permute-start.94 = (bf16[512,768]{1,0:T(8,128)(2,1)S(1)}, bf16[512,768]{1,0:T(8,128)(2,1)S(1)}, u32[]{:S(2)}, u32[]{:S(2)}) collective-permute-start(bf16[512,768]{1,0:T(8,128)(2,1)S(1)} %get-tuple-element.592.refs_4_), channel_id=1, source_target_pairs={{8,16},{16,8},{9,17},{17,9},{10,18},{18,10},{11,19},{19,11},{12,20... | collective-permute-start | bytes 2359304 | tf_op jit(solution)/shard_map/ppermute | solution.py:784
  300.3 11.6 %collective-permute-start.90 = (bf16[160,1024]{1,0:T(8,128)(2,1)S(1)}, bf16[160,1024]{1,0:T(8,128)(2,1)S(1)}, u32[]{:S(2)}, u32[]{:S(2)}) collective-permute-start(bf16[160,1024]{1,0:T(8,128)(2,1)S(1)} %get-tuple-element.585), channel_id=1, source_target_pairs={{0,1},{1,0},{2,3},{3,2},{4,5},{5,4},{6,7},{7,6},{8,9},{9,8},{10,11... | collective-permute-start | bytes 983048 | tf_op jit(solution)/shard_map/ppermute | solution.py:27
  300.5 14.2 %collective-permute-start.89 = (bf16[256,1024]{1,0:T(8,128)(2,1)S(1)}, bf16[256,1024]{1,0:T(8,128)(2,1)S(1)}, u32[]{:S(2)}, u32[]{:S(2)}) collective-permute-start(bf16[256,1024]{1,0:T(8,128)(2,1)S(1)} %get-tuple-element.580), channel_id=1, source_target_pairs={{0,2},{2,0},{1,3},{3,1},{4,6},{6,4},{5,7},{7,5},{8,10},{10,8},{9,1... | collective-permute-start | bytes 1572872 | tf_op jit(solution)/shard_map/ppermute | solution.py:31
  302.6 11.9 %collective-permute-start.91 = (bf16[160,1024]{1,0:T(8,128)(2,1)S(1)}, bf16[160,1024]{1,0:T(8,128)(2,1)S(1)}, u32[]{:S(2)}, u32[]{:S(2)}) collective-permute-start(bf16[160,1024]{1,0:T(8,128)(2,1)S(1)} %get-tuple-element.586), channel_id=1, source_target_pairs={{0,1},{1,0},{2,3},{3,2},{4,5},{5,4},{6,7},{7,6},{8,9},{9,8},{10,11... | collective-permute-start | bytes 983048 | tf_op jit(solution)/shard_map/ppermute | solution.py:27
  306.9 20.1 %collective-permute-start.101 = (bf16[512,768]{1,0:T(8,128)(2,1)S(1)}, bf16[512,768]{1,0:T(8,128)(2,1)S(1)}, u32[]{:S(2)}, u32[]{:S(2)}) collective-permute-start(bf16[512,768]{1,0:T(8,128)(2,1)S(1)} %bitcast.42), channel_id=1, source_target_pairs={{0,4},{4,0},{1,5},{5,1},{2,6},{6,2},{3,7},{7,3},{8,12},{12,8},{9,1... | collective-permute-start | bytes 2359304 | tf_op jit(solution)/shard_map/ppermute | solution.py:41
  308.5 19.5 %collective-permute-start.100 = (bf16[512,768]{1,0:T(8,128)(2,1)S(1)}, bf16[512,768]{1,0:T(8,128)(2,1)S(1)}, u32[]{:S(2)}, u32[]{:S(2)}) collective-permute-start(bf16[512,768]{1,0:T(8,128)(2,1)S(1)} %get-tuple-element.614), channel_id=1, source_target_pairs={{0,8},{8,0},{16,24},{24,16},{1,9},{9,1},{17,25},{25,17},{2,10},{10... | collective-permute-start | bytes 2359304 | tf_op jit(solution)/shard_map/ppermute | solution.py:786
  311.8 16.2 %collective-permute-start.102 = (bf16[512,768]{1,0:T(8,128)(2,1)S(1)}, bf16[512,768]{1,0:T(8,128)(2,1)S(1)}, u32[]{:S(2)}, u32[]{:S(2)}) collective-permute-start(bf16[512,768]{1,0:T(8,128)(2,1)S(1)} %get-tuple-element.619.refs_4_), channel_id=1, source_target_pairs={{8,16},{16,8},{9,17},{17,9},{10,18},{18,10},{11,19},{19,11},{12,20... | collective-permute-start | bytes 2359304 | tf_op jit(solution)/shard_map/ppermute | solution.py:784
  317.3 17.6 %collective-permute-start.97 = (bf16[320,1024]{1,0:T(8,128)(2,1)S(1)}, bf16[320,1024]{1,0:T(8,128)(2,1)S(1)}, u32[]{:S(2)}, u32[]{:S(2)}) collective-permute-start(bf16[320,1024]{1,0:T(8,128)(2,1)S(1)} %get-tuple-element.603), channel_id=1, source_target_pairs={{0,2},{2,0},{1,3},{3,1},{4,6},{6,4},{5,7},{7,5},{8,10},{10,8},{9,1... | collective-permute-start | bytes 1966088 | tf_op jit(solution)/shard_map/ppermute | solution.py:31
  327.0 23.3 %collective-permute-start.106 = (bf16[512,768]{1,0:T(8,128)(2,1)S(1)}, bf16[512,768]{1,0:T(8,128)(2,1)S(1)}, u32[]{:S(2)}, u32[]{:S(2)}) collective-permute-start(bf16[512,768]{1,0:T(8,128)(2,1)S(1)} %bitcast.40), channel_id=1, source_target_pairs={{0,4},{4,0},{1,5},{5,1},{2,6},{6,2},{3,7},{7,3},{8,12},{12,8},{9,1... | collective-permute-start | bytes 2359304 | tf_op jit(solution)/shard_map/ppermute | solution.py:41
  328.7 21.6 %collective-permute-start.107 = (bf16[512,768]{1,0:T(8,128)(2,1)S(1)}, bf16[512,768]{1,0:T(8,128)(2,1)S(1)}, u32[]{:S(2)}, u32[]{:S(2)}) collective-permute-start(bf16[512,768]{1,0:T(8,128)(2,1)S(1)} %get-tuple-element.652), channel_id=1, source_target_pairs={{0,8},{8,0},{16,24},{24,16},{1,9},{9,1},{17,25},{25,17},{2,10},{10... | collective-permute-start | bytes 2359304 | tf_op jit(solution)/shard_map/ppermute | solution.py:786
  332.2 18.1 %collective-permute-start.108 = (bf16[512,768]{1,0:T(8,128)(2,1)S(1)}, bf16[512,768]{1,0:T(8,128)(2,1)S(1)}, u32[]{:S(2)}, u32[]{:S(2)}) collective-permute-start(bf16[512,768]{1,0:T(8,128)(2,1)S(1)} %get-tuple-element.653.refs_4_), channel_id=1, source_target_pairs={{8,16},{16,8},{9,17},{17,9},{10,18},{18,10},{11,19},{19,11},{12,20... | collective-permute-start | bytes 2359304 | tf_op jit(solution)/shard_map/ppermute | solution.py:784
  347.9 25.0 %collective-permute-start.105 = (bf16[512,768]{1,0:T(8,128)(2,1)S(1)}, bf16[512,768]{1,0:T(8,128)(2,1)S(1)}, u32[]{:S(2)}, u32[]{:S(2)}) collective-permute-start(bf16[512,768]{1,0:T(8,128)(2,1)S(1)} %bitcast.41), channel_id=1, source_target_pairs={{0,4},{4,0},{1,5},{5,1},{2,6},{6,2},{3,7},{7,3},{8,12},{12,8},{9,1... | collective-permute-start | bytes 2359304 | tf_op jit(solution)/shard_map/ppermute | solution.py:41
  351.0 20.6 %collective-permute-start.109 = (bf16[512,768]{1,0:T(8,128)(2,1)S(1)}, bf16[512,768]{1,0:T(8,128)(2,1)S(1)}, u32[]{:S(2)}, u32[]{:S(2)}) collective-permute-start(bf16[512,768]{1,0:T(8,128)(2,1)S(1)} %get-tuple-element.656), channel_id=1, source_target_pairs={{0,8},{8,0},{16,24},{24,16},{1,9},{9,1},{17,25},{25,17},{2,10},{10... | collective-permute-start | bytes 2359304 | tf_op jit(solution)/shard_map/ppermute | solution.py:786
  354.5 18.4 %collective-permute-start.110 = (bf16[512,768]{1,0:T(8,128)(2,1)S(1)}, bf16[512,768]{1,0:T(8,128)(2,1)S(1)}, u32[]{:S(2)}, u32[]{:S(2)}) collective-permute-start(bf16[512,768]{1,0:T(8,128)(2,1)S(1)} %get-tuple-element.657.refs_4_), channel_id=1, source_target_pairs={{8,16},{16,8},{9,17},{17,9},{10,18},{18,10},{11,19},{19,11},{12,20... | collective-permute-start | bytes 2359304 | tf_op jit(solution)/shard_map/ppermute | solution.py:784
  355.5 22.3 %collective-permute-start.60 = (bf16[576,1024]{1,0:T(8,128)(2,1)S(1)}, bf16[576,1024]{1,0:T(8,128)(2,1)S(1)}, u32[]{:S(2)}, u32[]{:S(2)}) collective-permute-start(bf16[576,1024]{1,0:T(8,128)(2,1)S(1)} %constant_dynamic-update-slice_fusion.refs_0_), channel_id=1, source_target_pairs={{0,1},{1,0},{2,3},{3,2},{4,5},{5,4},{6,7},{7,6},{8,9},{9,8},{10,11... | collective-permute-start | bytes 3538952 | tf_op jit(solution)/shard_map/ppermute | solution.py:27
  362.9 30.7 %collective-permute-start.115 = (bf16[528,768]{1,0:T(8,128)(2,1)S(1)}, bf16[528,768]{1,0:T(8,128)(2,1)S(1)}, u32[]{:S(2)}, u32[]{:S(2)}) collective-permute-start(bf16[528,768]{1,0:T(8,128)(2,1)S(1)} %bitcast.39), channel_id=1, source_target_pairs={{0,4},{4,0},{1,5},{5,1},{2,6},{6,2},{3,7},{7,3},{8,12},{12,8},{9,1... | collective-permute-start | bytes 2433032 | tf_op jit(solution)/shard_map/ppermute | solution.py:41
  373.6 18.5 %collective-permute-start.116 = (bf16[512,768]{1,0:T(8,128)(2,1)S(1)}, bf16[512,768]{1,0:T(8,128)(2,1)S(1)}, u32[]{:S(2)}, u32[]{:S(2)}) collective-permute-start(bf16[512,768]{1,0:T(8,128)(2,1)S(1)} %get-tuple-element.690), channel_id=1, source_target_pairs={{0,8},{8,0},{16,24},{24,16},{1,9},{9,1},{17,25},{25,17},{2,10},{10... | collective-permute-start | bytes 2359304 | tf_op jit(solution)/shard_map/ppermute | solution.py:786
  376.0 17.6 %collective-permute-start.117 = (bf16[512,768]{1,0:T(8,128)(2,1)S(1)}, bf16[512,768]{1,0:T(8,128)(2,1)S(1)}, u32[]{:S(2)}, u32[]{:S(2)}) collective-permute-start(bf16[512,768]{1,0:T(8,128)(2,1)S(1)} %get-tuple-element.691.refs_4_), channel_id=1, source_target_pairs={{8,16},{16,8},{9,17},{17,9},{10,18},{18,10},{11,19},{19,11},{12,20... | collective-permute-start | bytes 2359304 | tf_op jit(solution)/shard_map/ppermute | solution.py:784
  376.7 26.4 %collective-permute-start.118 = (bf16[320,1024]{1,0:T(8,128)(2,1)S(1)}, bf16[320,1024]{1,0:T(8,128)(2,1)S(1)}, u32[]{:S(2)}, u32[]{:S(2)}) collective-permute-start(bf16[320,1024]{1,0:T(8,128)(2,1)S(1)} %get-tuple-element.698), channel_id=1, source_target_pairs={{0,2},{2,0},{1,3},{3,1},{4,6},{6,4},{5,7},{7,5},{8,10},{10,8},{9,1... | collective-permute-start | bytes 1966088 | tf_op jit(solution)/shard_map/ppermute | solution.py:31
  377.8 25.0 %collective-permute-start.114 = (bf16[256,1024]{1,0:T(8,128)(2,1)S(1)}, bf16[256,1024]{1,0:T(8,128)(2,1)S(1)}, u32[]{:S(2)}, u32[]{:S(2)}) collective-permute-start(bf16[256,1024]{1,0:T(8,128)(2,1)S(1)} %get-tuple-element.685), channel_id=1, source_target_pairs={{0,2},{2,0},{1,3},{3,1},{4,6},{6,4},{5,7},{7,5},{8,10},{10,8},{9,1... | collective-permute-start | bytes 1572872 | tf_op jit(solution)/shard_map/ppermute | solution.py:31
  394.3 18.0 %collective-permute-start.120 = (bf16[528,768]{1,0:T(8,128)(2,1)S(1)}, bf16[528,768]{1,0:T(8,128)(2,1)S(1)}, u32[]{:S(2)}, u32[]{:S(2)}) collective-permute-start(bf16[528,768]{1,0:T(8,128)(2,1)S(1)} %get-tuple-element.703), channel_id=1, source_target_pairs={{0,8},{8,0},{16,24},{24,16},{1,9},{9,1},{17,25},{25,17},{2,10},{10... | collective-permute-start | bytes 2433032 | tf_op jit(solution)/shard_map/ppermute | solution.py:786
  396.5 17.1 %collective-permute-start.121 = (bf16[512,768]{1,0:T(8,128)(2,1)S(1)}, bf16[512,768]{1,0:T(8,128)(2,1)S(1)}, u32[]{:S(2)}, u32[]{:S(2)}) collective-permute-start(bf16[512,768]{1,0:T(8,128)(2,1)S(1)} %get-tuple-element.704.refs_2_), channel_id=1, source_target_pairs={{8,16},{16,8},{9,17},{17,9},{10,18},{18,10},{11,19},{19,11},{12,20... | collective-permute-start | bytes 2359304 | tf_op jit(solution)/shard_map/ppermute | solution.py:784
  403.4 12.5 %collective-permute-start.119 = (bf16[576,1024]{1,0:T(8,128)(2,1)S(1)}, bf16[576,1024]{1,0:T(8,128)(2,1)S(1)}, u32[]{:S(2)}, u32[]{:S(2)}) collective-permute-start(bf16[576,1024]{1,0:T(8,128)(2,1)S(1)} %constant_dynamic-update-slice_fusion.4.refs_0_), channel_id=1, source_target_pairs={{0,1},{1,0},{2,3},{3,2},{4,5},{5,4},{6,7},{7,6},{8,9},{9,8},{10,11... | collective-permute-start | bytes 3538952 | tf_op jit(solution)/shard_map/ppermute | solution.py:27
  414.0 20.7 %collective-permute-start.122 = (bf16[528,768]{1,0:T(8,128)(2,1)S(1)}, bf16[528,768]{1,0:T(8,128)(2,1)S(1)}, u32[]{:S(2)}, u32[]{:S(2)}) collective-permute-start(bf16[528,768]{1,0:T(8,128)(2,1)S(1)} %get-tuple-element.712.refs_0_), channel_id=1, source_target_pairs={{8,16},{16,8},{9,17},{17,9},{10,18},{18,10},{11,19},{19,11},{12,20... | collective-permute-start | bytes 2433032 | tf_op jit(solution)/shard_map/ppermute | solution.py:784
  414.7 18.6 %collective-permute-start.123 = (bf16[512,768]{1,0:T(8,128)(2,1)S(1)}, bf16[512,768]{1,0:T(8,128)(2,1)S(1)}, u32[]{:S(2)}, u32[]{:S(2)}) collective-permute-start(bf16[512,768]{1,0:T(8,128)(2,1)S(1)} %get-tuple-element.713.refs_0_), channel_id=1, source_target_pairs={{8,0},{16,24},{9,1},{17,25},{10,2},{18,26},{11,3},{19,27},{12,4},{... | collective-permute-start | bytes 2359304 | tf_op jit(solution)/shard_map/ppermute | solution.py:790
  434.9 17.5 %collective-permute-start.124 = (bf16[528,768]{1,0:T(8,128)(2,1)S(1)}, bf16[528,768]{1,0:T(8,128)(2,1)S(1)}, u32[]{:S(2)}, u32[]{:S(2)}) collective-permute-start(bf16[528,768]{1,0:T(8,128)(2,1)S(1)} %get-tuple-element.718.refs_0_), channel_id=1, source_target_pairs={{8,0},{16,24},{9,1},{17,25},{10,2},{18,26},{11,3},{19,27},{12,4},{... | collective-permute-start | bytes 2433032 | tf_op jit(solution)/shard_map/ppermute | solution.py:790
  (212 other events, 941.7 us)

commit v5 on v4

--- a/solution.py
+++ b/solution.py
@@ -1024,9 +1024,9 @@
         zero, one = weights
         waits = {
             1: lambda: zero[2].early,
-            2: lambda: [*zero[3].early, *zero[2].late, *one[0].early, *one[1].early],
-            3: lambda: [*one[0].late, *one[1].late],
-            4: lambda: one[2].early,
+            2: lambda: [*zero[3].early, *zero[2].late, *one[0].early],
+            3: lambda: [*one[1].early, *one[0].late],
+            4: lambda: [*one[1].late, *one[2].early],
             5: lambda: [*one[2].late, *one[3].early],
             6: lambda: one[3].late,
         }

time: 464 us -> 459 us (0.989)
  waiting for transfers between devices: 146 us -> 140 us
    unnamed x310 -> x312, local copies, waits for them, and re-layouts: 43.6 us -> 42.9 us
  transfers between devices with their start and end apart: 125 -> 125, of which waited for: 61 -> 60; matrix products, arithmetic and copies ran while one was open for 0% -> 0% of each run, Pallas kernels for 33% -> 34%
where the time goes in v5:
time: 459 us; the launch traced here: 453 us
  Pallas kernels  163 us (36%)
  waiting for transfers between devices  140 us (31%)
  starting transfers between devices  99.9 us (22%)
  local copies, waits for them, and re-layouts  46.4 us (10%)
    pallas_call x95, Pallas kernels, call(): pl.pallas_call(kernel, grid=grid, in_specs=in_specs, out_specs=[*out_spec...  163 us
    unnamed x312, local copies, waits for them, and re-layouts  42.9 us
    ppermute x2, waiting for transfers between devices, step(): older['back'] = lax.ppermute(older['total'], DP, [(1, 0), (2, 3)])  32.7 us
    ppermute x6, waiting for transfers between devices, step(): lax.ppermute(found[-1], DP, [(0, 1), (1, 0), (2, 3), (3, 2)])  29.2 us
    ppermute x65, waiting for transfers between devices, to_core(): return lax.ppermute(value, TENSOR, CORE_SWAP)  24.2 us
    ppermute x17, waiting for transfers between devices, to_chip(): return lax.ppermute(value, TENSOR, CHIP_SWAP)  22.6 us
    ppermute x9, waiting for transfers between devices, from_fsdp(): lax.ppermute(value, FSDP, [((i + step) % size, i) for i in range(size)])  21 us
    ppermute x17, starting transfers between devices, to_chip(): return lax.ppermute(value, TENSOR, CHIP_SWAP)  17.6 us
  transfers between devices with their start and end apart: 125, of which 60 were waited for; matrix products, arithmetic and copies ran while one was open for 0% of the time, Pallas kernels for 34%

profile of v5, /device:TPU:0, one launch (start us, length us, event | category | flops | bytes accessed | tf_op | source)
XLA Modules:
  0.0 453.1 jit_solution(15124983403981922030)
XLA Ops:
  4.0 3.0 collective-permute-start
  7.0 9.1 %collective-permute-done.refs_4_.refs_1_.refs_3_.refs_5_ = bf16[3,256,256]{2,1,0:T(8,128)(2,1)S(1)} collective-permute-done((bf16[3,256,256]{2,1,0:T(8,128)(2,1)S(1)}, bf16[3,256,256]{2,1,0:T(8,128)(2,1)S(1)}, u32[]{:S(2)}, u32[]{:S(2)}) %collective-permute-start) | collective-permute-done | bytes 393248 | tf_op jit(solution)/shard_map/ppermute | solution.py:36
  16.1 1.8 collective-permute-start.1
  17.9 1.5 collective-permute-start.2
  19.4 1.7 copy-done.83
  33.6 1.6 collective-permute-start.4
  35.2 2.2 collective-permute-done.4
  37.9 1.8 copy-done.30
  40.6 1.6 collective-permute-start.8
  45.6 5.5 %attention_forward.4 = (bf16[128,1024]{1,0:T(8,128)(2,1)S(1)}, bf16[128,1024]{1,0:T(8,128)(2,1)S(1)}, bf16[256,1024]{1,0:T(8,128)(2,1)S(1)}, bf16[512,768]{1,0:T...) custom-call(bf16[256,1024]{1,0:T(8,128)(2,1)S(1)} %copy-done.32, ...), custom_call_target="tpu_custom_call" | custom-call | tf_op jit(solution)/shard_map/attention_forward/pallas_call | solution.py:131
  61.5 7.9 %attention_forward.5 = (bf16[160,1024]{1,0:T(8,128)(2,1)S(1)}, bf16[160,1024]{1,0:T(8,128)(2,1)}, bf16[320,1024]{1,0:T(8,128)(2,1)S(1)}, bf16[640,768]{1,0:T(8,1...) custom-call(bf16[320,1024]{1,0:T(8,128)(2,1)S(1)} %copy-done.19, ...), custom_call_target="tpu_custom_call" | custom-call | tf_op jit(solution)/shard_map/attention_forward/pallas_call | solution.py:131
  75.2 1.5 collective-permute-start.11
  81.5 5.0 %collective-permute-done.11.refs_8_.refs_5_ = bf16[3,256,256]{2,1,0:T(8,128)(2,1)} collective-permute-done((bf16[3,256,256]{2,1,0:T(8,128)(2,1)}, bf16[3,256,256]{2,1,0:T(8,128)(2,1)}, u32[]{:S(2)}, u32[]{:S(2)}) %collective-permute-start.11) | collective-permute-done | bytes 393248 | tf_op jit(solution)/shard_map/ppermute | solution.py:36
  90.5 1.7 norm_forward.8
  94.9 4.2 feed_forward.4
  101.4 3.9 collective-permute-done.23.refs_6_.refs_8_
  105.4 2.1 norm_forward.9
  112.7 5.1 %feed_forward.5 = (bf16[160,1024]{1,0:T(8,128)(2,1)S(1)}, bf16[160,1024]{1,0:T(8,128)(2,1)S(1)}, bf16[640,1024]{1,0:T(8,128)(2,1)S(1)}, bf16[640,1024]{1,0:T(8,1...) custom-call(bf16[160,1024]{1,0:T(8,128)(2,1)S(1)} %get-tuple-element.413.refs_0_.refs_14_.refs_4_, ...), custom_call_target="tpu_custom_call" | custom-call | tf_op jit(solution)/shard_map/feed_forward/pallas_call | solution.py:131
  122.6 2.3 collective-permute-done.24.refs_6_.refs_9_
  136.0 6.4 %attention_forward.6 = (bf16[128,1024]{1,0:T(8,128)(2,1)S(1)}, bf16[128,1024]{1,0:T(8,128)(2,1)S(1)}, bf16[256,1024]{1,0:T(8,128)(2,1)S(1)}, bf16[512,768]{1,0:T...) custom-call(bf16[128,1024]{1,0:T(8,128)(2,1)} %get-tuple-element.421.refs_0_,, ...), custom_call_target="tpu_custom_call" | custom-call | tf_op jit(solution)/shard_map/attention_forward/pallas_call | solution.py:131
  144.6 2.1 norm_forward.11
  148.2 2.1 collective-permute-start.36
  150.3 7.6 %attention_forward.7 = (bf16[160,1024]{1,0:T(8,128)(2,1)S(1)}, bf16[160,1024]{1,0:T(8,128)(2,1)S(1)}, bf16[320,1024]{1,0:T(8,128)(2,1)S(1)}, bf16[640,768]{1,0:T...) custom-call(bf16[160,1024]{1,0:T(8,128)(2,1)S(1)} %get-tuple-element, ...), custom_call_target="tpu_custom_call" | custom-call | tf_op jit(solution)/shard_map/attention_forward/pallas_call | solution.py:131
  165.2 4.0 feed_forward.6
  171.3 5.9 %collective-permute-done.50.refs_3_ = bf16[320,1024]{1,0:T(8,128)(2,1)S(1)} collective-permute-done((bf16[320,1024]{1,0:T(8,128)(2,1)S(1)}, bf16[320,1024]{1,0:T(8,128)(2,1)S(1)}, u32[]{:S(2)}, u32[]{:S(2)}) %collective-permute-start.50) | collective-permute-done | bytes 655392 | tf_op jit(solution)/shard_map/ppermute | solution.py:31
  180.2 4.7 %feed_forward.7 = (bf16[160,1024]{1,0:T(8,128)(2,1)S(1)}, bf16[160,1024]{1,0:T(8,128)(2,1)S(1)}, bf16[640,1024]{1,0:T(8,128)(2,1)S(1)}, bf16[640,1024]{1,0:T(8,1...) custom-call(bf16[160,1024]{1,0:T(8,128)(2,1)S(1)} %get-tuple-element.458.refs_0_.refs_14_.refs_4_, ...), custom_call_target="tpu_custom_call" | custom-call | tf_op jit(solution)/shard_map/feed_forward/pallas_call | solution.py:131
  188.2 5.2 %collective-permute-done.49.refs_3_ = bf16[256,1024]{1,0:T(8,128)(2,1)S(1)} collective-permute-done((bf16[256,1024]{1,0:T(8,128)(2,1)S(1)}, bf16[256,1024]{1,0:T(8,128)(2,1)S(1)}, u32[]{:S(2)}, u32[]{:S(2)}) %collective-permute-start.49) | collective-permute-done | bytes 524320 | tf_op jit(solution)/shard_map/ppermute | solution.py:31
  193.4 1.7 norm_forward.14
  197.7 3.9 feed_backward.4
  203.7 2.9 collective-permute-done.55.refs_3_
  206.6 1.9 norm_forward.15
  211.9 4.5 feed_backward.5
  218.2 1.6 collective-permute-start.70
  222.2 2.4 collective-permute-done.61.refs_3_
  227.5 6.6 %attention_backward.4 = (bf16[128,1024]{1,0:T(8,128)(2,1)S(1)}, bf16[128,1024]{1,0:T(8,128)(2,1)S(1)}, bf16[256,1024]{1,0:T(8,128)(2,1)S(1)}, bf16[512,768]{1,0:...) custom-call(bf16[128,1024]{1,0:T(8,128)(2,1)S(1)} %get-tuple-element.506.refs_0_.refs_10_, ...), custom_call_target="tpu_custom_call" | custom-call | tf_op jit(solution)/shard_map/attention_backward/pallas_call | solution.py:131
  235.9 2.1 collective-permute-start.77
  239.6 2.8 collective-permute-start.78
  245.9 8.1 %attention_backward.5 = (bf16[160,1024]{1,0:T(8,128)(2,1)S(1)}, bf16[160,1024]{1,0:T(8,128)(2,1)S(1)}, bf16[320,1024]{1,0:T(8,128)(2,1)S(1)}, bf16[640,768]{1,0:...) custom-call(bf16[160,1024]{1,0:T(8,128)(2,1)S(1)} %get-tuple-element.531.refs_0_.refs_14_, ...), custom_call_target="tpu_custom_call" | custom-call | tf_op jit(solution)/shard_map/attention_backward/pallas_call | solution.py:131
  255.9 1.7 collective-permute-start.84
  259.6 4.6 %collective-permute-start.85 = (bf16[512,768]{1,0:T(8,128)(2,1)S(1)}, bf16[512,768]{1,0:T(8,128)(2,1)S(1)}, u32[]{:S(2)}, u32[]{:S(2)}) collective-permute-start(bf16[512,768]{1,0:T(8,128)(2,1)S(1)} %get-tuple-element.566.refs_2_), channel_id=1, source_target_pairs={{0,8},{24,16},{1,9},{25,17},{2,10},{26,18},{3,11},{27,19},{4,12},{... | collective-permute-start | bytes 2359304 | tf_op jit(solution)/shard_map/ppermute | solution.py:788
  268.8 3.9 feed_backward.6
  272.7 2.8 collective-permute-done.84.refs_1_
  275.6 2.3 weight_grad.22
  277.9 2.2 collective-permute-done.85.refs_3_
  280.6 2.3 weight_grad.23
  283.6 2.6 collective-permute-start.92
  290.5 4.5 feed_backward.7
  296.1 1.8 collective-permute-done.93.refs_1_
  301.6 1.5 collective-permute-start.101
  303.8 3.2 collective-permute-start.100
  313.5 5.6 %attention_backward.6 = (bf16[128,1024]{1,0:T(8,128)(2,1)S(1)}, bf16[128,1024]{1,0:T(8,128)(2,1)S(1)}, bf16[256,1024]{1,0:T(8,128)(2,1)S(1)}, bf16[512,768]{1,0:...) custom-call(bf16[128,1024]{1,0:T(8,128)(2,1)S(1)} %get-tuple-element.601.refs_0_.refs_10_, ...), custom_call_target="tpu_custom_call" | custom-call | tf_op jit(solution)/shard_map/attention_backward/pallas_call | solution.py:131
  323.7 3.6 collective-permute-start.107
  334.1 7.1 %attention_backward.7 = (bf16[160,1024]{1,0:T(8,128)(2,1)S(1)}, bf16[160,1024]{1,0:T(8,128)(2,1)S(1)}, bf16[320,1024]{1,0:T(8,128)(2,1)S(1)}, bf16[640,768]{1,0:...) custom-call(bf16[160,1024]{1,0:T(8,128)(2,1)S(1)} %get-tuple-element.626.refs_0_.refs_14_, ...), custom_call_target="tpu_custom_call" | custom-call | tf_op jit(solution)/shard_map/attention_backward/pallas_call | solution.py:131
  346.1 3.4 collective-permute-start.109
  351.0 2.8 collective-permute-done.113.refs_2_
  359.9 6.8 %collective-permute-done.109.refs_1_.refs_3_ = bf16[512,768]{1,0:T(8,128)(2,1)S(1)} collective-permute-done((bf16[512,768]{1,0:T(8,128)(2,1)S(1)}, bf16[512,768]{1,0:T(8,128)(2,1)S(1)}, u32[]{:S(2)}, u32[]{:S(2)}) %collective-permute-start.109) | collective-permute-done | bytes 786464 | tf_op jit(solution)/shard_map/ppermute | solution.py:786
  368.7 2.4 collective-permute-start.116
  374.9 12.4 %collective-permute-done.116.refs_1_.refs_3_ = bf16[512,768]{1,0:T(8,128)(2,1)S(1)} collective-permute-done((bf16[512,768]{1,0:T(8,128)(2,1)S(1)}, bf16[512,768]{1,0:T(8,128)(2,1)S(1)}, u32[]{:S(2)}, u32[]{:S(2)}) %collective-permute-start.116) | collective-permute-done | bytes 786464 | tf_op jit(solution)/shard_map/ppermute | solution.py:786
  389.5 2.2 collective-permute-start.120
  392.4 5.6 %collective-permute-done.114.refs_3_ = bf16[256,1024]{1,0:T(8,128)(2,1)S(1)} collective-permute-done((bf16[256,1024]{1,0:T(8,128)(2,1)S(1)}, bf16[256,1024]{1,0:T(8,128)(2,1)S(1)}, u32[]{:S(2)}, u32[]{:S(2)}) %collective-permute-start.114) | collective-permute-done | bytes 524320 | tf_op jit(solution)/shard_map/ppermute | solution.py:31
  398.7 8.9 %collective-permute-done.120.refs_1_ = bf16[528,768]{1,0:T(8,128)(2,1)S(1)} collective-permute-done((bf16[528,768]{1,0:T(8,128)(2,1)S(1)}, bf16[528,768]{1,0:T(8,128)(2,1)S(1)}, u32[]{:S(2)}, u32[]{:S(2)}) %collective-permute-start.120) | collective-permute-done | bytes 811040 | tf_op jit(solution)/shard_map/ppermute | solution.py:786
  412.6 16.3 %collective-permute-done.123.refs_1_ = bf16[512,768]{1,0:T(8,128)(2,1)S(1)} collective-permute-done((bf16[512,768]{1,0:T(8,128)(2,1)S(1)}, bf16[512,768]{1,0:T(8,128)(2,1)S(1)}, u32[]{:S(2)}, u32[]{:S(2)}) %collective-permute-start.123) | collective-permute-done | bytes 786464 | tf_op jit(solution)/shard_map/ppermute | solution.py:790
  431.8 16.4 %collective-permute-done.124.refs_1_ = bf16[528,768]{1,0:T(8,128)(2,1)S(1)} collective-permute-done((bf16[528,768]{1,0:T(8,128)(2,1)S(1)}, bf16[528,768]{1,0:T(8,128)(2,1)S(1)}, u32[]{:S(2)}, u32[]{:S(2)}) %collective-permute-start.124) | collective-permute-done | bytes 811040 | tf_op jit(solution)/shard_map/ppermute | solution.py:790
  448.2 1.9 finish_proj.3
  (627 shorter events, 181.3 us)
Async XLA Ops:
  4.0 12.1 %collective-permute-start = (bf16[3,256,256]{2,1,0:T(8,128)(2,1)S(1)}, bf16[3,256,256]{2,1,0:T(8,128)(2,1)S(1)}, u32[]{:S(2)}, u32[]{:S(2)}) collective-permute-start(bf16[3,256,256]{2,1,0:T(8,128)(2,1)S(1)} %get-tuple-element.372), channel_id=1, source_target_pairs={{4,0},{0,4},{5,1},{1,5},{6,2},{2,6},{7,3},{3,7},{12,8},{8,12},{13,... | collective-permute-start | bytes 1179656 | tf_op jit(solution)/shard_map/ppermute | solution.py:36
  16.1 21.8 %collective-permute-start.1 = (bf16[3,256,256]{2,1,0:T(8,128)(2,1)S(1)}, bf16[3,256,256]{2,1,0:T(8,128)(2,1)S(1)}, u32[]{:S(2)}, u32[]{:S(2)}) collective-permute-start(bf16[3,256,256]{2,1,0:T(8,128)(2,1)S(1)} %collective-permute-done.refs_4_.refs_1_.refs_3_.refs_5_), channel_id=1, source_target_pairs={{0,8},{8,0},{16,24},{24,16},{1,9},{9,1},{17,25},{25,17},{2,10},{10... | collective-permute-start | bytes 1179656 | tf_op jit(solution)/shard_map/ppermute | solution.py:191
  31.4 22.2 %collective-permute-start.13 = (bf16[288,1024]{1,0:T(8,128)(2,1)}, bf16[288,1024]{1,0:T(8,128)(2,1)}, u32[]{:S(2)}, u32[]{:S(2)}) collective-permute-start(bf16[288,1024]{1,0:T(8,128)(2,1)} %get-tuple-element.390.refs_0_), channel_id=1, source_target_pairs={{0,2},{2,0},{1,3},{3,1},{4,6},{6,4},{5,7},{7,5},{8,10},{10,8},{9,1... | collective-permute-start | bytes 1769480 | tf_op jit(solution)/shard_map/ppermute | solution.py:31
  40.6 15.4 %collective-permute-start.8 = (bf16[256,1024]{1,0:T(8,128)(2,1)}, bf16[256,1024]{1,0:T(8,128)(2,1)S(1)}, u32[]{:S(2)}, u32[]{:S(2)}) collective-permute-start(bf16[256,1024]{1,0:T(8,128)(2,1)} %get-tuple-element.384), channel_id=1, source_target_pairs={{4,0},{0,4},{5,1},{1,5},{6,2},{2,6},{7,3},{3,7},{12,8},{8,12},{13,... | collective-permute-start | bytes 1572872 | tf_op jit(solution)/shard_map/ppermute | solution.py:36
  56.8 18.4 %collective-permute-start.9 = (bf16[1024,256]{1,0:T(8,128)(2,1)S(1)}, bf16[1024,256]{1,0:T(8,128)(2,1)}, u32[]{:S(2)}, u32[]{:S(2)}) collective-permute-start(bf16[1024,256]{1,0:T(8,128)(2,1)S(1)} %get-tuple-element.386), channel_id=1, source_target_pairs={{4,0},{0,4},{5,1},{1,5},{6,2},{2,6},{7,3},{3,7},{12,8},{8,12},{13,... | collective-permute-start | bytes 1572872 | tf_op jit(solution)/shard_map/ppermute | solution.py:36
  57.4 29.1 %collective-permute-start.7 = (bf16[256,1024]{1,0:T(8,128)(2,1)}, bf16[256,1024]{1,0:T(8,128)(2,1)}, u32[]{:S(2)}, u32[]{:S(2)}) collective-permute-start(bf16[256,1024]{1,0:T(8,128)(2,1)} %get-tuple-element.383), channel_id=1, source_target_pairs={{0,2},{2,0},{1,3},{3,1},{4,6},{6,4},{5,7},{7,5},{8,10},{10,8},{9,1... | collective-permute-start | bytes 1572872 | tf_op jit(solution)/shard_map/ppermute | solution.py:31
  57.9 28.6 %collective-permute-start.10 = (bf16[256,1024]{1,0:T(8,128)(2,1)S(1)}, bf16[256,1024]{1,0:T(8,128)(2,1)}, u32[]{:S(2)}, u32[]{:S(2)}) collective-permute-start(bf16[256,1024]{1,0:T(8,128)(2,1)S(1)} %collective-permute-done.8.refs_1_.refs_5_), channel_id=1, source_target_pairs={{0,8},{8,0},{16,24},{24,16},{1,9},{9,1},{17,25},{25,17},{2,10},{10... | collective-permute-start | bytes 1572872 | tf_op jit(solution)/shard_map/ppermute | solution.py:191
  75.2 11.3 %collective-permute-start.11 = (bf16[3,256,256]{2,1,0:T(8,128)(2,1)}, bf16[3,256,256]{2,1,0:T(8,128)(2,1)}, u32[]{:S(2)}, u32[]{:S(2)}) collective-permute-start(bf16[3,256,256]{2,1,0:T(8,128)(2,1)} %get-tuple-element.387), channel_id=1, source_target_pairs={{4,0},{0,4},{5,1},{1,5},{6,2},{2,6},{7,3},{3,7},{12,8},{8,12},{13,... | collective-permute-start | bytes 1179656 | tf_op jit(solution)/shard_map/ppermute | solution.py:36
  76.8 18.1 %collective-permute-start.19 = (bf16[1024,256]{1,0:T(8,128)(2,1)}, bf16[1024,256]{1,0:T(8,128)(2,1)}, u32[]{:S(2)}, u32[]{:S(2)}) collective-permute-start(bf16[1024,256]{1,0:T(8,128)(2,1)} %collective-permute-done.9.refs_6_.refs_8_), channel_id=1, source_target_pairs={{0,8},{8,0},{16,24},{24,16},{1,9},{9,1},{17,25},{25,17},{2,10},{10... | collective-permute-start | bytes 1572872 | tf_op jit(solution)/shard_map/ppermute | solution.py:191
  79.9 25.4 %collective-permute-start.26 = (bf16[320,1024]{1,0:T(8,128)(2,1)}, bf16[320,1024]{1,0:T(8,128)(2,1)}, u32[]{:S(2)}, u32[]{:S(2)}) collective-permute-start(bf16[320,1024]{1,0:T(8,128)(2,1)} %get-tuple-element.411), channel_id=1, source_target_pairs={{0,2},{2,0},{1,3},{3,1},{4,6},{6,4},{5,7},{7,5},{8,10},{10,8},{9,1... | collective-permute-start | bytes 1966088 | tf_op jit(solution)/shard_map/ppermute | solution.py:31
  93.5 11.8 %collective-permute-start.27 = (bf16[3,256,256]{2,1,0:T(8,128)(2,1)}, bf16[3,256,256]{2,1,0:T(8,128)(2,1)S(1)}, u32[]{:S(2)}, u32[]{:S(2)}) collective-permute-start(bf16[3,256,256]{2,1,0:T(8,128)(2,1)} %collective-permute-done.11.refs_8_.refs_5_), channel_id=1, source_target_pairs={{0,8},{8,0},{16,24},{24,16},{1,9},{9,1},{17,25},{25,17},{2,10},{10... | collective-permute-start | bytes 1179656 | tf_op jit(solution)/shard_map/ppermute | solution.py:191
  109.7 15.2 %collective-permute-start.25 = (bf16[256,1024]{1,0:T(8,128)(2,1)S(1)}, bf16[256,1024]{1,0:T(8,128)(2,1)}, u32[]{:S(2)}, u32[]{:S(2)}) collective-permute-start(bf16[256,1024]{1,0:T(8,128)(2,1)S(1)} %copy-done.145), channel_id=1, source_target_pairs={{4,0},{0,4},{5,1},{1,5},{6,2},{2,6},{7,3},{3,7},{12,8},{8,12},{13,... | collective-permute-start | bytes 1572872 | tf_op jit(solution)/shard_map/ppermute | solution.py:36
  111.2 13.7 %collective-permute-start.22 = (bf16[256,1024]{1,0:T(8,128)(2,1)S(1)}, bf16[256,1024]{1,0:T(8,128)(2,1)S(1)}, u32[]{:S(2)}, u32[]{:S(2)}) collective-permute-start(bf16[256,1024]{1,0:T(8,128)(2,1)S(1)} %get-tuple-element.407), channel_id=1, source_target_pairs={{0,2},{2,0},{1,3},{3,1},{4,6},{6,4},{5,7},{7,5},{8,10},{10,8},{9,1... | collective-permute-start | bytes 1572872 | tf_op jit(solution)/shard_map/ppermute | solution.py:31
  122.1 22.5 %collective-permute-start.39 = (bf16[320,1024]{1,0:T(8,128)(2,1)}, bf16[320,1024]{1,0:T(8,128)(2,1)}, u32[]{:S(2)}, u32[]{:S(2)}) collective-permute-start(bf16[320,1024]{1,0:T(8,128)(2,1)} %get-tuple-element.433), channel_id=1, source_target_pairs={{0,2},{2,0},{1,3},{3,1},{4,6},{6,4},{5,7},{7,5},{8,10},{10,8},{9,1... | collective-permute-start | bytes 1966088 | tf_op jit(solution)/shard_map/ppermute | solution.py:31
  129.4 15.2 %collective-permute-start.37 = (bf16[1024,256]{1,0:T(8,128)(2,1)}, bf16[1024,256]{1,0:T(8,128)(2,1)}, u32[]{:S(2)}, u32[]{:S(2)}) collective-permute-start(bf16[1024,256]{1,0:T(8,128)(2,1)} %get-tuple-element.432), channel_id=1, source_target_pairs={{4,0},{0,4},{5,1},{1,5},{6,2},{2,6},{7,3},{3,7},{12,8},{8,12},{13,... | collective-permute-start | bytes 1572872 | tf_op jit(solution)/shard_map/ppermute | solution.py:36
  129.9 14.7 %collective-permute-start.40 = (bf16[256,1024]{1,0:T(8,128)(2,1)}, bf16[256,1024]{1,0:T(8,128)(2,1)}, u32[]{:S(2)}, u32[]{:S(2)}) collective-permute-start(bf16[256,1024]{1,0:T(8,128)(2,1)} %collective-permute-done.25.refs_7_.refs_5_), channel_id=1, source_target_pairs={{0,8},{8,0},{16,24},{24,16},{1,9},{9,1},{17,25},{25,17},{2,10},{10... | collective-permute-start | bytes 1572872 | tf_op jit(solution)/shard_map/ppermute | solution.py:191
  147.3 14.2 %collective-permute-start.38 = (bf16[1024,256]{1,0:T(8,128)(2,1)}, bf16[1024,256]{1,0:T(8,128)(2,1)S(1)}, u32[]{:S(2)}, u32[]{:S(2)}) collective-permute-start(bf16[1024,256]{1,0:T(8,128)(2,1)} %collective-permute-done.37.refs_7_.refs_8_), channel_id=1, source_target_pairs={{0,8},{8,0},{16,24},{24,16},{1,9},{9,1},{17,25},{25,17},{2,10},{10... | collective-permute-start | bytes 1572872 | tf_op jit(solution)/shard_map/ppermute | solution.py:191
  148.2 14.0 %collective-permute-start.36 = (bf16[256,1024]{1,0:T(8,128)(2,1)S(1)}, bf16[256,1024]{1,0:T(8,128)(2,1)S(1)}, u32[]{:S(2)}, u32[]{:S(2)}) collective-permute-start(bf16[256,1024]{1,0:T(8,128)(2,1)S(1)} %get-tuple-element.430), channel_id=1, source_target_pairs={{0,2},{2,0},{1,3},{3,1},{4,6},{6,4},{5,7},{7,5},{8,10},{10,8},{9,1... | collective-permute-start | bytes 1572872 | tf_op jit(solution)/shard_map/ppermute | solution.py:31
  160.3 16.8 %collective-permute-start.50 = (bf16[320,1024]{1,0:T(8,128)(2,1)S(1)}, bf16[320,1024]{1,0:T(8,128)(2,1)S(1)}, u32[]{:S(2)}, u32[]{:S(2)}) collective-permute-start(bf16[320,1024]{1,0:T(8,128)(2,1)S(1)} %get-tuple-element.455), channel_id=1, source_target_pairs={{0,2},{2,0},{1,3},{3,1},{4,6},{6,4},{5,7},{7,5},{8,10},{10,8},{9,1... | collective-permute-start | bytes 1966088 | tf_op jit(solution)/shard_map/ppermute | solution.py:31
  178.6 14.8 %collective-permute-start.49 = (bf16[256,1024]{1,0:T(8,128)(2,1)S(1)}, bf16[256,1024]{1,0:T(8,128)(2,1)S(1)}, u32[]{:S(2)}, u32[]{:S(2)}) collective-permute-start(bf16[256,1024]{1,0:T(8,128)(2,1)S(1)} %get-tuple-element.453), channel_id=1, source_target_pairs={{0,2},{2,0},{1,3},{3,1},{4,6},{6,4},{5,7},{7,5},{8,10},{10,8},{9,1... | collective-permute-start | bytes 1572872 | tf_op jit(solution)/shard_map/ppermute | solution.py:31
  187.2 19.3 %collective-permute-start.55 = (bf16[320,1024]{1,0:T(8,128)(2,1)S(1)}, bf16[320,1024]{1,0:T(8,128)(2,1)S(1)}, u32[]{:S(2)}, u32[]{:S(2)}) collective-permute-start(bf16[320,1024]{1,0:T(8,128)(2,1)S(1)} %get-tuple-element.468), channel_id=1, source_target_pairs={{0,2},{2,0},{1,3},{3,1},{4,6},{6,4},{5,7},{7,5},{8,10},{10,8},{9,1... | collective-permute-start | bytes 1966088 | tf_op jit(solution)/shard_map/ppermute | solution.py:31
  210.3 14.3 %collective-permute-start.61 = (bf16[256,1024]{1,0:T(8,128)(2,1)S(1)}, bf16[256,1024]{1,0:T(8,128)(2,1)S(1)}, u32[]{:S(2)}, u32[]{:S(2)}) collective-permute-start(bf16[256,1024]{1,0:T(8,128)(2,1)S(1)} %get-tuple-element.485), channel_id=1, source_target_pairs={{0,2},{2,0},{1,3},{3,1},{4,6},{6,4},{5,7},{7,5},{8,10},{10,8},{9,1... | collective-permute-start | bytes 1572872 | tf_op jit(solution)/shard_map/ppermute | solution.py:31
  218.2 21.2 %collective-permute-start.70 = (bf16[512,768]{1,0:T(8,128)(2,1)S(1)}, bf16[512,768]{1,0:T(8,128)(2,1)S(1)}, u32[]{:S(2)}, u32[]{:S(2)}) collective-permute-start(bf16[512,768]{1,0:T(8,128)(2,1)S(1)} %bitcast.46), channel_id=1, source_target_pairs={{0,4},{4,0},{1,5},{5,1},{2,6},{6,2},{3,7},{7,3},{8,12},{12,8},{9,1... | collective-permute-start | bytes 2359304 | tf_op jit(solution)/shard_map/ppermute | solution.py:41
  221.3 21.4 %collective-permute-start.72 = (bf16[320,1024]{1,0:T(8,128)(2,1)S(1)}, bf16[320,1024]{1,0:T(8,128)(2,1)S(1)}, u32[]{:S(2)}, u32[]{:S(2)}) collective-permute-start(bf16[320,1024]{1,0:T(8,128)(2,1)S(1)} %get-tuple-element.526), channel_id=1, source_target_pairs={{0,2},{2,0},{1,3},{3,1},{4,6},{6,4},{5,7},{7,5},{8,10},{10,8},{9,1... | collective-permute-start | bytes 1966088 | tf_op jit(solution)/shard_map/ppermute | solution.py:31
  235.9 20.0 %collective-permute-start.77 = (bf16[512,768]{1,0:T(8,128)(2,1)S(1)}, bf16[512,768]{1,0:T(8,128)(2,1)S(1)}, u32[]{:S(2)}, u32[]{:S(2)}) collective-permute-start(bf16[512,768]{1,0:T(8,128)(2,1)S(1)} %bitcast.43), channel_id=1, source_target_pairs={{0,4},{4,0},{1,5},{5,1},{2,6},{6,2},{3,7},{7,3},{8,12},{12,8},{9,1... | collective-permute-start | bytes 2359304 | tf_op jit(solution)/shard_map/ppermute | solution.py:41
  239.6 19.6 %collective-permute-start.78 = (bf16[512,768]{1,0:T(8,128)(2,1)S(1)}, bf16[512,768]{1,0:T(8,128)(2,1)S(1)}, u32[]{:S(2)}, u32[]{:S(2)}) collective-permute-start(bf16[512,768]{1,0:T(8,128)(2,1)S(1)} %get-tuple-element.544.refs_2_), channel_id=1, source_target_pairs={{0,8},{24,16},{1,9},{25,17},{2,10},{26,18},{3,11},{27,19},{4,12},{... | collective-permute-start | bytes 2359304 | tf_op jit(solution)/shard_map/ppermute | solution.py:788
  244.3 21.0 %collective-permute-start.71 = (bf16[256,1024]{1,0:T(8,128)(2,1)S(1)}, bf16[256,1024]{1,0:T(8,128)(2,1)S(1)}, u32[]{:S(2)}, u32[]{:S(2)}) collective-permute-start(bf16[256,1024]{1,0:T(8,128)(2,1)S(1)} %get-tuple-element.522), channel_id=1, source_target_pairs={{0,2},{2,0},{1,3},{3,1},{4,6},{6,4},{5,7},{7,5},{8,10},{10,8},{9,1... | collective-permute-start | bytes 1572872 | tf_op jit(solution)/shard_map/ppermute | solution.py:31
  254.0 10.2 %collective-permute-start.75 = (bf16[160,1024]{1,0:T(8,128)(2,1)S(1)}, bf16[160,1024]{1,0:T(8,128)(2,1)S(1)}, u32[]{:S(2)}, u32[]{:S(2)}) collective-permute-start(bf16[160,1024]{1,0:T(8,128)(2,1)S(1)} %get-tuple-element.540), channel_id=1, source_target_pairs={{0,1},{1,0},{2,3},{3,2},{4,5},{5,4},{6,7},{7,6},{8,9},{9,8},{10,11... | collective-permute-start | bytes 983048 | tf_op jit(solution)/shard_map/ppermute | solution.py:27
  254.2 10.9 %collective-permute-start.76 = (bf16[160,1024]{1,0:T(8,128)(2,1)S(1)}, bf16[160,1024]{1,0:T(8,128)(2,1)S(1)}, u32[]{:S(2)}, u32[]{:S(2)}) collective-permute-start(bf16[160,1024]{1,0:T(8,128)(2,1)S(1)} %get-tuple-element.541), channel_id=1, source_target_pairs={{0,1},{1,0},{2,3},{3,2},{4,5},{5,4},{6,7},{7,6},{8,9},{9,8},{10,11... | collective-permute-start | bytes 983048 | tf_op jit(solution)/shard_map/ppermute | solution.py:27
  255.9 19.6 %collective-permute-start.84 = (bf16[512,768]{1,0:T(8,128)(2,1)S(1)}, bf16[512,768]{1,0:T(8,128)(2,1)S(1)}, u32[]{:S(2)}, u32[]{:S(2)}) collective-permute-start(bf16[512,768]{1,0:T(8,128)(2,1)S(1)} %bitcast.44), channel_id=1, source_target_pairs={{0,4},{4,0},{1,5},{5,1},{2,6},{6,2},{3,7},{7,3},{8,12},{12,8},{9,1... | collective-permute-start | bytes 2359304 | tf_op jit(solution)/shard_map/ppermute | solution.py:41
  259.6 20.4 %collective-permute-start.85 = (bf16[512,768]{1,0:T(8,128)(2,1)S(1)}, bf16[512,768]{1,0:T(8,128)(2,1)S(1)}, u32[]{:S(2)}, u32[]{:S(2)}) collective-permute-start(bf16[512,768]{1,0:T(8,128)(2,1)S(1)} %get-tuple-element.566.refs_2_), channel_id=1, source_target_pairs={{0,8},{24,16},{1,9},{25,17},{2,10},{26,18},{3,11},{27,19},{4,12},{... | collective-permute-start | bytes 2359304 | tf_op jit(solution)/shard_map/ppermute | solution.py:788
  264.2 18.7 %collective-permute-start.86 = (bf16[512,768]{1,0:T(8,128)(2,1)S(1)}, bf16[512,768]{1,0:T(8,128)(2,1)S(1)}, u32[]{:S(2)}, u32[]{:S(2)}) collective-permute-start(bf16[512,768]{1,0:T(8,128)(2,1)S(1)} %get-tuple-element.567.refs_4_), channel_id=1, source_target_pairs={{8,16},{16,8},{9,17},{17,9},{10,18},{18,10},{11,19},{19,11},{12,20... | collective-permute-start | bytes 2359304 | tf_op jit(solution)/shard_map/ppermute | solution.py:784
  267.9 19.4 %collective-permute-start.81 = (bf16[320,1024]{1,0:T(8,128)(2,1)S(1)}, bf16[320,1024]{1,0:T(8,128)(2,1)S(1)}, u32[]{:S(2)}, u32[]{:S(2)}) collective-permute-start(bf16[320,1024]{1,0:T(8,128)(2,1)S(1)} %get-tuple-element.557), channel_id=1, source_target_pairs={{0,2},{2,0},{1,3},{3,1},{4,6},{6,4},{5,7},{7,5},{8,10},{10,8},{9,1... | collective-permute-start | bytes 1966088 | tf_op jit(solution)/shard_map/ppermute | solution.py:31
  272.6 13.5 %collective-permute-start.82 = (bf16[128,1024]{1,0:T(8,128)(2,1)S(1)}, bf16[128,1024]{1,0:T(8,128)(2,1)S(1)}, u32[]{:S(2)}, u32[]{:S(2)}) collective-permute-start(bf16[128,1024]{1,0:T(8,128)(2,1)S(1)} %get-tuple-element.562), channel_id=1, source_target_pairs={{0,1},{1,0},{2,3},{3,2},{4,5},{5,4},{6,7},{7,6},{8,9},{9,8},{10,11... | collective-permute-start | bytes 786440 | tf_op jit(solution)/shard_map/ppermute | solution.py:27
  275.6 11.5 %collective-permute-start.83 = (bf16[128,1024]{1,0:T(8,128)(2,1)S(1)}, bf16[128,1024]{1,0:T(8,128)(2,1)S(1)}, u32[]{:S(2)}, u32[]{:S(2)}) collective-permute-start(bf16[128,1024]{1,0:T(8,128)(2,1)S(1)} %get-tuple-element.563), channel_id=1, source_target_pairs={{0,1},{1,0},{2,3},{3,2},{4,5},{5,4},{6,7},{7,6},{8,9},{9,8},{10,11... | collective-permute-start | bytes 786440 | tf_op jit(solution)/shard_map/ppermute | solution.py:27
  280.1 17.9 %collective-permute-start.93 = (bf16[512,768]{1,0:T(8,128)(2,1)S(1)}, bf16[512,768]{1,0:T(8,128)(2,1)S(1)}, u32[]{:S(2)}, u32[]{:S(2)}) collective-permute-start(bf16[512,768]{1,0:T(8,128)(2,1)S(1)} %bitcast.45), channel_id=1, source_target_pairs={{0,4},{4,0},{1,5},{5,1},{2,6},{6,2},{3,7},{7,3},{8,12},{12,8},{9,1... | collective-permute-start | bytes 2359304 | tf_op jit(solution)/shard_map/ppermute | solution.py:41
  283.6 18.0 %collective-permute-start.92 = (bf16[512,768]{1,0:T(8,128)(2,1)S(1)}, bf16[512,768]{1,0:T(8,128)(2,1)S(1)}, u32[]{:S(2)}, u32[]{:S(2)}) collective-permute-start(bf16[512,768]{1,0:T(8,128)(2,1)S(1)} %get-tuple-element.588), channel_id=1, source_target_pairs={{0,8},{8,0},{16,24},{24,16},{1,9},{9,1},{17,25},{25,17},{2,10},{10... | collective-permute-start | bytes 2359304 | tf_op jit(solution)/shard_map/ppermute | solution.py:786
  286.1 17.0 %collective-permute-start.94 = (bf16[512,768]{1,0:T(8,128)(2,1)S(1)}, bf16[512,768]{1,0:T(8,128)(2,1)S(1)}, u32[]{:S(2)}, u32[]{:S(2)}) collective-permute-start(bf16[512,768]{1,0:T(8,128)(2,1)S(1)} %get-tuple-element.592.refs_4_), channel_id=1, source_target_pairs={{8,16},{16,8},{9,17},{17,9},{10,18},{18,10},{11,19},{19,11},{12,20... | collective-permute-start | bytes 2359304 | tf_op jit(solution)/shard_map/ppermute | solution.py:784
  295.0 12.0 %collective-permute-start.90 = (bf16[160,1024]{1,0:T(8,128)(2,1)S(1)}, bf16[160,1024]{1,0:T(8,128)(2,1)S(1)}, u32[]{:S(2)}, u32[]{:S(2)}) collective-permute-start(bf16[160,1024]{1,0:T(8,128)(2,1)S(1)} %get-tuple-element.585), channel_id=1, source_target_pairs={{0,1},{1,0},{2,3},{3,2},{4,5},{5,4},{6,7},{7,6},{8,9},{9,8},{10,11... | collective-permute-start | bytes 983048 | tf_op jit(solution)/shard_map/ppermute | solution.py:27
  295.2 14.7 %collective-permute-start.89 = (bf16[256,1024]{1,0:T(8,128)(2,1)S(1)}, bf16[256,1024]{1,0:T(8,128)(2,1)S(1)}, u32[]{:S(2)}, u32[]{:S(2)}) collective-permute-start(bf16[256,1024]{1,0:T(8,128)(2,1)S(1)} %get-tuple-element.580), channel_id=1, source_target_pairs={{0,2},{2,0},{1,3},{3,1},{4,6},{6,4},{5,7},{7,5},{8,10},{10,8},{9,1... | collective-permute-start | bytes 1572872 | tf_op jit(solution)/shard_map/ppermute | solution.py:31
  297.9 11.8 %collective-permute-start.91 = (bf16[160,1024]{1,0:T(8,128)(2,1)S(1)}, bf16[160,1024]{1,0:T(8,128)(2,1)S(1)}, u32[]{:S(2)}, u32[]{:S(2)}) collective-permute-start(bf16[160,1024]{1,0:T(8,128)(2,1)S(1)} %get-tuple-element.586), channel_id=1, source_target_pairs={{0,1},{1,0},{2,3},{3,2},{4,5},{5,4},{6,7},{7,6},{8,9},{9,8},{10,11... | collective-permute-start | bytes 983048 | tf_op jit(solution)/shard_map/ppermute | solution.py:27
  301.6 20.2 %collective-permute-start.101 = (bf16[512,768]{1,0:T(8,128)(2,1)S(1)}, bf16[512,768]{1,0:T(8,128)(2,1)S(1)}, u32[]{:S(2)}, u32[]{:S(2)}) collective-permute-start(bf16[512,768]{1,0:T(8,128)(2,1)S(1)} %bitcast.42), channel_id=1, source_target_pairs={{0,4},{4,0},{1,5},{5,1},{2,6},{6,2},{3,7},{7,3},{8,12},{12,8},{9,1... | collective-permute-start | bytes 2359304 | tf_op jit(solution)/shard_map/ppermute | solution.py:41
  303.8 19.2 %collective-permute-start.100 = (bf16[512,768]{1,0:T(8,128)(2,1)S(1)}, bf16[512,768]{1,0:T(8,128)(2,1)S(1)}, u32[]{:S(2)}, u32[]{:S(2)}) collective-permute-start(bf16[512,768]{1,0:T(8,128)(2,1)S(1)} %get-tuple-element.614), channel_id=1, source_target_pairs={{0,8},{8,0},{16,24},{24,16},{1,9},{9,1},{17,25},{25,17},{2,10},{10... | collective-permute-start | bytes 2359304 | tf_op jit(solution)/shard_map/ppermute | solution.py:786
  307.0 16.0 %collective-permute-start.102 = (bf16[512,768]{1,0:T(8,128)(2,1)S(1)}, bf16[512,768]{1,0:T(8,128)(2,1)S(1)}, u32[]{:S(2)}, u32[]{:S(2)}) collective-permute-start(bf16[512,768]{1,0:T(8,128)(2,1)S(1)} %get-tuple-element.619.refs_4_), channel_id=1, source_target_pairs={{8,16},{16,8},{9,17},{17,9},{10,18},{18,10},{11,19},{19,11},{12,20... | collective-permute-start | bytes 2359304 | tf_op jit(solution)/shard_map/ppermute | solution.py:784
  312.4 17.4 %collective-permute-start.97 = (bf16[320,1024]{1,0:T(8,128)(2,1)S(1)}, bf16[320,1024]{1,0:T(8,128)(2,1)S(1)}, u32[]{:S(2)}, u32[]{:S(2)}) collective-permute-start(bf16[320,1024]{1,0:T(8,128)(2,1)S(1)} %get-tuple-element.603), channel_id=1, source_target_pairs={{0,2},{2,0},{1,3},{3,1},{4,6},{6,4},{5,7},{7,5},{8,10},{10,8},{9,1... | collective-permute-start | bytes 1966088 | tf_op jit(solution)/shard_map/ppermute | solution.py:31
  321.8 23.5 %collective-permute-start.106 = (bf16[512,768]{1,0:T(8,128)(2,1)S(1)}, bf16[512,768]{1,0:T(8,128)(2,1)S(1)}, u32[]{:S(2)}, u32[]{:S(2)}) collective-permute-start(bf16[512,768]{1,0:T(8,128)(2,1)S(1)} %bitcast.40), channel_id=1, source_target_pairs={{0,4},{4,0},{1,5},{5,1},{2,6},{6,2},{3,7},{7,3},{8,12},{12,8},{9,1... | collective-permute-start | bytes 2359304 | tf_op jit(solution)/shard_map/ppermute | solution.py:41
  323.7 21.7 %collective-permute-start.107 = (bf16[512,768]{1,0:T(8,128)(2,1)S(1)}, bf16[512,768]{1,0:T(8,128)(2,1)S(1)}, u32[]{:S(2)}, u32[]{:S(2)}) collective-permute-start(bf16[512,768]{1,0:T(8,128)(2,1)S(1)} %get-tuple-element.652), channel_id=1, source_target_pairs={{0,8},{8,0},{16,24},{24,16},{1,9},{9,1},{17,25},{25,17},{2,10},{10... | collective-permute-start | bytes 2359304 | tf_op jit(solution)/shard_map/ppermute | solution.py:786
  327.2 18.1 %collective-permute-start.108 = (bf16[512,768]{1,0:T(8,128)(2,1)S(1)}, bf16[512,768]{1,0:T(8,128)(2,1)S(1)}, u32[]{:S(2)}, u32[]{:S(2)}) collective-permute-start(bf16[512,768]{1,0:T(8,128)(2,1)S(1)} %get-tuple-element.653.refs_4_), channel_id=1, source_target_pairs={{8,16},{16,8},{9,17},{17,9},{10,18},{18,10},{11,19},{19,11},{12,20... | collective-permute-start | bytes 2359304 | tf_op jit(solution)/shard_map/ppermute | solution.py:784
  341.2 9.3 %collective-permute-start.112 = (bf16[160,1024]{1,0:T(8,128)(2,1)S(1)}, bf16[160,1024]{1,0:T(8,128)(2,1)S(1)}, u32[]{:S(2)}, u32[]{:S(2)}) collective-permute-start(bf16[160,1024]{1,0:T(8,128)(2,1)S(1)} %get-tuple-element.671), channel_id=1, source_target_pairs={{0,1},{1,0},{2,3},{3,2},{4,5},{5,4},{6,7},{7,6},{8,9},{9,8},{10,11... | collective-permute-start | bytes 983048 | tf_op jit(solution)/shard_map/ppermute | solution.py:27
  342.9 25.0 %collective-permute-start.105 = (bf16[512,768]{1,0:T(8,128)(2,1)S(1)}, bf16[512,768]{1,0:T(8,128)(2,1)S(1)}, u32[]{:S(2)}, u32[]{:S(2)}) collective-permute-start(bf16[512,768]{1,0:T(8,128)(2,1)S(1)} %bitcast.41), channel_id=1, source_target_pairs={{0,4},{4,0},{1,5},{5,1},{2,6},{6,2},{3,7},{7,3},{8,12},{12,8},{9,1... | collective-permute-start | bytes 2359304 | tf_op jit(solution)/shard_map/ppermute | solution.py:41
  346.1 20.6 %collective-permute-start.109 = (bf16[512,768]{1,0:T(8,128)(2,1)S(1)}, bf16[512,768]{1,0:T(8,128)(2,1)S(1)}, u32[]{:S(2)}, u32[]{:S(2)}) collective-permute-start(bf16[512,768]{1,0:T(8,128)(2,1)S(1)} %get-tuple-element.656), channel_id=1, source_target_pairs={{0,8},{8,0},{16,24},{24,16},{1,9},{9,1},{17,25},{25,17},{2,10},{10... | collective-permute-start | bytes 2359304 | tf_op jit(solution)/shard_map/ppermute | solution.py:786
  349.5 18.5 %collective-permute-start.110 = (bf16[512,768]{1,0:T(8,128)(2,1)S(1)}, bf16[512,768]{1,0:T(8,128)(2,1)S(1)}, u32[]{:S(2)}, u32[]{:S(2)}) collective-permute-start(bf16[512,768]{1,0:T(8,128)(2,1)S(1)} %get-tuple-element.657.refs_4_), channel_id=1, source_target_pairs={{8,16},{16,8},{9,17},{17,9},{10,18},{18,10},{11,19},{19,11},{12,20... | collective-permute-start | bytes 2359304 | tf_op jit(solution)/shard_map/ppermute | solution.py:784
  350.4 22.4 %collective-permute-start.60 = (bf16[576,1024]{1,0:T(8,128)(2,1)S(1)}, bf16[576,1024]{1,0:T(8,128)(2,1)S(1)}, u32[]{:S(2)}, u32[]{:S(2)}) collective-permute-start(bf16[576,1024]{1,0:T(8,128)(2,1)S(1)} %constant_dynamic-update-slice_fusion.refs_0_), channel_id=1, source_target_pairs={{0,1},{1,0},{2,3},{3,2},{4,5},{5,4},{6,7},{7,6},{8,9},{9,8},{10,11... | collective-permute-start | bytes 3538952 | tf_op jit(solution)/shard_map/ppermute | solution.py:27
  357.9 30.9 %collective-permute-start.115 = (bf16[528,768]{1,0:T(8,128)(2,1)S(1)}, bf16[528,768]{1,0:T(8,128)(2,1)S(1)}, u32[]{:S(2)}, u32[]{:S(2)}) collective-permute-start(bf16[528,768]{1,0:T(8,128)(2,1)S(1)} %bitcast.39), channel_id=1, source_target_pairs={{0,4},{4,0},{1,5},{5,1},{2,6},{6,2},{3,7},{7,3},{8,12},{12,8},{9,1... | collective-permute-start | bytes 2433032 | tf_op jit(solution)/shard_map/ppermute | solution.py:41
  368.7 18.6 %collective-permute-start.116 = (bf16[512,768]{1,0:T(8,128)(2,1)S(1)}, bf16[512,768]{1,0:T(8,128)(2,1)S(1)}, u32[]{:S(2)}, u32[]{:S(2)}) collective-permute-start(bf16[512,768]{1,0:T(8,128)(2,1)S(1)} %get-tuple-element.690), channel_id=1, source_target_pairs={{0,8},{8,0},{16,24},{24,16},{1,9},{9,1},{17,25},{25,17},{2,10},{10... | collective-permute-start | bytes 2359304 | tf_op jit(solution)/shard_map/ppermute | solution.py:786
  371.0 17.8 %collective-permute-start.117 = (bf16[512,768]{1,0:T(8,128)(2,1)S(1)}, bf16[512,768]{1,0:T(8,128)(2,1)S(1)}, u32[]{:S(2)}, u32[]{:S(2)}) collective-permute-start(bf16[512,768]{1,0:T(8,128)(2,1)S(1)} %get-tuple-element.691.refs_4_), channel_id=1, source_target_pairs={{8,16},{16,8},{9,17},{17,9},{10,18},{18,10},{11,19},{19,11},{12,20... | collective-permute-start | bytes 2359304 | tf_op jit(solution)/shard_map/ppermute | solution.py:784
  371.7 26.5 %collective-permute-start.118 = (bf16[320,1024]{1,0:T(8,128)(2,1)S(1)}, bf16[320,1024]{1,0:T(8,128)(2,1)S(1)}, u32[]{:S(2)}, u32[]{:S(2)}) collective-permute-start(bf16[320,1024]{1,0:T(8,128)(2,1)S(1)} %get-tuple-element.698), channel_id=1, source_target_pairs={{0,2},{2,0},{1,3},{3,1},{4,6},{6,4},{5,7},{7,5},{8,10},{10,8},{9,1... | collective-permute-start | bytes 1966088 | tf_op jit(solution)/shard_map/ppermute | solution.py:31
  372.8 25.1 %collective-permute-start.114 = (bf16[256,1024]{1,0:T(8,128)(2,1)S(1)}, bf16[256,1024]{1,0:T(8,128)(2,1)S(1)}, u32[]{:S(2)}, u32[]{:S(2)}) collective-permute-start(bf16[256,1024]{1,0:T(8,128)(2,1)S(1)} %get-tuple-element.685), channel_id=1, source_target_pairs={{0,2},{2,0},{1,3},{3,1},{4,6},{6,4},{5,7},{7,5},{8,10},{10,8},{9,1... | collective-permute-start | bytes 1572872 | tf_op jit(solution)/shard_map/ppermute | solution.py:31
  389.5 18.1 %collective-permute-start.120 = (bf16[528,768]{1,0:T(8,128)(2,1)S(1)}, bf16[528,768]{1,0:T(8,128)(2,1)S(1)}, u32[]{:S(2)}, u32[]{:S(2)}) collective-permute-start(bf16[528,768]{1,0:T(8,128)(2,1)S(1)} %get-tuple-element.703), channel_id=1, source_target_pairs={{0,8},{8,0},{16,24},{24,16},{1,9},{9,1},{17,25},{25,17},{2,10},{10... | collective-permute-start | bytes 2433032 | tf_op jit(solution)/shard_map/ppermute | solution.py:786
  391.7 17.2 %collective-permute-start.121 = (bf16[512,768]{1,0:T(8,128)(2,1)S(1)}, bf16[512,768]{1,0:T(8,128)(2,1)S(1)}, u32[]{:S(2)}, u32[]{:S(2)}) collective-permute-start(bf16[512,768]{1,0:T(8,128)(2,1)S(1)} %get-tuple-element.704.refs_2_), channel_id=1, source_target_pairs={{8,16},{16,8},{9,17},{17,9},{10,18},{18,10},{11,19},{19,11},{12,20... | collective-permute-start | bytes 2359304 | tf_op jit(solution)/shard_map/ppermute | solution.py:784
  398.6 12.7 %collective-permute-start.119 = (bf16[576,1024]{1,0:T(8,128)(2,1)S(1)}, bf16[576,1024]{1,0:T(8,128)(2,1)S(1)}, u32[]{:S(2)}, u32[]{:S(2)}) collective-permute-start(bf16[576,1024]{1,0:T(8,128)(2,1)S(1)} %constant_dynamic-update-slice_fusion.4.refs_0_), channel_id=1, source_target_pairs={{0,1},{1,0},{2,3},{3,2},{4,5},{5,4},{6,7},{7,6},{8,9},{9,8},{10,11... | collective-permute-start | bytes 3538952 | tf_op jit(solution)/shard_map/ppermute | solution.py:27
  409.3 21.0 %collective-permute-start.122 = (bf16[528,768]{1,0:T(8,128)(2,1)S(1)}, bf16[528,768]{1,0:T(8,128)(2,1)S(1)}, u32[]{:S(2)}, u32[]{:S(2)}) collective-permute-start(bf16[528,768]{1,0:T(8,128)(2,1)S(1)} %get-tuple-element.712.refs_0_), channel_id=1, source_target_pairs={{8,16},{16,8},{9,17},{17,9},{10,18},{18,10},{11,19},{19,11},{12,20... | collective-permute-start | bytes 2433032 | tf_op jit(solution)/shard_map/ppermute | solution.py:784
  410.0 18.9 %collective-permute-start.123 = (bf16[512,768]{1,0:T(8,128)(2,1)S(1)}, bf16[512,768]{1,0:T(8,128)(2,1)S(1)}, u32[]{:S(2)}, u32[]{:S(2)}) collective-permute-start(bf16[512,768]{1,0:T(8,128)(2,1)S(1)} %get-tuple-element.713.refs_0_), channel_id=1, source_target_pairs={{8,0},{16,24},{9,1},{17,25},{10,2},{18,26},{11,3},{19,27},{12,4},{... | collective-permute-start | bytes 2359304 | tf_op jit(solution)/shard_map/ppermute | solution.py:790
  430.5 17.7 %collective-permute-start.124 = (bf16[528,768]{1,0:T(8,128)(2,1)S(1)}, bf16[528,768]{1,0:T(8,128)(2,1)S(1)}, u32[]{:S(2)}, u32[]{:S(2)}) collective-permute-start(bf16[528,768]{1,0:T(8,128)(2,1)S(1)} %get-tuple-element.718.refs_0_), channel_id=1, source_target_pairs={{8,0},{16,24},{9,1},{17,25},{10,2},{18,26},{11,3},{19,27},{12,4},{... | collective-permute-start | bytes 2433032 | tf_op jit(solution)/shard_map/ppermute | solution.py:790
  (213 other events, 928.4 us)

commit v6 on v5

--- a/solution.py
+++ b/solution.py
@@ -163,12 +163,12 @@
 
 
 class Weight:
-    def __init__(self, order, whole, layer, axis):
+    def __init__(self, order, whole, layer, axis, direct=False):
         self.order, self.whole, self.layer, self.axis = order, whole, layer, axis
         self.size = lax.axis_size(FSDP)
         shape = whole.shape[1:]
         width = shape[axis]
-        self.halved = self.size == 2 and lax.axis_size(DP) % 2 == 0 and width % 256 == 0
+        self.halved = not direct and self.size == 2 and lax.axis_size(DP) % 2 == 0 and width % 256 == 0
         self.widths = [width] + ([width // 2] * 2 if self.halved else [width] * (self.size - 1))
         self.shape = shape
 
@@ -1001,7 +1001,7 @@
     weights = [
         [
             Weight(order, w_qkv, layer, 1),
-            Weight(order, w_out, layer, 1),
+            Weight(order, w_out, layer, 1, layer > 0),
             Weight(order, w_up, layer, 0),
             Weight(order, w_down, layer, 1),
         ]

time: 459 us -> 464 us (1.011)
  waiting for transfers between devices: 140 us -> 147 us
    unnamed x312 -> x304, local copies, waits for them, and re-layouts: 42.9 us -> 42.5 us
  transfers between devices with their start and end apart: 125 -> 124, of which waited for: 60 -> 64; matrix products, arithmetic and copies ran while one was open for 0% -> 0% of each run, Pallas kernels for 34% -> 33%
where the time goes in v6:
time: 464 us; the launch traced here: 458 us
  Pallas kernels  163 us (35%)
  waiting for transfers between devices  147 us (32%)
  starting transfers between devices  99 us (21%)
  local copies, waits for them, and re-layouts  46 us (10%)
    pallas_call x95, Pallas kernels, call(): pl.pallas_call(kernel, grid=grid, in_specs=in_specs, out_specs=[*out_spec...  163 us
    unnamed x304, local copies, waits for them, and re-layouts  42.5 us
    ppermute x2, waiting for transfers between devices, step(): older['back'] = lax.ppermute(older['total'], DP, [(1, 0), (2, 3)])  34.8 us
    ppermute x6, waiting for transfers between devices, step(): lax.ppermute(found[-1], DP, [(0, 1), (1, 0), (2, 3), (3, 2)])  30.7 us
    ppermute x65, waiting for transfers between devices, to_core(): return lax.ppermute(value, TENSOR, CORE_SWAP)  25.1 us
    ppermute x9, waiting for transfers between devices, from_fsdp(): lax.ppermute(value, FSDP, [((i + step) % size, i) for i in range(size)])  24.1 us
    ppermute x17, waiting for transfers between devices, to_chip(): return lax.ppermute(value, TENSOR, CHIP_SWAP)  22.8 us
    ppermute x6, starting transfers between devices, step(): lax.ppermute(found[-1], DP, [(0, 1), (1, 0), (2, 3), (3, 2)])  18.1 us
  transfers between devices with their start and end apart: 124, of which 64 were waited for; matrix products, arithmetic and copies ran while one was open for 0% of the time, Pallas kernels for 33%

profile of v6, /device:TPU:0, one launch (start us, length us, event | category | flops | bytes accessed | tf_op | source)
XLA Modules:
  0.0 458.2 jit_solution(16336126021276484176)
XLA Ops:
  4.0 3.0 collective-permute-start
  7.0 9.1 %collective-permute-done.refs_4_.refs_1_.refs_3_.refs_5_ = bf16[3,256,256]{2,1,0:T(8,128)(2,1)S(1)} collective-permute-done((bf16[3,256,256]{2,1,0:T(8,128)(2,1)S(1)}, bf16[3,256,256]{2,1,0:T(8,128)(2,1)S(1)}, u32[]{:S(2)}, u32[]{:S(2)}) %collective-permute-start) | collective-permute-done | bytes 393248 | tf_op jit(solution)/shard_map/ppermute | solution.py:36
  16.1 1.8 collective-permute-start.1
  17.9 1.5 collective-permute-start.2
  19.4 1.7 copy-done.81
  33.6 1.6 collective-permute-start.4
  35.2 2.2 collective-permute-done.4
  37.9 1.8 copy-done.30
  40.6 1.6 collective-permute-start.8
  45.5 5.5 %attention_forward.4 = (bf16[128,1024]{1,0:T(8,128)(2,1)S(1)}, bf16[128,1024]{1,0:T(8,128)(2,1)S(1)}, bf16[256,1024]{1,0:T(8,128)(2,1)S(1)}, bf16[512,768]{1,0:T...) custom-call(bf16[256,1024]{1,0:T(8,128)(2,1)S(1)} %copy-done.32, ...), custom_call_target="tpu_custom_call" | custom-call | tf_op jit(solution)/shard_map/attention_forward/pallas_call | solution.py:131
  61.5 7.9 %attention_forward.5 = (bf16[160,1024]{1,0:T(8,128)(2,1)S(1)}, bf16[160,1024]{1,0:T(8,128)(2,1)}, bf16[320,1024]{1,0:T(8,128)(2,1)S(1)}, bf16[640,768]{1,0:T(8,1...) custom-call(bf16[320,1024]{1,0:T(8,128)(2,1)S(1)} %copy-done.19, ...), custom_call_target="tpu_custom_call" | custom-call | tf_op jit(solution)/shard_map/attention_forward/pallas_call | solution.py:131
  75.2 1.5 collective-permute-start.11
  79.9 1.5 collective-permute-start.24
  81.5 5.0 %collective-permute-done.11.refs_8_.refs_5_ = bf16[3,256,256]{2,1,0:T(8,128)(2,1)} collective-permute-done((bf16[3,256,256]{2,1,0:T(8,128)(2,1)}, bf16[3,256,256]{2,1,0:T(8,128)(2,1)}, u32[]{:S(2)}, u32[]{:S(2)}) %collective-permute-start.11) | collective-permute-done | bytes 393248 | tf_op jit(solution)/shard_map/ppermute | solution.py:36
  90.5 1.7 norm_forward.8
  94.9 4.1 feed_forward.4
  99.7 1.5 collective-permute-start.25
  101.4 6.7 %collective-permute-done.25.refs_6_.refs_8_ = bf16[256,512]{1,0:T(8,128)(2,1)S(1)} collective-permute-done((bf16[256,512]{1,0:T(8,128)(2,1)S(1)}, bf16[256,512]{1,0:T(8,128)(2,1)S(1)}, u32[]{:S(2)}, u32[]{:S(2)}) %collective-permute-start.25) | collective-permute-done | bytes 262176 | tf_op jit(solution)/shard_map/ppermute | solution.py:36
  108.2 2.1 norm_forward.9
  112.5 1.5 collective-permute-start.23
  115.6 5.1 %feed_forward.5 = (bf16[160,1024]{1,0:T(8,128)(2,1)S(1)}, bf16[160,1024]{1,0:T(8,128)(2,1)S(1)}, bf16[640,1024]{1,0:T(8,128)(2,1)S(1)}, bf16[640,1024]{1,0:T(8,1...) custom-call(bf16[160,1024]{1,0:T(8,128)(2,1)S(1)} %get-tuple-element.412.refs_0_.refs_14_.refs_4_, ...), custom_call_target="tpu_custom_call" | custom-call | tf_op jit(solution)/shard_map/feed_forward/pallas_call | solution.py:131
  137.9 6.4 %attention_forward.6 = (bf16[128,1024]{1,0:T(8,128)(2,1)S(1)}, bf16[128,1024]{1,0:T(8,128)(2,1)S(1)}, bf16[256,1024]{1,0:T(8,128)(2,1)S(1)}, bf16[512,768]{1,0:T...) custom-call(bf16[128,1024]{1,0:T(8,128)(2,1)} %get-tuple-element.420.refs_0_,, ...), custom_call_target="tpu_custom_call" | custom-call | tf_op jit(solution)/shard_map/attention_forward/pallas_call | solution.py:131
  146.5 2.1 norm_forward.11
  151.6 7.6 %attention_forward.7 = (bf16[160,1024]{1,0:T(8,128)(2,1)S(1)}, bf16[160,1024]{1,0:T(8,128)(2,1)S(1)}, bf16[320,1024]{1,0:T(8,128)(2,1)S(1)}, bf16[640,768]{1,0:T...) custom-call(bf16[160,1024]{1,0:T(8,128)(2,1)S(1)} %get-tuple-element, ...), custom_call_target="tpu_custom_call" | custom-call | tf_op jit(solution)/shard_map/attention_forward/pallas_call | solution.py:131
  166.7 4.0 feed_forward.6
  172.8 5.6 %collective-permute-done.49.refs_3_ = bf16[320,1024]{1,0:T(8,128)(2,1)S(1)} collective-permute-done((bf16[320,1024]{1,0:T(8,128)(2,1)S(1)}, bf16[320,1024]{1,0:T(8,128)(2,1)S(1)}, u32[]{:S(2)}, u32[]{:S(2)}) %collective-permute-start.49) | collective-permute-done | bytes 655392 | tf_op jit(solution)/shard_map/ppermute | solution.py:31
  181.5 4.7 %feed_forward.7 = (bf16[160,1024]{1,0:T(8,128)(2,1)S(1)}, bf16[160,1024]{1,0:T(8,128)(2,1)S(1)}, bf16[640,1024]{1,0:T(8,128)(2,1)S(1)}, bf16[640,1024]{1,0:T(8,1...) custom-call(bf16[160,1024]{1,0:T(8,128)(2,1)S(1)} %get-tuple-element.456.refs_0_.refs_14_.refs_4_, ...), custom_call_target="tpu_custom_call" | custom-call | tf_op jit(solution)/shard_map/feed_forward/pallas_call | solution.py:131
  189.5 5.2 %collective-permute-done.48.refs_3_ = bf16[256,1024]{1,0:T(8,128)(2,1)S(1)} collective-permute-done((bf16[256,1024]{1,0:T(8,128)(2,1)S(1)}, bf16[256,1024]{1,0:T(8,128)(2,1)S(1)}, u32[]{:S(2)}, u32[]{:S(2)}) %collective-permute-start.48) | collective-permute-done | bytes 524320 | tf_op jit(solution)/shard_map/ppermute | solution.py:31
  194.7 1.7 norm_forward.14
  199.0 3.9 feed_backward.4
  205.0 2.9 collective-permute-done.54.refs_3_
  207.8 1.9 norm_forward.15
  213.2 4.5 feed_backward.5
  219.5 1.6 collective-permute-start.69
  223.5 2.4 collective-permute-done.60.refs_3_
  228.7 6.6 %attention_backward.4 = (bf16[128,1024]{1,0:T(8,128)(2,1)S(1)}, bf16[128,1024]{1,0:T(8,128)(2,1)S(1)}, bf16[256,1024]{1,0:T(8,128)(2,1)S(1)}, bf16[512,768]{1,0:...) custom-call(bf16[128,1024]{1,0:T(8,128)(2,1)S(1)} %get-tuple-element.504.refs_0_.refs_10_, ...), custom_call_target="tpu_custom_call" | custom-call | tf_op jit(solution)/shard_map/attention_backward/pallas_call | solution.py:131
  237.2 2.1 collective-permute-start.76
  241.0 3.1 collective-permute-start.77
  247.5 8.1 %attention_backward.5 = (bf16[160,1024]{1,0:T(8,128)(2,1)S(1)}, bf16[160,1024]{1,0:T(8,128)(2,1)S(1)}, bf16[320,1024]{1,0:T(8,128)(2,1)S(1)}, bf16[640,768]{1,0:...) custom-call(bf16[160,1024]{1,0:T(8,128)(2,1)S(1)} %get-tuple-element.529.refs_0_.refs_14_, ...), custom_call_target="tpu_custom_call" | custom-call | tf_op jit(solution)/shard_map/attention_backward/pallas_call | solution.py:131
  261.2 4.6 collective-permute-start.84
  270.3 3.9 feed_backward.6
  274.2 2.9 collective-permute-done.83.refs_1_
  277.1 2.3 weight_grad.22
  279.5 2.2 collective-permute-done.84.refs_3_
  282.3 2.3 weight_grad.23
  285.3 2.5 collective-permute-start.91
  292.3 4.4 feed_backward.7
  297.8 1.7 collective-permute-done.92.refs_1_
  302.1 1.6 collective-permute-done.91.refs_3_.refs_1_
  306.6 5.8 %collective-permute-start.99 = (bf16[512,768]{1,0:T(8,128)(2,1)S(1)}, bf16[512,768]{1,0:T(8,128)(2,1)S(1)}, u32[]{:S(2)}, u32[]{:S(2)}) collective-permute-start(bf16[512,768]{1,0:T(8,128)(2,1)S(1)} %get-tuple-element.612), channel_id=1, source_target_pairs={{0,8},{8,0},{16,24},{24,16},{1,9},{9,1},{17,25},{25,17},{2,10},{10... | collective-permute-start | bytes 2359304 | tf_op jit(solution)/shard_map/ppermute | solution.py:786
  317.7 5.6 %attention_backward.6 = (bf16[128,1024]{1,0:T(8,128)(2,1)S(1)}, bf16[128,1024]{1,0:T(8,128)(2,1)S(1)}, bf16[256,1024]{1,0:T(8,128)(2,1)S(1)}, bf16[512,768]{1,0:...) custom-call(bf16[128,1024]{1,0:T(8,128)(2,1)S(1)} %get-tuple-element.599.refs_0_.refs_10_, ...), custom_call_target="tpu_custom_call" | custom-call | tf_op jit(solution)/shard_map/attention_backward/pallas_call | solution.py:131
  328.7 1.8 collective-permute-start.106
  337.3 7.1 %attention_backward.7 = (bf16[160,1024]{1,0:T(8,128)(2,1)S(1)}, bf16[160,1024]{1,0:T(8,128)(2,1)S(1)}, bf16[320,1024]{1,0:T(8,128)(2,1)S(1)}, bf16[640,768]{1,0:...) custom-call(bf16[160,1024]{1,0:T(8,128)(2,1)S(1)} %get-tuple-element.624.refs_0_.refs_14_, ...), custom_call_target="tpu_custom_call" | custom-call | tf_op jit(solution)/shard_map/attention_backward/pallas_call | solution.py:131
  349.4 2.6 collective-permute-start.108
  353.5 2.8 collective-permute-done.112.refs_2_
  362.7 6.1 %collective-permute-done.108.refs_1_.refs_3_ = bf16[512,768]{1,0:T(8,128)(2,1)S(1)} collective-permute-done((bf16[512,768]{1,0:T(8,128)(2,1)S(1)}, bf16[512,768]{1,0:T(8,128)(2,1)S(1)}, u32[]{:S(2)}, u32[]{:S(2)}) %collective-permute-start.108) | collective-permute-done | bytes 786464 | tf_op jit(solution)/shard_map/ppermute | solution.py:786
  370.8 2.4 collective-permute-start.115
  377.0 12.1 %collective-permute-done.115.refs_1_.refs_3_ = bf16[512,768]{1,0:T(8,128)(2,1)S(1)} collective-permute-done((bf16[512,768]{1,0:T(8,128)(2,1)S(1)}, bf16[512,768]{1,0:T(8,128)(2,1)S(1)}, u32[]{:S(2)}, u32[]{:S(2)}) %collective-permute-start.115) | collective-permute-done | bytes 786464 | tf_op jit(solution)/shard_map/ppermute | solution.py:786
  391.3 3.0 collective-permute-start.119
  395.0 4.8 %collective-permute-done.113.refs_3_ = bf16[256,1024]{1,0:T(8,128)(2,1)S(1)} collective-permute-done((bf16[256,1024]{1,0:T(8,128)(2,1)S(1)}, bf16[256,1024]{1,0:T(8,128)(2,1)S(1)}, u32[]{:S(2)}, u32[]{:S(2)}) %collective-permute-start.113) | collective-permute-done | bytes 524320 | tf_op jit(solution)/shard_map/ppermute | solution.py:31
  400.5 10.0 %collective-permute-done.119.refs_1_ = bf16[528,768]{1,0:T(8,128)(2,1)S(1)} collective-permute-done((bf16[528,768]{1,0:T(8,128)(2,1)S(1)}, bf16[528,768]{1,0:T(8,128)(2,1)S(1)}, u32[]{:S(2)}, u32[]{:S(2)}) %collective-permute-start.119) | collective-permute-done | bytes 811040 | tf_op jit(solution)/shard_map/ppermute | solution.py:786
  415.6 18.0 %collective-permute-done.122.refs_1_ = bf16[512,768]{1,0:T(8,128)(2,1)S(1)} collective-permute-done((bf16[512,768]{1,0:T(8,128)(2,1)S(1)}, bf16[512,768]{1,0:T(8,128)(2,1)S(1)}, u32[]{:S(2)}, u32[]{:S(2)}) %collective-permute-start.122) | collective-permute-done | bytes 786464 | tf_op jit(solution)/shard_map/ppermute | solution.py:790
  436.5 16.8 %collective-permute-done.123.refs_1_ = bf16[528,768]{1,0:T(8,128)(2,1)S(1)} collective-permute-done((bf16[528,768]{1,0:T(8,128)(2,1)S(1)}, bf16[528,768]{1,0:T(8,128)(2,1)S(1)}, u32[]{:S(2)}, u32[]{:S(2)}) %collective-permute-start.123) | collective-permute-done | bytes 811040 | tf_op jit(solution)/shard_map/ppermute | solution.py:790
  453.3 1.9 finish_proj.3
  (617 shorter events, 182.7 us)
Async XLA Ops:
  4.0 12.1 %collective-permute-start = (bf16[3,256,256]{2,1,0:T(8,128)(2,1)S(1)}, bf16[3,256,256]{2,1,0:T(8,128)(2,1)S(1)}, u32[]{:S(2)}, u32[]{:S(2)}) collective-permute-start(bf16[3,256,256]{2,1,0:T(8,128)(2,1)S(1)} %get-tuple-element.371), channel_id=1, source_target_pairs={{4,0},{0,4},{5,1},{1,5},{6,2},{2,6},{7,3},{3,7},{12,8},{8,12},{13,... | collective-permute-start | bytes 1179656 | tf_op jit(solution)/shard_map/ppermute | solution.py:36
  16.1 21.8 %collective-permute-start.1 = (bf16[3,256,256]{2,1,0:T(8,128)(2,1)S(1)}, bf16[3,256,256]{2,1,0:T(8,128)(2,1)S(1)}, u32[]{:S(2)}, u32[]{:S(2)}) collective-permute-start(bf16[3,256,256]{2,1,0:T(8,128)(2,1)S(1)} %collective-permute-done.refs_4_.refs_1_.refs_3_.refs_5_), channel_id=1, source_target_pairs={{0,8},{8,0},{16,24},{24,16},{1,9},{9,1},{17,25},{25,17},{2,10},{10... | collective-permute-start | bytes 1179656 | tf_op jit(solution)/shard_map/ppermute | solution.py:191
  31.4 22.2 %collective-permute-start.13 = (bf16[288,1024]{1,0:T(8,128)(2,1)}, bf16[288,1024]{1,0:T(8,128)(2,1)}, u32[]{:S(2)}, u32[]{:S(2)}) collective-permute-start(bf16[288,1024]{1,0:T(8,128)(2,1)} %get-tuple-element.389.refs_0_), channel_id=1, source_target_pairs={{0,2},{2,0},{1,3},{3,1},{4,6},{6,4},{5,7},{7,5},{8,10},{10,8},{9,1... | collective-permute-start | bytes 1769480 | tf_op jit(solution)/shard_map/ppermute | solution.py:31
  40.6 15.4 %collective-permute-start.8 = (bf16[256,1024]{1,0:T(8,128)(2,1)}, bf16[256,1024]{1,0:T(8,128)(2,1)S(1)}, u32[]{:S(2)}, u32[]{:S(2)}) collective-permute-start(bf16[256,1024]{1,0:T(8,128)(2,1)} %get-tuple-element.383), channel_id=1, source_target_pairs={{4,0},{0,4},{5,1},{1,5},{6,2},{2,6},{7,3},{3,7},{12,8},{8,12},{13,... | collective-permute-start | bytes 1572872 | tf_op jit(solution)/shard_map/ppermute | solution.py:36
  56.8 18.4 %collective-permute-start.9 = (bf16[1024,256]{1,0:T(8,128)(2,1)S(1)}, bf16[1024,256]{1,0:T(8,128)(2,1)}, u32[]{:S(2)}, u32[]{:S(2)}) collective-permute-start(bf16[1024,256]{1,0:T(8,128)(2,1)S(1)} %get-tuple-element.385), channel_id=1, source_target_pairs={{4,0},{0,4},{5,1},{1,5},{6,2},{2,6},{7,3},{3,7},{12,8},{8,12},{13,... | collective-permute-start | bytes 1572872 | tf_op jit(solution)/shard_map/ppermute | solution.py:36
  57.4 29.2 %collective-permute-start.7 = (bf16[256,1024]{1,0:T(8,128)(2,1)}, bf16[256,1024]{1,0:T(8,128)(2,1)}, u32[]{:S(2)}, u32[]{:S(2)}) collective-permute-start(bf16[256,1024]{1,0:T(8,128)(2,1)} %get-tuple-element.382), channel_id=1, source_target_pairs={{0,2},{2,0},{1,3},{3,1},{4,6},{6,4},{5,7},{7,5},{8,10},{10,8},{9,1... | collective-permute-start | bytes 1572872 | tf_op jit(solution)/shard_map/ppermute | solution.py:31
  57.9 28.7 %collective-permute-start.10 = (bf16[256,1024]{1,0:T(8,128)(2,1)S(1)}, bf16[256,1024]{1,0:T(8,128)(2,1)}, u32[]{:S(2)}, u32[]{:S(2)}) collective-permute-start(bf16[256,1024]{1,0:T(8,128)(2,1)S(1)} %collective-permute-done.8.refs_1_.refs_5_), channel_id=1, source_target_pairs={{0,8},{8,0},{16,24},{24,16},{1,9},{9,1},{17,25},{25,17},{2,10},{10... | collective-permute-start | bytes 1572872 | tf_op jit(solution)/shard_map/ppermute | solution.py:191
  75.2 11.3 %collective-permute-start.11 = (bf16[3,256,256]{2,1,0:T(8,128)(2,1)}, bf16[3,256,256]{2,1,0:T(8,128)(2,1)}, u32[]{:S(2)}, u32[]{:S(2)}) collective-permute-start(bf16[3,256,256]{2,1,0:T(8,128)(2,1)} %get-tuple-element.386), channel_id=1, source_target_pairs={{4,0},{0,4},{5,1},{1,5},{6,2},{2,6},{7,3},{3,7},{12,8},{8,12},{13,... | collective-permute-start | bytes 1179656 | tf_op jit(solution)/shard_map/ppermute | solution.py:36
  76.8 18.1 %collective-permute-start.19 = (bf16[1024,256]{1,0:T(8,128)(2,1)}, bf16[1024,256]{1,0:T(8,128)(2,1)}, u32[]{:S(2)}, u32[]{:S(2)}) collective-permute-start(bf16[1024,256]{1,0:T(8,128)(2,1)} %collective-permute-done.9.refs_6_.refs_8_), channel_id=1, source_target_pairs={{0,8},{8,0},{16,24},{24,16},{1,9},{9,1},{17,25},{25,17},{2,10},{10... | collective-permute-start | bytes 1572872 | tf_op jit(solution)/shard_map/ppermute | solution.py:191
  79.9 28.2 %collective-permute-start.24 = (bf16[320,1024]{1,0:T(8,128)(2,1)}, bf16[320,1024]{1,0:T(8,128)(2,1)}, u32[]{:S(2)}, u32[]{:S(2)}) collective-permute-start(bf16[320,1024]{1,0:T(8,128)(2,1)} %get-tuple-element.409), channel_id=1, source_target_pairs={{0,2},{2,0},{1,3},{3,1},{4,6},{6,4},{5,7},{7,5},{8,10},{10,8},{9,1... | collective-permute-start | bytes 1966088 | tf_op jit(solution)/shard_map/ppermute | solution.py:31
  93.5 14.5 %collective-permute-start.26 = (bf16[3,256,256]{2,1,0:T(8,128)(2,1)}, bf16[3,256,256]{2,1,0:T(8,128)(2,1)S(1)}, u32[]{:S(2)}, u32[]{:S(2)}) collective-permute-start(bf16[3,256,256]{2,1,0:T(8,128)(2,1)} %collective-permute-done.11.refs_8_.refs_5_), channel_id=1, source_target_pairs={{0,8},{8,0},{16,24},{24,16},{1,9},{9,1},{17,25},{25,17},{2,10},{10... | collective-permute-start | bytes 1179656 | tf_op jit(solution)/shard_map/ppermute | solution.py:191
  112.5 14.0 %collective-permute-start.23 = (bf16[256,1024]{1,0:T(8,128)(2,1)S(1)}, bf16[256,1024]{1,0:T(8,128)(2,1)}, u32[]{:S(2)}, u32[]{:S(2)}) collective-permute-start(bf16[256,1024]{1,0:T(8,128)(2,1)S(1)} %copy-done.143), channel_id=1, source_target_pairs={{4,0},{0,4},{5,1},{1,5},{6,2},{2,6},{7,3},{3,7},{12,8},{8,12},{13,... | collective-permute-start | bytes 1572872 | tf_op jit(solution)/shard_map/ppermute | solution.py:36
  114.1 13.6 %collective-permute-start.22 = (bf16[256,1024]{1,0:T(8,128)(2,1)S(1)}, bf16[256,1024]{1,0:T(8,128)(2,1)S(1)}, u32[]{:S(2)}, u32[]{:S(2)}) collective-permute-start(bf16[256,1024]{1,0:T(8,128)(2,1)S(1)} %get-tuple-element.406), channel_id=1, source_target_pairs={{0,2},{2,0},{1,3},{3,1},{4,6},{6,4},{5,7},{7,5},{8,10},{10,8},{9,1... | collective-permute-start | bytes 1572872 | tf_op jit(solution)/shard_map/ppermute | solution.py:31
  125.7 20.8 %collective-permute-start.38 = (bf16[320,1024]{1,0:T(8,128)(2,1)}, bf16[320,1024]{1,0:T(8,128)(2,1)}, u32[]{:S(2)}, u32[]{:S(2)}) collective-permute-start(bf16[320,1024]{1,0:T(8,128)(2,1)} %get-tuple-element.431), channel_id=1, source_target_pairs={{0,2},{2,0},{1,3},{3,1},{4,6},{6,4},{5,7},{7,5},{8,10},{10,8},{9,1... | collective-permute-start | bytes 1966088 | tf_op jit(solution)/shard_map/ppermute | solution.py:31
  132.1 14.3 %collective-permute-start.36 = (bf16[1024,256]{1,0:T(8,128)(2,1)}, bf16[1024,256]{1,0:T(8,128)(2,1)}, u32[]{:S(2)}, u32[]{:S(2)}) collective-permute-start(bf16[1024,256]{1,0:T(8,128)(2,1)} %get-tuple-element.430), channel_id=1, source_target_pairs={{4,0},{0,4},{5,1},{1,5},{6,2},{2,6},{7,3},{3,7},{12,8},{8,12},{13,... | collective-permute-start | bytes 1572872 | tf_op jit(solution)/shard_map/ppermute | solution.py:36
  132.6 13.9 %collective-permute-start.39 = (bf16[256,1024]{1,0:T(8,128)(2,1)}, bf16[256,1024]{1,0:T(8,128)(2,1)}, u32[]{:S(2)}, u32[]{:S(2)}) collective-permute-start(bf16[256,1024]{1,0:T(8,128)(2,1)} %collective-permute-done.23.refs_6_.refs_5_), channel_id=1, source_target_pairs={{0,8},{8,0},{16,24},{24,16},{1,9},{9,1},{17,25},{25,17},{2,10},{10... | collective-permute-start | bytes 1572872 | tf_op jit(solution)/shard_map/ppermute | solution.py:191
  149.2 14.1 %collective-permute-start.37 = (bf16[1024,256]{1,0:T(8,128)(2,1)}, bf16[1024,256]{1,0:T(8,128)(2,1)S(1)}, u32[]{:S(2)}, u32[]{:S(2)}) collective-permute-start(bf16[1024,256]{1,0:T(8,128)(2,1)} %collective-permute-done.36.refs_7_.refs_8_), channel_id=1, source_target_pairs={{0,8},{8,0},{16,24},{24,16},{1,9},{9,1},{17,25},{25,17},{2,10},{10... | collective-permute-start | bytes 1572872 | tf_op jit(solution)/shard_map/ppermute | solution.py:191
  150.1 13.7 %collective-permute-start.35 = (bf16[256,1024]{1,0:T(8,128)(2,1)S(1)}, bf16[256,1024]{1,0:T(8,128)(2,1)S(1)}, u32[]{:S(2)}, u32[]{:S(2)}) collective-permute-start(bf16[256,1024]{1,0:T(8,128)(2,1)S(1)} %get-tuple-element.428), channel_id=1, source_target_pairs={{0,2},{2,0},{1,3},{3,1},{4,6},{6,4},{5,7},{7,5},{8,10},{10,8},{9,1... | collective-permute-start | bytes 1572872 | tf_op jit(solution)/shard_map/ppermute | solution.py:31
  161.6 16.8 %collective-permute-start.49 = (bf16[320,1024]{1,0:T(8,128)(2,1)S(1)}, bf16[320,1024]{1,0:T(8,128)(2,1)S(1)}, u32[]{:S(2)}, u32[]{:S(2)}) collective-permute-start(bf16[320,1024]{1,0:T(8,128)(2,1)S(1)} %get-tuple-element.453), channel_id=1, source_target_pairs={{0,2},{2,0},{1,3},{3,1},{4,6},{6,4},{5,7},{7,5},{8,10},{10,8},{9,1... | collective-permute-start | bytes 1966088 | tf_op jit(solution)/shard_map/ppermute | solution.py:31
  179.9 14.8 %collective-permute-start.48 = (bf16[256,1024]{1,0:T(8,128)(2,1)S(1)}, bf16[256,1024]{1,0:T(8,128)(2,1)S(1)}, u32[]{:S(2)}, u32[]{:S(2)}) collective-permute-start(bf16[256,1024]{1,0:T(8,128)(2,1)S(1)} %get-tuple-element.451), channel_id=1, source_target_pairs={{0,2},{2,0},{1,3},{3,1},{4,6},{6,4},{5,7},{7,5},{8,10},{10,8},{9,1... | collective-permute-start | bytes 1572872 | tf_op jit(solution)/shard_map/ppermute | solution.py:31
  188.5 19.3 %collective-permute-start.54 = (bf16[320,1024]{1,0:T(8,128)(2,1)S(1)}, bf16[320,1024]{1,0:T(8,128)(2,1)S(1)}, u32[]{:S(2)}, u32[]{:S(2)}) collective-permute-start(bf16[320,1024]{1,0:T(8,128)(2,1)S(1)} %get-tuple-element.466), channel_id=1, source_target_pairs={{0,2},{2,0},{1,3},{3,1},{4,6},{6,4},{5,7},{7,5},{8,10},{10,8},{9,1... | collective-permute-start | bytes 1966088 | tf_op jit(solution)/shard_map/ppermute | solution.py:31
  211.6 14.3 %collective-permute-start.60 = (bf16[256,1024]{1,0:T(8,128)(2,1)S(1)}, bf16[256,1024]{1,0:T(8,128)(2,1)S(1)}, u32[]{:S(2)}, u32[]{:S(2)}) collective-permute-start(bf16[256,1024]{1,0:T(8,128)(2,1)S(1)} %get-tuple-element.483), channel_id=1, source_target_pairs={{0,2},{2,0},{1,3},{3,1},{4,6},{6,4},{5,7},{7,5},{8,10},{10,8},{9,1... | collective-permute-start | bytes 1572872 | tf_op jit(solution)/shard_map/ppermute | solution.py:31
  219.5 21.3 %collective-permute-start.69 = (bf16[512,768]{1,0:T(8,128)(2,1)S(1)}, bf16[512,768]{1,0:T(8,128)(2,1)S(1)}, u32[]{:S(2)}, u32[]{:S(2)}) collective-permute-start(bf16[512,768]{1,0:T(8,128)(2,1)S(1)} %bitcast.46), channel_id=1, source_target_pairs={{0,4},{4,0},{1,5},{5,1},{2,6},{6,2},{3,7},{7,3},{8,12},{12,8},{9,1... | collective-permute-start | bytes 2359304 | tf_op jit(solution)/shard_map/ppermute | solution.py:41
  222.6 21.6 %collective-permute-start.71 = (bf16[320,1024]{1,0:T(8,128)(2,1)S(1)}, bf16[320,1024]{1,0:T(8,128)(2,1)S(1)}, u32[]{:S(2)}, u32[]{:S(2)}) collective-permute-start(bf16[320,1024]{1,0:T(8,128)(2,1)S(1)} %get-tuple-element.524), channel_id=1, source_target_pairs={{0,2},{2,0},{1,3},{3,1},{4,6},{6,4},{5,7},{7,5},{8,10},{10,8},{9,1... | collective-permute-start | bytes 1966088 | tf_op jit(solution)/shard_map/ppermute | solution.py:31
  235.3 8.7 %collective-permute-start.67 = (bf16[128,1024]{1,0:T(8,128)(2,1)S(1)}, bf16[128,1024]{1,0:T(8,128)(2,1)S(1)}, u32[]{:S(2)}, u32[]{:S(2)}) collective-permute-start(bf16[128,1024]{1,0:T(8,128)(2,1)S(1)} %get-tuple-element.510), channel_id=1, source_target_pairs={{0,1},{1,0},{2,3},{3,2},{4,5},{5,4},{6,7},{7,6},{8,9},{9,8},{10,11... | collective-permute-start | bytes 786440 | tf_op jit(solution)/shard_map/ppermute | solution.py:27
  237.2 20.3 %collective-permute-start.76 = (bf16[512,768]{1,0:T(8,128)(2,1)S(1)}, bf16[512,768]{1,0:T(8,128)(2,1)S(1)}, u32[]{:S(2)}, u32[]{:S(2)}) collective-permute-start(bf16[512,768]{1,0:T(8,128)(2,1)S(1)} %bitcast.44), channel_id=1, source_target_pairs={{0,4},{4,0},{1,5},{5,1},{2,6},{6,2},{3,7},{7,3},{8,12},{12,8},{9,1... | collective-permute-start | bytes 2359304 | tf_op jit(solution)/shard_map/ppermute | solution.py:41
  241.0 19.8 %collective-permute-start.77 = (bf16[512,768]{1,0:T(8,128)(2,1)S(1)}, bf16[512,768]{1,0:T(8,128)(2,1)S(1)}, u32[]{:S(2)}, u32[]{:S(2)}) collective-permute-start(bf16[512,768]{1,0:T(8,128)(2,1)S(1)} %get-tuple-element.542.refs_2_), channel_id=1, source_target_pairs={{0,8},{24,16},{1,9},{25,17},{2,10},{26,18},{3,11},{27,19},{4,12},{... | collective-permute-start | bytes 2359304 | tf_op jit(solution)/shard_map/ppermute | solution.py:788
  245.9 21.0 %collective-permute-start.70 = (bf16[256,1024]{1,0:T(8,128)(2,1)S(1)}, bf16[256,1024]{1,0:T(8,128)(2,1)S(1)}, u32[]{:S(2)}, u32[]{:S(2)}) collective-permute-start(bf16[256,1024]{1,0:T(8,128)(2,1)S(1)} %get-tuple-element.520), channel_id=1, source_target_pairs={{0,2},{2,0},{1,3},{3,1},{4,6},{6,4},{5,7},{7,5},{8,10},{10,8},{9,1... | collective-permute-start | bytes 1572872 | tf_op jit(solution)/shard_map/ppermute | solution.py:31
  255.6 10.2 %collective-permute-start.74 = (bf16[160,1024]{1,0:T(8,128)(2,1)S(1)}, bf16[160,1024]{1,0:T(8,128)(2,1)S(1)}, u32[]{:S(2)}, u32[]{:S(2)}) collective-permute-start(bf16[160,1024]{1,0:T(8,128)(2,1)S(1)} %get-tuple-element.538), channel_id=1, source_target_pairs={{0,1},{1,0},{2,3},{3,2},{4,5},{5,4},{6,7},{7,6},{8,9},{9,8},{10,11... | collective-permute-start | bytes 983048 | tf_op jit(solution)/shard_map/ppermute | solution.py:27
  255.8 10.9 %collective-permute-start.75 = (bf16[160,1024]{1,0:T(8,128)(2,1)S(1)}, bf16[160,1024]{1,0:T(8,128)(2,1)S(1)}, u32[]{:S(2)}, u32[]{:S(2)}) collective-permute-start(bf16[160,1024]{1,0:T(8,128)(2,1)S(1)} %get-tuple-element.539), channel_id=1, source_target_pairs={{0,1},{1,0},{2,3},{3,2},{4,5},{5,4},{6,7},{7,6},{8,9},{9,8},{10,11... | collective-permute-start | bytes 983048 | tf_op jit(solution)/shard_map/ppermute | solution.py:27
  257.5 19.7 %collective-permute-start.83 = (bf16[512,768]{1,0:T(8,128)(2,1)S(1)}, bf16[512,768]{1,0:T(8,128)(2,1)S(1)}, u32[]{:S(2)}, u32[]{:S(2)}) collective-permute-start(bf16[512,768]{1,0:T(8,128)(2,1)S(1)} %bitcast.43), channel_id=1, source_target_pairs={{0,4},{4,0},{1,5},{5,1},{2,6},{6,2},{3,7},{7,3},{8,12},{12,8},{9,1... | collective-permute-start | bytes 2359304 | tf_op jit(solution)/shard_map/ppermute | solution.py:41
  261.2 20.5 %collective-permute-start.84 = (bf16[512,768]{1,0:T(8,128)(2,1)S(1)}, bf16[512,768]{1,0:T(8,128)(2,1)S(1)}, u32[]{:S(2)}, u32[]{:S(2)}) collective-permute-start(bf16[512,768]{1,0:T(8,128)(2,1)S(1)} %get-tuple-element.564.refs_2_), channel_id=1, source_target_pairs={{0,8},{24,16},{1,9},{25,17},{2,10},{26,18},{3,11},{27,19},{4,12},{... | collective-permute-start | bytes 2359304 | tf_op jit(solution)/shard_map/ppermute | solution.py:788
  265.8 18.8 %collective-permute-start.85 = (bf16[512,768]{1,0:T(8,128)(2,1)S(1)}, bf16[512,768]{1,0:T(8,128)(2,1)S(1)}, u32[]{:S(2)}, u32[]{:S(2)}) collective-permute-start(bf16[512,768]{1,0:T(8,128)(2,1)S(1)} %get-tuple-element.565.refs_4_), channel_id=1, source_target_pairs={{8,16},{16,8},{9,17},{17,9},{10,18},{18,10},{11,19},{19,11},{12,20... | collective-permute-start | bytes 2359304 | tf_op jit(solution)/shard_map/ppermute | solution.py:784
  269.5 19.5 %collective-permute-start.80 = (bf16[320,1024]{1,0:T(8,128)(2,1)S(1)}, bf16[320,1024]{1,0:T(8,128)(2,1)S(1)}, u32[]{:S(2)}, u32[]{:S(2)}) collective-permute-start(bf16[320,1024]{1,0:T(8,128)(2,1)S(1)} %get-tuple-element.555), channel_id=1, source_target_pairs={{0,2},{2,0},{1,3},{3,1},{4,6},{6,4},{5,7},{7,5},{8,10},{10,8},{9,1... | collective-permute-start | bytes 1966088 | tf_op jit(solution)/shard_map/ppermute | solution.py:31
  274.2 13.7 %collective-permute-start.81 = (bf16[128,1024]{1,0:T(8,128)(2,1)S(1)}, bf16[128,1024]{1,0:T(8,128)(2,1)S(1)}, u32[]{:S(2)}, u32[]{:S(2)}) collective-permute-start(bf16[128,1024]{1,0:T(8,128)(2,1)S(1)} %get-tuple-element.560), channel_id=1, source_target_pairs={{0,1},{1,0},{2,3},{3,2},{4,5},{5,4},{6,7},{7,6},{8,9},{9,8},{10,11... | collective-permute-start | bytes 786440 | tf_op jit(solution)/shard_map/ppermute | solution.py:27
  277.1 11.7 %collective-permute-start.82 = (bf16[128,1024]{1,0:T(8,128)(2,1)S(1)}, bf16[128,1024]{1,0:T(8,128)(2,1)S(1)}, u32[]{:S(2)}, u32[]{:S(2)}) collective-permute-start(bf16[128,1024]{1,0:T(8,128)(2,1)S(1)} %get-tuple-element.561), channel_id=1, source_target_pairs={{0,1},{1,0},{2,3},{3,2},{4,5},{5,4},{6,7},{7,6},{8,9},{9,8},{10,11... | collective-permute-start | bytes 786440 | tf_op jit(solution)/shard_map/ppermute | solution.py:27
  281.7 17.8 %collective-permute-start.92 = (bf16[512,768]{1,0:T(8,128)(2,1)S(1)}, bf16[512,768]{1,0:T(8,128)(2,1)S(1)}, u32[]{:S(2)}, u32[]{:S(2)}) collective-permute-start(bf16[512,768]{1,0:T(8,128)(2,1)S(1)} %bitcast.45), channel_id=1, source_target_pairs={{0,4},{4,0},{1,5},{5,1},{2,6},{6,2},{3,7},{7,3},{8,12},{12,8},{9,1... | collective-permute-start | bytes 2359304 | tf_op jit(solution)/shard_map/ppermute | solution.py:41
  285.3 18.4 %collective-permute-start.91 = (bf16[512,768]{1,0:T(8,128)(2,1)S(1)}, bf16[512,768]{1,0:T(8,128)(2,1)S(1)}, u32[]{:S(2)}, u32[]{:S(2)}) collective-permute-start(bf16[512,768]{1,0:T(8,128)(2,1)S(1)} %get-tuple-element.586), channel_id=1, source_target_pairs={{0,8},{8,0},{16,24},{24,16},{1,9},{9,1},{17,25},{25,17},{2,10},{10... | collective-permute-start | bytes 2359304 | tf_op jit(solution)/shard_map/ppermute | solution.py:786
  287.9 16.9 %collective-permute-start.93 = (bf16[512,768]{1,0:T(8,128)(2,1)S(1)}, bf16[512,768]{1,0:T(8,128)(2,1)S(1)}, u32[]{:S(2)}, u32[]{:S(2)}) collective-permute-start(bf16[512,768]{1,0:T(8,128)(2,1)S(1)} %get-tuple-element.590.refs_4_), channel_id=1, source_target_pairs={{8,16},{16,8},{9,17},{17,9},{10,18},{18,10},{11,19},{19,11},{12,20... | collective-permute-start | bytes 2359304 | tf_op jit(solution)/shard_map/ppermute | solution.py:784
  296.7 9.9 %collective-permute-start.89 = (bf16[160,1024]{1,0:T(8,128)(2,1)S(1)}, bf16[160,1024]{1,0:T(8,128)(2,1)S(1)}, u32[]{:S(2)}, u32[]{:S(2)}) collective-permute-start(bf16[160,1024]{1,0:T(8,128)(2,1)S(1)} %get-tuple-element.583), channel_id=1, source_target_pairs={{0,1},{1,0},{2,3},{3,2},{4,5},{5,4},{6,7},{7,6},{8,9},{9,8},{10,11... | collective-permute-start | bytes 983048 | tf_op jit(solution)/shard_map/ppermute | solution.py:27
  296.9 17.2 %collective-permute-start.88 = (bf16[256,1024]{1,0:T(8,128)(2,1)S(1)}, bf16[256,1024]{1,0:T(8,128)(2,1)S(1)}, u32[]{:S(2)}, u32[]{:S(2)}) collective-permute-start(bf16[256,1024]{1,0:T(8,128)(2,1)S(1)} %get-tuple-element.578), channel_id=1, source_target_pairs={{0,2},{2,0},{1,3},{3,1},{4,6},{6,4},{5,7},{7,5},{8,10},{10,8},{9,1... | collective-permute-start | bytes 1572872 | tf_op jit(solution)/shard_map/ppermute | solution.py:31
  299.5 14.5 %collective-permute-start.90 = (bf16[160,1024]{1,0:T(8,128)(2,1)S(1)}, bf16[160,1024]{1,0:T(8,128)(2,1)S(1)}, u32[]{:S(2)}, u32[]{:S(2)}) collective-permute-start(bf16[160,1024]{1,0:T(8,128)(2,1)S(1)} %get-tuple-element.584), channel_id=1, source_target_pairs={{0,1},{1,0},{2,3},{3,2},{4,5},{5,4},{6,7},{7,6},{8,9},{9,8},{10,11... | collective-permute-start | bytes 983048 | tf_op jit(solution)/shard_map/ppermute | solution.py:27
  303.7 22.4 %collective-permute-start.100 = (bf16[512,768]{1,0:T(8,128)(2,1)S(1)}, bf16[512,768]{1,0:T(8,128)(2,1)S(1)}, u32[]{:S(2)}, u32[]{:S(2)}) collective-permute-start(bf16[512,768]{1,0:T(8,128)(2,1)S(1)} %bitcast.42), channel_id=1, source_target_pairs={{0,4},{4,0},{1,5},{5,1},{2,6},{6,2},{3,7},{7,3},{8,12},{12,8},{9,1... | collective-permute-start | bytes 2359304 | tf_op jit(solution)/shard_map/ppermute | solution.py:41
  305.5 21.7 %collective-permute-start.101 = (bf16[512,768]{1,0:T(8,128)(2,1)S(1)}, bf16[512,768]{1,0:T(8,128)(2,1)S(1)}, u32[]{:S(2)}, u32[]{:S(2)}) collective-permute-start(bf16[512,768]{1,0:T(8,128)(2,1)S(1)} %get-tuple-element.617.refs_4_), channel_id=1, source_target_pairs={{8,16},{16,8},{9,17},{17,9},{10,18},{18,10},{11,19},{19,11},{12,20... | collective-permute-start | bytes 2359304 | tf_op jit(solution)/shard_map/ppermute | solution.py:784
  306.6 21.4 %collective-permute-start.99 = (bf16[512,768]{1,0:T(8,128)(2,1)S(1)}, bf16[512,768]{1,0:T(8,128)(2,1)S(1)}, u32[]{:S(2)}, u32[]{:S(2)}) collective-permute-start(bf16[512,768]{1,0:T(8,128)(2,1)S(1)} %get-tuple-element.612), channel_id=1, source_target_pairs={{0,8},{8,0},{16,24},{24,16},{1,9},{9,1},{17,25},{25,17},{2,10},{10... | collective-permute-start | bytes 2359304 | tf_op jit(solution)/shard_map/ppermute | solution.py:786
  316.7 16.8 %collective-permute-start.96 = (bf16[320,1024]{1,0:T(8,128)(2,1)S(1)}, bf16[320,1024]{1,0:T(8,128)(2,1)S(1)}, u32[]{:S(2)}, u32[]{:S(2)}) collective-permute-start(bf16[320,1024]{1,0:T(8,128)(2,1)S(1)} %get-tuple-element.601), channel_id=1, source_target_pairs={{0,2},{2,0},{1,3},{3,1},{4,6},{6,4},{5,7},{7,5},{8,10},{10,8},{9,1... | collective-permute-start | bytes 1966088 | tf_op jit(solution)/shard_map/ppermute | solution.py:31
  326.1 22.6 %collective-permute-start.105 = (bf16[512,768]{1,0:T(8,128)(2,1)S(1)}, bf16[512,768]{1,0:T(8,128)(2,1)S(1)}, u32[]{:S(2)}, u32[]{:S(2)}) collective-permute-start(bf16[512,768]{1,0:T(8,128)(2,1)S(1)} %bitcast.40), channel_id=1, source_target_pairs={{0,4},{4,0},{1,5},{5,1},{2,6},{6,2},{3,7},{7,3},{8,12},{12,8},{9,1... | collective-permute-start | bytes 2359304 | tf_op jit(solution)/shard_map/ppermute | solution.py:41
  328.7 20.0 %collective-permute-start.106 = (bf16[512,768]{1,0:T(8,128)(2,1)S(1)}, bf16[512,768]{1,0:T(8,128)(2,1)S(1)}, u32[]{:S(2)}, u32[]{:S(2)}) collective-permute-start(bf16[512,768]{1,0:T(8,128)(2,1)S(1)} %get-tuple-element.650), channel_id=1, source_target_pairs={{0,8},{8,0},{16,24},{24,16},{1,9},{9,1},{17,25},{25,17},{2,10},{10... | collective-permute-start | bytes 2359304 | tf_op jit(solution)/shard_map/ppermute | solution.py:786
  330.5 18.2 %collective-permute-start.107 = (bf16[512,768]{1,0:T(8,128)(2,1)S(1)}, bf16[512,768]{1,0:T(8,128)(2,1)S(1)}, u32[]{:S(2)}, u32[]{:S(2)}) collective-permute-start(bf16[512,768]{1,0:T(8,128)(2,1)S(1)} %get-tuple-element.651.refs_4_), channel_id=1, source_target_pairs={{8,16},{16,8},{9,17},{17,9},{10,18},{18,10},{11,19},{19,11},{12,20... | collective-permute-start | bytes 2359304 | tf_op jit(solution)/shard_map/ppermute | solution.py:784
  346.2 23.9 %collective-permute-start.104 = (bf16[512,768]{1,0:T(8,128)(2,1)S(1)}, bf16[512,768]{1,0:T(8,128)(2,1)S(1)}, u32[]{:S(2)}, u32[]{:S(2)}) collective-permute-start(bf16[512,768]{1,0:T(8,128)(2,1)S(1)} %bitcast.41), channel_id=1, source_target_pairs={{0,4},{4,0},{1,5},{5,1},{2,6},{6,2},{3,7},{7,3},{8,12},{12,8},{9,1... | collective-permute-start | bytes 2359304 | tf_op jit(solution)/shard_map/ppermute | solution.py:41
  349.4 19.4 %collective-permute-start.108 = (bf16[512,768]{1,0:T(8,128)(2,1)S(1)}, bf16[512,768]{1,0:T(8,128)(2,1)S(1)}, u32[]{:S(2)}, u32[]{:S(2)}) collective-permute-start(bf16[512,768]{1,0:T(8,128)(2,1)S(1)} %get-tuple-element.654), channel_id=1, source_target_pairs={{0,8},{8,0},{16,24},{24,16},{1,9},{9,1},{17,25},{25,17},{2,10},{10... | collective-permute-start | bytes 2359304 | tf_op jit(solution)/shard_map/ppermute | solution.py:786
  351.9 18.2 %collective-permute-start.109 = (bf16[512,768]{1,0:T(8,128)(2,1)S(1)}, bf16[512,768]{1,0:T(8,128)(2,1)S(1)}, u32[]{:S(2)}, u32[]{:S(2)}) collective-permute-start(bf16[512,768]{1,0:T(8,128)(2,1)S(1)} %get-tuple-element.655.refs_4_), channel_id=1, source_target_pairs={{8,16},{16,8},{9,17},{17,9},{10,18},{18,10},{11,19},{19,11},{12,20... | collective-permute-start | bytes 2359304 | tf_op jit(solution)/shard_map/ppermute | solution.py:784
  352.9 21.8 %collective-permute-start.59 = (bf16[576,1024]{1,0:T(8,128)(2,1)S(1)}, bf16[576,1024]{1,0:T(8,128)(2,1)S(1)}, u32[]{:S(2)}, u32[]{:S(2)}) collective-permute-start(bf16[576,1024]{1,0:T(8,128)(2,1)S(1)} %constant_dynamic-update-slice_fusion.refs_0_), channel_id=1, source_target_pairs={{0,1},{1,0},{2,3},{3,2},{4,5},{5,4},{6,7},{7,6},{8,9},{9,8},{10,11... | collective-permute-start | bytes 3538952 | tf_op jit(solution)/shard_map/ppermute | solution.py:27
  360.4 30.2 %collective-permute-start.114 = (bf16[528,768]{1,0:T(8,128)(2,1)S(1)}, bf16[528,768]{1,0:T(8,128)(2,1)S(1)}, u32[]{:S(2)}, u32[]{:S(2)}) collective-permute-start(bf16[528,768]{1,0:T(8,128)(2,1)S(1)} %bitcast.39), channel_id=1, source_target_pairs={{0,4},{4,0},{1,5},{5,1},{2,6},{6,2},{3,7},{7,3},{8,12},{12,8},{9,1... | collective-permute-start | bytes 2433032 | tf_op jit(solution)/shard_map/ppermute | solution.py:41
  370.8 18.3 %collective-permute-start.115 = (bf16[512,768]{1,0:T(8,128)(2,1)S(1)}, bf16[512,768]{1,0:T(8,128)(2,1)S(1)}, u32[]{:S(2)}, u32[]{:S(2)}) collective-permute-start(bf16[512,768]{1,0:T(8,128)(2,1)S(1)} %get-tuple-element.688), channel_id=1, source_target_pairs={{0,8},{8,0},{16,24},{24,16},{1,9},{9,1},{17,25},{25,17},{2,10},{10... | collective-permute-start | bytes 2359304 | tf_op jit(solution)/shard_map/ppermute | solution.py:786
  373.2 17.4 %collective-permute-start.116 = (bf16[512,768]{1,0:T(8,128)(2,1)S(1)}, bf16[512,768]{1,0:T(8,128)(2,1)S(1)}, u32[]{:S(2)}, u32[]{:S(2)}) collective-permute-start(bf16[512,768]{1,0:T(8,128)(2,1)S(1)} %get-tuple-element.689.refs_4_), channel_id=1, source_target_pairs={{8,16},{16,8},{9,17},{17,9},{10,18},{18,10},{11,19},{19,11},{12,20... | collective-permute-start | bytes 2359304 | tf_op jit(solution)/shard_map/ppermute | solution.py:784
  373.9 26.2 %collective-permute-start.117 = (bf16[320,1024]{1,0:T(8,128)(2,1)S(1)}, bf16[320,1024]{1,0:T(8,128)(2,1)S(1)}, u32[]{:S(2)}, u32[]{:S(2)}) collective-permute-start(bf16[320,1024]{1,0:T(8,128)(2,1)S(1)} %get-tuple-element.696), channel_id=1, source_target_pairs={{0,2},{2,0},{1,3},{3,1},{4,6},{6,4},{5,7},{7,5},{8,10},{10,8},{9,1... | collective-permute-start | bytes 1966088 | tf_op jit(solution)/shard_map/ppermute | solution.py:31
  374.7 25.0 %collective-permute-start.113 = (bf16[256,1024]{1,0:T(8,128)(2,1)S(1)}, bf16[256,1024]{1,0:T(8,128)(2,1)S(1)}, u32[]{:S(2)}, u32[]{:S(2)}) collective-permute-start(bf16[256,1024]{1,0:T(8,128)(2,1)S(1)} %get-tuple-element.683), channel_id=1, source_target_pairs={{0,2},{2,0},{1,3},{3,1},{4,6},{6,4},{5,7},{7,5},{8,10},{10,8},{9,1... | collective-permute-start | bytes 1572872 | tf_op jit(solution)/shard_map/ppermute | solution.py:31
  391.3 19.3 %collective-permute-start.119 = (bf16[528,768]{1,0:T(8,128)(2,1)S(1)}, bf16[528,768]{1,0:T(8,128)(2,1)S(1)}, u32[]{:S(2)}, u32[]{:S(2)}) collective-permute-start(bf16[528,768]{1,0:T(8,128)(2,1)S(1)} %get-tuple-element.701), channel_id=1, source_target_pairs={{0,8},{8,0},{16,24},{24,16},{1,9},{9,1},{17,25},{25,17},{2,10},{10... | collective-permute-start | bytes 2433032 | tf_op jit(solution)/shard_map/ppermute | solution.py:786
  394.2 17.6 %collective-permute-start.120 = (bf16[512,768]{1,0:T(8,128)(2,1)S(1)}, bf16[512,768]{1,0:T(8,128)(2,1)S(1)}, u32[]{:S(2)}, u32[]{:S(2)}) collective-permute-start(bf16[512,768]{1,0:T(8,128)(2,1)S(1)} %get-tuple-element.702.refs_2_), channel_id=1, source_target_pairs={{8,16},{16,8},{9,17},{17,9},{10,18},{18,10},{11,19},{19,11},{12,20... | collective-permute-start | bytes 2359304 | tf_op jit(solution)/shard_map/ppermute | solution.py:784
  400.4 13.8 %collective-permute-start.118 = (bf16[576,1024]{1,0:T(8,128)(2,1)S(1)}, bf16[576,1024]{1,0:T(8,128)(2,1)S(1)}, u32[]{:S(2)}, u32[]{:S(2)}) collective-permute-start(bf16[576,1024]{1,0:T(8,128)(2,1)S(1)} %constant_dynamic-update-slice_fusion.4.refs_0_), channel_id=1, source_target_pairs={{0,1},{1,0},{2,3},{3,2},{4,5},{5,4},{6,7},{7,6},{8,9},{9,8},{10,11... | collective-permute-start | bytes 3538952 | tf_op jit(solution)/shard_map/ppermute | solution.py:27
  412.3 22.7 %collective-permute-start.121 = (bf16[528,768]{1,0:T(8,128)(2,1)S(1)}, bf16[528,768]{1,0:T(8,128)(2,1)S(1)}, u32[]{:S(2)}, u32[]{:S(2)}) collective-permute-start(bf16[528,768]{1,0:T(8,128)(2,1)S(1)} %get-tuple-element.710.refs_0_), channel_id=1, source_target_pairs={{8,16},{16,8},{9,17},{17,9},{10,18},{18,10},{11,19},{19,11},{12,20... | collective-permute-start | bytes 2433032 | tf_op jit(solution)/shard_map/ppermute | solution.py:784
  413.0 20.6 %collective-permute-start.122 = (bf16[512,768]{1,0:T(8,128)(2,1)S(1)}, bf16[512,768]{1,0:T(8,128)(2,1)S(1)}, u32[]{:S(2)}, u32[]{:S(2)}) collective-permute-start(bf16[512,768]{1,0:T(8,128)(2,1)S(1)} %get-tuple-element.711.refs_0_), channel_id=1, source_target_pairs={{8,0},{16,24},{9,1},{17,25},{10,2},{18,26},{11,3},{19,27},{12,4},{... | collective-permute-start | bytes 2359304 | tf_op jit(solution)/shard_map/ppermute | solution.py:790
  435.2 18.1 %collective-permute-start.123 = (bf16[528,768]{1,0:T(8,128)(2,1)S(1)}, bf16[528,768]{1,0:T(8,128)(2,1)S(1)}, u32[]{:S(2)}, u32[]{:S(2)}) collective-permute-start(bf16[528,768]{1,0:T(8,128)(2,1)S(1)} %get-tuple-element.716.refs_0_), channel_id=1, source_target_pairs={{8,0},{16,24},{9,1},{17,25},{10,2},{18,26},{11,3},{19,27},{12,4},{... | collective-permute-start | bytes 2433032 | tf_op jit(solution)/shard_map/ppermute | solution.py:790
  (208 other events, 909.6 us)
